TPU v7x, 32 devices: a whole 2x2x4 slice. The times are simulated.
32 devices in a mesh: ctx: 16 (over z, x, core), head: 2 (over y).
Axes of the slice: x: 2, y: 2, z: 4, core: 2. Of those that a mesh axis runs over, the one named last changes fastest.
Arguments:
- q_ret: bfloat16 [2048, 1024], P('ctx', 'head'), may hold values from -6 to 6
- k_ret: bfloat16 [2048, 1024], P('ctx', 'head'), may hold values from -6 to 6
- v_ret: bfloat16 [2048, 1024], P('ctx', 'head'), may hold values from -6 to 6
- gate_ret: bfloat16 [2048, 1024], P('ctx', 'head'), may hold values from -6 to 6
- log_decay: float32 [2048, 4], P('ctx', 'head'), may hold values from -2 to 0
- q_cross: bfloat16 [2048, 1024], P('ctx', 'head'), may hold values from -32 to 32
- cache_k: bfloat16 [2048, 512], P(('ctx', 'head')), may hold values from -16 to 16
- cache_v: bfloat16 [2048, 512], P(('ctx', 'head')), may hold values from -6 to 6
Outputs:
- o_ret: bfloat16 [2048, 1024], P('ctx', 'head')
- o_cross: bfloat16 [2048, 1024], P('ctx', 'head')
All inputs are finite; a program needn't handle non-finite values.
Results may differ from a plain program's by a relative error of at most 0.0039.
Values may be sent and summed in bfloat16 or wider, within the bound.
No kernel may reach another device: no remote copies, remote signals or barrier semaphores. Data moves between devices by JAX's collectives and lax.ppermute only.
A program may use at most 128 MiB of HBM per device.

v0:
```python
import math

import jax
import jax.numpy as jnp
from jax import lax
from jax.sharding import PartitionSpec as P

HD = 256


neg_large = -1e30
norm_eps = 1e-06
highest = lax.Precision.HIGHEST


def entering(value, axis, join, neutral):
    count, mine = (lax.axis_size(axis), lax.axis_index(axis))
    pieces = jax.tree.map(lambda part: lax.all_gather(part, axis), value)
    running = jax.tree.map(
        lambda part, zero: jnp.full_like(part, 0) + jnp.asarray(zero, part.dtype), value, neutral
    )

    def lap(position, running):
        longer = join(running, jax.tree.map(lambda part: part[position], pieces))
        return jax.tree.map(lambda new, old: jnp.where(position < mine, new, old), longer, running)

    return lax.fori_loop(0, count - 1, lap, running)


def split_heads(matrix_in):
    return matrix_in.reshape(matrix_in.shape[0], matrix_in.shape[1] // HD, HD).transpose(1, 0, 2)


def join_heads(stacked):
    return stacked.transpose(1, 0, 2).reshape(stacked.shape[1], stacked.shape[0] * stacked.shape[2])


def chain_combine(earlier_part, later_part):
    return (
        earlier_part[0] * later_part[0],
        later_part[0][:, None, None] * earlier_part[1] + later_part[1],
    )


def retention_block(q_ret, k_ret, v_ret, gate_ret, log_decay):
    row_count = q_ret.shape[0]
    queries = split_heads(q_ret)
    key_heads = split_heads(k_ret)
    value_heads = split_heads(v_ret)
    decay_sum = jnp.cumsum(log_decay, axis=0).T
    scores = jnp.einsum("hrd,hsd->hrs", queries, key_heads, preferred_element_type=jnp.float32)
    position = lax.iota(jnp.int32, row_count)
    causal = position[:, None] >= position[None, :]
    spread = jnp.minimum(decay_sum[:, :, None] - decay_sum[:, None, :], 0.0)
    weight_matrix = jnp.where(causal[None], jnp.exp(spread) * scores, 0.0).astype(jnp.bfloat16)
    within_block = jnp.einsum(
        "hrs,hsd->hrd", weight_matrix, value_heads, preferred_element_type=jnp.float32
    )
    final_sum = decay_sum[:, -1]
    carried = (
        key_heads.astype(jnp.float32) * jnp.exp(final_sum[:, None] - decay_sum)[:, :, None]
    ).astype(jnp.bfloat16)
    summary = jnp.einsum("hsd,hse->hde", carried, value_heads, preferred_element_type=jnp.float32)
    total_decay = jnp.exp(final_sum)
    identity = (jnp.ones_like(total_decay), jnp.zeros_like(summary))
    prior_decay, prior_state = entering((total_decay, summary), "ctx", chain_combine, identity)
    from_before = jnp.einsum(
        "hrd,hde->hre", queries.astype(jnp.float32), prior_state, precision=highest
    )
    retained = within_block + jnp.exp(decay_sum)[:, :, None] * from_before
    normed = retained * lax.rsqrt(jnp.mean(retained * retained, axis=2, keepdims=True) + norm_eps)
    gated_out = normed * jax.nn.silu(split_heads(gate_ret).astype(jnp.float32))
    return join_heads(gated_out).astype(jnp.bfloat16)


def pick_block(length):
    size_now = min(length, 1024)
    while length % size_now != 0:
        size_now = size_now - 1
    return size_now


def attend_keys(state_now, key_block, value_block, offset, flat_queries, row_position, score_scale):
    top_score, run_total, running_sum = state_now
    scores = (
        jnp.einsum("rd,kd->rk", flat_queries, key_block, preferred_element_type=jnp.float32)
        * score_scale
    )
    key_position = offset + lax.iota(jnp.int32, key_block.shape[0])
    allowed = row_position[:, None] >= key_position[None, :]
    masked = jnp.where(allowed, scores, neg_large)
    new_top = jnp.maximum(top_score, jnp.max(masked, axis=1))
    weight_matrix = jnp.where(allowed, jnp.exp(masked - new_top[:, None]), 0.0)
    rescale = jnp.exp(top_score - new_top)
    run_total = run_total * rescale + jnp.sum(weight_matrix, axis=1)
    running_sum = running_sum * rescale[:, None] + jnp.dot(
        weight_matrix.astype(jnp.bfloat16), value_block, preferred_element_type=jnp.float32
    )
    return (new_top, run_total, running_sum)


def fold_piece(carries, cache_piece, query_sets, score_scale):
    key_piece, value_piece = cache_piece
    length = key_piece.shape[0]
    size_now = pick_block(length)
    blocks = length // size_now
    key_blocks = key_piece.reshape(blocks, size_now, key_piece.shape[1])
    value_blocks = value_piece.reshape(blocks, size_now, value_piece.shape[1])
    offsets = size_now * lax.iota(jnp.int32, blocks)
    results = []
    for carry_one, query_set in zip(carries, query_sets):
        flat_queries, row_position = query_set
        last_query = jnp.max(row_position)

        def one_block(state_now, inputs):
            key_block, value_block, offset = inputs

            def active(current):
                return attend_keys(
                    current, key_block, value_block, offset, flat_queries, row_position, score_scale
                )

            def passive(current):
                return current

            return (lax.cond(offset <= last_query, active, passive, state_now), None)

        carry_one, unused = lax.scan(one_block, carry_one, (key_blocks, value_blocks, offsets))
        results.append(carry_one)
    return tuple(results)


def make_queries(q_block, first_position):
    head_count = q_block.shape[1] // HD
    flat_queries = split_heads(q_block).reshape(head_count * q_block.shape[0], HD)
    position = first_position + lax.iota(jnp.int32, q_block.shape[0])
    return (flat_queries, jnp.tile(position, head_count))


def start_state(row_total):
    return (
        jnp.full((row_total,), neg_large, jnp.float32),
        jnp.zeros((row_total,), jnp.float32),
        jnp.zeros((row_total, HD), jnp.float32),
    )


def finish(state_now, head_count):
    top_score, run_total, running_sum = state_now
    mixed_out = running_sum / run_total[:, None]
    row_count = mixed_out.shape[0] // head_count
    return join_heads(mixed_out.reshape(head_count, row_count, HD)).astype(jnp.bfloat16)


def per_device(q_ret, k_ret, v_ret, gate_ret, log_decay, q_cross, cache_k, cache_v):
    o_ret = retention_block(q_ret, k_ret, v_ret, gate_ret, log_decay)
    key_rows, value_rows = (
        lax.all_to_all(cache_k, "head", split_axis=1, concat_axis=0, tiled=True),
        lax.all_to_all(cache_v, "head", split_axis=1, concat_axis=0, tiled=True),
    )
    row_count = q_cross.shape[0]
    head_count = q_cross.shape[1] // HD
    score_scale = 1.0 / math.sqrt(HD)
    index_ctx = lax.axis_index("ctx")
    first_row = index_ctx * row_count
    query_sets = (make_queries(q_cross, first_row),)
    initial = tuple(
        (start_state(flat_queries.shape[0]) for flat_queries, row_position in query_sets)
    )
    states = fold_piece(
        initial,
        (
            lax.all_gather(key_rows, "ctx", axis=0, tiled=True),
            lax.all_gather(value_rows, "ctx", axis=0, tiled=True),
        ),
        query_sets,
        score_scale,
    )
    o_cross = finish(states[0], head_count)
    return (o_ret, o_cross)


def solution(mesh):
    placed = (
        P("ctx", "head"),
        P("ctx", "head"),
        P("ctx", "head"),
        P("ctx", "head"),
        P("ctx", "head"),
        P("ctx", "head"),
        P(("ctx", "head"), None),
        P(("ctx", "head"), None),
    )
    return jax.shard_map(
        per_device,
        mesh=mesh,
        in_specs=placed,
        out_specs=(P("ctx", "head"), P("ctx", "head")),
        check_vma=False,
    )
```

profile of v0, /device:TPU:0, one launch (start us, length us, event | category | flops | bytes accessed | tf_op | source)
XLA Modules:
  0.0 196.7 jit_solution(16261993351074165631)
XLA Ops:
  7.2 0.8 copy.185
  8.1 8.2 %all_to_all.38 = bf16[64,2,256]{2,0,1:T(8,128)(2,1)} all-to-all(bf16[64,2,256]{2,0,1:T(8,128)(2,1)S(1)} %bitcast.129), channel_id=1, replica_groups=mesh['ctx'=16,'head'=2] {'head'}, dimensions={1} | all-to-all | bytes 131072 | tf_op jit(solution)/shard_map/all_to_all | solution.py:158
  16.4 0.8 copy.184
  17.2 7.1 %all_to_all.39 = bf16[64,2,256]{2,0,1:T(8,128)(2,1)} all-to-all(bf16[64,2,256]{2,0,1:T(8,128)(2,1)S(1)} %bitcast.130), channel_id=1, replica_groups=mesh['ctx'=16,'head'=2] {'head'}, dimensions={1} | all-to-all | bytes 131072 | tf_op jit(solution)/shard_map/all_to_all | solution.py:159
  24.4 0.8 copy.130
  25.2 0.2 reduce_window_sum.11
  25.5 1.0 copy.152
  26.5 0.2 slice_reduce_fusion
  26.8 2.0 fusion.28
  28.8 1.2 dynamic-slice
  30.7 0.2 dynamic-update-slice
  31.0 31.6 %all-reduce = f32[32]{0:T(128)S(1)} all-reduce(f32[32]{0:T(128)S(1)} %dynamic-update-slice), channel_id=2, replica_groups=mesh['ctx'=16,'head'=2] {'ctx'}, use_global_device_ids=true, to_apply=%add | all-reduce | flops 32 | bytes 256
  62.7 1.0 copy.140
  63.9 0.9 copy.183
  64.8 0.6 broadcast_reduce_fusion
  65.5 28.6 %all-gather.8.cloned.1.call-done = bf16[2048,256]{1,0:T(8,128)(2,1)} async-done(((bf16[128,256]{1,0:T(8,128)(2,1)}), bf16[2048,256]{1,0:T(8,128)(2,1)}) %all-gather.8.cloned.1.call-update) | async-done | bytes 1048592 | tf_op jit(solution)/shard_map/all_gather | solution.py:174
  94.2 7.5 %while.29 = (s32[]{:T(128)}, f32[256]{0:T(256)S(1)}, f32[256]{0:T(256)S(1)}, f32[256,256]{1,0:T(8,128)S(1)}, s32[2]{0:T(128)S(1)}, /*index=5*/s32[]{:T(128)}, bf...) while((s32[]{:T(128)}, f32[256]{0:T(256)S(1)}, ...), condition=%wide.region_10.11_spmd.clone, body=%wide.region_5.10_spmd.clone.sunk | while | flops 271713792 | bytes 4888331 | solution.py:128
  94.2 0.6 dynamic_slice.53
  96.0 3.9 %conditional.3 = ((f32[256]{0:T(256)S(1)}, f32[256]{0:T(256)S(1)}, f32[256,256]{1,0:T(8,128)S(1)})) conditional(s32[]{:T(128)} %convert_element_type.70, (f32[256]{0:T(256)S(1)}, f32[256]{0:T(256)S(1)}, f32[256,256]{1,0:T(8,128)S(1)}) %tuple.77, (s32[128]{0:T(128)S(1)}, s32[]{:T(128)}, bf16[2,1024,256]{2,1,0:T(8,128)(2,1)}, s32[]{:T(128)}, ...), branch_computations={%region_6.6_spmd, %region_7.9_spmd} | conditional | flops 271713792 | bytes 4888100 | solution.py:126
  96.0 0.5 iota_add_fusion
  96.5 1.4 fusion.44
  98.0 0.2 fusion.5
  98.3 1.6 convolution_add_fusion
  99.9 0.6 dynamic_slice.53
  101.9 0.1 copy.147
  102.0 0.7 copy.158
  102.7 67.5 %all-gather.10.cloned.1.call-done = f32[32,256,256]{2,1,0:T(8,128)} async-done(((f32[2,256,256]{2,1,0:T(8,128)}), f32[32,256,256]{2,1,0:T(8,128)}) %all-gather.10.cloned.1.call-update) | async-done | bytes 8388624 | tf_op jit(solution)/shard_map/all_gather | solution.py:18
  170.2 18.1 %while.30 = (s32[]{:T(128)}, f32[2,256,256]{2,1,0:T(8,128)S(1)}, s32[]{:T(128)}, f32[16,2]{1,0:T(8,128)S(1)}, f32[16,2,256,256]{3,2,1,0:T(8,128)}, /*index=5*/s32[]{:T(128)}, s32[]{:T(128)}) while((s32[]{:T(128)}, f32[2,256,256]{2,1,0:T(8,128)S(1)}, s32[]{:T(128)}, f32[16,2]{1,0:T(8,128)S(1)}, f32[16,2,256,256]{3,2,1,0:T(8,128)}, ...), condition=%wide.region_2.3_spmd.clone, body=%wide.region_1.2_spmd.clone.sunk | while | flops 524292 | bytes 1572993 | solution.py:27
  170.2 1.2 fusion.49
  171.4 1.2 fusion.49
  172.6 1.2 fusion.49
  173.8 1.2 fusion.49
  175.0 1.2 fusion.49
  176.2 1.2 fusion.49
  177.5 1.2 fusion.49
  178.7 1.2 fusion.49
  179.9 1.2 fusion.49
  181.1 1.2 fusion.49
  182.3 1.2 fusion.49
  183.5 1.2 fusion.49
  184.7 1.2 fusion.49
  185.9 1.2 fusion.49
  187.1 1.2 fusion.49
  188.3 0.3 fusion.29
  188.7 0.4 fusion.23
  189.1 0.1 fusion.27
  189.3 0.1 copy.143
  189.4 0.8 copy.148
  (47 shorter events, 1.0 us)
Async XLA Ops:
  7.2 58.4 %all-gather.6.cloned.1.call-start = ((), (), s32[]{:S(2)}) async-start(), calls=%async_computation.2 | async-start | bytes 1114112 | tf_op jit(solution)/shard_map/all_gather | solution.py:173
  16.3 77.8 %all-gather.8.cloned.1.call-start = ((), (), s32[]{:S(2)}) async-start(), calls=%async_computation.3 | async-start | bytes 1114112 | tf_op jit(solution)/shard_map/all_gather | solution.py:174
  24.4 145.8 %all-gather.10.cloned.1.call-start = ((), (), s32[]{:S(2)}) async-start(), calls=%async_computation.4 | async-start | bytes 8912896 | tf_op jit(solution)/shard_map/all_gather | solution.py:18
  101.7 86.6 %copy-start = (bf16[128,512]{1,0:T(8,128)(2,1)S(1)}, bf16[128,512]{1,0:T(8,128)(2,1)}, u32[]{:S(2)}) copy-start(bf16[128,512]{1,0:T(8,128)(2,1)} %param.14) | copy-start | bytes 393220
  101.7 87.0 %copy-start.1 = (bf16[128,512]{1,0:T(8,128)(2,1)S(1)}, bf16[128,512]{1,0:T(8,128)(2,1)}, u32[]{:S(2)}) copy-start(bf16[128,512]{1,0:T(8,128)(2,1)} %param.16) | copy-start | bytes 393220
Sparse Core Ops, SparseCore 0:
  16.4 38.5 all-gather.5
  57.2 36.8 all-gather.7
  96.3 73.8 all-gather.9
where the time goes:
time: 198 us; the launch traced here: 197 us
  waiting for transfers between devices  96.2 us (49%)
  blocking collectives  47 us (24%)
  other arithmetic  19.5 us (10%)
  between operations  14.6 us (7%)
  local copies, waits for them, and re-layouts  10.5 us (5%)
  matrix products  5.78 us (3%)
  loops' own time  2.96 us (1%)
    all_gather x1, waiting for transfers between devices, entering(): pieces = jax.tree.map(lambda part: lax.all_gather(part, axis), value)  67.5 us
    unnamed x1, blocking collectives  31.6 us
    all_gather x1, waiting for transfers between devices, per_device(): lax.all_gather(value_rows, 'ctx', axis=0, tiled=True)  28.6 us
    select_n x15, other arithmetic, lap(): jnp.where(position < mine, new, old)  17.6 us
    all_to_all x1, blocking collectives, per_device(): lax.all_to_all(cache_k, 'head', split_axis=1, concat_axis=0, tiled=True)  8.25 us
    all_to_all x1, blocking collectives, per_device(): lax.all_to_all(cache_v, 'head', split_axis=1, concat_axis=0, tiled=True)  7.14 us
    unnamed x11, local copies, waits for them, and re-layouts  4.78 us
  transfers between devices with their start and end apart: 3, of which 2 were waited for; matrix products, arithmetic and copies ran while one was open for 8% of the time, Pallas kernels for 0%

commit v1 on v0

v1 whole, which is shorter than its diff:
```python
import functools
import math

import jax
import jax.numpy as jnp
from jax import lax
from jax.experimental import pallas as pl
from jax.experimental.pallas import tpu as pltpu
from jax.sharding import PartitionSpec as P

HD = 256
FAR = -1e30
NEAR = -1e29
EPS = 1e-06
F32 = jnp.float32
BF16 = jnp.bfloat16
PAD = 16
LANES = 128
VMEM = pl.BlockSpec(memory_space=pltpu.VMEM)


def call(body, outs, args, scratch=(), flops=1_000_000, name=None):
    moved = sum(math.prod(a.shape) * a.dtype.itemsize for a in (*args, *outs))
    single = len(outs) == 1
    return pl.pallas_call(
        body,
        out_shape=outs[0] if single else tuple(outs),
        in_specs=[VMEM] * len(args),
        out_specs=VMEM if single else tuple(VMEM for _ in outs),
        scratch_shapes=scratch,
        compiler_params=pltpu.CompilerParams(vmem_limit_bytes=40 * 1024 * 1024),
        cost_estimate=pl.CostEstimate(flops=flops, bytes_accessed=moved, transcendentals=0),
        name=name,
    )(*args)


def shape(dims, dtype=BF16):
    return jax.ShapeDtypeStruct(dims, dtype)


def dot(a, b, contract, precision=None):
    return lax.dot_general(
        a, b, (contract, ((), ())), preferred_element_type=F32, precision=precision
    )


def thirds(value):
    high = value.astype(BF16).astype(F32)
    rest = value - high
    middle = rest.astype(BF16).astype(F32)
    return high, middle, rest - middle


def decay_sums(log_decay):
    rows = log_decay.shape[0]
    below = lax.broadcasted_iota(jnp.int32, (rows, rows), 0) >= lax.broadcasted_iota(
        jnp.int32, (rows, rows), 1
    )
    lower = jnp.where(below, 1.0, 0.0).astype(F32)
    return dot(lower, log_decay, ((1,), (0,)), lax.Precision.HIGHEST), below


def split_cache(n, k_ref, v_ref, *pieces):
    width = pieces[0].shape[2]
    here = lax.axis_index("head")
    for e, piece in enumerate(pieces):
        target = lax.rem(here + e, n)
        columns = pl.ds(pl.multiple_of(target * width, LANES), width)
        piece[0] = k_ref[:, columns]
        piece[1] = v_ref[:, columns]


def write_total(out, head, at, total):
    row = lax.broadcasted_iota(jnp.int32, (PAD, HD), 0)
    high, middle, low = thirds(total)
    tile = jnp.where(row == 0, high, jnp.where(row == 1, middle, jnp.where(row == 2, low, 0.0)))
    out[head, pl.ds(at, PAD), :] = tile.astype(BF16)


def read_total(ref, head, at):
    tile = ref[head, pl.ds(at, PAD), :].astype(F32)
    return tile[0:1, :] + tile[1:2, :] + tile[2:3, :]


def summarize(plane, k_ref, v_ref, d_ref, *rest):
    outs, (held,) = rest[:-1], rest[-1:]
    heads = d_ref.shape[1]
    part = HD // plane
    mine = lax.rem(lax.axis_index("ctx"), plane)
    sums, _ = decay_sums(d_ref[...])
    rows = sums.shape[0]
    for head in range(heads):
        columns = pl.ds(head * HD, HD)
        column = sums[:, head : head + 1]
        last = column[rows - 1 : rows, :]
        carried = (k_ref[:, columns].astype(F32) * jnp.exp(last - column)).astype(BF16)
        held[head] = dot(carried, v_ref[:, columns], ((0,), (0,)))
        total = jnp.broadcast_to(last, (1, HD))
        for s, out in enumerate(outs):
            slot = jnp.bitwise_xor(mine, s)
            piece = held[head, pl.ds(pl.multiple_of(slot * part, part), part), :]
            out[head, pl.ds(0, part), :] = piece.astype(BF16)
            write_total(out, head, part, total)


def plane_total(plane, *refs):
    ins, out = refs[:plane], refs[plane]
    heads, part = out.shape[0], out.shape[1] - PAD
    mine = lax.rem(lax.axis_index("ctx"), plane)
    place = [jnp.bitwise_xor(mine, s) for s in range(plane)]
    for head in range(heads):
        totals = [read_total(ref, head, part) for ref in ins]
        sum_now = jnp.zeros((part, HD), F32)
        for s in range(plane):
            later = jnp.zeros((1, HD), F32)
            for t in range(plane):
                later = later + jnp.where(place[t] > place[s], totals[t], 0.0)
            sum_now = sum_now + jnp.exp(later) * ins[s][head, pl.ds(0, part), :].astype(F32)
        out[head, pl.ds(0, part), :] = sum_now.astype(BF16)
        write_total(out, head, part, functools.reduce(jnp.add, totals))


def priors(plane, far, *refs):
    ins, planes, outs = refs[:plane], refs[plane : plane + far], refs[plane + far :]
    heads, part = outs[0].shape[0], outs[0].shape[1]
    mine = lax.rem(lax.axis_index("ctx"), plane)
    place = [jnp.bitwise_xor(mine, s) for s in range(plane)]
    for head in range(heads):
        totals = [read_total(ref, head, part) for ref in ins]
        entering = jnp.zeros((part, HD), F32)
        between = jnp.zeros((1, HD), F32)
        for ref in planes:
            entering = entering + jnp.exp(between) * ref[head, pl.ds(0, part), :].astype(F32)
            between = between + read_total(ref, head, part)
        blocks = [ref[head, pl.ds(0, part), :].astype(F32) for ref in ins]
        for r, out in enumerate(outs):
            before = jnp.zeros((1, HD), F32)
            for t in range(plane):
                before = before + jnp.where(place[t] < place[r], totals[t], 0.0)
            state = jnp.exp(before) * entering
            for s in range(plane):
                if s == r:
                    continue
                gap = jnp.zeros((1, HD), F32)
                for t in range(plane):
                    inside = jnp.logical_and(place[t] > place[s], place[t] < place[r])
                    gap = gap + jnp.where(inside, totals[t], 0.0)
                state = state + jnp.where(place[s] < place[r], jnp.exp(gap), 0.0) * blocks[s]
            out[head] = state.astype(BF16)


def retain_inside(q_ref, k_ref, v_ref, d_ref, inside_ref, factor_ref):
    heads = d_ref.shape[1]
    sums, below = decay_sums(d_ref[...])
    rows = sums.shape[0]
    same = lax.broadcasted_iota(jnp.int32, (rows, rows), 0) == lax.broadcasted_iota(
        jnp.int32, (rows, rows), 1
    )
    factor_ref[...] = jnp.exp(sums)
    for head in range(heads):
        columns = pl.ds(head * HD, HD)
        column = jnp.broadcast_to(sums[:, head : head + 1], (rows, rows))
        across = jnp.sum(jnp.where(same, column, 0.0), axis=0, keepdims=True)
        spread = jnp.exp(jnp.minimum(column - across, 0.0))
        scores = dot(q_ref[:, columns], k_ref[:, columns], ((1,), (1,)))
        weights = jnp.where(below, spread * scores, 0.0).astype(BF16)
        inside_ref[:, columns] = dot(weights, v_ref[:, columns], ((1,), (0,)))


def retain_finish(plane, q_ref, gate_ref, inside_ref, factor_ref, *refs):
    states, out, held = refs[:plane], refs[plane], refs[plane + 1]
    heads = factor_ref.shape[1]
    part = HD // plane
    mine = lax.rem(lax.axis_index("ctx"), plane)
    for head in range(heads):
        columns = pl.ds(head * HD, HD)
        for s, ref in enumerate(states):
            slot = jnp.bitwise_xor(mine, s)
            held[head, pl.ds(pl.multiple_of(slot * part, part), part), :] = ref[head]
        before = dot(q_ref[:, columns], held[head], ((1,), (0,)))
        retained = inside_ref[:, columns] + factor_ref[:, head : head + 1] * before
        scale = lax.rsqrt(jnp.mean(retained * retained, axis=1, keepdims=True) + EPS)
        gate = gate_ref[:, columns].astype(F32)
        silu = gate / (1.0 + jnp.exp(-gate))
        out[:, columns] = (retained * scale * silu).astype(BF16)


def attend(plane, far, n, *refs):
    queries = refs[:plane]
    pieces = refs[plane : plane + far * n]
    outs = refs[plane + far * n : 2 * plane + far * n]
    keys, values = refs[2 * plane + far * n :]
    rows = queries[0].shape[0]
    heads = queries[0].shape[1] // HD
    length, width = pieces[0].shape[1:]
    group = heads * HD // width
    total = far * n * length
    index = lax.axis_index("ctx")
    mine, depth = lax.rem(index, plane), lax.div(index, plane)
    here = lax.axis_index("head")
    for i, piece in enumerate(pieces):
        keys[pl.ds(i * length, length), :] = piece[0]
        values[pl.ds(i * length, length), :] = piece[1]
    column = lax.broadcasted_iota(jnp.int32, (1, total), 1)
    limit = jnp.zeros((1, total), jnp.int32)
    for i in range(far * n):
        s, e = divmod(i, n)
        inside = jnp.logical_and(column >= i * length, column < (i + 1) * length)
        if s == 0:
            first = mine * rows + lax.rem(here + n - e, n) * length - i * length
            at = column + first
        else:
            at = jnp.where(depth >= s, -1, plane * rows)
        limit = jnp.where(inside, at, limit)
    scale = 1.0 / (math.sqrt(HD) * math.log(2.0))
    row = lax.broadcasted_iota(jnp.int32, (rows, total), 0)
    lane = lax.broadcasted_iota(jnp.int32, (rows, LANES), 1)
    for r in range(plane):
        position = row + jnp.bitwise_xor(mine, r) * rows
        allowed = position >= limit
        stats = jnp.zeros((rows, LANES), F32)
        for head in range(heads):
            columns = pl.ds(head * HD, HD)
            shared = pl.ds((head // group) * HD, HD)
            scores = dot(queries[r][:, columns], keys[:, shared], ((1,), (1,))) * scale
            masked = jnp.where(allowed, scores, FAR)
            top = jnp.maximum(jnp.max(masked, axis=1, keepdims=True), NEAR)
            weights = jnp.exp2(masked - top)
            summed = jnp.sum(weights, axis=1, keepdims=True)
            mixed = dot(weights.astype(BF16), values[:, shared], ((1,), (0,)))
            some = summed > 0.0
            safe = jnp.where(some, summed, 1.0)
            outs[r][:, columns] = (mixed / safe).astype(BF16)
            level = jnp.where(some, top + jnp.log2(safe), FAR)
            for i, third in enumerate(thirds(level)):
                stats = jnp.where(lane == 3 * head + i, third, stats)
        outs[r][:, pl.ds(heads * HD, LANES)] = stats.astype(BF16)


def merge(plane, *refs):
    ins, out = refs[:plane], refs[plane]
    heads = out.shape[1] // HD
    stats = [ref[:, pl.ds(heads * HD, LANES)].astype(F32) for ref in ins]
    for head in range(heads):
        columns = pl.ds(head * HD, HD)
        levels = [
            tile[:, 3 * head : 3 * head + 1]
            + tile[:, 3 * head + 1 : 3 * head + 2]
            + tile[:, 3 * head + 2 : 3 * head + 3]
            for tile in stats
        ]
        top = functools.reduce(jnp.maximum, levels)
        weights = [jnp.exp2(level - top) for level in levels]
        summed = functools.reduce(jnp.add, weights)
        mixed = functools.reduce(
            jnp.add, [w * ref[:, columns].astype(F32) for w, ref in zip(weights, ins)]
        )
        out[:, columns] = (mixed / summed).astype(BF16)


def per_device(count, n, q_ret, k_ret, v_ret, gate_ret, log_decay, q_cross, cache_k, cache_v):
    plane = math.gcd(count, 4)
    far = count // plane
    rows, wide = q_cross.shape
    heads = wide // HD
    length, width = cache_k.shape[0], cache_k.shape[1] // n
    part = HD // plane

    def in_plane(value, s):
        return lax.ppermute(value, "ctx", [(b, b ^ s) for b in range(count)])

    def onward(value, s):
        return lax.ppermute(value, "ctx", [(b, b + s * plane) for b in range(count - s * plane)])

    def to_head(value, s, e):
        table = [
            (b * n + y, (b + s * plane) * n + (y + e) % n)
            for b in range(count - s * plane)
            for y in range(n)
        ]
        return lax.ppermute(value, ("ctx", "head"), table)

    pieces = call(
        functools.partial(split_cache, n),
        [shape((2, length, width))] * n,
        (cache_k, cache_v),
        name="split_cache",
    )
    if n == 1:
        pieces = (pieces,)
    arrived = []
    for s in range(far):
        for e in range(n):
            arrived.append(pieces[e] if s == 0 and e == 0 else to_head(pieces[e], s, e))
    queries = [q_cross] + [in_plane(q_cross, s) for s in range(1, plane)]

    message = shape((heads, part + PAD, HD))
    sent = call(
        functools.partial(summarize, plane),
        [message] * plane,
        (k_ret, v_ret, log_decay),
        scratch=[pltpu.VMEM((heads, HD, HD), F32)],
        flops=2 * rows * HD * HD * heads,
        name="summarize",
    )
    slices = [sent[0]] + [in_plane(sent[s], s) for s in range(1, plane)]

    inside, factor = call(
        retain_inside,
        [shape((rows, wide), F32), shape((rows, heads), F32)],
        (q_ret, k_ret, v_ret, log_decay),
        flops=4 * rows * rows * HD * heads,
        name="retain_inside",
    )
    whole = call(functools.partial(plane_total, plane), [message], slices, name="plane_total")
    planes = [onward(whole, s) for s in range(1, far)]
    given = call(
        functools.partial(priors, plane, len(planes)),
        [shape((heads, part, HD))] * plane,
        (*slices, *planes),
        name="priors",
    )
    states = [given[0]] + [in_plane(given[s], s) for s in range(1, plane)]

    partial_outs = call(
        functools.partial(attend, plane, far, n),
        [shape((rows, wide + LANES))] * plane,
        (*queries, *arrived),
        scratch=[pltpu.VMEM((far * n * length, width), BF16) for _ in range(2)],
        flops=4 * rows * plane * heads * far * n * length * HD,
        name="attend",
    )
    returned = [partial_outs[0]] + [in_plane(partial_outs[s], s) for s in range(1, plane)]

    o_ret = call(
        functools.partial(retain_finish, plane),
        [shape((rows, wide))],
        (q_ret, gate_ret, inside, factor, *states),
        scratch=[pltpu.VMEM((heads, HD, HD), BF16)],
        flops=2 * rows * HD * HD * heads,
        name="retain_finish",
    )
    o_cross = call(functools.partial(merge, plane), [shape((rows, wide))], returned, name="merge")
    return o_ret, o_cross


def solution(mesh):
    split = P("ctx", "head")
    rows = P(("ctx", "head"), None)
    return jax.shard_map(
        functools.partial(per_device, mesh.shape["ctx"], mesh.shape["head"]),
        mesh=mesh,
        in_specs=(split,) * 6 + (rows,) * 2,
        out_specs=(split, split),
        check_vma=False,
    )
```

time: 198 us -> 60.8 us (0.31)
  waiting for transfers between devices: 96.2 us -> 10.2 us
  blocking collectives: 47 us -> 0 us
  starting transfers between devices: 0.12 us -> 40 us
  other arithmetic: 19.5 us -> 0 us
  between operations: 14.6 us -> 0.86 us
  local copies, waits for them, and re-layouts: 10.5 us -> 2.74 us
  Pallas kernels: 0 us -> 6.58 us
  matrix products: 5.78 us -> 0 us
  loops' own time: 2.96 us -> 0 us
    all_gather x3 -> x0, waiting for transfers between devices: 96.2 us -> none  [the longest x1 67.5 us: entering(): pieces = jax.tree.map(lambda part: lax.all_gather(part, axis), value)]
    ppermute x0 -> x22, starting transfers between devices: none -> 40 us  [the longest x7 23.1 us: to_head(): return lax.ppermute(value, ('ctx', 'head'), table)]
    unnamed x1 -> x0, blocking collectives: 31.6 us -> none
    select_n x15 -> x0, other arithmetic: 17.6 us -> none  [lap(): jnp.where(position < mine, new, old)]
    all_to_all x2 -> x0, blocking collectives: 15.4 us -> none  [the longest x1 8.25 us: per_device(): lax.all_to_all(cache_k, 'head', split_axis=1, concat_axis=0, tiled=True)]
    ppermute x0 -> x22, waiting for transfers between devices: none -> 10.2 us  [the longest x12 9.37 us: in_plane(): return lax.ppermute(value, 'ctx', [(b, b ^ s) for b in range(count)])]
    pallas_call x0 -> x8, Pallas kernels: none -> 6.58 us  [call(): pl.pallas_call(body, out_shape=outs[0] if single else tuple(outs), in_spe...]
    dot_general x5 -> x0, matrix products: 5.78 us -> none  [the longest x1 1.96 us: retention_block(): jnp.einsum('hsd,hse->hde', carried, value_heads, preferred_element_type=j...]
  transfers between devices with their start and end apart: 3 -> 22, of which waited for: 2 -> 6; matrix products, arithmetic and copies ran while one was open for 8% -> 0% of each run, Pallas kernels for 0% -> 9%
where the time goes in v1:
time: 60.8 us; the launch traced here: 60.4 us
  starting transfers between devices  40 us (66%)
  waiting for transfers between devices  10.2 us (17%)
  Pallas kernels  6.58 us (11%)
  local copies, waits for them, and re-layouts  2.74 us (5%)
  between operations  0.86 us (1%)
    ppermute x7, starting transfers between devices, to_head(): return lax.ppermute(value, ('ctx', 'head'), table)  23.1 us
    ppermute x3, starting transfers between devices, onward(): lax.ppermute(value, 'ctx', [(b, b + s * plane) for b in range(count - s *...  9.87 us
    ppermute x12, waiting for transfers between devices, in_plane(): return lax.ppermute(value, 'ctx', [(b, b ^ s) for b in range(count)])  9.37 us
    ppermute x12, starting transfers between devices, in_plane(): return lax.ppermute(value, 'ctx', [(b, b ^ s) for b in range(count)])  7.02 us
    pallas_call x8, Pallas kernels, call(): pl.pallas_call(body, out_shape=outs[0] if single else tuple(outs), in_spe...  6.58 us
    unnamed x19, local copies, waits for them, and re-layouts  2.74 us
  transfers between devices with their start and end apart: 22, of which 6 were waited for; matrix products, arithmetic and copies ran while one was open for 0% of the time, Pallas kernels for 9%

profile of v1, /device:TPU:0, one launch (start us, length us, event | category | flops | bytes accessed | tf_op | source)
XLA Modules:
  0.0 60.4 jit_solution(12799856473970612186)
XLA Ops:
  0.7 0.9 %copy-done.5 = bf16[64,512]{1,0:T(8,128)(2,1)S(1)} copy-done((bf16[64,512]{1,0:T(8,128)(2,1)S(1)}, bf16[64,512]{1,0:T(8,128)(2,1)}, u32[]{:S(2)}) %copy-start.5) | copy-done | bytes 65560
  1.5 0.8 %copy-done.6 = bf16[64,512]{1,0:T(8,128)(2,1)S(1)} copy-done((bf16[64,512]{1,0:T(8,128)(2,1)S(1)}, bf16[64,512]{1,0:T(8,128)(2,1)}, u32[]{:S(2)}) %copy-start.6) | copy-done | bytes 65560
  2.4 0.0 copy-start.8
  2.4 3.0 %collective-permute-start.12 = (bf16[2,64,256]{2,1,0:T(8,128)(2,1)S(1)}, bf16[2,64,256]{2,1,0:T(8,128)(2,1)S(1)}, u32[]{:S(2)}, u32[]{:S(2)}) collective-permute-start(bf16[2,64,256]{2,1,0:T(8,128)(2,1)S(1)} %get-tuple-element.29), channel_id=1, source_target_pairs={{0,1},{1,0},{2,3},{3,2},{4,5},{5,4},{6,7},{7,6},{8,9},{9,8},{10,11... | collective-permute-start | bytes 196616 | tf_op jit(solution)/shard_map/ppermute | solution.py:281
  5.4 3.5 %collective-permute-start.13 = (bf16[2,64,256]{2,1,0:T(8,128)(2,1)S(1)}, bf16[2,64,256]{2,1,0:T(8,128)(2,1)S(1)}, u32[]{:S(2)}, u32[]{:S(2)}) collective-permute-start(bf16[2,64,256]{2,1,0:T(8,128)(2,1)S(1)} %get-tuple-element.28.refs_4_), channel_id=1, source_target_pairs={{0,8},{1,9},{2,10},{3,11},{4,12},{5,13},{6,14},{7,15},{8,16},{9,17... | collective-permute-start | bytes 196616 | tf_op jit(solution)/shard_map/ppermute | solution.py:281
  8.9 3.4 %collective-permute-start.14 = (bf16[2,64,256]{2,1,0:T(8,128)(2,1)S(1)}, bf16[2,64,256]{2,1,0:T(8,128)(2,1)S(1)}, u32[]{:S(2)}, u32[]{:S(2)}) collective-permute-start(bf16[2,64,256]{2,1,0:T(8,128)(2,1)S(1)} %get-tuple-element.29), channel_id=1, source_target_pairs={{0,9},{1,8},{2,11},{3,10},{4,13},{5,12},{6,15},{7,14},{8,17},{9,16... | collective-permute-start | bytes 196616 | tf_op jit(solution)/shard_map/ppermute | solution.py:281
  12.3 0.1 copy.10.d_ref
  12.5 0.0 copy-start.2
  12.5 0.9 %copy-done.2 = bf16[128,512]{1,0:T(8,128)(2,1)S(1)} copy-done((bf16[128,512]{1,0:T(8,128)(2,1)S(1)}, bf16[128,512]{1,0:T(8,128)(2,1)}, u32[]{:S(2)}) %copy-start.2) | copy-done | bytes 131096
  13.4 0.7 %summarize.1 = (bf16[2,80,256]{2,1,0:T(8,128)(2,1)S(1)}, bf16[2,80,256]{2,1,0:T(8,128)(2,1)S(1)}, bf16[2,80,256]{2,1,0:T(8,128)(2,1)S(1)}, bf16[2,80,256]{2,1,0:T(8,128)(2,1)S(1)}) custom-call(bf16[128,512]{1,0:T(8,128)(2,1)S(1)} %copy-done.1, bf16[128,512]{1,0:T(8,128)(2,1)S(1)} %copy-done.2, f32[128,2]{1,0:T(8,128)S(1)} %copy.10.d_ref), custom_call_target="tpu_custom_call" | custom-call | flops 33554432 | bytes 590848 | tf_op jit(solution)/shard_map/summarize/pallas_call | solution.py:25
  14.0 0.1 collective-permute-start
  14.1 3.0 %collective-permute-start.15 = (bf16[2,64,256]{2,1,0:T(8,128)(2,1)S(1)}, bf16[2,64,256]{2,1,0:T(8,128)(2,1)S(1)}, u32[]{:S(2)}, u32[]{:S(2)}) collective-permute-start(bf16[2,64,256]{2,1,0:T(8,128)(2,1)S(1)} %get-tuple-element.28.refs_4_), channel_id=1, source_target_pairs={{0,16},{1,17},{2,18},{3,19},{4,20},{5,21},{6,22},{7,23},{8,24},{9,... | collective-permute-start | bytes 196616 | tf_op jit(solution)/shard_map/ppermute | solution.py:281
  17.1 1.6 %collective-permute-start.16 = (bf16[2,64,256]{2,1,0:T(8,128)(2,1)S(1)}, bf16[2,64,256]{2,1,0:T(8,128)(2,1)S(1)}, u32[]{:S(2)}, u32[]{:S(2)}) collective-permute-start(bf16[2,64,256]{2,1,0:T(8,128)(2,1)S(1)} %get-tuple-element.29), channel_id=1, source_target_pairs={{0,17},{1,16},{2,19},{3,18},{4,21},{5,20},{6,23},{7,22},{8,25},{9,... | collective-permute-start | bytes 196616 | tf_op jit(solution)/shard_map/ppermute | solution.py:281
  18.7 0.0 collective-permute-done.13.refs_6_
  18.7 1.6 %collective-permute-start.1 = (bf16[2,80,256]{2,1,0:T(8,128)(2,1)S(1)}, bf16[2,80,256]{2,1,0:T(8,128)(2,1)S(1)}, u32[]{:S(2)}, u32[]{:S(2)}) collective-permute-start(bf16[2,80,256]{2,1,0:T(8,128)(2,1)S(1)} %get-tuple-element.22), channel_id=1, source_target_pairs={{0,4},{2,6},{4,0},{6,2},{8,12},{10,14},{12,8},{14,10},{16,20},{18,... | collective-permute-start | bytes 245768 | tf_op jit(solution)/shard_map/ppermute | solution.py:270
  20.3 0.1 collective-permute-start.2
  20.3 1.5 %collective-permute-start.10 = (bf16[128,512]{1,0:T(8,128)(2,1)S(1)}, bf16[128,512]{1,0:T(8,128)(2,1)S(1)}, u32[]{:S(2)}, u32[]{:S(2)}) collective-permute-start(bf16[128,512]{1,0:T(8,128)(2,1)S(1)} %copy-done.7), channel_id=1, source_target_pairs={{0,4},{2,6},{4,0},{6,2},{8,12},{10,14},{12,8},{14,10},{16,20},{18,... | collective-permute-start | bytes 393224 | tf_op jit(solution)/shard_map/ppermute | solution.py:270
  21.8 0.4 collective-permute-start.11
  22.3 0.2 collective-permute-start.9
  22.5 0.9 %collective-permute-done.1.refs_2_ = bf16[2,80,256]{2,1,0:T(8,128)(2,1)S(1)} collective-permute-done((bf16[2,80,256]{2,1,0:T(8,128)(2,1)S(1)}, bf16[2,80,256]{2,1,0:T(8,128)(2,1)S(1)}, u32[]{:S(2)}, u32[]{:S(2)}) %collective-permute-start.1) | collective-permute-done | bytes 81952 | tf_op jit(solution)/shard_map/ppermute | solution.py:270
  23.4 7.3 %collective-permute-start.17 = (bf16[2,64,256]{2,1,0:T(8,128)(2,1)S(1)}, bf16[2,64,256]{2,1,0:T(8,128)(2,1)S(1)}, u32[]{:S(2)}, u32[]{:S(2)}) collective-permute-start(bf16[2,64,256]{2,1,0:T(8,128)(2,1)S(1)} %get-tuple-element.28.refs_4_), channel_id=1, source_target_pairs={{0,24},{1,25},{2,26},{3,27},{4,28},{5,29},{6,30},{7,31}} | collective-permute-start | bytes 196616 | tf_op jit(solution)/shard_map/ppermute | solution.py:281
  30.8 1.3 %collective-permute-start.18 = (bf16[2,64,256]{2,1,0:T(8,128)(2,1)S(1)}, bf16[2,64,256]{2,1,0:T(8,128)(2,1)S(1)}, u32[]{:S(2)}, u32[]{:S(2)}) collective-permute-start(bf16[2,64,256]{2,1,0:T(8,128)(2,1)S(1)} %get-tuple-element.29), channel_id=1, source_target_pairs={{0,25},{1,24},{2,27},{3,26},{4,29},{5,28},{6,31},{7,30}} | collective-permute-start | bytes 196616 | tf_op jit(solution)/shard_map/ppermute | solution.py:281
  32.1 0.1 plane_total.1
  32.2 0.8 %collective-permute-done.17.refs_10_ = bf16[2,64,256]{2,1,0:T(8,128)(2,1)S(1)} collective-permute-done((bf16[2,64,256]{2,1,0:T(8,128)(2,1)S(1)}, bf16[2,64,256]{2,1,0:T(8,128)(2,1)S(1)}, u32[]{:S(2)}, u32[]{:S(2)}) %collective-permute-start.17) | collective-permute-done | bytes 65568 | tf_op jit(solution)/shard_map/ppermute | solution.py:281
  32.9 1.3 %collective-permute-start.3 = (bf16[2,80,256]{2,1,0:T(8,128)(2,1)S(1)}, bf16[2,80,256]{2,1,0:T(8,128)(2,1)S(1)}, u32[]{:S(2)}, u32[]{:S(2)}) collective-permute-start(bf16[2,80,256]{2,1,0:T(8,128)(2,1)S(1)} %plane_total.1), channel_id=1, source_target_pairs={{0,8},{2,10},{4,12},{6,14},{8,16},{10,18},{12,20},{14,22},{16,24},... | collective-permute-start | bytes 245768 | tf_op jit(solution)/shard_map/ppermute | solution.py:273
  34.2 0.1 collective-permute-done.18.refs_11_
  34.3 7.3 %collective-permute-start.4 = (bf16[2,80,256]{2,1,0:T(8,128)(2,1)S(1)}, bf16[2,80,256]{2,1,0:T(8,128)(2,1)S(1)}, u32[]{:S(2)}, u32[]{:S(2)}) collective-permute-start(bf16[2,80,256]{2,1,0:T(8,128)(2,1)S(1)} %plane_total.1), channel_id=1, source_target_pairs={{0,16},{2,18},{4,20},{6,22},{8,24},{10,26},{12,28},{14,30},{1,17},... | collective-permute-start | bytes 245768 | tf_op jit(solution)/shard_map/ppermute | solution.py:273
  41.6 1.3 %collective-permute-start.5 = (bf16[2,80,256]{2,1,0:T(8,128)(2,1)S(1)}, bf16[2,80,256]{2,1,0:T(8,128)(2,1)S(1)}, u32[]{:S(2)}, u32[]{:S(2)}) collective-permute-start(bf16[2,80,256]{2,1,0:T(8,128)(2,1)S(1)} %plane_total.1), channel_id=1, source_target_pairs={{0,24},{2,26},{4,28},{6,30},{1,25},{3,27},{5,29},{7,31}} | collective-permute-start | bytes 245768 | tf_op jit(solution)/shard_map/ppermute | solution.py:273
  42.9 0.0 collective-permute-done.11.refs_3_
  42.9 0.0 collective-permute-done.9.refs_1_
  43.0 2.9 %attend.1 = (bf16[128,640]{1,0:T(8,128)(2,1)S(1)}, bf16[128,640]{1,0:T(8,128)(2,1)S(1)}, bf16[128,640]{1,0:T(8,128)(2,1)S(1)}, bf16[128,640]{1,0:T(8,128)(2,1)S(1)}) custom-call(bf16[128,512]{1,0:T(8,128)(2,1)S(1)} %copy-done.7, bf16[128,512]{1,0:T(8,128)(2,1)S(1)} %collective-permute-done.9.refs_1_, bf16[128,512]{1,0:T(8,128)(2,1)S(1)} %collective-permute-done.10.refs_2_, ...), custom_call_target="tpu_custom_call" | custom-call | flops 536870912 | bytes 1703936 | tf_op jit(solution)/shard_map/attend/pallas_call | solution.py:25
  45.8 0.1 collective-permute-start.19
  45.9 0.3 collective-permute-start.20
  46.2 1.6 %collective-permute-start.21 = (bf16[128,640]{1,0:T(8,128)(2,1)S(1)}, bf16[128,640]{1,0:T(8,128)(2,1)S(1)}, u32[]{:S(2)}, u32[]{:S(2)}) collective-permute-start(bf16[128,640]{1,0:T(8,128)(2,1)S(1)} %get-tuple-element.33), channel_id=1, source_target_pairs={{0,6},{2,4},{4,2},{6,0},{8,14},{10,12},{12,10},{14,8},{16,22},{18,... | collective-permute-start | bytes 491528 | tf_op jit(solution)/shard_map/ppermute | solution.py:270
  47.8 0.0 collective-permute-done.4.refs_5_
  47.8 0.0 collective-permute-done.5.refs_6_
  47.8 0.3 priors.1
  48.1 0.4 collective-permute-start.6
  48.5 0.2 collective-permute-start.7
  48.7 0.7 %collective-permute-done.6.refs_1_ = bf16[2,64,256]{2,1,0:T(8,128)(2,1)S(1)} collective-permute-done((bf16[2,64,256]{2,1,0:T(8,128)(2,1)S(1)}, bf16[2,64,256]{2,1,0:T(8,128)(2,1)S(1)}, u32[]{:S(2)}, u32[]{:S(2)}) %collective-permute-start.6) | collective-permute-done | bytes 65568 | tf_op jit(solution)/shard_map/ppermute | solution.py:270
  49.4 0.6 %collective-permute-start.8 = (bf16[2,64,256]{2,1,0:T(8,128)(2,1)S(1)}, bf16[2,64,256]{2,1,0:T(8,128)(2,1)S(1)}, u32[]{:S(2)}, u32[]{:S(2)}) collective-permute-start(bf16[2,64,256]{2,1,0:T(8,128)(2,1)S(1)} %get-tuple-element.27), channel_id=1, source_target_pairs={{0,6},{2,4},{4,2},{6,0},{8,14},{10,12},{12,10},{14,8},{16,22},{18,... | collective-permute-start | bytes 196616 | tf_op jit(solution)/shard_map/ppermute | solution.py:270
  50.0 0.6 %retain_inside.1 = (f32[128,512]{1,0:T(8,128)S(1)}, f32[128,2]{1,0:T(8,128)S(1)}) custom-call(bf16[128,512]{1,0:T(8,128)(2,1)S(1)} %copy-done, bf16[128,512]{1,0:T(8,128)(2,1)S(1)} %copy-done.1, bf16[128,512]{1,0:T(8,128)(2,1)S(1)} %copy-done.3, f32[128,2]{1,0:T(8,128)S(1)} %copy.10.d_ref), custom_call_target="tpu_custom_call" | custom-call | flops 33554432 | bytes 657408 | tf_op jit(solution)/shard_map/retain_inside/pallas_call | solution.py:25
  50.6 7.3 %collective-permute-done.7.refs_2_ = bf16[2,64,256]{2,1,0:T(8,128)(2,1)S(1)} collective-permute-done((bf16[2,64,256]{2,1,0:T(8,128)(2,1)S(1)}, bf16[2,64,256]{2,1,0:T(8,128)(2,1)S(1)}, u32[]{:S(2)}, u32[]{:S(2)}) %collective-permute-start.7) | collective-permute-done | bytes 65568 | tf_op jit(solution)/shard_map/ppermute | solution.py:270
  57.9 0.5 collective-permute-done.8.refs_3_
  58.4 1.0 %retain_finish.1 = bf16[128,512]{1,0:T(8,128)(2,1)} custom-call(bf16[128,512]{1,0:T(8,128)(2,1)S(1)} %copy-done, bf16[128,512]{1,0:T(8,128)(2,1)S(1)} %copy-done.4, f32[128,512]{1,0:T(8,128)S(1)} %get-tuple-element.18.inside_ref, f32[128,2]{1,0:T(8,128)S(1)} %get-tuple-element.19.factor_ref, bf16[2,64,256]{2,1,0:T(8,128)(2,1)S(1)} %get-tuple-element.24.refs_0_, ...), custom_call_target="tpu_custom_call" | custom-call | flops 33554432 | bytes 918528 | tf_op jit(solution)/shard_map/retain_finish/pallas_call | solution.py:25
  59.4 0.0 collective-permute-done.19.refs_1_
  59.4 0.0 collective-permute-done.20.refs_2_
  59.4 1.1 %merge.1 = bf16[128,512]{1,0:T(8,128)(2,1)} custom-call(bf16[128,640]{1,0:T(8,128)(2,1)S(1)} %get-tuple-element.30.refs_0_, bf16[128,640]{1,0:T(8,128)(2,1)S(1)} %collective-permute-done.19.refs_1_, bf16[128,640]{1,0:T(8,128)(2,1)S(1)} %collective-permute-done.20.refs_2_, bf16[128,640]{1,0:T(8,128)(2,1)S(1)} %collective-permute-done.21.refs_3_), custom_call_target="tpu_custom_call" | custom-call | flops 1000000 | bytes 786432 | tf_op jit(solution)/shard_map/merge/pallas_call | solution.py:25
  (23 shorter events, 0.1 us)
Async XLA Ops:
  0.6 11.8 %copy-start.1 = (bf16[128,512]{1,0:T(8,128)(2,1)S(1)}, bf16[128,512]{1,0:T(8,128)(2,1)}, u32[]{:S(2)}) copy-start(bf16[128,512]{1,0:T(8,128)(2,1)} %k_ref.4) | copy-start | bytes 393220
  0.6 0.9 %copy-start.5 = (bf16[64,512]{1,0:T(8,128)(2,1)S(1)}, bf16[64,512]{1,0:T(8,128)(2,1)}, u32[]{:S(2)}) copy-start(bf16[64,512]{1,0:T(8,128)(2,1)} %k_ref.5) | copy-start | bytes 196612
  1.5 0.8 %copy-start.6 = (bf16[64,512]{1,0:T(8,128)(2,1)S(1)}, bf16[64,512]{1,0:T(8,128)(2,1)}, u32[]{:S(2)}) copy-start(bf16[64,512]{1,0:T(8,128)(2,1)} %v_ref.5) | copy-start | bytes 196612
  2.4 10.0 %copy-start.8 = (f32[128,2]{0,1:T(2,128)S(1)}, f32[128,2]{0,1:T(2,128)}, u32[]{:S(2)}) copy-start(f32[128,2]{0,1:T(2,128)} %param.12) | copy-start | bytes 3076
  2.4 14.7 %collective-permute-start.12 = (bf16[2,64,256]{2,1,0:T(8,128)(2,1)S(1)}, bf16[2,64,256]{2,1,0:T(8,128)(2,1)S(1)}, u32[]{:S(2)}, u32[]{:S(2)}) collective-permute-start(bf16[2,64,256]{2,1,0:T(8,128)(2,1)S(1)} %get-tuple-element.29), channel_id=1, source_target_pairs={{0,1},{1,0},{2,3},{3,2},{4,5},{5,4},{6,7},{7,6},{8,9},{9,8},{10,11... | collective-permute-start | bytes 196616 | tf_op jit(solution)/shard_map/ppermute | solution.py:281
  5.4 13.3 %collective-permute-start.13 = (bf16[2,64,256]{2,1,0:T(8,128)(2,1)S(1)}, bf16[2,64,256]{2,1,0:T(8,128)(2,1)S(1)}, u32[]{:S(2)}, u32[]{:S(2)}) collective-permute-start(bf16[2,64,256]{2,1,0:T(8,128)(2,1)S(1)} %get-tuple-element.28.refs_4_), channel_id=1, source_target_pairs={{0,8},{1,9},{2,10},{3,11},{4,12},{5,13},{6,14},{7,15},{8,16},{9,17... | collective-permute-start | bytes 196616 | tf_op jit(solution)/shard_map/ppermute | solution.py:281
  8.9 11.4 %collective-permute-start.14 = (bf16[2,64,256]{2,1,0:T(8,128)(2,1)S(1)}, bf16[2,64,256]{2,1,0:T(8,128)(2,1)S(1)}, u32[]{:S(2)}, u32[]{:S(2)}) collective-permute-start(bf16[2,64,256]{2,1,0:T(8,128)(2,1)S(1)} %get-tuple-element.29), channel_id=1, source_target_pairs={{0,9},{1,8},{2,11},{3,10},{4,13},{5,12},{6,15},{7,14},{8,17},{9,16... | collective-permute-start | bytes 196616 | tf_op jit(solution)/shard_map/ppermute | solution.py:281
  12.5 0.9 %copy-start.2 = (bf16[128,512]{1,0:T(8,128)(2,1)S(1)}, bf16[128,512]{1,0:T(8,128)(2,1)}, u32[]{:S(2)}) copy-start(bf16[128,512]{1,0:T(8,128)(2,1)} %v_ref.4) | copy-start | bytes 393220
  13.4 7.0 %copy-start.7 = (bf16[128,512]{1,0:T(8,128)(2,1)S(1)}, bf16[128,512]{1,0:T(8,128)(2,1)}, u32[]{:S(2)}) copy-start(bf16[128,512]{1,0:T(8,128)(2,1)} %refs_0_.1) | copy-start | bytes 393220
  14.0 8.2 %collective-permute-start = (bf16[2,80,256]{2,1,0:T(8,128)(2,1)S(1)}, bf16[2,80,256]{2,1,0:T(8,128)(2,1)S(1)}, u32[]{:S(2)}, u32[]{:S(2)}) collective-permute-start(bf16[2,80,256]{2,1,0:T(8,128)(2,1)S(1)} %get-tuple-element.21), channel_id=1, source_target_pairs={{0,2},{2,0},{4,6},{6,4},{8,10},{10,8},{12,14},{14,12},{16,18},{18,... | collective-permute-start | bytes 245768 | tf_op jit(solution)/shard_map/ppermute | solution.py:270
  14.1 6.2 %collective-permute-start.15 = (bf16[2,64,256]{2,1,0:T(8,128)(2,1)S(1)}, bf16[2,64,256]{2,1,0:T(8,128)(2,1)S(1)}, u32[]{:S(2)}, u32[]{:S(2)}) collective-permute-start(bf16[2,64,256]{2,1,0:T(8,128)(2,1)S(1)} %get-tuple-element.28.refs_4_), channel_id=1, source_target_pairs={{0,16},{1,17},{2,18},{3,19},{4,20},{5,21},{6,22},{7,23},{8,24},{9,... | collective-permute-start | bytes 196616 | tf_op jit(solution)/shard_map/ppermute | solution.py:281
  17.1 4.7 %collective-permute-start.16 = (bf16[2,64,256]{2,1,0:T(8,128)(2,1)S(1)}, bf16[2,64,256]{2,1,0:T(8,128)(2,1)S(1)}, u32[]{:S(2)}, u32[]{:S(2)}) collective-permute-start(bf16[2,64,256]{2,1,0:T(8,128)(2,1)S(1)} %get-tuple-element.29), channel_id=1, source_target_pairs={{0,17},{1,16},{2,19},{3,18},{4,21},{5,20},{6,23},{7,22},{8,25},{9,... | collective-permute-start | bytes 196616 | tf_op jit(solution)/shard_map/ppermute | solution.py:281
  18.7 4.7 %collective-permute-start.1 = (bf16[2,80,256]{2,1,0:T(8,128)(2,1)S(1)}, bf16[2,80,256]{2,1,0:T(8,128)(2,1)S(1)}, u32[]{:S(2)}, u32[]{:S(2)}) collective-permute-start(bf16[2,80,256]{2,1,0:T(8,128)(2,1)S(1)} %get-tuple-element.22), channel_id=1, source_target_pairs={{0,4},{2,6},{4,0},{6,2},{8,12},{10,14},{12,8},{14,10},{16,20},{18,... | collective-permute-start | bytes 245768 | tf_op jit(solution)/shard_map/ppermute | solution.py:270
  20.3 10.5 %collective-permute-start.2 = (bf16[2,80,256]{2,1,0:T(8,128)(2,1)S(1)}, bf16[2,80,256]{2,1,0:T(8,128)(2,1)S(1)}, u32[]{:S(2)}, u32[]{:S(2)}) collective-permute-start(bf16[2,80,256]{2,1,0:T(8,128)(2,1)S(1)} %get-tuple-element.23), channel_id=1, source_target_pairs={{0,6},{2,4},{4,2},{6,0},{8,14},{10,12},{12,10},{14,8},{16,22},{18,... | collective-permute-start | bytes 245768 | tf_op jit(solution)/shard_map/ppermute | solution.py:270
  20.3 21.3 %collective-permute-start.10 = (bf16[128,512]{1,0:T(8,128)(2,1)S(1)}, bf16[128,512]{1,0:T(8,128)(2,1)S(1)}, u32[]{:S(2)}, u32[]{:S(2)}) collective-permute-start(bf16[128,512]{1,0:T(8,128)(2,1)S(1)} %copy-done.7), channel_id=1, source_target_pairs={{0,4},{2,6},{4,0},{6,2},{8,12},{10,14},{12,8},{14,10},{16,20},{18,... | collective-permute-start | bytes 393224 | tf_op jit(solution)/shard_map/ppermute | solution.py:270
  21.8 21.1 %collective-permute-start.11 = (bf16[128,512]{1,0:T(8,128)(2,1)S(1)}, bf16[128,512]{1,0:T(8,128)(2,1)S(1)}, u32[]{:S(2)}, u32[]{:S(2)}) collective-permute-start(bf16[128,512]{1,0:T(8,128)(2,1)S(1)} %copy-done.7), channel_id=1, source_target_pairs={{0,6},{2,4},{4,2},{6,0},{8,14},{10,12},{12,10},{14,8},{16,22},{18,... | collective-permute-start | bytes 393224 | tf_op jit(solution)/shard_map/ppermute | solution.py:270
  22.3 20.7 %collective-permute-start.9 = (bf16[128,512]{1,0:T(8,128)(2,1)S(1)}, bf16[128,512]{1,0:T(8,128)(2,1)S(1)}, u32[]{:S(2)}, u32[]{:S(2)}) collective-permute-start(bf16[128,512]{1,0:T(8,128)(2,1)S(1)} %copy-done.7), channel_id=1, source_target_pairs={{0,2},{2,0},{4,6},{6,4},{8,10},{10,8},{12,14},{14,12},{16,18},{18,... | collective-permute-start | bytes 393224 | tf_op jit(solution)/shard_map/ppermute | solution.py:270
  23.4 9.6 %collective-permute-start.17 = (bf16[2,64,256]{2,1,0:T(8,128)(2,1)S(1)}, bf16[2,64,256]{2,1,0:T(8,128)(2,1)S(1)}, u32[]{:S(2)}, u32[]{:S(2)}) collective-permute-start(bf16[2,64,256]{2,1,0:T(8,128)(2,1)S(1)} %get-tuple-element.28.refs_4_), channel_id=1, source_target_pairs={{0,24},{1,25},{2,26},{3,27},{4,28},{5,29},{6,30},{7,31}} | collective-permute-start | bytes 196616 | tf_op jit(solution)/shard_map/ppermute | solution.py:281
  30.8 3.6 %collective-permute-start.18 = (bf16[2,64,256]{2,1,0:T(8,128)(2,1)S(1)}, bf16[2,64,256]{2,1,0:T(8,128)(2,1)S(1)}, u32[]{:S(2)}, u32[]{:S(2)}) collective-permute-start(bf16[2,64,256]{2,1,0:T(8,128)(2,1)S(1)} %get-tuple-element.29), channel_id=1, source_target_pairs={{0,25},{1,24},{2,27},{3,26},{4,29},{5,28},{6,31},{7,30}} | collective-permute-start | bytes 196616 | tf_op jit(solution)/shard_map/ppermute | solution.py:281
  32.9 13.2 %collective-permute-start.3 = (bf16[2,80,256]{2,1,0:T(8,128)(2,1)S(1)}, bf16[2,80,256]{2,1,0:T(8,128)(2,1)S(1)}, u32[]{:S(2)}, u32[]{:S(2)}) collective-permute-start(bf16[2,80,256]{2,1,0:T(8,128)(2,1)S(1)} %plane_total.1), channel_id=1, source_target_pairs={{0,8},{2,10},{4,12},{6,14},{8,16},{10,18},{12,20},{14,22},{16,24},... | collective-permute-start | bytes 245768 | tf_op jit(solution)/shard_map/ppermute | solution.py:273
  34.3 13.4 %collective-permute-start.4 = (bf16[2,80,256]{2,1,0:T(8,128)(2,1)S(1)}, bf16[2,80,256]{2,1,0:T(8,128)(2,1)S(1)}, u32[]{:S(2)}, u32[]{:S(2)}) collective-permute-start(bf16[2,80,256]{2,1,0:T(8,128)(2,1)S(1)} %plane_total.1), channel_id=1, source_target_pairs={{0,16},{2,18},{4,20},{6,22},{8,24},{10,26},{12,28},{14,30},{1,17},... | collective-permute-start | bytes 245768 | tf_op jit(solution)/shard_map/ppermute | solution.py:273
  41.6 6.1 %collective-permute-start.5 = (bf16[2,80,256]{2,1,0:T(8,128)(2,1)S(1)}, bf16[2,80,256]{2,1,0:T(8,128)(2,1)S(1)}, u32[]{:S(2)}, u32[]{:S(2)}) collective-permute-start(bf16[2,80,256]{2,1,0:T(8,128)(2,1)S(1)} %plane_total.1), channel_id=1, source_target_pairs={{0,24},{2,26},{4,28},{6,30},{1,25},{3,27},{5,29},{7,31}} | collective-permute-start | bytes 245768 | tf_op jit(solution)/shard_map/ppermute | solution.py:273
  45.8 13.6 %collective-permute-start.19 = (bf16[128,640]{1,0:T(8,128)(2,1)S(1)}, bf16[128,640]{1,0:T(8,128)(2,1)S(1)}, u32[]{:S(2)}, u32[]{:S(2)}) collective-permute-start(bf16[128,640]{1,0:T(8,128)(2,1)S(1)} %get-tuple-element.31), channel_id=1, source_target_pairs={{0,2},{2,0},{4,6},{6,4},{8,10},{10,8},{12,14},{14,12},{16,18},{18,... | collective-permute-start | bytes 491528 | tf_op jit(solution)/shard_map/ppermute | solution.py:270
  45.9 13.5 %collective-permute-start.20 = (bf16[128,640]{1,0:T(8,128)(2,1)S(1)}, bf16[128,640]{1,0:T(8,128)(2,1)S(1)}, u32[]{:S(2)}, u32[]{:S(2)}) collective-permute-start(bf16[128,640]{1,0:T(8,128)(2,1)S(1)} %get-tuple-element.32), channel_id=1, source_target_pairs={{0,4},{2,6},{4,0},{6,2},{8,12},{10,14},{12,8},{14,10},{16,20},{18,... | collective-permute-start | bytes 491528 | tf_op jit(solution)/shard_map/ppermute | solution.py:270
  46.2 3.8 %copy-start = (bf16[128,512]{1,0:T(8,128)(2,1)S(1)}, bf16[128,512]{1,0:T(8,128)(2,1)}, u32[]{:S(2)}) copy-start(bf16[128,512]{1,0:T(8,128)(2,1)} %q_ref.3) | copy-start | bytes 393220
  46.2 3.8 %copy-start.3 = (bf16[128,512]{1,0:T(8,128)(2,1)S(1)}, bf16[128,512]{1,0:T(8,128)(2,1)}, u32[]{:S(2)}) copy-start(bf16[128,512]{1,0:T(8,128)(2,1)} %v_ref.4) | copy-start | bytes 393220
  46.2 13.2 %collective-permute-start.21 = (bf16[128,640]{1,0:T(8,128)(2,1)S(1)}, bf16[128,640]{1,0:T(8,128)(2,1)S(1)}, u32[]{:S(2)}, u32[]{:S(2)}) collective-permute-start(bf16[128,640]{1,0:T(8,128)(2,1)S(1)} %get-tuple-element.33), channel_id=1, source_target_pairs={{0,6},{2,4},{4,2},{6,0},{8,14},{10,12},{12,10},{14,8},{16,22},{18,... | collective-permute-start | bytes 491528 | tf_op jit(solution)/shard_map/ppermute | solution.py:270
  48.1 1.3 %collective-permute-start.6 = (bf16[2,64,256]{2,1,0:T(8,128)(2,1)S(1)}, bf16[2,64,256]{2,1,0:T(8,128)(2,1)S(1)}, u32[]{:S(2)}, u32[]{:S(2)}) collective-permute-start(bf16[2,64,256]{2,1,0:T(8,128)(2,1)S(1)} %get-tuple-element.25), channel_id=1, source_target_pairs={{0,2},{2,0},{4,6},{6,4},{8,10},{10,8},{12,14},{14,12},{16,18},{18,... | collective-permute-start | bytes 196616 | tf_op jit(solution)/shard_map/ppermute | solution.py:270
  48.5 9.4 %collective-permute-start.7 = (bf16[2,64,256]{2,1,0:T(8,128)(2,1)S(1)}, bf16[2,64,256]{2,1,0:T(8,128)(2,1)S(1)}, u32[]{:S(2)}, u32[]{:S(2)}) collective-permute-start(bf16[2,64,256]{2,1,0:T(8,128)(2,1)S(1)} %get-tuple-element.26), channel_id=1, source_target_pairs={{0,4},{2,6},{4,0},{6,2},{8,12},{10,14},{12,8},{14,10},{16,20},{18,... | collective-permute-start | bytes 196616 | tf_op jit(solution)/shard_map/ppermute | solution.py:270
  49.4 9.0 %copy-start.4 = (bf16[128,512]{1,0:T(8,128)(2,1)S(1)}, bf16[128,512]{1,0:T(8,128)(2,1)}, u32[]{:S(2)}) copy-start(bf16[128,512]{1,0:T(8,128)(2,1)} %gate_ref.1) | copy-start | bytes 393220
  49.4 9.0 %collective-permute-start.8 = (bf16[2,64,256]{2,1,0:T(8,128)(2,1)S(1)}, bf16[2,64,256]{2,1,0:T(8,128)(2,1)S(1)}, u32[]{:S(2)}, u32[]{:S(2)}) collective-permute-start(bf16[2,64,256]{2,1,0:T(8,128)(2,1)S(1)} %get-tuple-element.27), channel_id=1, source_target_pairs={{0,6},{2,4},{4,2},{6,0},{8,14},{10,12},{12,10},{14,8},{16,22},{18,... | collective-permute-start | bytes 196616 | tf_op jit(solution)/shard_map/ppermute | solution.py:270

commit v2 on v1

v2 whole, which is shorter than its diff:
```python
import functools
import math

import jax
import jax.numpy as jnp
from jax import lax
from jax.experimental import pallas as pl
from jax.experimental.pallas import tpu as pltpu
from jax.sharding import PartitionSpec as P

HD = 256
FAR = -1e30
NEAR = -1e29
EPS = 1e-06
F32 = jnp.float32
BF16 = jnp.bfloat16
PAD = 16
LANES = 128
VMEM = pl.BlockSpec(memory_space=pltpu.VMEM)


def call(body, outs, args, scratch=(), flops=1_000_000, name=None):
    moved = sum(math.prod(a.shape) * a.dtype.itemsize for a in (*args, *outs))
    single = len(outs) == 1
    return pl.pallas_call(
        body,
        out_shape=outs[0] if single else tuple(outs),
        in_specs=[VMEM] * len(args),
        out_specs=VMEM if single else tuple(VMEM for _ in outs),
        scratch_shapes=scratch,
        compiler_params=pltpu.CompilerParams(vmem_limit_bytes=40 * 1024 * 1024),
        cost_estimate=pl.CostEstimate(flops=flops, bytes_accessed=moved, transcendentals=0),
        name=name,
    )(*args)


def shape(dims, dtype=BF16):
    return jax.ShapeDtypeStruct(dims, dtype)


def dot(a, b, contract, precision=None):
    return lax.dot_general(
        a, b, (contract, ((), ())), preferred_element_type=F32, precision=precision
    )


def thirds(value):
    high = value.astype(BF16).astype(F32)
    rest = value - high
    middle = rest.astype(BF16).astype(F32)
    return high, middle, rest - middle


def decay_sums(log_decay):
    rows = log_decay.shape[0]
    below = lax.broadcasted_iota(jnp.int32, (rows, rows), 0) >= lax.broadcasted_iota(
        jnp.int32, (rows, rows), 1
    )
    lower = jnp.where(below, 1.0, 0.0).astype(F32)
    return dot(lower, log_decay, ((1,), (0,)), lax.Precision.HIGHEST), below


def split_cache(n, k_ref, v_ref, *pieces):
    width = k_ref.shape[1] // n
    here = lax.axis_index("head")
    for e, piece in enumerate(pieces):
        target = lax.rem(here + e, n)
        columns = pl.ds(pl.multiple_of(target * width, LANES), width)
        piece[:, pl.ds(0, width)] = k_ref[:, columns]
        piece[:, pl.ds(width, width)] = v_ref[:, columns]


def join_rows(n, *refs):
    pieces, out = refs[:n], refs[n]
    length = pieces[0].shape[0]
    here = lax.axis_index("head")
    for e, piece in enumerate(pieces):
        place = lax.rem(here + n - e, n)
        out[pl.ds(pl.multiple_of(place * length, PAD), length), :] = piece[...]


def bits():
    index = lax.axis_index("ctx")
    low = lax.rem(index, 2)
    return low, lax.rem(lax.div(index, 2), 2), lax.div(index, 4)


def put_total(out, at, total):
    wide = out.shape[1]
    if out.dtype == F32:
        out[pl.ds(at, PAD), :] = jnp.broadcast_to(total, (PAD, wide))
        return
    row = lax.broadcasted_iota(jnp.int32, (PAD, wide), 0)
    high, middle, low = thirds(total)
    tile = jnp.where(row == 0, high, jnp.where(row == 1, middle, jnp.where(row == 2, low, 0.0)))
    out[pl.ds(at, PAD), :] = tile.astype(out.dtype)


def total_of(ref):
    tile = ref[pl.ds(ref.shape[0] - PAD, PAD), :].astype(F32)
    if ref.dtype == F32:
        return tile[0:1, :]
    return tile[0:1, :] + tile[1:2, :] + tile[2:3, :]


def state_of(ref):
    return ref[pl.ds(0, ref.shape[0] - PAD), :].astype(F32)


def part_of(held, which, rows):
    return held[pl.ds(pl.multiple_of(which * rows, rows), rows), :]


def summarize(k_ref, v_ref, d_ref, send, keep, held):
    low, _, _ = bits()
    half = HD // 2
    sums, _ = decay_sums(d_ref[...])
    rows = sums.shape[0]
    totals = []
    for head in range(d_ref.shape[1]):
        columns = pl.ds(head * HD, HD)
        column = sums[:, head : head + 1]
        last = column[rows - 1 : rows, :]
        carried = (k_ref[:, columns].astype(F32) * jnp.exp(last - column)).astype(BF16)
        held[:, columns] = dot(carried, v_ref[:, columns], ((0,), (0,)))
        totals.append(jnp.broadcast_to(last, (1, HD)))
    total = jnp.concatenate(totals, axis=1)
    for out, which in ((send, 1 - low), (keep, low)):
        out[pl.ds(0, half), :] = part_of(held, which, half).astype(out.dtype)
        put_total(out, half, total)


def pair_total(first, keep_ref, other_ref):
    kept, other = state_of(keep_ref), state_of(other_ref)
    kept_total, other_total = total_of(keep_ref), total_of(other_ref)
    late = jnp.where(first, other_total, kept_total)
    earlier, later = jnp.where(first, kept, other), jnp.where(first, other, kept)
    return jnp.exp(late) * earlier + later, kept_total + other_total


def chip_total(keep_ref, other_ref, send, keep, held):
    low, high, _ = bits()
    quarter = HD // 4
    held[...], total = pair_total(low == 0, keep_ref, other_ref)
    for out, which in ((send, 1 - high), (keep, high)):
        out[pl.ds(0, quarter), :] = part_of(held, which, quarter).astype(out.dtype)
        put_total(out, quarter, total)


def plane_total(keep_ref, other_ref, out):
    _, high, _ = bits()
    state, total = pair_total(high == 0, keep_ref, other_ref)
    out[pl.ds(0, state.shape[0]), :] = state.astype(out.dtype)
    put_total(out, state.shape[0], total)


def chip_priors(keep_ref, other_ref, *refs):
    planes, send, keep = refs[:-2], refs[-2], refs[-1]
    _, high, _ = bits()
    entering = jnp.zeros(send.shape, F32)
    between = jnp.zeros((1, send.shape[1]), F32)
    for ref in planes:
        entering = entering + jnp.exp(between) * state_of(ref)
        between = between + total_of(ref)
    first = high == 0
    early = jnp.where(first, state_of(keep_ref), state_of(other_ref))
    early_total = jnp.where(first, total_of(keep_ref), total_of(other_ref))
    second = jnp.exp(early_total) * entering + early
    send[...] = jnp.where(first, second, entering).astype(send.dtype)
    keep[...] = jnp.where(first, entering, second).astype(keep.dtype)


def block_priors(keep_ref, other_ref, prior_ref, prior_other_ref, send, keep, held):
    low, high, _ = bits()
    quarter = prior_ref.shape[0]
    for ref, which in ((prior_ref, high), (prior_other_ref, 1 - high)):
        held[pl.ds(pl.multiple_of(which * quarter, quarter), quarter), :] = ref[...].astype(F32)
    first = low == 0
    early = jnp.where(first, state_of(keep_ref), state_of(other_ref))
    early_total = jnp.where(first, total_of(keep_ref), total_of(other_ref))
    entering = held[...]
    second = jnp.exp(early_total) * entering + early
    send[...] = jnp.where(first, second, entering).astype(send.dtype)
    keep[...] = jnp.where(first, entering, second).astype(keep.dtype)


def retain_inside(q_ref, k_ref, v_ref, d_ref, inside_ref, factor_ref):
    heads = d_ref.shape[1]
    sums, below = decay_sums(d_ref[...])
    rows = sums.shape[0]
    same = lax.broadcasted_iota(jnp.int32, (rows, rows), 0) == lax.broadcasted_iota(
        jnp.int32, (rows, rows), 1
    )
    factor_ref[...] = jnp.exp(sums)
    for head in range(heads):
        columns = pl.ds(head * HD, HD)
        column = jnp.broadcast_to(sums[:, head : head + 1], (rows, rows))
        across = jnp.sum(jnp.where(same, column, 0.0), axis=0, keepdims=True)
        spread = jnp.exp(jnp.minimum(column - across, 0.0))
        scores = dot(q_ref[:, columns], k_ref[:, columns], ((1,), (1,)))
        weights = jnp.where(below, spread * scores, 0.0).astype(BF16)
        inside_ref[:, columns] = dot(weights, v_ref[:, columns], ((1,), (0,)))


def retain_finish(q_ref, gate_ref, inside_ref, factor_ref, keep_ref, other_ref, out, held):
    low, _, _ = bits()
    half = keep_ref.shape[0]
    for ref, which in ((keep_ref, low), (other_ref, 1 - low)):
        held[pl.ds(pl.multiple_of(which * half, half), half), :] = ref[...]
    for head in range(factor_ref.shape[1]):
        columns = pl.ds(head * HD, HD)
        before = dot(q_ref[:, columns], held[:, columns], ((1,), (0,)))
        retained = inside_ref[:, columns] + factor_ref[:, head : head + 1] * before
        scale = lax.rsqrt(jnp.mean(retained * retained, axis=1, keepdims=True) + EPS)
        gate = gate_ref[:, columns].astype(F32)
        silu = gate / (1.0 + jnp.exp(-gate))
        out[:, columns] = (retained * scale * silu).astype(BF16)


def attend(far, q_ref, q_other_ref, *refs):
    blocks, (send, keep, keys, values) = refs[: 2 * far], refs[2 * far :]
    rows, wide = q_ref.shape
    heads = wide // HD
    length, width = blocks[0].shape[0], blocks[0].shape[1] // 2
    group = wide // width
    total = 2 * far * length
    low, high, depth = bits()
    for i, block in enumerate(blocks):
        keys[pl.ds(i * length, length), :] = block[:, pl.ds(0, width)]
        values[pl.ds(i * length, length), :] = block[:, pl.ds(width, width)]
    column = lax.broadcasted_iota(jnp.int32, (1, total), 1)
    limit = jnp.zeros((1, total), jnp.int32)
    for i in range(2 * far):
        s, t = divmod(i, 2)
        if s == 0:
            core = low if t == 0 else 1 - low
            at = column + ((2 * high + core) * length - i * length)
        else:
            at = jnp.where(depth >= s, -1, 4 * rows)
        limit = jnp.where(column >= i * length, at, limit)
    scale = 1.0 / (math.sqrt(HD) * math.log(2.0))
    row = lax.broadcasted_iota(jnp.int32, (rows, total), 0)
    lane = lax.broadcasted_iota(jnp.int32, (rows, LANES), 1)
    for query, out, place in ((q_other_ref, send, 1 - high), (q_ref, keep, high)):
        allowed = row + (2 * place + low) * rows >= limit
        stats = jnp.zeros((rows, LANES), F32)
        for head in range(heads):
            columns = pl.ds(head * HD, HD)
            shared = pl.ds((head // group) * HD, HD)
            scores = dot(query[:, columns], keys[:, shared], ((1,), (1,))) * scale
            masked = jnp.where(allowed, scores, FAR)
            top = jnp.maximum(jnp.max(masked, axis=1, keepdims=True), NEAR)
            weights = jnp.exp2(masked - top)
            summed = jnp.sum(weights, axis=1, keepdims=True)
            mixed = dot(weights.astype(BF16), values[:, shared], ((1,), (0,)))
            some = summed > 0.0
            safe = jnp.where(some, summed, 1.0)
            out[:, columns] = (mixed / safe).astype(out.dtype)
            level = jnp.where(some, top + jnp.log2(safe), FAR)
            for i, third in enumerate(thirds(level)):
                stats = jnp.where(lane == 3 * head + i, third, stats)
        out[:, pl.ds(wide, LANES)] = stats.astype(out.dtype)


def merge(keep_ref, other_ref, out):
    wide = out.shape[1]
    ins = (keep_ref, other_ref)
    stats = [ref[:, pl.ds(wide, LANES)].astype(F32) for ref in ins]
    for head in range(wide // HD):
        columns = pl.ds(head * HD, HD)
        levels = [
            tile[:, 3 * head : 3 * head + 1]
            + tile[:, 3 * head + 1 : 3 * head + 2]
            + tile[:, 3 * head + 2 : 3 * head + 3]
            for tile in stats
        ]
        top = functools.reduce(jnp.maximum, levels)
        weights = [jnp.exp2(level - top) for level in levels]
        share = 1.0 / functools.reduce(jnp.add, weights)
        mixed = functools.reduce(
            jnp.add, [(w * share) * ref[:, columns].astype(F32) for w, ref in zip(weights, ins)]
        )
        out[:, columns] = mixed.astype(BF16)


def per_device(count, n, q_ret, k_ret, v_ret, gate_ret, log_decay, q_cross, cache_k, cache_v):
    far = count // 4
    rows, wide = q_cross.shape
    heads = wide // HD
    length, width = cache_k.shape[0], cache_k.shape[1] // n
    half, quarter = HD // 2, HD // 4

    def swap(value, bit):
        return lax.ppermute(value, "ctx", [(b, b ^ bit) for b in range(count)])

    def onward(value, s):
        return lax.ppermute(value, "ctx", [(b, b + s * 4) for b in range(count - s * 4)])

    def to_head(value, e):
        return lax.ppermute(value, "head", [(y, (y + e) % n) for y in range(n)])

    pieces = call(
        functools.partial(split_cache, n),
        [shape((length, 2 * width))] * n,
        (cache_k, cache_v),
        name="split_cache",
    )
    arrived = [pieces[0]] + [to_head(pieces[e], e) for e in range(1, n)]
    sum_send, sum_keep = call(
        summarize,
        [shape((half + PAD, wide)), shape((half + PAD, wide), F32)],
        (k_ret, v_ret, log_decay),
        scratch=[pltpu.VMEM((HD, wide), F32)],
        flops=2 * rows * HD * HD * heads,
        name="summarize",
    )
    sum_other = swap(sum_send, 1)
    block = call(
        functools.partial(join_rows, n), [shape((n * length, 2 * width))], arrived, name="join_rows"
    )
    blocks = [block] + [onward(block, s) for s in range(1, far)]
    chip_send, chip_keep = call(
        chip_total,
        [shape((quarter + PAD, wide)), shape((quarter + PAD, wide), F32)],
        (sum_keep, sum_other),
        scratch=[pltpu.VMEM((half, wide), F32)],
        name="chip_total",
    )
    chip_other = swap(chip_send, 2)
    q_other = swap(q_cross, 2)
    whole = call(plane_total, [shape((quarter + PAD, wide))], (chip_keep, chip_other), name="plane_total")
    planes = [onward(whole, s) for s in range(1, far)]
    inside, factor = call(
        retain_inside,
        [shape((rows, wide), F32), shape((rows, heads), F32)],
        (q_ret, k_ret, v_ret, log_decay),
        flops=4 * rows * rows * HD * heads,
        name="retain_inside",
    )
    both = []
    for one in blocks:
        both += [one, swap(one, 1)]
    part_send, part_keep = call(
        functools.partial(attend, far),
        [shape((rows, wide + LANES)), shape((rows, wide + LANES), F32)],
        (q_cross, q_other, *both),
        scratch=[pltpu.VMEM((2 * far * n * length, width), BF16) for _ in range(2)],
        flops=8 * rows * heads * 2 * far * n * length * HD,
        name="attend",
    )
    part_other = swap(part_send, 2)
    prior_send, prior_keep = call(
        chip_priors,
        [shape((quarter, wide)), shape((quarter, wide), F32)],
        (chip_keep, chip_other, *planes),
        name="chip_priors",
    )
    prior_other = swap(prior_send, 2)
    state_send, state_keep = call(
        block_priors,
        [shape((half, wide)), shape((half, wide))],
        (sum_keep, sum_other, prior_keep, prior_other),
        scratch=[pltpu.VMEM((half, wide), F32)],
        name="block_priors",
    )
    state_other = swap(state_send, 1)
    o_ret = call(
        retain_finish,
        [shape((rows, wide))],
        (q_ret, gate_ret, inside, factor, state_keep, state_other),
        scratch=[pltpu.VMEM((HD, wide), BF16)],
        flops=2 * rows * HD * HD * heads,
        name="retain_finish",
    )
    o_cross = call(merge, [shape((rows, wide))], (part_keep, part_other), name="merge")
    return o_ret, o_cross


def solution(mesh):
    split = P("ctx", "head")
    rows = P(("ctx", "head"), None)
    return jax.shard_map(
        functools.partial(per_device, mesh.shape["ctx"], mesh.shape["head"]),
        mesh=mesh,
        in_specs=(split,) * 6 + (rows,) * 2,
        out_specs=(split, split),
        check_vma=False,
    )
```

time: 60.8 us -> 44.7 us (0.74)
  the two profiles are of different devices: /device:TPU:0 before, /device:TPU:24 now
where the time goes in v2:
time: 44.7 us; the launch traced here: 44.4 us
  waiting for transfers between devices  19.7 us (44%)
  starting transfers between devices  14.8 us (33%)
  Pallas kernels  5.55 us (12%)
  local copies, waits for them, and re-layouts  3.49 us (8%)
  between operations  0.79 us (2%)
    ppermute x6, waiting for transfers between devices, onward(): lax.ppermute(value, 'ctx', [(b, b + s * 4) for b in range(count - s * 4)])  12.3 us
    ppermute x6, starting transfers between devices, onward(): lax.ppermute(value, 'ctx', [(b, b + s * 4) for b in range(count - s * 4)])  7.87 us
    pallas_call x11, Pallas kernels, call(): pl.pallas_call(body, out_shape=outs[0] if single else tuple(outs), in_spe...  5.55 us
    ppermute x10, starting transfers between devices, swap(): return lax.ppermute(value, 'ctx', [(b, b ^ bit) for b in range(count)])  5.34 us
    ppermute x10, waiting for transfers between devices, swap(): return lax.ppermute(value, 'ctx', [(b, b ^ bit) for b in range(count)])  4.53 us
    unnamed x19, local copies, waits for them, and re-layouts  3.49 us
    ppermute x1, waiting for transfers between devices, to_head(): return lax.ppermute(value, 'head', [(y, (y + e) % n) for y in range(n)])  2.91 us
    ppermute x1, starting transfers between devices, to_head(): return lax.ppermute(value, 'head', [(y, (y + e) % n) for y in range(n)])  1.58 us
  transfers between devices with their start and end apart: 17, of which 7 were waited for; matrix products, arithmetic and copies ran while one was open for 0% of the time, Pallas kernels for 9%

profile of v2, /device:TPU:24, one launch (start us, length us, event | category | flops | bytes accessed | tf_op | source)
XLA Modules:
  0.0 44.4 jit_solution(1861412516120187910)
XLA Ops:
  0.6 0.8 %copy.10.d_ref = f32[128,2]{1,0:T(8,128)S(1)} copy(f32[128,2]{0,1:T(2,128)} %param.12) | data formatting | bytes 2048 | tf_op args[4]
  1.4 0.9 %copy-done.1 = bf16[128,512]{1,0:T(8,128)(2,1)S(1)} copy-done((bf16[128,512]{1,0:T(8,128)(2,1)S(1)}, bf16[128,512]{1,0:T(8,128)(2,1)}, u32[]{:S(2)}) %copy-start.1) | copy-done | bytes 131096
  2.3 0.9 %copy-done.3 = bf16[128,512]{1,0:T(8,128)(2,1)S(1)} copy-done((bf16[128,512]{1,0:T(8,128)(2,1)S(1)}, bf16[128,512]{1,0:T(8,128)(2,1)}, u32[]{:S(2)}) %copy-start.3) | copy-done | bytes 131096
  3.2 0.7 %summarize.1 = (bf16[144,512]{1,0:T(8,128)(2,1)S(1)}, f32[144,512]{1,0:T(8,128)S(1)}) custom-call(bf16[128,512]{1,0:T(8,128)(2,1)S(1)} %copy-done.1, bf16[128,512]{1,0:T(8,128)(2,1)S(1)} %copy-done.3, f32[128,2]{1,0:T(8,128)S(1)} %copy.10.d_ref), custom_call_target="tpu_custom_call" | custom-call | flops 33554432 | bytes 705536 | tf_op jit(solution)/shard_map/summarize/pallas_call | solution.py:25
  3.9 0.1 collective-permute-start
  4.0 0.1 copy-done.6
  4.1 0.0 copy-done.7
  4.1 1.6 %collective-permute-start.8 = (bf16[64,512]{1,0:T(8,128)(2,1)S(1)}, bf16[64,512]{1,0:T(8,128)(2,1)S(1)}, u32[]{:S(2)}, u32[]{:S(2)}) collective-permute-start(bf16[64,512]{1,0:T(8,128)(2,1)S(1)} %get-tuple-element.27), channel_id=1, source_target_pairs={{0,1},{1,0},{2,3},{3,2},{4,5},{5,4},{6,7},{7,6},{8,9},{9,8},{10,11... | collective-permute-start | bytes 196616 | tf_op jit(solution)/shard_map/ppermute | solution.py:300
  5.7 2.9 %collective-permute-done.8.refs_1_ = bf16[64,512]{1,0:T(8,128)(2,1)S(1)} collective-permute-done((bf16[64,512]{1,0:T(8,128)(2,1)S(1)}, bf16[64,512]{1,0:T(8,128)(2,1)S(1)}, u32[]{:S(2)}, u32[]{:S(2)}) %collective-permute-start.8) | collective-permute-done | bytes 65568 | tf_op jit(solution)/shard_map/ppermute | solution.py:300
  8.6 1.3 %collective-permute-start.10 = (bf16[128,512]{1,0:T(8,128)(2,1)S(1)}, bf16[128,512]{1,0:T(8,128)(2,1)S(1)}, u32[]{:S(2)}, u32[]{:S(2)}) collective-permute-start(bf16[128,512]{1,0:T(8,128)(2,1)S(1)} %join_rows.1.refs_0_), channel_id=1, source_target_pairs={{0,8},{2,10},{4,12},{6,14},{8,16},{10,18},{12,20},{14,22},{16,24},... | collective-permute-start | bytes 393224 | tf_op jit(solution)/shard_map/ppermute | solution.py:297
  9.9 0.0 collective-permute-done.other_ref
  9.9 0.1 chip_total.1
  10.1 1.6 %collective-permute-start.1 = (bf16[80,512]{1,0:T(8,128)(2,1)S(1)}, bf16[80,512]{1,0:T(8,128)(2,1)S(1)}, u32[]{:S(2)}, u32[]{:S(2)}) collective-permute-start(bf16[80,512]{1,0:T(8,128)(2,1)S(1)} %get-tuple-element.21), channel_id=1, source_target_pairs={{0,4},{2,6},{4,0},{6,2},{8,12},{10,14},{12,8},{14,10},{16,20},{18,... | collective-permute-start | bytes 245768 | tf_op jit(solution)/shard_map/ppermute | solution.py:294
  11.6 1.3 %collective-permute-start.12 = (bf16[128,512]{1,0:T(8,128)(2,1)S(1)}, bf16[128,512]{1,0:T(8,128)(2,1)S(1)}, u32[]{:S(2)}, u32[]{:S(2)}) collective-permute-start(bf16[128,512]{1,0:T(8,128)(2,1)S(1)} %join_rows.1.refs_0_), channel_id=1, source_target_pairs={{0,16},{2,18},{4,20},{6,22},{8,24},{10,26},{12,28},{14,30},{1,17},... | collective-permute-start | bytes 393224 | tf_op jit(solution)/shard_map/ppermute | solution.py:297
  12.9 1.3 %collective-permute-start.14 = (bf16[128,512]{1,0:T(8,128)(2,1)S(1)}, bf16[128,512]{1,0:T(8,128)(2,1)S(1)}, u32[]{:S(2)}, u32[]{:S(2)}) collective-permute-start(bf16[128,512]{1,0:T(8,128)(2,1)S(1)} %join_rows.1.refs_0_), channel_id=1, source_target_pairs={{0,24},{2,26},{4,28},{6,30},{1,25},{3,27},{5,29},{7,31}} | collective-permute-start | bytes 393224 | tf_op jit(solution)/shard_map/ppermute | solution.py:297
  14.2 0.4 collective-permute-done.1.other_ref
  14.6 1.4 %collective-permute-start.2 = (bf16[80,512]{1,0:T(8,128)(2,1)S(1)}, bf16[80,512]{1,0:T(8,128)(2,1)S(1)}, u32[]{:S(2)}, u32[]{:S(2)}) collective-permute-start(bf16[80,512]{1,0:T(8,128)(2,1)S(1)} %plane_total.1), channel_id=1, source_target_pairs={{0,8},{2,10},{4,12},{6,14},{8,16},{10,18},{12,20},{14,22},{16,24},... | collective-permute-start | bytes 245768 | tf_op jit(solution)/shard_map/ppermute | solution.py:297
  16.1 1.3 %collective-permute-start.3 = (bf16[80,512]{1,0:T(8,128)(2,1)S(1)}, bf16[80,512]{1,0:T(8,128)(2,1)S(1)}, u32[]{:S(2)}, u32[]{:S(2)}) collective-permute-start(bf16[80,512]{1,0:T(8,128)(2,1)S(1)} %plane_total.1), channel_id=1, source_target_pairs={{0,16},{2,18},{4,20},{6,22},{8,24},{10,26},{12,28},{14,30},{1,17},... | collective-permute-start | bytes 245768 | tf_op jit(solution)/shard_map/ppermute | solution.py:297
  17.4 0.0 collective-permute-done.10.refs_2_
  17.4 1.3 %collective-permute-start.4 = (bf16[80,512]{1,0:T(8,128)(2,1)S(1)}, bf16[80,512]{1,0:T(8,128)(2,1)S(1)}, u32[]{:S(2)}, u32[]{:S(2)}) collective-permute-start(bf16[80,512]{1,0:T(8,128)(2,1)S(1)} %plane_total.1), channel_id=1, source_target_pairs={{0,24},{2,26},{4,28},{6,30},{1,25},{3,27},{5,29},{7,31}} | collective-permute-start | bytes 245768 | tf_op jit(solution)/shard_map/ppermute | solution.py:297
  18.7 10.9 %collective-permute-done.12.refs_4_ = bf16[128,512]{1,0:T(8,128)(2,1)S(1)} collective-permute-done((bf16[128,512]{1,0:T(8,128)(2,1)S(1)}, bf16[128,512]{1,0:T(8,128)(2,1)S(1)}, u32[]{:S(2)}, u32[]{:S(2)}) %collective-permute-start.12) | collective-permute-done | bytes 131104 | tf_op jit(solution)/shard_map/ppermute | solution.py:297
  29.6 0.5 %collective-permute-start.7 = (bf16[128,512]{1,0:T(8,128)(2,1)S(1)}, bf16[128,512]{1,0:T(8,128)(2,1)S(1)}, u32[]{:S(2)}, u32[]{:S(2)}) collective-permute-start(bf16[128,512]{1,0:T(8,128)(2,1)S(1)} %copy-done.8), channel_id=1, source_target_pairs={{0,4},{2,6},{4,0},{6,2},{8,12},{10,14},{12,8},{14,10},{16,20},{18,... | collective-permute-start | bytes 393224 | tf_op jit(solution)/shard_map/ppermute | solution.py:294
  30.2 0.0 collective-permute-done.14.refs_6_
  30.2 0.0 collective-permute-start.9
  30.2 0.0 collective-permute-done.2.refs_0_
  30.2 0.5 %collective-permute-start.11 = (bf16[128,512]{1,0:T(8,128)(2,1)S(1)}, bf16[128,512]{1,0:T(8,128)(2,1)S(1)}, u32[]{:S(2)}, u32[]{:S(2)}) collective-permute-start(bf16[128,512]{1,0:T(8,128)(2,1)S(1)} %collective-permute-done.10.refs_2_), channel_id=1, source_target_pairs={{0,2},{2,0},{4,6},{6,4},{8,10},{10,8},{12,14},{14,12},{16,18},{18,... | collective-permute-start | bytes 393224 | tf_op jit(solution)/shard_map/ppermute | solution.py:294
  30.7 1.3 %collective-permute-done.3.refs_1_ = bf16[80,512]{1,0:T(8,128)(2,1)S(1)} collective-permute-done((bf16[80,512]{1,0:T(8,128)(2,1)S(1)}, bf16[80,512]{1,0:T(8,128)(2,1)S(1)}, u32[]{:S(2)}, u32[]{:S(2)}) %collective-permute-start.3) | collective-permute-done | bytes 81952 | tf_op jit(solution)/shard_map/ppermute | solution.py:297
  32.0 0.0 collective-permute-start.13
  32.0 0.0 collective-permute-done.4.refs_2_
  32.0 0.5 %collective-permute-start.15 = (bf16[128,512]{1,0:T(8,128)(2,1)S(1)}, bf16[128,512]{1,0:T(8,128)(2,1)S(1)}, u32[]{:S(2)}, u32[]{:S(2)}) collective-permute-start(bf16[128,512]{1,0:T(8,128)(2,1)S(1)} %collective-permute-done.14.refs_6_), channel_id=1, source_target_pairs={{0,2},{2,0},{4,6},{6,4},{8,10},{10,8},{12,14},{14,12},{16,18},{18,... | collective-permute-start | bytes 393224 | tf_op jit(solution)/shard_map/ppermute | solution.py:294
  32.5 0.1 chip_priors.1
  32.6 2.0 %collective-permute-done.7.q_other_ref = bf16[128,512]{1,0:T(8,128)(2,1)S(1)} collective-permute-done((bf16[128,512]{1,0:T(8,128)(2,1)S(1)}, bf16[128,512]{1,0:T(8,128)(2,1)S(1)}, u32[]{:S(2)}, u32[]{:S(2)}) %collective-permute-start.7) | collective-permute-done | bytes 131104 | tf_op jit(solution)/shard_map/ppermute | solution.py:294
  34.6 0.5 %collective-permute-start.5 = (bf16[64,512]{1,0:T(8,128)(2,1)S(1)}, bf16[64,512]{1,0:T(8,128)(2,1)S(1)}, u32[]{:S(2)}, u32[]{:S(2)}) collective-permute-start(bf16[64,512]{1,0:T(8,128)(2,1)S(1)} %get-tuple-element.23), channel_id=1, source_target_pairs={{0,4},{2,6},{4,0},{6,2},{8,12},{10,14},{12,8},{14,10},{16,20},{18,... | collective-permute-start | bytes 196616 | tf_op jit(solution)/shard_map/ppermute | solution.py:294
  35.1 0.0 collective-permute-done.11.refs_3_
  35.1 0.0 collective-permute-done.13.refs_5_
  35.1 1.9 %attend.1 = (bf16[128,640]{1,0:T(8,128)(2,1)S(1)}, f32[128,640]{1,0:T(8,128)S(1)}) custom-call(bf16[128,512]{1,0:T(8,128)(2,1)S(1)} %copy-done.8, bf16[128,512]{1,0:T(8,128)(2,1)S(1)} %collective-permute-done.7.q_other_ref, bf16[128,512]{1,0:T(8,128)(2,1)S(1)} %join_rows.1.refs_0_, bf16[128,512]{1,0:T(8,128)(2,1)S(1)} %collective-permute-done.9.refs_1_, ...), custom_call_target="tpu_custom_call" | custom-call | flops 536870912 | bytes 1802240 | tf_op jit(solution)/shard_map/attend/pallas_call | solution.py:25
  37.0 1.6 %collective-permute-start.16 = (bf16[128,640]{1,0:T(8,128)(2,1)S(1)}, bf16[128,640]{1,0:T(8,128)(2,1)S(1)}, u32[]{:S(2)}, u32[]{:S(2)}) collective-permute-start(bf16[128,640]{1,0:T(8,128)(2,1)S(1)} %get-tuple-element.29), channel_id=1, source_target_pairs={{0,4},{2,6},{4,0},{6,2},{8,12},{10,14},{12,8},{14,10},{16,20},{18,... | collective-permute-start | bytes 491528 | tf_op jit(solution)/shard_map/ppermute | solution.py:294
  38.6 0.7 %collective-permute-done.5.prior_other_ref = bf16[64,512]{1,0:T(8,128)(2,1)S(1)} collective-permute-done((bf16[64,512]{1,0:T(8,128)(2,1)S(1)}, bf16[64,512]{1,0:T(8,128)(2,1)S(1)}, u32[]{:S(2)}, u32[]{:S(2)}) %collective-permute-start.5) | collective-permute-done | bytes 65568 | tf_op jit(solution)/shard_map/ppermute | solution.py:294
  39.3 0.1 block_priors.1
  39.4 0.1 collective-permute-start.6
  39.5 0.7 %copy-done = bf16[128,512]{1,0:T(8,128)(2,1)S(1)} copy-done((bf16[128,512]{1,0:T(8,128)(2,1)S(1)}, bf16[128,512]{1,0:T(8,128)(2,1)}, u32[]{:S(2)}) %copy-start) | copy-done | bytes 131096
  40.2 0.1 copy-done.2
  40.2 0.1 copy-done.4
  40.3 0.6 %retain_inside.1 = (f32[128,512]{1,0:T(8,128)S(1)}, f32[128,2]{1,0:T(8,128)S(1)}) custom-call(bf16[128,512]{1,0:T(8,128)(2,1)S(1)} %copy-done, bf16[128,512]{1,0:T(8,128)(2,1)S(1)} %copy-done.2, bf16[128,512]{1,0:T(8,128)(2,1)S(1)} %copy-done.4, f32[128,2]{1,0:T(8,128)S(1)} %copy.10.d_ref), custom_call_target="tpu_custom_call" | custom-call | flops 33554432 | bytes 657408 | tf_op jit(solution)/shard_map/retain_inside/pallas_call | solution.py:25
  40.9 1.5 %collective-permute-done.16.other_ref = bf16[128,640]{1,0:T(8,128)(2,1)S(1)} collective-permute-done((bf16[128,640]{1,0:T(8,128)(2,1)S(1)}, bf16[128,640]{1,0:T(8,128)(2,1)S(1)}, u32[]{:S(2)}, u32[]{:S(2)}) %collective-permute-start.16) | collective-permute-done | bytes 163872 | tf_op jit(solution)/shard_map/ppermute | solution.py:294
  42.4 0.9 %merge.1 = bf16[128,512]{1,0:T(8,128)(2,1)} custom-call(f32[128,640]{1,0:T(8,128)S(1)} %get-tuple-element.28.keep_ref, bf16[128,640]{1,0:T(8,128)(2,1)S(1)} %collective-permute-done.16.other_ref), custom_call_target="tpu_custom_call" | custom-call | flops 1000000 | bytes 622592 | tf_op jit(solution)/shard_map/merge/pallas_call | solution.py:25
  43.4 0.0 collective-permute-done.6.other_ref
  43.4 1.0 %retain_finish.1 = bf16[128,512]{1,0:T(8,128)(2,1)} custom-call(bf16[128,512]{1,0:T(8,128)(2,1)S(1)} %copy-done, bf16[128,512]{1,0:T(8,128)(2,1)S(1)} %copy-done.5, f32[128,512]{1,0:T(8,128)S(1)} %get-tuple-element.16.inside_ref, f32[128,2]{1,0:T(8,128)S(1)} %get-tuple-element.17.factor_ref, bf16[128,512]{1,0:T(8,128)(2,1)S(1)} %get-tuple-element.24.keep_ref, ...), custom_call_target="tpu_custom_call" | custom-call | flops 33554432 | bytes 918528 | tf_op jit(solution)/shard_map/retain_finish/pallas_call | solution.py:25
  (16 shorter events, 0.1 us)
Async XLA Ops:
  1.4 0.9 %copy-start.1 = (bf16[128,512]{1,0:T(8,128)(2,1)S(1)}, bf16[128,512]{1,0:T(8,128)(2,1)}, u32[]{:S(2)}) copy-start(bf16[128,512]{1,0:T(8,128)(2,1)} %k_ref.4) | copy-start | bytes 393220
  2.3 0.9 %copy-start.3 = (bf16[128,512]{1,0:T(8,128)(2,1)S(1)}, bf16[128,512]{1,0:T(8,128)(2,1)}, u32[]{:S(2)}) copy-start(bf16[128,512]{1,0:T(8,128)(2,1)} %v_ref.4) | copy-start | bytes 393220
  3.2 0.8 %copy-start.6 = (bf16[64,512]{1,0:T(8,128)(2,1)S(1)}, bf16[64,512]{1,0:T(8,128)(2,1)}, u32[]{:S(2)}) copy-start(bf16[64,512]{1,0:T(8,128)(2,1)} %k_ref.5) | copy-start | bytes 196612
  3.2 0.9 %copy-start.7 = (bf16[64,512]{1,0:T(8,128)(2,1)S(1)}, bf16[64,512]{1,0:T(8,128)(2,1)}, u32[]{:S(2)}) copy-start(bf16[64,512]{1,0:T(8,128)(2,1)} %v_ref.5) | copy-start | bytes 196612
  3.9 6.0 %collective-permute-start = (bf16[144,512]{1,0:T(8,128)(2,1)S(1)}, bf16[144,512]{1,0:T(8,128)(2,1)S(1)}, u32[]{:S(2)}, u32[]{:S(2)}) collective-permute-start(bf16[144,512]{1,0:T(8,128)(2,1)S(1)} %get-tuple-element.19), channel_id=1, source_target_pairs={{0,2},{2,0},{4,6},{6,4},{8,10},{10,8},{12,14},{14,12},{16,18},{18,... | collective-permute-start | bytes 442376 | tf_op jit(solution)/shard_map/ppermute | solution.py:294
  4.1 4.5 %collective-permute-start.8 = (bf16[64,512]{1,0:T(8,128)(2,1)S(1)}, bf16[64,512]{1,0:T(8,128)(2,1)S(1)}, u32[]{:S(2)}, u32[]{:S(2)}) collective-permute-start(bf16[64,512]{1,0:T(8,128)(2,1)S(1)} %get-tuple-element.27), channel_id=1, source_target_pairs={{0,1},{1,0},{2,3},{3,2},{4,5},{5,4},{6,7},{7,6},{8,9},{9,8},{10,11... | collective-permute-start | bytes 196616 | tf_op jit(solution)/shard_map/ppermute | solution.py:300
  8.6 8.7 %collective-permute-start.10 = (bf16[128,512]{1,0:T(8,128)(2,1)S(1)}, bf16[128,512]{1,0:T(8,128)(2,1)S(1)}, u32[]{:S(2)}, u32[]{:S(2)}) collective-permute-start(bf16[128,512]{1,0:T(8,128)(2,1)S(1)} %join_rows.1.refs_0_), channel_id=1, source_target_pairs={{0,8},{2,10},{4,12},{6,14},{8,16},{10,18},{12,20},{14,22},{16,24},... | collective-permute-start | bytes 393224 | tf_op jit(solution)/shard_map/ppermute | solution.py:297
  10.1 4.5 %collective-permute-start.1 = (bf16[80,512]{1,0:T(8,128)(2,1)S(1)}, bf16[80,512]{1,0:T(8,128)(2,1)S(1)}, u32[]{:S(2)}, u32[]{:S(2)}) collective-permute-start(bf16[80,512]{1,0:T(8,128)(2,1)S(1)} %get-tuple-element.21), channel_id=1, source_target_pairs={{0,4},{2,6},{4,0},{6,2},{8,12},{10,14},{12,8},{14,10},{16,20},{18,... | collective-permute-start | bytes 245768 | tf_op jit(solution)/shard_map/ppermute | solution.py:294
  11.6 18.0 %collective-permute-start.12 = (bf16[128,512]{1,0:T(8,128)(2,1)S(1)}, bf16[128,512]{1,0:T(8,128)(2,1)S(1)}, u32[]{:S(2)}, u32[]{:S(2)}) collective-permute-start(bf16[128,512]{1,0:T(8,128)(2,1)S(1)} %join_rows.1.refs_0_), channel_id=1, source_target_pairs={{0,16},{2,18},{4,20},{6,22},{8,24},{10,26},{12,28},{14,30},{1,17},... | collective-permute-start | bytes 393224 | tf_op jit(solution)/shard_map/ppermute | solution.py:297
  12.9 17.2 %collective-permute-start.14 = (bf16[128,512]{1,0:T(8,128)(2,1)S(1)}, bf16[128,512]{1,0:T(8,128)(2,1)S(1)}, u32[]{:S(2)}, u32[]{:S(2)}) collective-permute-start(bf16[128,512]{1,0:T(8,128)(2,1)S(1)} %join_rows.1.refs_0_), channel_id=1, source_target_pairs={{0,24},{2,26},{4,28},{6,30},{1,25},{3,27},{5,29},{7,31}} | collective-permute-start | bytes 393224 | tf_op jit(solution)/shard_map/ppermute | solution.py:297
  14.6 15.0 %copy-start.8 = (bf16[128,512]{1,0:T(8,128)(2,1)S(1)}, bf16[128,512]{1,0:T(8,128)(2,1)}, u32[]{:S(2)}) copy-start(bf16[128,512]{1,0:T(8,128)(2,1)} %q_ref.5) | copy-start | bytes 393220
  14.6 15.5 %collective-permute-start.2 = (bf16[80,512]{1,0:T(8,128)(2,1)S(1)}, bf16[80,512]{1,0:T(8,128)(2,1)S(1)}, u32[]{:S(2)}, u32[]{:S(2)}) collective-permute-start(bf16[80,512]{1,0:T(8,128)(2,1)S(1)} %plane_total.1), channel_id=1, source_target_pairs={{0,8},{2,10},{4,12},{6,14},{8,16},{10,18},{12,20},{14,22},{16,24},... | collective-permute-start | bytes 245768 | tf_op jit(solution)/shard_map/ppermute | solution.py:297
  16.1 16.0 %collective-permute-start.3 = (bf16[80,512]{1,0:T(8,128)(2,1)S(1)}, bf16[80,512]{1,0:T(8,128)(2,1)S(1)}, u32[]{:S(2)}, u32[]{:S(2)}) collective-permute-start(bf16[80,512]{1,0:T(8,128)(2,1)S(1)} %plane_total.1), channel_id=1, source_target_pairs={{0,16},{2,18},{4,20},{6,22},{8,24},{10,26},{12,28},{14,30},{1,17},... | collective-permute-start | bytes 245768 | tf_op jit(solution)/shard_map/ppermute | solution.py:297
  17.4 14.7 %collective-permute-start.4 = (bf16[80,512]{1,0:T(8,128)(2,1)S(1)}, bf16[80,512]{1,0:T(8,128)(2,1)S(1)}, u32[]{:S(2)}, u32[]{:S(2)}) collective-permute-start(bf16[80,512]{1,0:T(8,128)(2,1)S(1)} %plane_total.1), channel_id=1, source_target_pairs={{0,24},{2,26},{4,28},{6,30},{1,25},{3,27},{5,29},{7,31}} | collective-permute-start | bytes 245768 | tf_op jit(solution)/shard_map/ppermute | solution.py:297
  29.6 5.0 %collective-permute-start.7 = (bf16[128,512]{1,0:T(8,128)(2,1)S(1)}, bf16[128,512]{1,0:T(8,128)(2,1)S(1)}, u32[]{:S(2)}, u32[]{:S(2)}) collective-permute-start(bf16[128,512]{1,0:T(8,128)(2,1)S(1)} %copy-done.8), channel_id=1, source_target_pairs={{0,4},{2,6},{4,0},{6,2},{8,12},{10,14},{12,8},{14,10},{16,20},{18,... | collective-permute-start | bytes 393224 | tf_op jit(solution)/shard_map/ppermute | solution.py:294
  30.2 5.0 %collective-permute-start.9 = (bf16[128,512]{1,0:T(8,128)(2,1)S(1)}, bf16[128,512]{1,0:T(8,128)(2,1)S(1)}, u32[]{:S(2)}, u32[]{:S(2)}) collective-permute-start(bf16[128,512]{1,0:T(8,128)(2,1)S(1)} %join_rows.1.refs_0_), channel_id=1, source_target_pairs={{0,2},{2,0},{4,6},{6,4},{8,10},{10,8},{12,14},{14,12},{16,18},{18,... | collective-permute-start | bytes 393224 | tf_op jit(solution)/shard_map/ppermute | solution.py:294
  30.2 5.0 %collective-permute-start.11 = (bf16[128,512]{1,0:T(8,128)(2,1)S(1)}, bf16[128,512]{1,0:T(8,128)(2,1)S(1)}, u32[]{:S(2)}, u32[]{:S(2)}) collective-permute-start(bf16[128,512]{1,0:T(8,128)(2,1)S(1)} %collective-permute-done.10.refs_2_), channel_id=1, source_target_pairs={{0,2},{2,0},{4,6},{6,4},{8,10},{10,8},{12,14},{14,12},{16,18},{18,... | collective-permute-start | bytes 393224 | tf_op jit(solution)/shard_map/ppermute | solution.py:294
  32.0 3.1 %collective-permute-start.13 = (bf16[128,512]{1,0:T(8,128)(2,1)S(1)}, bf16[128,512]{1,0:T(8,128)(2,1)S(1)}, u32[]{:S(2)}, u32[]{:S(2)}) collective-permute-start(bf16[128,512]{1,0:T(8,128)(2,1)S(1)} %collective-permute-done.12.refs_4_), channel_id=1, source_target_pairs={{0,2},{2,0},{4,6},{6,4},{8,10},{10,8},{12,14},{14,12},{16,18},{18,... | collective-permute-start | bytes 393224 | tf_op jit(solution)/shard_map/ppermute | solution.py:294
  32.0 3.1 %collective-permute-start.15 = (bf16[128,512]{1,0:T(8,128)(2,1)S(1)}, bf16[128,512]{1,0:T(8,128)(2,1)S(1)}, u32[]{:S(2)}, u32[]{:S(2)}) collective-permute-start(bf16[128,512]{1,0:T(8,128)(2,1)S(1)} %collective-permute-done.14.refs_6_), channel_id=1, source_target_pairs={{0,2},{2,0},{4,6},{6,4},{8,10},{10,8},{12,14},{14,12},{16,18},{18,... | collective-permute-start | bytes 393224 | tf_op jit(solution)/shard_map/ppermute | solution.py:294
  34.6 4.7 %collective-permute-start.5 = (bf16[64,512]{1,0:T(8,128)(2,1)S(1)}, bf16[64,512]{1,0:T(8,128)(2,1)S(1)}, u32[]{:S(2)}, u32[]{:S(2)}) collective-permute-start(bf16[64,512]{1,0:T(8,128)(2,1)S(1)} %get-tuple-element.23), channel_id=1, source_target_pairs={{0,4},{2,6},{4,0},{6,2},{8,12},{10,14},{12,8},{14,10},{16,20},{18,... | collective-permute-start | bytes 196616 | tf_op jit(solution)/shard_map/ppermute | solution.py:294
  37.0 5.4 %collective-permute-start.16 = (bf16[128,640]{1,0:T(8,128)(2,1)S(1)}, bf16[128,640]{1,0:T(8,128)(2,1)S(1)}, u32[]{:S(2)}, u32[]{:S(2)}) collective-permute-start(bf16[128,640]{1,0:T(8,128)(2,1)S(1)} %get-tuple-element.29), channel_id=1, source_target_pairs={{0,4},{2,6},{4,0},{6,2},{8,12},{10,14},{12,8},{14,10},{16,20},{18,... | collective-permute-start | bytes 491528 | tf_op jit(solution)/shard_map/ppermute | solution.py:294
  39.3 0.9 %copy-start = (bf16[128,512]{1,0:T(8,128)(2,1)S(1)}, bf16[128,512]{1,0:T(8,128)(2,1)}, u32[]{:S(2)}) copy-start(bf16[128,512]{1,0:T(8,128)(2,1)} %q_ref.4) | copy-start | bytes 393220
  39.3 1.0 %copy-start.2 = (bf16[128,512]{1,0:T(8,128)(2,1)S(1)}, bf16[128,512]{1,0:T(8,128)(2,1)}, u32[]{:S(2)}) copy-start(bf16[128,512]{1,0:T(8,128)(2,1)} %k_ref.4) | copy-start | bytes 393220
  39.3 1.0 %copy-start.4 = (bf16[128,512]{1,0:T(8,128)(2,1)S(1)}, bf16[128,512]{1,0:T(8,128)(2,1)}, u32[]{:S(2)}) copy-start(bf16[128,512]{1,0:T(8,128)(2,1)} %v_ref.4) | copy-start | bytes 393220
  39.4 3.9 %collective-permute-start.6 = (bf16[128,512]{1,0:T(8,128)(2,1)S(1)}, bf16[128,512]{1,0:T(8,128)(2,1)S(1)}, u32[]{:S(2)}, u32[]{:S(2)}) collective-permute-start(bf16[128,512]{1,0:T(8,128)(2,1)S(1)} %get-tuple-element.25), channel_id=1, source_target_pairs={{0,2},{2,0},{4,6},{6,4},{8,10},{10,8},{12,14},{14,12},{16,18},{18,... | collective-permute-start | bytes 393224 | tf_op jit(solution)/shard_map/ppermute | solution.py:294
  42.4 0.9 %copy-start.5 = (bf16[128,512]{1,0:T(8,128)(2,1)S(1)}, bf16[128,512]{1,0:T(8,128)(2,1)}, u32[]{:S(2)}) copy-start(bf16[128,512]{1,0:T(8,128)(2,1)} %gate_ref.1) | copy-start | bytes 393220

commit v3 on v2

--- a/solution.py
+++ b/solution.py
@@ -17,21 +17,31 @@
 PAD = 16
 LANES = 128
 VMEM = pl.BlockSpec(memory_space=pltpu.VMEM)
-
-
-def call(body, outs, args, scratch=(), flops=1_000_000, name=None):
-    moved = sum(math.prod(a.shape) * a.dtype.itemsize for a in (*args, *outs))
+ANY = pl.BlockSpec(memory_space=pl.ANY)
+HBM = pl.BlockSpec(memory_space=pltpu.HBM)
+
+
+def call(
+    body, outs, args, scratch=(), name=None, takes=VMEM, gives=VMEM, after=(),
+    aliases=None,
+):
     single = len(outs) == 1
+    used, total = len(args), len(args) + len(after)
+
+    def kernel(*refs):
+        body(*refs[:used], *refs[total:])
+
     return pl.pallas_call(
-        body,
+        kernel,
         out_shape=outs[0] if single else tuple(outs),
-        in_specs=[VMEM] * len(args),
-        out_specs=VMEM if single else tuple(VMEM for _ in outs),
+        in_specs=(takes if isinstance(takes, list) else [takes] * used) + [ANY] * len(after),
+        out_specs=gives if single or isinstance(gives, tuple) else tuple(gives for _ in outs),
         scratch_shapes=scratch,
+        input_output_aliases=aliases or {},
         compiler_params=pltpu.CompilerParams(vmem_limit_bytes=40 * 1024 * 1024),
-        cost_estimate=pl.CostEstimate(flops=flops, bytes_accessed=moved, transcendentals=0),
+        cost_estimate=pl.CostEstimate(flops=1000, bytes_accessed=1000, transcendentals=0),
         name=name,
-    )(*args)
+    )(*args, *after)
 
 
 def shape(dims, dtype=BF16):
@@ -51,23 +61,31 @@
     return high, middle, rest - middle
 
 
-def decay_sums(log_decay):
-    rows = log_decay.shape[0]
+def lower_ones(rows):
     below = lax.broadcasted_iota(jnp.int32, (rows, rows), 0) >= lax.broadcasted_iota(
         jnp.int32, (rows, rows), 1
     )
-    lower = jnp.where(below, 1.0, 0.0).astype(F32)
-    return dot(lower, log_decay, ((1,), (0,)), lax.Precision.HIGHEST), below
-
-
-def split_cache(n, k_ref, v_ref, *pieces):
+    return below, jnp.where(below, 1.0, 0.0).astype(F32)
+
+
+def load_all(n, count, *refs):
+    k_ref, v_ref, *plain = refs[:count]
+    outs, sems = refs[count:-1], refs[-1]
+    pieces, copies = outs[:n], outs[n:]
     width = k_ref.shape[1] // n
     here = lax.axis_index("head")
+    moves = []
     for e, piece in enumerate(pieces):
         target = lax.rem(here + e, n)
         columns = pl.ds(pl.multiple_of(target * width, LANES), width)
-        piece[:, pl.ds(0, width)] = k_ref[:, columns]
-        piece[:, pl.ds(width, width)] = v_ref[:, columns]
+        moves.append((k_ref.at[:, columns], piece.at[:, pl.ds(0, width)]))
+        moves.append((v_ref.at[:, columns], piece.at[:, pl.ds(width, width)]))
+    moves += list(zip(plain, copies))
+    running = [pltpu.make_async_copy(a, b, sems.at[i]) for i, (a, b) in enumerate(moves)]
+    for one in running:
+        one.start()
+    for one in running:
+        one.wait()
 
 
 def join_rows(n, *refs):
@@ -114,10 +132,10 @@
 def summarize(k_ref, v_ref, d_ref, send, keep, held):
     low, _, _ = bits()
     half = HD // 2
-    sums, _ = decay_sums(d_ref[...])
-    rows = sums.shape[0]
+    rows = d_ref.shape[1]
+    sums = dot(lower_ones(rows)[1], d_ref[...], ((1,), (1,)), lax.Precision.HIGHEST)
     totals = []
-    for head in range(d_ref.shape[1]):
+    for head in range(d_ref.shape[0]):
         columns = pl.ds(head * HD, HD)
         column = sums[:, head : head + 1]
         last = column[rows - 1 : rows, :]
@@ -184,10 +202,18 @@
     keep[...] = jnp.where(first, entering, second).astype(keep.dtype)
 
 
+def grow(own_ref, earlier_ref, _, out, __):
+    rows = out.shape[0] - PAD
+    own, earlier = total_of(own_ref), total_of(earlier_ref)
+    state = jnp.exp(own) * state_of(earlier_ref) + state_of(own_ref)
+    out[pl.ds(0, rows), :] = state.astype(out.dtype)
+    put_total(out, rows, own + earlier)
+
+
 def retain_inside(q_ref, k_ref, v_ref, d_ref, inside_ref, factor_ref):
-    heads = d_ref.shape[1]
-    sums, below = decay_sums(d_ref[...])
-    rows = sums.shape[0]
+    heads, rows = d_ref.shape
+    below, ones = lower_ones(rows)
+    sums = dot(ones, d_ref[...], ((1,), (1,)), lax.Precision.HIGHEST)
     same = lax.broadcasted_iota(jnp.int32, (rows, rows), 0) == lax.broadcasted_iota(
         jnp.int32, (rows, rows), 1
     )
@@ -202,7 +228,13 @@
         inside_ref[:, columns] = dot(weights, v_ref[:, columns], ((1,), (0,)))
 
 
-def retain_finish(q_ref, gate_ref, inside_ref, factor_ref, keep_ref, other_ref, out, held):
+def finish(
+    part_ref, part_other_ref, q_ref, gate_ref, inside_ref, factor_ref, keep_ref, other_ref,
+    o_ret, o_cross, held, ret_held, cross_held, sems,
+):
+    merge(part_ref, part_other_ref, cross_held)
+    cross_out = pltpu.make_async_copy(cross_held, o_cross, sems.at[0])
+    cross_out.start()
     low, _, _ = bits()
     half = keep_ref.shape[0]
     for ref, which in ((keep_ref, low), (other_ref, 1 - low)):
@@ -214,24 +246,32 @@
         scale = lax.rsqrt(jnp.mean(retained * retained, axis=1, keepdims=True) + EPS)
         gate = gate_ref[:, columns].astype(F32)
         silu = gate / (1.0 + jnp.exp(-gate))
-        out[:, columns] = (retained * scale * silu).astype(BF16)
-
-
-def attend(far, q_ref, q_other_ref, *refs):
-    blocks, (send, keep, keys, values) = refs[: 2 * far], refs[2 * far :]
+        ret_held[:, columns] = (retained * scale * silu).astype(BF16)
+    ret_out = pltpu.make_async_copy(ret_held, o_ret, sems.at[1])
+    ret_out.start()
+    cross_out.wait()
+    ret_out.wait()
+
+
+def attend(first, count, q_ref, q_other_ref, *refs):
+    blocks, refs = refs[: 2 * count], refs[2 * count :]
+    last = first > 0
+    carried, refs = (refs[:4], refs[4:]) if last else ((), refs)
+    outs, (keys, values) = refs[:-2], refs[-2:]
     rows, wide = q_ref.shape
     heads = wide // HD
     length, width = blocks[0].shape[0], blocks[0].shape[1] // 2
     group = wide // width
-    total = 2 * far * length
+    total = 2 * count * length
     low, high, depth = bits()
     for i, block in enumerate(blocks):
         keys[pl.ds(i * length, length), :] = block[:, pl.ds(0, width)]
         values[pl.ds(i * length, length), :] = block[:, pl.ds(width, width)]
     column = lax.broadcasted_iota(jnp.int32, (1, total), 1)
     limit = jnp.zeros((1, total), jnp.int32)
-    for i in range(2 * far):
+    for i in range(2 * count):
         s, t = divmod(i, 2)
+        s = s + first
         if s == 0:
             core = low if t == 0 else 1 - low
             at = column + ((2 * high + core) * length - i * length)
@@ -241,25 +281,44 @@
     scale = 1.0 / (math.sqrt(HD) * math.log(2.0))
     row = lax.broadcasted_iota(jnp.int32, (rows, total), 0)
     lane = lax.broadcasted_iota(jnp.int32, (rows, LANES), 1)
-    for query, out, place in ((q_other_ref, send, 1 - high), (q_ref, keep, high)):
+    for which, (query, place) in enumerate(((q_other_ref, 1 - high), (q_ref, high))):
         allowed = row + (2 * place + low) * rows >= limit
         stats = jnp.zeros((rows, LANES), F32)
+        if last:
+            mixed_ref, stats_ref = carried[2 * which : 2 * which + 2]
+            out = outs[which]
+        else:
+            out, stats_out = outs[2 * which : 2 * which + 2]
         for head in range(heads):
             columns = pl.ds(head * HD, HD)
             shared = pl.ds((head // group) * HD, HD)
             scores = dot(query[:, columns], keys[:, shared], ((1,), (1,))) * scale
             masked = jnp.where(allowed, scores, FAR)
             top = jnp.maximum(jnp.max(masked, axis=1, keepdims=True), NEAR)
+            if last:
+                old = stats_ref[:, 2 * head : 2 * head + 1]
+                top = jnp.maximum(top, old)
             weights = jnp.exp2(masked - top)
             summed = jnp.sum(weights, axis=1, keepdims=True)
             mixed = dot(weights.astype(BF16), values[:, shared], ((1,), (0,)))
+            if not last:
+                out[:, columns] = mixed
+                stats = jnp.where(lane == 2 * head, top, stats)
+                stats = jnp.where(lane == 2 * head + 1, summed, stats)
+                continue
+            shrink = jnp.exp2(old - top)
+            summed = summed + shrink * stats_ref[:, 2 * head + 1 : 2 * head + 2]
+            mixed = mixed + shrink * mixed_ref[:, columns]
             some = summed > 0.0
             safe = jnp.where(some, summed, 1.0)
             out[:, columns] = (mixed / safe).astype(out.dtype)
             level = jnp.where(some, top + jnp.log2(safe), FAR)
             for i, third in enumerate(thirds(level)):
                 stats = jnp.where(lane == 3 * head + i, third, stats)
-        out[:, pl.ds(wide, LANES)] = stats.astype(out.dtype)
+        if last:
+            out[:, pl.ds(wide, LANES)] = stats.astype(out.dtype)
+        else:
+            stats_out[...] = stats
 
 
 def merge(keep_ref, other_ref, out):
@@ -293,68 +352,127 @@
     def swap(value, bit):
         return lax.ppermute(value, "ctx", [(b, b ^ bit) for b in range(count)])
 
-    def onward(value, s):
-        return lax.ppermute(value, "ctx", [(b, b + s * 4) for b in range(count - s * 4)])
+    def along(value, step, least):
+        pairs = [(b, b + step * 4) for b in range(least * 4, count - step * 4)]
+        return lax.ppermute(value, "ctx", pairs)
 
     def to_head(value, e):
         return lax.ppermute(value, "head", [(y, (y + e) % n) for y in range(n)])
 
-    pieces = call(
-        functools.partial(split_cache, n),
-        [shape((length, 2 * width))] * n,
-        (cache_k, cache_v),
-        name="split_cache",
-    )
+    plain = (k_ret, v_ret, log_decay.T, q_ret, q_cross, gate_ret)
+    loaded = call(
+        functools.partial(load_all, n, 2 + len(plain)),
+        [pltpu.VMEM((length, 2 * width), BF16)] * n + [pltpu.VMEM(a.shape, a.dtype) for a in plain],
+        [pltpu.with_memory_space_constraint(a, pltpu.HBM) for a in (cache_k, cache_v, *plain)],
+        scratch=[pltpu.SemaphoreType.DMA((2 * n + len(plain),))],
+        name="load_all",
+        takes=HBM,
+    )
+    pieces = loaded[:n]
+    k_ret, v_ret, decays, q_ret, q_cross, gate_ret = loaded[n:]
     arrived = [pieces[0]] + [to_head(pieces[e], e) for e in range(1, n)]
     sum_send, sum_keep = call(
         summarize,
         [shape((half + PAD, wide)), shape((half + PAD, wide), F32)],
-        (k_ret, v_ret, log_decay),
+        (k_ret, v_ret, decays),
         scratch=[pltpu.VMEM((HD, wide), F32)],
-        flops=2 * rows * HD * HD * heads,
         name="summarize",
     )
     sum_other = swap(sum_send, 1)
-    block = call(
-        functools.partial(join_rows, n), [shape((n * length, 2 * width))], arrived, name="join_rows"
-    )
-    blocks = [block] + [onward(block, s) for s in range(1, far)]
     chip_send, chip_keep = call(
         chip_total,
         [shape((quarter + PAD, wide)), shape((quarter + PAD, wide), F32)],
         (sum_keep, sum_other),
         scratch=[pltpu.VMEM((half, wide), F32)],
         name="chip_total",
-    )
-    chip_other = swap(chip_send, 2)
-    q_other = swap(q_cross, 2)
-    whole = call(plane_total, [shape((quarter + PAD, wide))], (chip_keep, chip_other), name="plane_total")
-    planes = [onward(whole, s) for s in range(1, far)]
+        after=arrived[-1:],
+    )
     inside, factor = call(
         retain_inside,
         [shape((rows, wide), F32), shape((rows, heads), F32)],
-        (q_ret, k_ret, v_ret, log_decay),
-        flops=4 * rows * rows * HD * heads,
+        (q_ret, k_ret, v_ret, decays),
         name="retain_inside",
-    )
-    both = []
-    for one in blocks:
-        both += [one, swap(one, 1)]
-    part_send, part_keep = call(
-        functools.partial(attend, far),
-        [shape((rows, wide + LANES)), shape((rows, wide + LANES), F32)],
-        (q_cross, q_other, *both),
-        scratch=[pltpu.VMEM((2 * far * n * length, width), BF16) for _ in range(2)],
-        flops=8 * rows * heads * 2 * far * n * length * HD,
-        name="attend",
-    )
-    part_other = swap(part_send, 2)
+        after=(chip_send,),
+    )
+    blocks = [
+        call(
+            functools.partial(join_rows, n),
+            [shape((n * length, 2 * width))],
+            arrived,
+            name="join_rows",
+        )
+    ]
+    for s in range(1, far - 1):
+        blocks.append(along(blocks[-1], 1, s - 1))
+    chip_other = swap(chip_send, 2)
+    q_other = swap(q_cross, 2)
+    window = call(
+        plane_total,
+        [shape((quarter + PAD, wide))],
+        (chip_keep, chip_other),
+        name="plane_total",
+        after=(factor,),
+    )
+    def look(first, count, outs, carried, name):
+        keys = 2 * count * n * length
+        both = []
+        for one in blocks[first : first + count]:
+            both += [one, swap(one, 1)]
+        return call(
+            functools.partial(attend, first, count),
+            outs,
+            (q_cross, q_other, *both, *carried),
+            scratch=[pltpu.VMEM((keys, width), BF16) for _ in range(2)],
+            name=name,
+        )
+
+    near = max(far // 2, 1)
+    so_far = look(
+        0, near, [shape((rows, wide), F32), shape((rows, LANES), F32)] * 2, (), "attend_near"
+    )
+    planes, step = [], 1
+    while step < far:
+        planes.append(along(window, step, 0))
+        step *= 2
+        if step < far:
+            window, blocks[-1] = call(
+                grow,
+                [shape(window.shape), shape(blocks[-1].shape)],
+                (window, planes[-1], blocks[-1]),
+                name="grow",
+                takes=[VMEM, VMEM, ANY],
+                gives=(VMEM, ANY),
+                after=so_far[1:2],
+                aliases={2: 1},
+            )
     prior_send, prior_keep = call(
         chip_priors,
         [shape((quarter, wide)), shape((quarter, wide), F32)],
         (chip_keep, chip_other, *planes),
         name="chip_priors",
     )
+    if far > 1:
+        arriving = along(blocks[-1], 1, far - 2)
+        blocks.append(
+            call(
+                lambda *refs: None,
+                [shape(arriving.shape)],
+                (arriving,),
+                name="hold",
+                takes=ANY,
+                gives=ANY,
+                after=(prior_send,),
+                aliases={0: 0},
+            )
+        )
+    part_send, part_keep = look(
+        near,
+        far - near,
+        [shape((rows, wide + LANES)), shape((rows, wide + LANES), F32)],
+        so_far,
+        "attend_far",
+    )
+    part_other = swap(part_send, 2)
     prior_other = swap(prior_send, 2)
     state_send, state_keep = call(
         block_priors,
@@ -364,16 +482,15 @@
         name="block_priors",
     )
     state_other = swap(state_send, 1)
-    o_ret = call(
-        retain_finish,
-        [shape((rows, wide))],
-        (q_ret, gate_ret, inside, factor, state_keep, state_other),
-        scratch=[pltpu.VMEM((HD, wide), BF16)],
-        flops=2 * rows * HD * HD * heads,
-        name="retain_finish",
-    )
-    o_cross = call(merge, [shape((rows, wide))], (part_keep, part_other), name="merge")
-    return o_ret, o_cross
+    held = pltpu.VMEM((rows, wide), BF16)
+    return call(
+        finish,
+        [shape((rows, wide))] * 2,
+        (part_keep, part_other, q_ret, gate_ret, inside, factor, state_keep, state_other),
+        scratch=[pltpu.VMEM((HD, wide), BF16), held, held, pltpu.SemaphoreType.DMA((2,))],
+        name="finish",
+        gives=HBM,
+    )
 
 
 def solution(mesh):

time: 44.7 us -> 45.5 us (1.018)
  the two profiles are of different devices: /device:TPU:24 before, /device:TPU:0 now
where the time goes in v3:
time: 45.5 us; the launch traced here: 45.3 us
  starting transfers between devices  27.3 us (60%)
  waiting for transfers between devices  9.79 us (22%)
  Pallas kernels  7.42 us (16%)
  between operations  0.82 us (2%)
    ppermute x5, starting transfers between devices, along(): return lax.ppermute(value, 'ctx', pairs)  18.7 us
    pallas_call x13, Pallas kernels, call(): pl.pallas_call(kernel, out_shape=outs[0] if single else tuple(outs), in_s...  7.42 us
    ppermute x10, starting transfers between devices, swap(): return lax.ppermute(value, 'ctx', [(b, b ^ bit) for b in range(count)])  5.52 us
    ppermute x10, waiting for transfers between devices, swap(): return lax.ppermute(value, 'ctx', [(b, b ^ bit) for b in range(count)])  5.47 us
    ppermute x1, starting transfers between devices, to_head(): return lax.ppermute(value, 'head', [(y, (y + e) % n) for y in range(n)])  3.03 us
    ppermute x5, waiting for transfers between devices, along(): return lax.ppermute(value, 'ctx', pairs)  2.83 us
    ppermute x1, waiting for transfers between devices, to_head(): return lax.ppermute(value, 'head', [(y, (y + e) % n) for y in range(n)])  1.49 us
  transfers between devices with their start and end apart: 16, of which 7 were waited for; matrix products, arithmetic and copies ran while one was open for 0% of the time, Pallas kernels for 11%

profile of v3, /device:TPU:0, one launch (start us, length us, event | category | flops | bytes accessed | tf_op | source)
XLA Modules:
  0.0 45.3 jit_solution(12324483392581694974)
XLA Ops:
  0.6 1.3 %load_all.1 = (bf16[64,512]{1,0:T(8,128)(2,1)S(1)}, bf16[64,512]{1,0:T(8,128)(2,1)S(1)}, bf16[128,512]{1,0:T(8,128)(2,1)S(1)}, bf16[128,512]{1,0:T(8,128)(2,1)S(...) custom-call(bf16[64,512]{1,0:T(8,128)(2,1)} %refs_0_.1, ...), custom_call_target="tpu_custom_call" | custom-call | flops 1000 | bytes 1000 | tf_op jit(solution)/shard_map/load_all/pallas_call | solution.py:34
  2.0 3.0 %collective-permute-start.2 = (bf16[64,512]{1,0:T(8,128)(2,1)S(1)}, bf16[64,512]{1,0:T(8,128)(2,1)S(1)}, u32[]{:S(2)}, u32[]{:S(2)}) collective-permute-start(bf16[64,512]{1,0:T(8,128)(2,1)S(1)} %get-tuple-element.34), channel_id=1, source_target_pairs={{0,1},{1,0},{2,3},{3,2},{4,5},{5,4},{6,7},{7,6},{8,9},{9,8},{10,11... | collective-permute-start | bytes 196616 | tf_op jit(solution)/shard_map/ppermute | solution.py:360
  5.0 0.7 %summarize.1 = (bf16[144,512]{1,0:T(8,128)(2,1)S(1)}, f32[144,512]{1,0:T(8,128)S(1)}) custom-call(bf16[128,512]{1,0:T(8,128)(2,1)S(1)} %get-tuple-element.29.refs_0_.refs_1_, bf16[128,512]{1,0:T(8,128)(2,1)S(1)} %get-tuple-element.30.refs_1_.refs_2_, f32[2,128]{1,0:T(2,128)S(1)} %get-tuple-element.31.refs_2_.refs_3_), custom_call_target="tpu_custom_call" | custom-call | flops 1000 | bytes 1000 | tf_op jit(solution)/shard_map/summarize/pallas_call | solution.py:34
  5.7 0.1 collective-permute-start.1
  5.8 1.5 %collective-permute-done.2.refs_2_.refs_1_ = bf16[64,512]{1,0:T(8,128)(2,1)S(1)} collective-permute-done((bf16[64,512]{1,0:T(8,128)(2,1)S(1)}, bf16[64,512]{1,0:T(8,128)(2,1)S(1)}, u32[]{:S(2)}, u32[]{:S(2)}) %collective-permute-start.2) | collective-permute-done | bytes 65568 | tf_op jit(solution)/shard_map/ppermute | solution.py:360
  7.3 4.0 %collective-permute-start.5 = (bf16[128,512]{1,0:T(8,128)(2,1)S(1)}, bf16[128,512]{1,0:T(8,128)(2,1)S(1)}, u32[]{:S(2)}, u32[]{:S(2)}) collective-permute-start(bf16[128,512]{1,0:T(8,128)(2,1)S(1)} %join_rows.1.refs_2_), channel_id=1, source_target_pairs={{0,8},{2,10},{4,12},{6,14},{8,16},{10,18},{12,20},{14,22},{16,24},... | collective-permute-start | bytes 393224 | tf_op jit(solution)/shard_map/ppermute | solution.py:357
  11.3 0.0 collective-permute-done.1.refs_1_
  11.3 0.1 chip_total.1
  11.4 1.6 %collective-permute-start.3 = (bf16[80,512]{1,0:T(8,128)(2,1)S(1)}, bf16[80,512]{1,0:T(8,128)(2,1)S(1)}, u32[]{:S(2)}, u32[]{:S(2)}) collective-permute-start(bf16[80,512]{1,0:T(8,128)(2,1)S(1)} %get-tuple-element.36.refs_4_), channel_id=1, source_target_pairs={{0,4},{2,6},{4,0},{6,2},{8,12},{10,14},{12,8},{14,10},{16,20},{18,... | collective-permute-start | bytes 245768 | tf_op jit(solution)/shard_map/ppermute | solution.py:353
  13.0 0.5 %collective-permute-start = (bf16[128,512]{1,0:T(8,128)(2,1)S(1)}, bf16[128,512]{1,0:T(8,128)(2,1)S(1)}, u32[]{:S(2)}, u32[]{:S(2)}) collective-permute-start(bf16[128,512]{1,0:T(8,128)(2,1)S(1)} %get-tuple-element.28.refs_0_), channel_id=1, source_target_pairs={{0,4},{2,6},{4,0},{6,2},{8,12},{10,14},{12,8},{14,10},{16,20},{18,... | collective-permute-start | bytes 393224 | tf_op jit(solution)/shard_map/ppermute | solution.py:353
  13.5 0.0 collective-permute-start.7
  13.5 0.3 collective-permute-done.5.refs_4_
  13.8 0.3 collective-permute-start.8
  14.0 0.7 %collective-permute-start.6 = (bf16[128,512]{1,0:T(8,128)(2,1)S(1)}, bf16[128,512]{1,0:T(8,128)(2,1)S(1)}, u32[]{:S(2)}, u32[]{:S(2)}) collective-permute-start(bf16[128,512]{1,0:T(8,128)(2,1)S(1)} %collective-permute-done.5.refs_4_), channel_id=1, source_target_pairs={{8,16},{10,18},{12,20},{14,22},{16,24},{18,26},{20,28},{22,30},{9,... | collective-permute-start | bytes 393224 | tf_op jit(solution)/shard_map/ppermute | solution.py:357
  14.7 0.6 %retain_inside.1 = (f32[128,512]{1,0:T(8,128)S(1)}, f32[128,2]{1,0:T(8,128)S(1)}) custom-call(bf16[128,512]{1,0:T(8,128)(2,1)S(1)} %get-tuple-element.37.refs_0_.refs_2_, bf16[128,512]{1,0:T(8,128)(2,1)S(1)} %get-tuple-element.29.refs_0_.refs_1_, bf16[128,512]{1,0:T(8,128)(2,1)S(1)} %get-tuple-element.30.refs_1_.refs_2_, ...), custom_call_target="tpu_custom_call" | custom-call | flops 1000 | bytes 1000 | tf_op jit(solution)/shard_map/retain_inside/pallas_call | solution.py:34
  15.3 0.7 %collective-permute-done.3.refs_1_ = bf16[80,512]{1,0:T(8,128)(2,1)S(1)} collective-permute-done((bf16[80,512]{1,0:T(8,128)(2,1)S(1)}, bf16[80,512]{1,0:T(8,128)(2,1)S(1)}, u32[]{:S(2)}, u32[]{:S(2)}) %collective-permute-start.3) | collective-permute-done | bytes 81952 | tf_op jit(solution)/shard_map/ppermute | solution.py:353
  16.0 6.3 %collective-permute-start.4 = (bf16[80,512]{1,0:T(8,128)(2,1)S(1)}, bf16[80,512]{1,0:T(8,128)(2,1)S(1)}, u32[]{:S(2)}, u32[]{:S(2)}) collective-permute-start(bf16[80,512]{1,0:T(8,128)(2,1)S(1)} %plane_total.1.refs_0_), channel_id=1, source_target_pairs={{0,8},{2,10},{4,12},{6,14},{8,16},{10,18},{12,20},{14,22},{16,24},... | collective-permute-start | bytes 245768 | tf_op jit(solution)/shard_map/ppermute | solution.py:357
  22.3 0.0 collective-permute-done.refs_1_
  22.3 0.0 collective-permute-done.7.refs_3_
  22.3 0.0 collective-permute-done.8.refs_5_
  22.3 1.4 %attend_near.1 = (f32[128,512]{1,0:T(8,128)S(1)}, f32[128,128]{1,0:T(8,128)S(1)}, f32[128,512]{1,0:T(8,128)S(1)}, f32[128,128]{1,0:T(8,128)S(1)}) custom-call(bf16[128,512]{1,0:T(8,128)(2,1)S(1)} %get-tuple-element.28.refs_0_, bf16[128,512]{1,0:T(8,128)(2,1)S(1)} %collective-permute-done.refs_1_, bf16[128,512]{1,0:T(8,128)(2,1)S(1)} %join_rows.1.refs_2_, ...), custom_call_target="tpu_custom_call" | custom-call | flops 1000 | bytes 1000 | tf_op jit(solution)/shard_map/attend_near/pallas_call | solution.py:34
  23.7 0.6 %collective-permute-done.4.refs_1_.refs_2_ = bf16[80,512]{1,0:T(8,128)(2,1)S(1)} collective-permute-done((bf16[80,512]{1,0:T(8,128)(2,1)S(1)}, bf16[80,512]{1,0:T(8,128)(2,1)S(1)}, u32[]{:S(2)}, u32[]{:S(2)}) %collective-permute-start.4) | collective-permute-done | bytes 81952 | tf_op jit(solution)/shard_map/ppermute | solution.py:357
  24.4 0.0 collective-permute-done.6.refs_2_
  24.4 0.7 %collective-permute-start.10 = (bf16[128,512]{1,0:T(8,128)(2,1)S(1)}, bf16[128,512]{1,0:T(8,128)(2,1)S(1)}, u32[]{:S(2)}, u32[]{:S(2)}) collective-permute-start(bf16[128,512]{1,0:T(8,128)(2,1)S(1)} %get-tuple-element.41.refs_2_), channel_id=1, source_target_pairs={{16,24},{18,26},{20,28},{22,30},{17,25},{19,27},{21,29},{23,31}} | collective-permute-start | bytes 393224 | tf_op jit(solution)/shard_map/ppermute | solution.py:357
  25.1 7.1 %collective-permute-start.11 = (bf16[80,512]{1,0:T(8,128)(2,1)S(1)}, bf16[80,512]{1,0:T(8,128)(2,1)S(1)}, u32[]{:S(2)}, u32[]{:S(2)}) collective-permute-start(bf16[80,512]{1,0:T(8,128)(2,1)S(1)} %get-tuple-element.42), channel_id=1, source_target_pairs={{0,16},{2,18},{4,20},{6,22},{8,24},{10,26},{12,28},{14,30},{1,17},... | collective-permute-start | bytes 245768 | tf_op jit(solution)/shard_map/ppermute | solution.py:357
  32.2 0.1 collective-permute-start.9
  32.3 2.0 %collective-permute-done.11.refs_3_ = bf16[80,512]{1,0:T(8,128)(2,1)S(1)} collective-permute-done((bf16[80,512]{1,0:T(8,128)(2,1)S(1)}, bf16[80,512]{1,0:T(8,128)(2,1)S(1)}, u32[]{:S(2)}, u32[]{:S(2)}) %collective-permute-start.11) | collective-permute-done | bytes 81952 | tf_op jit(solution)/shard_map/ppermute | solution.py:357
  34.3 0.1 chip_priors.1
  34.3 0.0 collective-permute-done.10.refs_0_
  34.4 0.1 collective-permute-start.12
  34.4 1.6 %collective-permute-start.14 = (bf16[64,512]{1,0:T(8,128)(2,1)S(1)}, bf16[64,512]{1,0:T(8,128)(2,1)S(1)}, u32[]{:S(2)}, u32[]{:S(2)}) collective-permute-start(bf16[64,512]{1,0:T(8,128)(2,1)S(1)} %get-tuple-element.43.refs_1_), channel_id=1, source_target_pairs={{0,4},{2,6},{4,0},{6,2},{8,12},{10,14},{12,8},{14,10},{16,20},{18,... | collective-permute-start | bytes 196616 | tf_op jit(solution)/shard_map/ppermute | solution.py:353
  36.0 0.0 collective-permute-done.9.refs_3_
  36.0 0.0 collective-permute-done.12.refs_5_
  36.0 1.8 %attend_far.1 = (bf16[128,640]{1,0:T(8,128)(2,1)S(1)}, f32[128,640]{1,0:T(8,128)S(1)}) custom-call(bf16[128,512]{1,0:T(8,128)(2,1)S(1)} %get-tuple-element.28.refs_0_, bf16[128,512]{1,0:T(8,128)(2,1)S(1)} %collective-permute-done.refs_1_, bf16[128,512]{1,0:T(8,128)(2,1)S(1)} %get-tuple-element.41.refs_2_, ...), custom_call_target="tpu_custom_call" | custom-call | flops 1000 | bytes 1000 | tf_op jit(solution)/shard_map/attend_far/pallas_call | solution.py:34
  37.9 1.3 %collective-permute-start.13 = (bf16[128,640]{1,0:T(8,128)(2,1)S(1)}, bf16[128,640]{1,0:T(8,128)(2,1)S(1)}, u32[]{:S(2)}, u32[]{:S(2)}) collective-permute-start(bf16[128,640]{1,0:T(8,128)(2,1)S(1)} %get-tuple-element.48), channel_id=1, source_target_pairs={{0,4},{2,6},{4,0},{6,2},{8,12},{10,14},{12,8},{14,10},{16,20},{18,... | collective-permute-start | bytes 491528 | tf_op jit(solution)/shard_map/ppermute | solution.py:353
  39.2 0.0 collective-permute-done.14.refs_3_
  39.2 0.1 block_priors.1
  39.3 0.1 collective-permute-start.15
  39.4 1.3 %collective-permute-done.15.refs_7_ = bf16[128,512]{1,0:T(8,128)(2,1)S(1)} collective-permute-done((bf16[128,512]{1,0:T(8,128)(2,1)S(1)}, bf16[128,512]{1,0:T(8,128)(2,1)S(1)}, u32[]{:S(2)}, u32[]{:S(2)}) %collective-permute-start.15) | collective-permute-done | bytes 131104 | tf_op jit(solution)/shard_map/ppermute | solution.py:353
  40.7 3.4 %collective-permute-done.13.refs_1_ = bf16[128,640]{1,0:T(8,128)(2,1)S(1)} collective-permute-done((bf16[128,640]{1,0:T(8,128)(2,1)S(1)}, bf16[128,640]{1,0:T(8,128)(2,1)S(1)}, u32[]{:S(2)}, u32[]{:S(2)}) %collective-permute-start.13) | collective-permute-done | bytes 163872 | tf_op jit(solution)/shard_map/ppermute | solution.py:353
  44.2 1.1 %finish.1 = (bf16[128,512]{1,0:T(8,128)(2,1)}, bf16[128,512]{1,0:T(8,128)(2,1)}) custom-call(f32[128,640]{1,0:T(8,128)S(1)} %get-tuple-element.47.refs_0_, bf16[128,640]{1,0:T(8,128)(2,1)S(1)} %collective-permute-done.13.refs_1_, bf16[128,512]{1,0:T(8,128)(2,1)S(1)} %get-tuple-element.37.refs_0_.refs_2_, bf16[128,512]{1,0:T(8,128)(2,1)S(1)} %get-tuple-element.49.refs_3_, ...), custom_call_target="tpu_custom_call" | custom-call | flops 1000 | bytes 1000 | tf_op jit(solution)/shard_map/finish/pallas_call | solution.py:34
  (4 shorter events, 0.1 us)
Async XLA Ops:
  2.0 5.3 %collective-permute-start.2 = (bf16[64,512]{1,0:T(8,128)(2,1)S(1)}, bf16[64,512]{1,0:T(8,128)(2,1)S(1)}, u32[]{:S(2)}, u32[]{:S(2)}) collective-permute-start(bf16[64,512]{1,0:T(8,128)(2,1)S(1)} %get-tuple-element.34), channel_id=1, source_target_pairs={{0,1},{1,0},{2,3},{3,2},{4,5},{5,4},{6,7},{7,6},{8,9},{9,8},{10,11... | collective-permute-start | bytes 196616 | tf_op jit(solution)/shard_map/ppermute | solution.py:360
  5.7 5.6 %collective-permute-start.1 = (bf16[144,512]{1,0:T(8,128)(2,1)S(1)}, bf16[144,512]{1,0:T(8,128)(2,1)S(1)}, u32[]{:S(2)}, u32[]{:S(2)}) collective-permute-start(bf16[144,512]{1,0:T(8,128)(2,1)S(1)} %get-tuple-element.33), channel_id=1, source_target_pairs={{0,2},{2,0},{4,6},{6,4},{8,10},{10,8},{12,14},{14,12},{16,18},{18,... | collective-permute-start | bytes 442376 | tf_op jit(solution)/shard_map/ppermute | solution.py:353
  7.3 6.5 %collective-permute-start.5 = (bf16[128,512]{1,0:T(8,128)(2,1)S(1)}, bf16[128,512]{1,0:T(8,128)(2,1)S(1)}, u32[]{:S(2)}, u32[]{:S(2)}) collective-permute-start(bf16[128,512]{1,0:T(8,128)(2,1)S(1)} %join_rows.1.refs_2_), channel_id=1, source_target_pairs={{0,8},{2,10},{4,12},{6,14},{8,16},{10,18},{12,20},{14,22},{16,24},... | collective-permute-start | bytes 393224 | tf_op jit(solution)/shard_map/ppermute | solution.py:357
  11.4 4.6 %collective-permute-start.3 = (bf16[80,512]{1,0:T(8,128)(2,1)S(1)}, bf16[80,512]{1,0:T(8,128)(2,1)S(1)}, u32[]{:S(2)}, u32[]{:S(2)}) collective-permute-start(bf16[80,512]{1,0:T(8,128)(2,1)S(1)} %get-tuple-element.36.refs_4_), channel_id=1, source_target_pairs={{0,4},{2,6},{4,0},{6,2},{8,12},{10,14},{12,8},{14,10},{16,20},{18,... | collective-permute-start | bytes 245768 | tf_op jit(solution)/shard_map/ppermute | solution.py:353
  13.0 9.3 %collective-permute-start = (bf16[128,512]{1,0:T(8,128)(2,1)S(1)}, bf16[128,512]{1,0:T(8,128)(2,1)S(1)}, u32[]{:S(2)}, u32[]{:S(2)}) collective-permute-start(bf16[128,512]{1,0:T(8,128)(2,1)S(1)} %get-tuple-element.28.refs_0_), channel_id=1, source_target_pairs={{0,4},{2,6},{4,0},{6,2},{8,12},{10,14},{12,8},{14,10},{16,20},{18,... | collective-permute-start | bytes 393224 | tf_op jit(solution)/shard_map/ppermute | solution.py:353
  13.5 8.8 %collective-permute-start.7 = (bf16[128,512]{1,0:T(8,128)(2,1)S(1)}, bf16[128,512]{1,0:T(8,128)(2,1)S(1)}, u32[]{:S(2)}, u32[]{:S(2)}) collective-permute-start(bf16[128,512]{1,0:T(8,128)(2,1)S(1)} %join_rows.1.refs_2_), channel_id=1, source_target_pairs={{0,2},{2,0},{4,6},{6,4},{8,10},{10,8},{12,14},{14,12},{16,18},{18,... | collective-permute-start | bytes 393224 | tf_op jit(solution)/shard_map/ppermute | solution.py:353
  13.8 8.5 %collective-permute-start.8 = (bf16[128,512]{1,0:T(8,128)(2,1)S(1)}, bf16[128,512]{1,0:T(8,128)(2,1)S(1)}, u32[]{:S(2)}, u32[]{:S(2)}) collective-permute-start(bf16[128,512]{1,0:T(8,128)(2,1)S(1)} %collective-permute-done.5.refs_4_), channel_id=1, source_target_pairs={{0,2},{2,0},{4,6},{6,4},{8,10},{10,8},{12,14},{14,12},{16,18},{18,... | collective-permute-start | bytes 393224 | tf_op jit(solution)/shard_map/ppermute | solution.py:353
  14.0 10.3 %collective-permute-start.6 = (bf16[128,512]{1,0:T(8,128)(2,1)S(1)}, bf16[128,512]{1,0:T(8,128)(2,1)S(1)}, u32[]{:S(2)}, u32[]{:S(2)}) collective-permute-start(bf16[128,512]{1,0:T(8,128)(2,1)S(1)} %collective-permute-done.5.refs_4_), channel_id=1, source_target_pairs={{8,16},{10,18},{12,20},{14,22},{16,24},{18,26},{20,28},{22,30},{9,... | collective-permute-start | bytes 393224 | tf_op jit(solution)/shard_map/ppermute | solution.py:357
  16.0 8.3 %collective-permute-start.4 = (bf16[80,512]{1,0:T(8,128)(2,1)S(1)}, bf16[80,512]{1,0:T(8,128)(2,1)S(1)}, u32[]{:S(2)}, u32[]{:S(2)}) collective-permute-start(bf16[80,512]{1,0:T(8,128)(2,1)S(1)} %plane_total.1.refs_0_), channel_id=1, source_target_pairs={{0,8},{2,10},{4,12},{6,14},{8,16},{10,18},{12,20},{14,22},{16,24},... | collective-permute-start | bytes 245768 | tf_op jit(solution)/shard_map/ppermute | solution.py:357
  24.4 9.9 %collective-permute-start.10 = (bf16[128,512]{1,0:T(8,128)(2,1)S(1)}, bf16[128,512]{1,0:T(8,128)(2,1)S(1)}, u32[]{:S(2)}, u32[]{:S(2)}) collective-permute-start(bf16[128,512]{1,0:T(8,128)(2,1)S(1)} %get-tuple-element.41.refs_2_), channel_id=1, source_target_pairs={{16,24},{18,26},{20,28},{22,30},{17,25},{19,27},{21,29},{23,31}} | collective-permute-start | bytes 393224 | tf_op jit(solution)/shard_map/ppermute | solution.py:357
  25.1 9.2 %collective-permute-start.11 = (bf16[80,512]{1,0:T(8,128)(2,1)S(1)}, bf16[80,512]{1,0:T(8,128)(2,1)S(1)}, u32[]{:S(2)}, u32[]{:S(2)}) collective-permute-start(bf16[80,512]{1,0:T(8,128)(2,1)S(1)} %get-tuple-element.42), channel_id=1, source_target_pairs={{0,16},{2,18},{4,20},{6,22},{8,24},{10,26},{12,28},{14,30},{1,17},... | collective-permute-start | bytes 245768 | tf_op jit(solution)/shard_map/ppermute | solution.py:357
  32.2 3.8 %collective-permute-start.9 = (bf16[128,512]{1,0:T(8,128)(2,1)S(1)}, bf16[128,512]{1,0:T(8,128)(2,1)S(1)}, u32[]{:S(2)}, u32[]{:S(2)}) collective-permute-start(bf16[128,512]{1,0:T(8,128)(2,1)S(1)} %get-tuple-element.41.refs_2_), channel_id=1, source_target_pairs={{0,2},{2,0},{4,6},{6,4},{8,10},{10,8},{12,14},{14,12},{16,18},{18,... | collective-permute-start | bytes 393224 | tf_op jit(solution)/shard_map/ppermute | solution.py:353
  34.4 1.6 %collective-permute-start.12 = (bf16[128,512]{1,0:T(8,128)(2,1)S(1)}, bf16[128,512]{1,0:T(8,128)(2,1)S(1)}, u32[]{:S(2)}, u32[]{:S(2)}) collective-permute-start(bf16[128,512]{1,0:T(8,128)(2,1)S(1)} %hold.1.refs_4_), channel_id=1, source_target_pairs={{0,2},{2,0},{4,6},{6,4},{8,10},{10,8},{12,14},{14,12},{16,18},{18,... | collective-permute-start | bytes 393224 | tf_op jit(solution)/shard_map/ppermute | solution.py:353
  34.4 4.7 %collective-permute-start.14 = (bf16[64,512]{1,0:T(8,128)(2,1)S(1)}, bf16[64,512]{1,0:T(8,128)(2,1)S(1)}, u32[]{:S(2)}, u32[]{:S(2)}) collective-permute-start(bf16[64,512]{1,0:T(8,128)(2,1)S(1)} %get-tuple-element.43.refs_1_), channel_id=1, source_target_pairs={{0,4},{2,6},{4,0},{6,2},{8,12},{10,14},{12,8},{14,10},{16,20},{18,... | collective-permute-start | bytes 196616 | tf_op jit(solution)/shard_map/ppermute | solution.py:353
  37.9 6.3 %collective-permute-start.13 = (bf16[128,640]{1,0:T(8,128)(2,1)S(1)}, bf16[128,640]{1,0:T(8,128)(2,1)S(1)}, u32[]{:S(2)}, u32[]{:S(2)}) collective-permute-start(bf16[128,640]{1,0:T(8,128)(2,1)S(1)} %get-tuple-element.48), channel_id=1, source_target_pairs={{0,4},{2,6},{4,0},{6,2},{8,12},{10,14},{12,8},{14,10},{16,20},{18,... | collective-permute-start | bytes 491528 | tf_op jit(solution)/shard_map/ppermute | solution.py:353
  39.3 1.4 %collective-permute-start.15 = (bf16[128,512]{1,0:T(8,128)(2,1)S(1)}, bf16[128,512]{1,0:T(8,128)(2,1)S(1)}, u32[]{:S(2)}, u32[]{:S(2)}) collective-permute-start(bf16[128,512]{1,0:T(8,128)(2,1)S(1)} %get-tuple-element.53), channel_id=1, source_target_pairs={{0,2},{2,0},{4,6},{6,4},{8,10},{10,8},{12,14},{14,12},{16,18},{18,... | collective-permute-start | bytes 393224 | tf_op jit(solution)/shard_map/ppermute | solution.py:353

commit v4 on v3

--- a/solution.py
+++ b/solution.py
@@ -42,6 +42,19 @@
         cost_estimate=pl.CostEstimate(flops=1000, bytes_accessed=1000, transcendentals=0),
         name=name,
     )(*args, *after)
+
+
+def pass_on(value, *after):
+    return call(
+        lambda *refs: None,
+        [shape(value.shape, value.dtype)],
+        (value,),
+        name="pass_on",
+        takes=ANY,
+        gives=ANY,
+        after=after,
+        aliases={0: 0},
+    )
 
 
 def shape(dims, dtype=BF16):
@@ -174,12 +187,13 @@
 
 def chip_priors(keep_ref, other_ref, *refs):
     planes, send, keep = refs[:-2], refs[-2], refs[-1]
-    _, high, _ = bits()
+    _, high, depth = bits()
     entering = jnp.zeros(send.shape, F32)
     between = jnp.zeros((1, send.shape[1]), F32)
-    for ref in planes:
-        entering = entering + jnp.exp(between) * state_of(ref)
-        between = between + total_of(ref)
+    for i, ref in enumerate(planes):
+        earlier = lax.rem(lax.div(depth, 2**i), 2) == 1
+        entering = entering + jnp.where(earlier, jnp.exp(between) * state_of(ref), 0.0)
+        between = between + jnp.where(earlier, total_of(ref), 0.0)
     first = high == 0
     early = jnp.where(first, state_of(keep_ref), state_of(other_ref))
     early_total = jnp.where(first, total_of(keep_ref), total_of(other_ref))
@@ -202,12 +216,12 @@
     keep[...] = jnp.where(first, entering, second).astype(keep.dtype)
 
 
-def grow(own_ref, earlier_ref, _, out, __):
+def grow(bit, own_ref, other_ref, out):
     rows = out.shape[0] - PAD
-    own, earlier = total_of(own_ref), total_of(earlier_ref)
-    state = jnp.exp(own) * state_of(earlier_ref) + state_of(own_ref)
+    first = lax.rem(lax.div(bits()[2], bit), 2) == 0
+    state, total = pair_total(first, own_ref, other_ref)
     out[pl.ds(0, rows), :] = state.astype(out.dtype)
-    put_total(out, rows, own + earlier)
+    put_total(out, rows, total)
 
 
 def retain_inside(q_ref, k_ref, v_ref, d_ref, inside_ref, factor_ref):
@@ -253,9 +267,9 @@
     ret_out.wait()
 
 
-def attend(first, count, q_ref, q_other_ref, *refs):
+def attend(hops, last, q_ref, q_other_ref, *refs):
+    count = len(hops)
     blocks, refs = refs[: 2 * count], refs[2 * count :]
-    last = first > 0
     carried, refs = (refs[:4], refs[4:]) if last else ((), refs)
     outs, (keys, values) = refs[:-2], refs[-2:]
     rows, wide = q_ref.shape
@@ -270,13 +284,12 @@
     column = lax.broadcasted_iota(jnp.int32, (1, total), 1)
     limit = jnp.zeros((1, total), jnp.int32)
     for i in range(2 * count):
-        s, t = divmod(i, 2)
-        s = s + first
+        s, t = hops[i // 2], i % 2
         if s == 0:
             core = low if t == 0 else 1 - low
             at = column + ((2 * high + core) * length - i * length)
         else:
-            at = jnp.where(depth >= s, -1, 4 * rows)
+            at = jnp.where(jnp.bitwise_xor(depth, s) < depth, -1, 4 * rows)
         limit = jnp.where(column >= i * length, at, limit)
     scale = 1.0 / (math.sqrt(HD) * math.log(2.0))
     row = lax.broadcasted_iota(jnp.int32, (rows, total), 0)
@@ -352,10 +365,6 @@
     def swap(value, bit):
         return lax.ppermute(value, "ctx", [(b, b ^ bit) for b in range(count)])
 
-    def along(value, step, least):
-        pairs = [(b, b + step * 4) for b in range(least * 4, count - step * 4)]
-        return lax.ppermute(value, "ctx", pairs)
-
     def to_head(value, e):
         return lax.ppermute(value, "head", [(y, (y + e) % n) for y in range(n)])
 
@@ -394,17 +403,16 @@
         name="retain_inside",
         after=(chip_send,),
     )
-    blocks = [
-        call(
+    blocks = {
+        0: call(
             functools.partial(join_rows, n),
             [shape((n * length, 2 * width))],
             arrived,
             name="join_rows",
         )
-    ]
-    for s in range(1, far - 1):
-        blocks.append(along(blocks[-1], 1, s - 1))
+    }
     chip_other = swap(chip_send, 2)
+    q_cross = pass_on(q_cross, chip_send)
     q_other = swap(q_cross, 2)
     window = call(
         plane_total,
@@ -413,66 +421,66 @@
         name="plane_total",
         after=(factor,),
     )
-    def look(first, count, outs, carried, name):
-        keys = 2 * count * n * length
+    bit = far // 2
+    while bit:
+        for s in list(blocks):
+            if s and bit == 1:
+                blocks[s] = pass_on(blocks[s], window)
+            blocks[s ^ bit] = swap(blocks[s], 4 * bit)
+        bit //= 2
+    planes, bit = [], 1
+    while bit < far:
+        planes.append(swap(window, 4 * bit))
+        if 2 * bit < far:
+            window = call(
+                functools.partial(grow, bit),
+                [shape(window.shape)],
+                (window, planes[-1]),
+                name="grow",
+                after=(q_other,),
+            )
+        bit *= 2
+
+    for s in blocks:
+        if s % 2 and s > 1:
+            blocks[s] = pass_on(blocks[s], window)
+    def look(hops, last, outs, carried, name):
+        keys = 2 * len(hops) * n * length
         both = []
-        for one in blocks[first : first + count]:
-            both += [one, swap(one, 1)]
+        for s in hops:
+            both += [blocks[s], swap(blocks[s], 1)]
         return call(
-            functools.partial(attend, first, count),
+            functools.partial(attend, hops, last),
             outs,
             (q_cross, q_other, *both, *carried),
             scratch=[pltpu.VMEM((keys, width), BF16) for _ in range(2)],
             name=name,
         )
 
-    near = max(far // 2, 1)
+    hops = list(blocks)
+    near = far // 2
     so_far = look(
-        0, near, [shape((rows, wide), F32), shape((rows, LANES), F32)] * 2, (), "attend_near"
-    )
-    planes, step = [], 1
-    while step < far:
-        planes.append(along(window, step, 0))
-        step *= 2
-        if step < far:
-            window, blocks[-1] = call(
-                grow,
-                [shape(window.shape), shape(blocks[-1].shape)],
-                (window, planes[-1], blocks[-1]),
-                name="grow",
-                takes=[VMEM, VMEM, ANY],
-                gives=(VMEM, ANY),
-                after=so_far[1:2],
-                aliases={2: 1},
-            )
+        hops[:near],
+        False,
+        [shape((rows, wide), F32), shape((rows, LANES), F32)] * 2,
+        (),
+        "attend_near",
+    )
+    part_send, part_keep = look(
+        hops[near:],
+        True,
+        [shape((rows, wide + LANES)), shape((rows, wide + LANES), F32)],
+        so_far,
+        "attend_far",
+    )
+    part_other = swap(part_send, 2)
     prior_send, prior_keep = call(
         chip_priors,
         [shape((quarter, wide)), shape((quarter, wide), F32)],
         (chip_keep, chip_other, *planes),
         name="chip_priors",
-    )
-    if far > 1:
-        arriving = along(blocks[-1], 1, far - 2)
-        blocks.append(
-            call(
-                lambda *refs: None,
-                [shape(arriving.shape)],
-                (arriving,),
-                name="hold",
-                takes=ANY,
-                gives=ANY,
-                after=(prior_send,),
-                aliases={0: 0},
-            )
-        )
-    part_send, part_keep = look(
-        near,
-        far - near,
-        [shape((rows, wide + LANES)), shape((rows, wide + LANES), F32)],
-        so_far,
-        "attend_far",
-    )
-    part_other = swap(part_send, 2)
+        after=so_far[1:2],
+    )
     prior_other = swap(prior_send, 2)
     state_send, state_keep = call(
         block_priors,

time: 45.5 us -> 42.6 us (0.936)
  starting transfers between devices: 27.3 us -> 18 us
  waiting for transfers between devices: 9.79 us -> 16.2 us
    ppermute x5 -> x0, starting transfers between devices: 18.7 us -> none  [along(): return lax.ppermute(value, 'ctx', pairs)]
    ppermute x10 -> x15, starting transfers between devices: 5.52 us -> 15.4 us  [swap(): return lax.ppermute(value, 'ctx', [(b, b ^ bit) for b in range(count)])]
    ppermute x10 -> x15, waiting for transfers between devices: 5.47 us -> 13.6 us  [swap(): return lax.ppermute(value, 'ctx', [(b, b ^ bit) for b in range(count)])]
    ppermute x5 -> x0, waiting for transfers between devices: 2.83 us -> none  [along(): return lax.ppermute(value, 'ctx', pairs)]
    ppermute x1, waiting for transfers between devices: 1.49 us -> 2.69 us  [to_head(): return lax.ppermute(value, 'head', [(y, (y + e) % n) for y in range(n)])]
    pallas_call x13 -> x15, Pallas kernels: 7.42 us -> 7.45 us  [call(): pl.pallas_call(kernel, out_shape=outs[0] if single else tuple(outs), in_s...]
  transfers between devices with their start and end apart: 16 -> 16, of which waited for: 7 -> 9; matrix products, arithmetic and copies ran while one was open for 0% -> 0% of each run, Pallas kernels for 11% -> 10%
where the time goes in v4:
time: 42.6 us; the launch traced here: 42.4 us
  starting transfers between devices  18 us (42%)
  waiting for transfers between devices  16.2 us (38%)
  Pallas kernels  7.45 us (17%)
  between operations  0.74 us (2%)
    ppermute x15, starting transfers between devices, swap(): return lax.ppermute(value, 'ctx', [(b, b ^ bit) for b in range(count)])  15.4 us
    ppermute x15, waiting for transfers between devices, swap(): return lax.ppermute(value, 'ctx', [(b, b ^ bit) for b in range(count)])  13.6 us
    pallas_call x15, Pallas kernels, call(): pl.pallas_call(kernel, out_shape=outs[0] if single else tuple(outs), in_s...  7.45 us
    ppermute x1, waiting for transfers between devices, to_head(): return lax.ppermute(value, 'head', [(y, (y + e) % n) for y in range(n)])  2.69 us
    ppermute x1, starting transfers between devices, to_head(): return lax.ppermute(value, 'head', [(y, (y + e) % n) for y in range(n)])  2.6 us
  transfers between devices with their start and end apart: 16, of which 9 were waited for; matrix products, arithmetic and copies ran while one was open for 0% of the time, Pallas kernels for 10%

profile of v4, /device:TPU:0, one launch (start us, length us, event | category | flops | bytes accessed | tf_op | source)
XLA Modules:
  0.0 42.4 jit_solution(10922924579499110501)
XLA Ops:
  0.6 1.3 %load_all.1 = (bf16[64,512]{1,0:T(8,128)(2,1)S(1)}, bf16[64,512]{1,0:T(8,128)(2,1)S(1)}, bf16[128,512]{1,0:T(8,128)(2,1)S(1)}, bf16[128,512]{1,0:T(8,128)(2,1)S(...) custom-call(bf16[64,512]{1,0:T(8,128)(2,1)} %refs_0_.1, ...), custom_call_target="tpu_custom_call" | custom-call | flops 1000 | bytes 1000 | tf_op jit(solution)/shard_map/load_all/pallas_call | solution.py:34
  2.0 0.7 %summarize.1 = (bf16[144,512]{1,0:T(8,128)(2,1)S(1)}, f32[144,512]{1,0:T(8,128)S(1)}) custom-call(bf16[128,512]{1,0:T(8,128)(2,1)S(1)} %get-tuple-element.27.refs_0_.refs_1_, bf16[128,512]{1,0:T(8,128)(2,1)S(1)} %get-tuple-element.28.refs_1_.refs_2_, f32[2,128]{1,0:T(2,128)S(1)} %get-tuple-element.29.refs_2_.refs_3_), custom_call_target="tpu_custom_call" | custom-call | flops 1000 | bytes 1000 | tf_op jit(solution)/shard_map/summarize/pallas_call | solution.py:34
  2.6 0.5 %collective-permute-start = (bf16[144,512]{1,0:T(8,128)(2,1)S(1)}, bf16[144,512]{1,0:T(8,128)(2,1)S(1)}, u32[]{:S(2)}, u32[]{:S(2)}) collective-permute-start(bf16[144,512]{1,0:T(8,128)(2,1)S(1)} %get-tuple-element.31), channel_id=1, source_target_pairs={{0,2},{2,0},{4,6},{6,4},{8,10},{10,8},{12,14},{14,12},{16,18},{18,... | collective-permute-start | bytes 442376 | tf_op jit(solution)/shard_map/ppermute | solution.py:366
  3.2 2.6 %collective-permute-start.1 = (bf16[64,512]{1,0:T(8,128)(2,1)S(1)}, bf16[64,512]{1,0:T(8,128)(2,1)S(1)}, u32[]{:S(2)}, u32[]{:S(2)}) collective-permute-start(bf16[64,512]{1,0:T(8,128)(2,1)S(1)} %get-tuple-element.32), channel_id=1, source_target_pairs={{0,1},{1,0},{2,3},{3,2},{4,5},{5,4},{6,7},{7,6},{8,9},{9,8},{10,11... | collective-permute-start | bytes 196616 | tf_op jit(solution)/shard_map/ppermute | solution.py:369
  5.8 2.7 %collective-permute-done.1.refs_2_.refs_1_ = bf16[64,512]{1,0:T(8,128)(2,1)S(1)} collective-permute-done((bf16[64,512]{1,0:T(8,128)(2,1)S(1)}, bf16[64,512]{1,0:T(8,128)(2,1)S(1)}, u32[]{:S(2)}, u32[]{:S(2)}) %collective-permute-start.1) | collective-permute-done | bytes 65568 | tf_op jit(solution)/shard_map/ppermute | solution.py:369
  8.5 2.9 %collective-permute-start.5 = (bf16[128,512]{1,0:T(8,128)(2,1)S(1)}, bf16[128,512]{1,0:T(8,128)(2,1)S(1)}, u32[]{:S(2)}, u32[]{:S(2)}) collective-permute-start(bf16[128,512]{1,0:T(8,128)(2,1)S(1)} %join_rows.1.refs_2_), channel_id=1, source_target_pairs={{0,16},{2,18},{4,20},{6,22},{8,24},{10,26},{12,28},{14,30},{16,0},... | collective-permute-start | bytes 393224 | tf_op jit(solution)/shard_map/ppermute | solution.py:366
  11.4 0.0 collective-permute-done.refs_1_
  11.4 0.1 chip_total.1
  11.5 1.6 %collective-permute-start.6 = (bf16[80,512]{1,0:T(8,128)(2,1)S(1)}, bf16[80,512]{1,0:T(8,128)(2,1)S(1)}, u32[]{:S(2)}, u32[]{:S(2)}) collective-permute-start(bf16[80,512]{1,0:T(8,128)(2,1)S(1)} %get-tuple-element.33.refs_1_.refs_4_), channel_id=1, source_target_pairs={{0,4},{2,6},{4,0},{6,2},{8,12},{10,14},{12,8},{14,10},{16,20},{18,... | collective-permute-start | bytes 245768 | tf_op jit(solution)/shard_map/ppermute | solution.py:366
  13.0 1.6 %collective-permute-start.3 = (bf16[128,512]{1,0:T(8,128)(2,1)S(1)}, bf16[128,512]{1,0:T(8,128)(2,1)S(1)}, u32[]{:S(2)}, u32[]{:S(2)}) collective-permute-start(bf16[128,512]{1,0:T(8,128)(2,1)S(1)} %join_rows.1.refs_2_), channel_id=1, source_target_pairs={{0,8},{2,10},{4,12},{6,14},{8,0},{10,2},{12,4},{14,6},{16,24},{18,... | collective-permute-start | bytes 393224 | tf_op jit(solution)/shard_map/ppermute | solution.py:366
  14.6 0.6 %retain_inside.1 = (f32[128,512]{1,0:T(8,128)S(1)}, f32[128,2]{1,0:T(8,128)S(1)}) custom-call(bf16[128,512]{1,0:T(8,128)(2,1)S(1)} %get-tuple-element.36.refs_0_.refs_2_, bf16[128,512]{1,0:T(8,128)(2,1)S(1)} %get-tuple-element.27.refs_0_.refs_1_, bf16[128,512]{1,0:T(8,128)(2,1)S(1)} %get-tuple-element.28.refs_1_.refs_2_, ...), custom_call_target="tpu_custom_call" | custom-call | flops 1000 | bytes 1000 | tf_op jit(solution)/shard_map/retain_inside/pallas_call | solution.py:34
  15.2 0.6 %collective-permute-start.2 = (bf16[128,512]{1,0:T(8,128)(2,1)S(1)}, bf16[128,512]{1,0:T(8,128)(2,1)S(1)}, u32[]{:S(2)}, u32[]{:S(2)}) collective-permute-start(bf16[128,512]{1,0:T(8,128)(2,1)S(1)} %pass_on.3.refs_0_), channel_id=1, source_target_pairs={{0,4},{2,6},{4,0},{6,2},{8,12},{10,14},{12,8},{14,10},{16,20},{18,... | collective-permute-start | bytes 393224 | tf_op jit(solution)/shard_map/ppermute | solution.py:366
  15.8 0.2 collective-permute-done.6.refs_1_
  16.0 1.6 %collective-permute-done.5.refs_0_ = bf16[128,512]{1,0:T(8,128)(2,1)S(1)} collective-permute-done((bf16[128,512]{1,0:T(8,128)(2,1)S(1)}, bf16[128,512]{1,0:T(8,128)(2,1)S(1)}, u32[]{:S(2)}, u32[]{:S(2)}) %collective-permute-start.5) | collective-permute-done | bytes 131104 | tf_op jit(solution)/shard_map/ppermute | solution.py:366
  17.6 0.7 %collective-permute-start.7 = (bf16[128,512]{1,0:T(8,128)(2,1)S(1)}, bf16[128,512]{1,0:T(8,128)(2,1)S(1)}, u32[]{:S(2)}, u32[]{:S(2)}) collective-permute-start(bf16[128,512]{1,0:T(8,128)(2,1)S(1)} %pass_on.4.refs_4_), channel_id=1, source_target_pairs={{0,8},{2,10},{4,12},{6,14},{8,0},{10,2},{12,4},{14,6},{16,24},{18,... | collective-permute-start | bytes 393224 | tf_op jit(solution)/shard_map/ppermute | solution.py:366
  18.3 1.4 %collective-permute-start.8 = (bf16[80,512]{1,0:T(8,128)(2,1)S(1)}, bf16[80,512]{1,0:T(8,128)(2,1)S(1)}, u32[]{:S(2)}, u32[]{:S(2)}) collective-permute-start(bf16[80,512]{1,0:T(8,128)(2,1)S(1)} %plane_total.1.refs_1_.refs_0_), channel_id=1, source_target_pairs={{0,8},{2,10},{4,12},{6,14},{8,0},{10,2},{12,4},{14,6},{16,24},{18,... | collective-permute-start | bytes 245768 | tf_op jit(solution)/shard_map/ppermute | solution.py:366
  19.7 0.0 collective-permute-start.10
  19.7 0.0 collective-permute-done.3.refs_2_
  19.7 0.5 %collective-permute-start.11 = (bf16[128,512]{1,0:T(8,128)(2,1)S(1)}, bf16[128,512]{1,0:T(8,128)(2,1)S(1)}, u32[]{:S(2)}, u32[]{:S(2)}) collective-permute-start(bf16[128,512]{1,0:T(8,128)(2,1)S(1)} %pass_on.4.refs_4_), channel_id=1, source_target_pairs={{0,2},{2,0},{4,6},{6,4},{8,10},{10,8},{12,14},{14,12},{16,18},{18,... | collective-permute-start | bytes 393224 | tf_op jit(solution)/shard_map/ppermute | solution.py:366
  20.2 0.1 collective-permute-done.2.refs_2_.refs_1_
  20.3 0.0 collective-permute-start.4
  20.3 3.5 %collective-permute-done.8.refs_1_.refs_2_ = bf16[80,512]{1,0:T(8,128)(2,1)S(1)} collective-permute-done((bf16[80,512]{1,0:T(8,128)(2,1)S(1)}, bf16[80,512]{1,0:T(8,128)(2,1)S(1)}, u32[]{:S(2)}, u32[]{:S(2)}) %collective-permute-start.8) | collective-permute-done | bytes 81952 | tf_op jit(solution)/shard_map/ppermute | solution.py:366
  23.7 0.1 grow.1.refs_1_
  23.8 0.0 collective-permute-done.7.refs_0_
  23.8 0.1 collective-permute-start.9
  23.9 3.4 %collective-permute-start.13 = (bf16[80,512]{1,0:T(8,128)(2,1)S(1)}, bf16[80,512]{1,0:T(8,128)(2,1)S(1)}, u32[]{:S(2)}, u32[]{:S(2)}) collective-permute-start(bf16[80,512]{1,0:T(8,128)(2,1)S(1)} %grow.1.refs_1_), channel_id=1, source_target_pairs={{0,16},{2,18},{4,20},{6,22},{8,24},{10,26},{12,28},{14,30},{16,0},... | collective-permute-start | bytes 245768 | tf_op jit(solution)/shard_map/ppermute | solution.py:366
  27.3 0.0 collective-permute-done.10.refs_3_
  27.3 0.0 collective-permute-done.11.refs_5_
  27.3 1.4 %attend_near.1 = (f32[128,512]{1,0:T(8,128)S(1)}, f32[128,128]{1,0:T(8,128)S(1)}, f32[128,512]{1,0:T(8,128)S(1)}, f32[128,128]{1,0:T(8,128)S(1)}) custom-call(bf16[128,512]{1,0:T(8,128)(2,1)S(1)} %pass_on.3.refs_0_, bf16[128,512]{1,0:T(8,128)(2,1)S(1)} %collective-permute-done.2.refs_2_.refs_1_, bf16[128,512]{1,0:T(8,128)(2,1)S(1)} %join_rows.1.refs_2_, ...), custom_call_target="tpu_custom_call" | custom-call | flops 1000 | bytes 1000 | tf_op jit(solution)/shard_map/attend_near/pallas_call | solution.py:34
  28.7 3.4 %collective-permute-done.13.refs_3_ = bf16[80,512]{1,0:T(8,128)(2,1)S(1)} collective-permute-done((bf16[80,512]{1,0:T(8,128)(2,1)S(1)}, bf16[80,512]{1,0:T(8,128)(2,1)S(1)}, u32[]{:S(2)}, u32[]{:S(2)}) %collective-permute-start.13) | collective-permute-done | bytes 81952 | tf_op jit(solution)/shard_map/ppermute | solution.py:366
  32.1 0.1 chip_priors.1
  32.2 1.5 %collective-permute-start.14 = (bf16[64,512]{1,0:T(8,128)(2,1)S(1)}, bf16[64,512]{1,0:T(8,128)(2,1)S(1)}, u32[]{:S(2)}, u32[]{:S(2)}) collective-permute-start(bf16[64,512]{1,0:T(8,128)(2,1)S(1)} %get-tuple-element.47), channel_id=1, source_target_pairs={{0,4},{2,6},{4,0},{6,2},{8,12},{10,14},{12,8},{14,10},{16,20},{18,... | collective-permute-start | bytes 196616 | tf_op jit(solution)/shard_map/ppermute | solution.py:366
  33.7 0.0 collective-permute-done.4.refs_3_
  33.7 0.0 collective-permute-done.9.refs_5_
  33.7 1.8 %attend_far.1 = (bf16[128,640]{1,0:T(8,128)(2,1)S(1)}, f32[128,640]{1,0:T(8,128)S(1)}) custom-call(bf16[128,512]{1,0:T(8,128)(2,1)S(1)} %pass_on.3.refs_0_, bf16[128,512]{1,0:T(8,128)(2,1)S(1)} %collective-permute-done.2.refs_2_.refs_1_, bf16[128,512]{1,0:T(8,128)(2,1)S(1)} %collective-permute-done.3.refs_2_, ...), custom_call_target="tpu_custom_call" | custom-call | flops 1000 | bytes 1000 | tf_op jit(solution)/shard_map/attend_far/pallas_call | solution.py:34
  35.6 0.6 %collective-permute-start.12 = (bf16[128,640]{1,0:T(8,128)(2,1)S(1)}, bf16[128,640]{1,0:T(8,128)(2,1)S(1)}, u32[]{:S(2)}, u32[]{:S(2)}) collective-permute-start(bf16[128,640]{1,0:T(8,128)(2,1)S(1)} %get-tuple-element.43), channel_id=1, source_target_pairs={{0,4},{2,6},{4,0},{6,2},{8,12},{10,14},{12,8},{14,10},{16,20},{18,... | collective-permute-start | bytes 491528 | tf_op jit(solution)/shard_map/ppermute | solution.py:366
  36.2 0.3 collective-permute-done.14.refs_3_
  36.5 0.1 block_priors.1
  36.7 0.1 collective-permute-start.15
  36.7 1.3 %collective-permute-done.15.refs_7_ = bf16[128,512]{1,0:T(8,128)(2,1)S(1)} collective-permute-done((bf16[128,512]{1,0:T(8,128)(2,1)S(1)}, bf16[128,512]{1,0:T(8,128)(2,1)S(1)}, u32[]{:S(2)}, u32[]{:S(2)}) %collective-permute-start.15) | collective-permute-done | bytes 131104 | tf_op jit(solution)/shard_map/ppermute | solution.py:366
  38.1 3.3 %collective-permute-done.12.refs_1_ = bf16[128,640]{1,0:T(8,128)(2,1)S(1)} collective-permute-done((bf16[128,640]{1,0:T(8,128)(2,1)S(1)}, bf16[128,640]{1,0:T(8,128)(2,1)S(1)}, u32[]{:S(2)}, u32[]{:S(2)}) %collective-permute-start.12) | collective-permute-done | bytes 163872 | tf_op jit(solution)/shard_map/ppermute | solution.py:366
  41.3 1.1 %finish.1 = (bf16[128,512]{1,0:T(8,128)(2,1)}, bf16[128,512]{1,0:T(8,128)(2,1)}) custom-call(f32[128,640]{1,0:T(8,128)S(1)} %get-tuple-element.42.refs_0_, bf16[128,640]{1,0:T(8,128)(2,1)S(1)} %collective-permute-done.12.refs_1_, bf16[128,512]{1,0:T(8,128)(2,1)S(1)} %get-tuple-element.36.refs_0_.refs_2_, bf16[128,512]{1,0:T(8,128)(2,1)S(1)} %get-tuple-element.44.refs_3_, ...), custom_call_target="tpu_custom_call" | custom-call | flops 1000 | bytes 1000 | tf_op jit(solution)/shard_map/finish/pallas_call | solution.py:34
  (5 shorter events, 0.1 us)
Async XLA Ops:
  2.6 8.7 %collective-permute-start = (bf16[144,512]{1,0:T(8,128)(2,1)S(1)}, bf16[144,512]{1,0:T(8,128)(2,1)S(1)}, u32[]{:S(2)}, u32[]{:S(2)}) collective-permute-start(bf16[144,512]{1,0:T(8,128)(2,1)S(1)} %get-tuple-element.31), channel_id=1, source_target_pairs={{0,2},{2,0},{4,6},{6,4},{8,10},{10,8},{12,14},{14,12},{16,18},{18,... | collective-permute-start | bytes 442376 | tf_op jit(solution)/shard_map/ppermute | solution.py:366
  3.2 5.3 %collective-permute-start.1 = (bf16[64,512]{1,0:T(8,128)(2,1)S(1)}, bf16[64,512]{1,0:T(8,128)(2,1)S(1)}, u32[]{:S(2)}, u32[]{:S(2)}) collective-permute-start(bf16[64,512]{1,0:T(8,128)(2,1)S(1)} %get-tuple-element.32), channel_id=1, source_target_pairs={{0,1},{1,0},{2,3},{3,2},{4,5},{5,4},{6,7},{7,6},{8,9},{9,8},{10,11... | collective-permute-start | bytes 196616 | tf_op jit(solution)/shard_map/ppermute | solution.py:369
  8.5 9.1 %collective-permute-start.5 = (bf16[128,512]{1,0:T(8,128)(2,1)S(1)}, bf16[128,512]{1,0:T(8,128)(2,1)S(1)}, u32[]{:S(2)}, u32[]{:S(2)}) collective-permute-start(bf16[128,512]{1,0:T(8,128)(2,1)S(1)} %join_rows.1.refs_2_), channel_id=1, source_target_pairs={{0,16},{2,18},{4,20},{6,22},{8,24},{10,26},{12,28},{14,30},{16,0},... | collective-permute-start | bytes 393224 | tf_op jit(solution)/shard_map/ppermute | solution.py:366
  11.5 4.5 %collective-permute-start.6 = (bf16[80,512]{1,0:T(8,128)(2,1)S(1)}, bf16[80,512]{1,0:T(8,128)(2,1)S(1)}, u32[]{:S(2)}, u32[]{:S(2)}) collective-permute-start(bf16[80,512]{1,0:T(8,128)(2,1)S(1)} %get-tuple-element.33.refs_1_.refs_4_), channel_id=1, source_target_pairs={{0,4},{2,6},{4,0},{6,2},{8,12},{10,14},{12,8},{14,10},{16,20},{18,... | collective-permute-start | bytes 245768 | tf_op jit(solution)/shard_map/ppermute | solution.py:366
  13.0 6.6 %collective-permute-start.3 = (bf16[128,512]{1,0:T(8,128)(2,1)S(1)}, bf16[128,512]{1,0:T(8,128)(2,1)S(1)}, u32[]{:S(2)}, u32[]{:S(2)}) collective-permute-start(bf16[128,512]{1,0:T(8,128)(2,1)S(1)} %join_rows.1.refs_2_), channel_id=1, source_target_pairs={{0,8},{2,10},{4,12},{6,14},{8,0},{10,2},{12,4},{14,6},{16,24},{18,... | collective-permute-start | bytes 393224 | tf_op jit(solution)/shard_map/ppermute | solution.py:366
  15.2 5.0 %collective-permute-start.2 = (bf16[128,512]{1,0:T(8,128)(2,1)S(1)}, bf16[128,512]{1,0:T(8,128)(2,1)S(1)}, u32[]{:S(2)}, u32[]{:S(2)}) collective-permute-start(bf16[128,512]{1,0:T(8,128)(2,1)S(1)} %pass_on.3.refs_0_), channel_id=1, source_target_pairs={{0,4},{2,6},{4,0},{6,2},{8,12},{10,14},{12,8},{14,10},{16,20},{18,... | collective-permute-start | bytes 393224 | tf_op jit(solution)/shard_map/ppermute | solution.py:366
  17.6 6.2 %collective-permute-start.7 = (bf16[128,512]{1,0:T(8,128)(2,1)S(1)}, bf16[128,512]{1,0:T(8,128)(2,1)S(1)}, u32[]{:S(2)}, u32[]{:S(2)}) collective-permute-start(bf16[128,512]{1,0:T(8,128)(2,1)S(1)} %pass_on.4.refs_4_), channel_id=1, source_target_pairs={{0,8},{2,10},{4,12},{6,14},{8,0},{10,2},{12,4},{14,6},{16,24},{18,... | collective-permute-start | bytes 393224 | tf_op jit(solution)/shard_map/ppermute | solution.py:366
  18.3 5.5 %collective-permute-start.8 = (bf16[80,512]{1,0:T(8,128)(2,1)S(1)}, bf16[80,512]{1,0:T(8,128)(2,1)S(1)}, u32[]{:S(2)}, u32[]{:S(2)}) collective-permute-start(bf16[80,512]{1,0:T(8,128)(2,1)S(1)} %plane_total.1.refs_1_.refs_0_), channel_id=1, source_target_pairs={{0,8},{2,10},{4,12},{6,14},{8,0},{10,2},{12,4},{14,6},{16,24},{18,... | collective-permute-start | bytes 245768 | tf_op jit(solution)/shard_map/ppermute | solution.py:366
  19.7 7.6 %collective-permute-start.10 = (bf16[128,512]{1,0:T(8,128)(2,1)S(1)}, bf16[128,512]{1,0:T(8,128)(2,1)S(1)}, u32[]{:S(2)}, u32[]{:S(2)}) collective-permute-start(bf16[128,512]{1,0:T(8,128)(2,1)S(1)} %join_rows.1.refs_2_), channel_id=1, source_target_pairs={{0,2},{2,0},{4,6},{6,4},{8,10},{10,8},{12,14},{14,12},{16,18},{18,... | collective-permute-start | bytes 393224 | tf_op jit(solution)/shard_map/ppermute | solution.py:366
  19.7 7.6 %collective-permute-start.11 = (bf16[128,512]{1,0:T(8,128)(2,1)S(1)}, bf16[128,512]{1,0:T(8,128)(2,1)S(1)}, u32[]{:S(2)}, u32[]{:S(2)}) collective-permute-start(bf16[128,512]{1,0:T(8,128)(2,1)S(1)} %pass_on.4.refs_4_), channel_id=1, source_target_pairs={{0,2},{2,0},{4,6},{6,4},{8,10},{10,8},{12,14},{14,12},{16,18},{18,... | collective-permute-start | bytes 393224 | tf_op jit(solution)/shard_map/ppermute | solution.py:366
  20.3 13.5 %collective-permute-start.4 = (bf16[128,512]{1,0:T(8,128)(2,1)S(1)}, bf16[128,512]{1,0:T(8,128)(2,1)S(1)}, u32[]{:S(2)}, u32[]{:S(2)}) collective-permute-start(bf16[128,512]{1,0:T(8,128)(2,1)S(1)} %collective-permute-done.3.refs_2_), channel_id=1, source_target_pairs={{0,2},{2,0},{4,6},{6,4},{8,10},{10,8},{12,14},{14,12},{16,18},{18,... | collective-permute-start | bytes 393224 | tf_op jit(solution)/shard_map/ppermute | solution.py:366
  23.8 9.9 %collective-permute-start.9 = (bf16[128,512]{1,0:T(8,128)(2,1)S(1)}, bf16[128,512]{1,0:T(8,128)(2,1)S(1)}, u32[]{:S(2)}, u32[]{:S(2)}) collective-permute-start(bf16[128,512]{1,0:T(8,128)(2,1)S(1)} %pass_on.5.refs_4_), channel_id=1, source_target_pairs={{0,2},{2,0},{4,6},{6,4},{8,10},{10,8},{12,14},{14,12},{16,18},{18,... | collective-permute-start | bytes 393224 | tf_op jit(solution)/shard_map/ppermute | solution.py:366
  23.9 8.2 %collective-permute-start.13 = (bf16[80,512]{1,0:T(8,128)(2,1)S(1)}, bf16[80,512]{1,0:T(8,128)(2,1)S(1)}, u32[]{:S(2)}, u32[]{:S(2)}) collective-permute-start(bf16[80,512]{1,0:T(8,128)(2,1)S(1)} %grow.1.refs_1_), channel_id=1, source_target_pairs={{0,16},{2,18},{4,20},{6,22},{8,24},{10,26},{12,28},{14,30},{16,0},... | collective-permute-start | bytes 245768 | tf_op jit(solution)/shard_map/ppermute | solution.py:366
  32.2 4.3 %collective-permute-start.14 = (bf16[64,512]{1,0:T(8,128)(2,1)S(1)}, bf16[64,512]{1,0:T(8,128)(2,1)S(1)}, u32[]{:S(2)}, u32[]{:S(2)}) collective-permute-start(bf16[64,512]{1,0:T(8,128)(2,1)S(1)} %get-tuple-element.47), channel_id=1, source_target_pairs={{0,4},{2,6},{4,0},{6,2},{8,12},{10,14},{12,8},{14,10},{16,20},{18,... | collective-permute-start | bytes 196616 | tf_op jit(solution)/shard_map/ppermute | solution.py:366
  35.6 5.7 %collective-permute-start.12 = (bf16[128,640]{1,0:T(8,128)(2,1)S(1)}, bf16[128,640]{1,0:T(8,128)(2,1)S(1)}, u32[]{:S(2)}, u32[]{:S(2)}) collective-permute-start(bf16[128,640]{1,0:T(8,128)(2,1)S(1)} %get-tuple-element.43), channel_id=1, source_target_pairs={{0,4},{2,6},{4,0},{6,2},{8,12},{10,14},{12,8},{14,10},{16,20},{18,... | collective-permute-start | bytes 491528 | tf_op jit(solution)/shard_map/ppermute | solution.py:366
  36.7 1.4 %collective-permute-start.15 = (bf16[128,512]{1,0:T(8,128)(2,1)S(1)}, bf16[128,512]{1,0:T(8,128)(2,1)S(1)}, u32[]{:S(2)}, u32[]{:S(2)}) collective-permute-start(bf16[128,512]{1,0:T(8,128)(2,1)S(1)} %get-tuple-element.49), channel_id=1, source_target_pairs={{0,2},{2,0},{4,6},{6,4},{8,10},{10,8},{12,14},{14,12},{16,18},{18,... | collective-permute-start | bytes 393224 | tf_op jit(solution)/shard_map/ppermute | solution.py:366

commit v5 on v4

--- a/solution.py
+++ b/solution.py
@@ -267,12 +267,18 @@
     ret_out.wait()
 
 
-def attend(hops, last, q_ref, q_other_ref, *refs):
+def copy_after(source, out):
+    out[...] = source[...]
+
+
+def attend(hops, last, sides, *refs):
     count = len(hops)
+    queries, refs = refs[: len(sides)], refs[len(sides) :]
     blocks, refs = refs[: 2 * count], refs[2 * count :]
-    carried, refs = (refs[:4], refs[4:]) if last else ((), refs)
+    taken = 2 * len(sides) if last else 0
+    carried, refs = refs[:taken], refs[taken:]
     outs, (keys, values) = refs[:-2], refs[-2:]
-    rows, wide = q_ref.shape
+    rows, wide = queries[0].shape
     heads = wide // HD
     length, width = blocks[0].shape[0], blocks[0].shape[1] // 2
     group = wide // width
@@ -294,7 +300,8 @@
     scale = 1.0 / (math.sqrt(HD) * math.log(2.0))
     row = lax.broadcasted_iota(jnp.int32, (rows, total), 0)
     lane = lax.broadcasted_iota(jnp.int32, (rows, LANES), 1)
-    for which, (query, place) in enumerate(((q_other_ref, 1 - high), (q_ref, high))):
+    for which, (query, side) in enumerate(zip(queries, sides)):
+        place = jnp.bitwise_xor(high, side)
         allowed = row + (2 * place + low) * rows >= limit
         stats = jnp.zeros((rows, LANES), F32)
         if last:
@@ -412,8 +419,13 @@
         )
     }
     chip_other = swap(chip_send, 2)
-    q_cross = pass_on(q_cross, chip_send)
     q_other = swap(q_cross, 2)
+    bit = far // 2
+    while bit > 1:
+        for s in list(blocks):
+            blocks[s ^ bit] = swap(blocks[s], 4 * bit)
+        bit //= 2
+    blocks[1] = swap(blocks[0], 4)
     window = call(
         plane_total,
         [shape((quarter + PAD, wide))],
@@ -421,13 +433,6 @@
         name="plane_total",
         after=(factor,),
     )
-    bit = far // 2
-    while bit:
-        for s in list(blocks):
-            if s and bit == 1:
-                blocks[s] = pass_on(blocks[s], window)
-            blocks[s ^ bit] = swap(blocks[s], 4 * bit)
-        bit //= 2
     planes, bit = [], 1
     while bit < far:
         planes.append(swap(window, 4 * bit))
@@ -437,43 +442,35 @@
                 [shape(window.shape)],
                 (window, planes[-1]),
                 name="grow",
-                after=(q_other,),
+                after=(q_other, *[blocks[s] for s in blocks if s]),
             )
         bit *= 2
 
-    for s in blocks:
-        if s % 2 and s > 1:
-            blocks[s] = pass_on(blocks[s], window)
-    def look(hops, last, outs, carried, name):
+    def look(hops, last, outs, queries, carried, name):
         keys = 2 * len(hops) * n * length
         both = []
         for s in hops:
-            both += [blocks[s], swap(blocks[s], 1)]
+            if s not in swapped:
+                swapped[s] = swap(blocks[s], 1)
+            both += [blocks[s], swapped[s]]
         return call(
-            functools.partial(attend, hops, last),
+            functools.partial(attend, hops, last, [side for _, side in queries]),
             outs,
-            (q_cross, q_other, *both, *carried),
+            (*[query for query, _ in queries], *both, *carried),
             scratch=[pltpu.VMEM((keys, width), BF16) for _ in range(2)],
             name=name,
         )
 
-    hops = list(blocks)
-    near = far // 2
+    swapped = {}
+    near = list(blocks)
     so_far = look(
-        hops[:near],
+        near,
         False,
         [shape((rows, wide), F32), shape((rows, LANES), F32)] * 2,
+        ((q_other, 1), (q_cross, 0)),
         (),
         "attend_near",
     )
-    part_send, part_keep = look(
-        hops[near:],
-        True,
-        [shape((rows, wide + LANES)), shape((rows, wide + LANES), F32)],
-        so_far,
-        "attend_far",
-    )
-    part_other = swap(part_send, 2)
     prior_send, prior_keep = call(
         chip_priors,
         [shape((quarter, wide)), shape((quarter, wide), F32)],
@@ -481,6 +478,15 @@
         name="chip_priors",
         after=so_far[1:2],
     )
+    for s in near:
+        if s > 1:
+            ready = call(copy_after, [shape(blocks[s].shape)], (blocks[s],), after=(window,))
+            blocks[s ^ 1] = pass_on(swap(ready, 4), prior_send)
+    hops = [s for s in blocks if s not in near]
+    packed = (rows, wide + LANES)
+    part_send = look(hops, True, [shape(packed)], ((q_other, 1),), so_far[:2], "attend_far")
+    part_keep = look(hops, True, [shape(packed, F32)], ((q_cross, 0),), so_far[2:], "attend_own")
+    part_other = swap(part_send, 2)
     prior_other = swap(prior_send, 2)
     state_send, state_keep = call(
         block_priors,

time: 42.6 us -> 38 us (0.89)
  starting transfers between devices: 18 us -> 15.5 us
  waiting for transfers between devices: 16.2 us -> 14 us
    ppermute x15, starting transfers between devices: 15.4 us -> 12.9 us  [swap(): return lax.ppermute(value, 'ctx', [(b, b ^ bit) for b in range(count)])]
    ppermute x15, waiting for transfers between devices: 13.6 us -> 11.3 us  [swap(): return lax.ppermute(value, 'ctx', [(b, b ^ bit) for b in range(count)])]
  transfers between devices with their start and end apart: 16 -> 16, of which waited for: 9 -> 10; matrix products, arithmetic and copies ran while one was open for 0% -> 0% of each run, Pallas kernels for 10% -> 12%
where the time goes in v5:
time: 38 us; the launch traced here: 37.9 us
  starting transfers between devices  15.5 us (41%)
  waiting for transfers between devices  14 us (37%)
  Pallas kernels  7.67 us (20%)
  between operations  0.76 us (2%)
    ppermute x15, starting transfers between devices, swap(): return lax.ppermute(value, 'ctx', [(b, b ^ bit) for b in range(count)])  12.9 us
    ppermute x15, waiting for transfers between devices, swap(): return lax.ppermute(value, 'ctx', [(b, b ^ bit) for b in range(count)])  11.3 us
    pallas_call x15, Pallas kernels, call(): pl.pallas_call(kernel, out_shape=outs[0] if single else tuple(outs), in_s...  7.67 us
    ppermute x1, waiting for transfers between devices, to_head(): return lax.ppermute(value, 'head', [(y, (y + e) % n) for y in range(n)])  2.69 us
    ppermute x1, starting transfers between devices, to_head(): return lax.ppermute(value, 'head', [(y, (y + e) % n) for y in range(n)])  2.6 us
  transfers between devices with their start and end apart: 16, of which 10 were waited for; matrix products, arithmetic and copies ran while one was open for 0% of the time, Pallas kernels for 12%

profile of v5, /device:TPU:0, one launch (start us, length us, event | category | flops | bytes accessed | tf_op | source)
XLA Modules:
  0.0 37.9 jit_solution(7041559487871929082)
XLA Ops:
  0.6 1.3 %load_all.1 = (bf16[64,512]{1,0:T(8,128)(2,1)S(1)}, bf16[64,512]{1,0:T(8,128)(2,1)S(1)}, bf16[128,512]{1,0:T(8,128)(2,1)S(1)}, bf16[128,512]{1,0:T(8,128)(2,1)S(...) custom-call(bf16[64,512]{1,0:T(8,128)(2,1)} %refs_0_.1, ...), custom_call_target="tpu_custom_call" | custom-call | flops 1000 | bytes 1000 | tf_op jit(solution)/shard_map/load_all/pallas_call | solution.py:34
  2.0 0.7 %summarize.1 = (bf16[144,512]{1,0:T(8,128)(2,1)S(1)}, f32[144,512]{1,0:T(8,128)S(1)}) custom-call(bf16[128,512]{1,0:T(8,128)(2,1)S(1)} %get-tuple-element.27.refs_0_.refs_1_, bf16[128,512]{1,0:T(8,128)(2,1)S(1)} %get-tuple-element.28.refs_1_.refs_2_, f32[2,128]{1,0:T(2,128)S(1)} %get-tuple-element.29.refs_2_.refs_3_), custom_call_target="tpu_custom_call" | custom-call | flops 1000 | bytes 1000 | tf_op jit(solution)/shard_map/summarize/pallas_call | solution.py:34
  2.6 0.5 %collective-permute-start.2 = (bf16[144,512]{1,0:T(8,128)(2,1)S(1)}, bf16[144,512]{1,0:T(8,128)(2,1)S(1)}, u32[]{:S(2)}, u32[]{:S(2)}) collective-permute-start(bf16[144,512]{1,0:T(8,128)(2,1)S(1)} %get-tuple-element.31), channel_id=1, source_target_pairs={{0,2},{2,0},{4,6},{6,4},{8,10},{10,8},{12,14},{14,12},{16,18},{18,... | collective-permute-start | bytes 442376 | tf_op jit(solution)/shard_map/ppermute | solution.py:373
  3.2 2.6 %collective-permute-start = (bf16[64,512]{1,0:T(8,128)(2,1)S(1)}, bf16[64,512]{1,0:T(8,128)(2,1)S(1)}, u32[]{:S(2)}, u32[]{:S(2)}) collective-permute-start(bf16[64,512]{1,0:T(8,128)(2,1)S(1)} %get-tuple-element.26), channel_id=1, source_target_pairs={{0,1},{1,0},{2,3},{3,2},{4,5},{5,4},{6,7},{7,6},{8,9},{9,8},{10,11... | collective-permute-start | bytes 196616 | tf_op jit(solution)/shard_map/ppermute | solution.py:376
  5.8 2.7 %collective-permute-done.refs_1_.refs_2_ = bf16[64,512]{1,0:T(8,128)(2,1)S(1)} collective-permute-done((bf16[64,512]{1,0:T(8,128)(2,1)S(1)}, bf16[64,512]{1,0:T(8,128)(2,1)S(1)}, u32[]{:S(2)}, u32[]{:S(2)}) %collective-permute-start) | collective-permute-done | bytes 65568 | tf_op jit(solution)/shard_map/ppermute | solution.py:376
  8.4 0.0 collective-permute-done.2.refs_1_
  8.4 0.1 chip_total.1
  8.6 1.8 %collective-permute-start.3 = (bf16[80,512]{1,0:T(8,128)(2,1)S(1)}, bf16[80,512]{1,0:T(8,128)(2,1)S(1)}, u32[]{:S(2)}, u32[]{:S(2)}) collective-permute-start(bf16[80,512]{1,0:T(8,128)(2,1)S(1)} %get-tuple-element.33.refs_4_), channel_id=1, source_target_pairs={{0,4},{2,6},{4,0},{6,2},{8,12},{10,14},{12,8},{14,10},{16,20},{18,... | collective-permute-start | bytes 245768 | tf_op jit(solution)/shard_map/ppermute | solution.py:373
  10.4 1.6 %collective-permute-start.6 = (bf16[128,512]{1,0:T(8,128)(2,1)S(1)}, bf16[128,512]{1,0:T(8,128)(2,1)S(1)}, u32[]{:S(2)}, u32[]{:S(2)}) collective-permute-start(bf16[128,512]{1,0:T(8,128)(2,1)S(1)} %join_rows.1.refs_2_), channel_id=1, source_target_pairs={{0,8},{2,10},{4,12},{6,14},{8,0},{10,2},{12,4},{14,6},{16,24},{18,... | collective-permute-start | bytes 393224 | tf_op jit(solution)/shard_map/ppermute | solution.py:373
  12.0 2.6 %collective-permute-start.1 = (bf16[128,512]{1,0:T(8,128)(2,1)S(1)}, bf16[128,512]{1,0:T(8,128)(2,1)S(1)}, u32[]{:S(2)}, u32[]{:S(2)}) collective-permute-start(bf16[128,512]{1,0:T(8,128)(2,1)S(1)} %join_rows.1.refs_2_), channel_id=1, source_target_pairs={{0,16},{2,18},{4,20},{6,22},{8,24},{10,26},{12,28},{14,30},{16,0},... | collective-permute-start | bytes 393224 | tf_op jit(solution)/shard_map/ppermute | solution.py:373
  14.6 0.5 %collective-permute-start.5 = (bf16[128,512]{1,0:T(8,128)(2,1)S(1)}, bf16[128,512]{1,0:T(8,128)(2,1)S(1)}, u32[]{:S(2)}, u32[]{:S(2)}) collective-permute-start(bf16[128,512]{1,0:T(8,128)(2,1)S(1)} %get-tuple-element.24.refs_1_.refs_0_), channel_id=1, source_target_pairs={{0,4},{2,6},{4,0},{6,2},{8,12},{10,14},{12,8},{14,10},{16,20},{18,... | collective-permute-start | bytes 393224 | tf_op jit(solution)/shard_map/ppermute | solution.py:373
  15.2 0.6 %retain_inside.1 = (f32[128,512]{1,0:T(8,128)S(1)}, f32[128,2]{1,0:T(8,128)S(1)}) custom-call(bf16[128,512]{1,0:T(8,128)(2,1)S(1)} %get-tuple-element.34.refs_0_.refs_2_, bf16[128,512]{1,0:T(8,128)(2,1)S(1)} %get-tuple-element.27.refs_0_.refs_1_, bf16[128,512]{1,0:T(8,128)(2,1)S(1)} %get-tuple-element.28.refs_1_.refs_2_, ...), custom_call_target="tpu_custom_call" | custom-call | flops 1000 | bytes 1000 | tf_op jit(solution)/shard_map/retain_inside/pallas_call | solution.py:34
  15.8 0.0 collective-permute-done.3.refs_1_
  15.8 0.5 %collective-permute-start.4 = (bf16[80,512]{1,0:T(8,128)(2,1)S(1)}, bf16[80,512]{1,0:T(8,128)(2,1)S(1)}, u32[]{:S(2)}, u32[]{:S(2)}) collective-permute-start(bf16[80,512]{1,0:T(8,128)(2,1)S(1)} %plane_total.1.refs_0_), channel_id=1, source_target_pairs={{0,8},{2,10},{4,12},{6,14},{8,0},{10,2},{12,4},{14,6},{16,24},{18,... | collective-permute-start | bytes 245768 | tf_op jit(solution)/shard_map/ppermute | solution.py:373
  16.3 0.0 collective-permute-start.9
  16.3 0.8 %collective-permute-done.6.refs_4_.refs_6_ = bf16[128,512]{1,0:T(8,128)(2,1)S(1)} collective-permute-done((bf16[128,512]{1,0:T(8,128)(2,1)S(1)}, bf16[128,512]{1,0:T(8,128)(2,1)S(1)}, u32[]{:S(2)}, u32[]{:S(2)}) %collective-permute-start.6) | collective-permute-done | bytes 131104 | tf_op jit(solution)/shard_map/ppermute | solution.py:373
  17.1 0.0 collective-permute-start.11
  17.1 1.8 %collective-permute-done.1.refs_3_.refs_0_.refs_4_ = bf16[128,512]{1,0:T(8,128)(2,1)S(1)} collective-permute-done((bf16[128,512]{1,0:T(8,128)(2,1)S(1)}, bf16[128,512]{1,0:T(8,128)(2,1)S(1)}, u32[]{:S(2)}, u32[]{:S(2)}) %collective-permute-start.1) | collective-permute-done | bytes 131104 | tf_op jit(solution)/shard_map/ppermute | solution.py:373
  18.9 0.0 collective-permute-start.10
  18.9 0.7 %collective-permute-done.5.refs_2_.refs_0_ = bf16[128,512]{1,0:T(8,128)(2,1)S(1)} collective-permute-done((bf16[128,512]{1,0:T(8,128)(2,1)S(1)}, bf16[128,512]{1,0:T(8,128)(2,1)S(1)}, u32[]{:S(2)}, u32[]{:S(2)}) %collective-permute-start.5) | collective-permute-done | bytes 131104 | tf_op jit(solution)/shard_map/ppermute | solution.py:373
  19.6 0.7 %collective-permute-done.4.refs_1_.refs_2_ = bf16[80,512]{1,0:T(8,128)(2,1)S(1)} collective-permute-done((bf16[80,512]{1,0:T(8,128)(2,1)S(1)}, bf16[80,512]{1,0:T(8,128)(2,1)S(1)}, u32[]{:S(2)}, u32[]{:S(2)}) %collective-permute-start.4) | collective-permute-done | bytes 81952 | tf_op jit(solution)/shard_map/ppermute | solution.py:373
  20.3 0.1 grow.1.refs_1_
  20.4 1.3 %collective-permute-start.7 = (bf16[128,512]{1,0:T(8,128)(2,1)S(1)}, bf16[128,512]{1,0:T(8,128)(2,1)S(1)}, u32[]{:S(2)}, u32[]{:S(2)}) collective-permute-start(bf16[128,512]{1,0:T(8,128)(2,1)S(1)} %shard_map.95), channel_id=1, source_target_pairs={{0,8},{2,10},{4,12},{6,14},{8,0},{10,2},{12,4},{14,6},{16,24},{18,... | collective-permute-start | bytes 393224 | tf_op jit(solution)/shard_map/ppermute | solution.py:373
  21.7 2.4 %collective-permute-start.8 = (bf16[80,512]{1,0:T(8,128)(2,1)S(1)}, bf16[80,512]{1,0:T(8,128)(2,1)S(1)}, u32[]{:S(2)}, u32[]{:S(2)}) collective-permute-start(bf16[80,512]{1,0:T(8,128)(2,1)S(1)} %grow.1.refs_1_), channel_id=1, source_target_pairs={{0,16},{2,18},{4,20},{6,22},{8,24},{10,26},{12,28},{14,30},{16,0},... | collective-permute-start | bytes 245768 | tf_op jit(solution)/shard_map/ppermute | solution.py:373
  24.1 0.0 collective-permute-done.9.refs_3_
  24.1 0.0 collective-permute-done.11.refs_7_
  24.1 0.0 collective-permute-done.10.refs_5_
  24.1 1.7 %attend_near.1 = (f32[128,512]{1,0:T(8,128)S(1)}, f32[128,128]{1,0:T(8,128)S(1)}, f32[128,512]{1,0:T(8,128)S(1)}, f32[128,128]{1,0:T(8,128)S(1)}) custom-call(bf16[128,512]{1,0:T(8,128)(2,1)S(1)} %collective-permute-done.5.refs_2_.refs_0_, bf16[128,512]{1,0:T(8,128)(2,1)S(1)} %get-tuple-element.24.refs_1_.refs_0_, bf16[128,512]{1,0:T(8,128)(2,1)S(1)} %join_rows.1.refs_2_, ...), custom_call_target="tpu_custom_call" | custom-call | flops 1000 | bytes 1000 | tf_op jit(solution)/shard_map/attend_near/pallas_call | solution.py:34
  25.8 2.2 %collective-permute-done.8.refs_3_ = bf16[80,512]{1,0:T(8,128)(2,1)S(1)} collective-permute-done((bf16[80,512]{1,0:T(8,128)(2,1)S(1)}, bf16[80,512]{1,0:T(8,128)(2,1)S(1)}, u32[]{:S(2)}, u32[]{:S(2)}) %collective-permute-start.8) | collective-permute-done | bytes 81952 | tf_op jit(solution)/shard_map/ppermute | solution.py:373
  28.0 0.1 chip_priors.1
  28.1 0.0 collective-permute-done.7.refs_0_
  28.1 0.1 collective-permute-start.12
  28.2 0.6 %collective-permute-start.14 = (bf16[64,512]{1,0:T(8,128)(2,1)S(1)}, bf16[64,512]{1,0:T(8,128)(2,1)S(1)}, u32[]{:S(2)}, u32[]{:S(2)}) collective-permute-start(bf16[64,512]{1,0:T(8,128)(2,1)S(1)} %get-tuple-element.37.refs_1_), channel_id=1, source_target_pairs={{0,4},{2,6},{4,0},{6,2},{8,12},{10,14},{12,8},{14,10},{16,20},{18,... | collective-permute-start | bytes 196616 | tf_op jit(solution)/shard_map/ppermute | solution.py:373
  28.8 0.7 %collective-permute-done.12.refs_2_ = bf16[128,512]{1,0:T(8,128)(2,1)S(1)} collective-permute-done((bf16[128,512]{1,0:T(8,128)(2,1)S(1)}, bf16[128,512]{1,0:T(8,128)(2,1)S(1)}, u32[]{:S(2)}, u32[]{:S(2)}) %collective-permute-start.12) | collective-permute-done | bytes 131104 | tf_op jit(solution)/shard_map/ppermute | solution.py:373
  29.5 0.9 %attend_far.1 = bf16[128,640]{1,0:T(8,128)(2,1)S(1)} custom-call(bf16[128,512]{1,0:T(8,128)(2,1)S(1)} %collective-permute-done.5.refs_2_.refs_0_, bf16[128,512]{1,0:T(8,128)(2,1)S(1)} %pass_on.1.refs_1_, bf16[128,512]{1,0:T(8,128)(2,1)S(1)} %collective-permute-done.12.refs_2_, f32[128,512]{1,0:T(8,128)S(1)} %get-tuple-element.40.refs_3_, ...), custom_call_target="tpu_custom_call" | custom-call | flops 1000 | bytes 1000 | tf_op jit(solution)/shard_map/attend_far/pallas_call | solution.py:34
  30.5 0.8 %collective-permute-start.13 = (bf16[128,640]{1,0:T(8,128)(2,1)S(1)}, bf16[128,640]{1,0:T(8,128)(2,1)S(1)}, u32[]{:S(2)}, u32[]{:S(2)}) collective-permute-start(bf16[128,640]{1,0:T(8,128)(2,1)S(1)} %attend_far.1), channel_id=1, source_target_pairs={{0,4},{2,6},{4,0},{6,2},{8,12},{10,14},{12,8},{14,10},{16,20},{18,... | collective-permute-start | bytes 491528 | tf_op jit(solution)/shard_map/ppermute | solution.py:373
  31.3 1.4 %collective-permute-done.14.refs_3_ = bf16[64,512]{1,0:T(8,128)(2,1)S(1)} collective-permute-done((bf16[64,512]{1,0:T(8,128)(2,1)S(1)}, bf16[64,512]{1,0:T(8,128)(2,1)S(1)}, u32[]{:S(2)}, u32[]{:S(2)}) %collective-permute-start.14) | collective-permute-done | bytes 65568 | tf_op jit(solution)/shard_map/ppermute | solution.py:373
  32.7 0.1 block_priors.1
  32.9 0.1 collective-permute-start.15
  33.0 0.9 %attend_own.1.refs_0_ = f32[128,640]{1,0:T(8,128)S(1)} custom-call(bf16[128,512]{1,0:T(8,128)(2,1)S(1)} %get-tuple-element.24.refs_1_.refs_0_, bf16[128,512]{1,0:T(8,128)(2,1)S(1)} %pass_on.1.refs_1_, bf16[128,512]{1,0:T(8,128)(2,1)S(1)} %collective-permute-done.12.refs_2_, f32[128,512]{1,0:T(8,128)S(1)} %get-tuple-element.38.refs_3_, ...), custom_call_target="tpu_custom_call" | custom-call | flops 1000 | bytes 1000 | tf_op jit(solution)/shard_map/attend_own/pallas_call | solution.py:34
  33.9 0.4 %collective-permute-done.15.refs_7_ = bf16[128,512]{1,0:T(8,128)(2,1)S(1)} collective-permute-done((bf16[128,512]{1,0:T(8,128)(2,1)S(1)}, bf16[128,512]{1,0:T(8,128)(2,1)S(1)}, u32[]{:S(2)}, u32[]{:S(2)}) %collective-permute-start.15) | collective-permute-done | bytes 131104 | tf_op jit(solution)/shard_map/ppermute | solution.py:373
  34.3 2.5 %collective-permute-done.13.refs_1_ = bf16[128,640]{1,0:T(8,128)(2,1)S(1)} collective-permute-done((bf16[128,640]{1,0:T(8,128)(2,1)S(1)}, bf16[128,640]{1,0:T(8,128)(2,1)S(1)}, u32[]{:S(2)}, u32[]{:S(2)}) %collective-permute-start.13) | collective-permute-done | bytes 163872 | tf_op jit(solution)/shard_map/ppermute | solution.py:373
  36.8 1.1 %finish.1 = (bf16[128,512]{1,0:T(8,128)(2,1)}, bf16[128,512]{1,0:T(8,128)(2,1)}) custom-call(f32[128,640]{1,0:T(8,128)S(1)} %attend_own.1.refs_0_, bf16[128,640]{1,0:T(8,128)(2,1)S(1)} %collective-permute-done.13.refs_1_, bf16[128,512]{1,0:T(8,128)(2,1)S(1)} %get-tuple-element.34.refs_0_.refs_2_, bf16[128,512]{1,0:T(8,128)(2,1)S(1)} %get-tuple-element.41.refs_3_, ...), custom_call_target="tpu_custom_call" | custom-call | flops 1000 | bytes 1000 | tf_op jit(solution)/shard_map/finish/pallas_call | solution.py:34
  (4 shorter events, 0.1 us)
Async XLA Ops:
  2.6 5.8 %collective-permute-start.2 = (bf16[144,512]{1,0:T(8,128)(2,1)S(1)}, bf16[144,512]{1,0:T(8,128)(2,1)S(1)}, u32[]{:S(2)}, u32[]{:S(2)}) collective-permute-start(bf16[144,512]{1,0:T(8,128)(2,1)S(1)} %get-tuple-element.31), channel_id=1, source_target_pairs={{0,2},{2,0},{4,6},{6,4},{8,10},{10,8},{12,14},{14,12},{16,18},{18,... | collective-permute-start | bytes 442376 | tf_op jit(solution)/shard_map/ppermute | solution.py:373
  3.2 5.3 %collective-permute-start = (bf16[64,512]{1,0:T(8,128)(2,1)S(1)}, bf16[64,512]{1,0:T(8,128)(2,1)S(1)}, u32[]{:S(2)}, u32[]{:S(2)}) collective-permute-start(bf16[64,512]{1,0:T(8,128)(2,1)S(1)} %get-tuple-element.26), channel_id=1, source_target_pairs={{0,1},{1,0},{2,3},{3,2},{4,5},{5,4},{6,7},{7,6},{8,9},{9,8},{10,11... | collective-permute-start | bytes 196616 | tf_op jit(solution)/shard_map/ppermute | solution.py:376
  8.6 7.2 %collective-permute-start.3 = (bf16[80,512]{1,0:T(8,128)(2,1)S(1)}, bf16[80,512]{1,0:T(8,128)(2,1)S(1)}, u32[]{:S(2)}, u32[]{:S(2)}) collective-permute-start(bf16[80,512]{1,0:T(8,128)(2,1)S(1)} %get-tuple-element.33.refs_4_), channel_id=1, source_target_pairs={{0,4},{2,6},{4,0},{6,2},{8,12},{10,14},{12,8},{14,10},{16,20},{18,... | collective-permute-start | bytes 245768 | tf_op jit(solution)/shard_map/ppermute | solution.py:373
  10.4 6.7 %collective-permute-start.6 = (bf16[128,512]{1,0:T(8,128)(2,1)S(1)}, bf16[128,512]{1,0:T(8,128)(2,1)S(1)}, u32[]{:S(2)}, u32[]{:S(2)}) collective-permute-start(bf16[128,512]{1,0:T(8,128)(2,1)S(1)} %join_rows.1.refs_2_), channel_id=1, source_target_pairs={{0,8},{2,10},{4,12},{6,14},{8,0},{10,2},{12,4},{14,6},{16,24},{18,... | collective-permute-start | bytes 393224 | tf_op jit(solution)/shard_map/ppermute | solution.py:373
  12.0 6.9 %collective-permute-start.1 = (bf16[128,512]{1,0:T(8,128)(2,1)S(1)}, bf16[128,512]{1,0:T(8,128)(2,1)S(1)}, u32[]{:S(2)}, u32[]{:S(2)}) collective-permute-start(bf16[128,512]{1,0:T(8,128)(2,1)S(1)} %join_rows.1.refs_2_), channel_id=1, source_target_pairs={{0,16},{2,18},{4,20},{6,22},{8,24},{10,26},{12,28},{14,30},{16,0},... | collective-permute-start | bytes 393224 | tf_op jit(solution)/shard_map/ppermute | solution.py:373
  14.6 5.0 %collective-permute-start.5 = (bf16[128,512]{1,0:T(8,128)(2,1)S(1)}, bf16[128,512]{1,0:T(8,128)(2,1)S(1)}, u32[]{:S(2)}, u32[]{:S(2)}) collective-permute-start(bf16[128,512]{1,0:T(8,128)(2,1)S(1)} %get-tuple-element.24.refs_1_.refs_0_), channel_id=1, source_target_pairs={{0,4},{2,6},{4,0},{6,2},{8,12},{10,14},{12,8},{14,10},{16,20},{18,... | collective-permute-start | bytes 393224 | tf_op jit(solution)/shard_map/ppermute | solution.py:373
  15.8 4.5 %collective-permute-start.4 = (bf16[80,512]{1,0:T(8,128)(2,1)S(1)}, bf16[80,512]{1,0:T(8,128)(2,1)S(1)}, u32[]{:S(2)}, u32[]{:S(2)}) collective-permute-start(bf16[80,512]{1,0:T(8,128)(2,1)S(1)} %plane_total.1.refs_0_), channel_id=1, source_target_pairs={{0,8},{2,10},{4,12},{6,14},{8,0},{10,2},{12,4},{14,6},{16,24},{18,... | collective-permute-start | bytes 245768 | tf_op jit(solution)/shard_map/ppermute | solution.py:373
  16.3 7.8 %collective-permute-start.9 = (bf16[128,512]{1,0:T(8,128)(2,1)S(1)}, bf16[128,512]{1,0:T(8,128)(2,1)S(1)}, u32[]{:S(2)}, u32[]{:S(2)}) collective-permute-start(bf16[128,512]{1,0:T(8,128)(2,1)S(1)} %join_rows.1.refs_2_), channel_id=1, source_target_pairs={{0,2},{2,0},{4,6},{6,4},{8,10},{10,8},{12,14},{14,12},{16,18},{18,... | collective-permute-start | bytes 393224 | tf_op jit(solution)/shard_map/ppermute | solution.py:373
  17.1 7.0 %collective-permute-start.11 = (bf16[128,512]{1,0:T(8,128)(2,1)S(1)}, bf16[128,512]{1,0:T(8,128)(2,1)S(1)}, u32[]{:S(2)}, u32[]{:S(2)}) collective-permute-start(bf16[128,512]{1,0:T(8,128)(2,1)S(1)} %collective-permute-done.6.refs_4_.refs_6_), channel_id=1, source_target_pairs={{0,2},{2,0},{4,6},{6,4},{8,10},{10,8},{12,14},{14,12},{16,18},{18,... | collective-permute-start | bytes 393224 | tf_op jit(solution)/shard_map/ppermute | solution.py:373
  18.9 5.2 %collective-permute-start.10 = (bf16[128,512]{1,0:T(8,128)(2,1)S(1)}, bf16[128,512]{1,0:T(8,128)(2,1)S(1)}, u32[]{:S(2)}, u32[]{:S(2)}) collective-permute-start(bf16[128,512]{1,0:T(8,128)(2,1)S(1)} %collective-permute-done.1.refs_3_.refs_0_.refs_4_), channel_id=1, source_target_pairs={{0,2},{2,0},{4,6},{6,4},{8,10},{10,8},{12,14},{14,12},{16,18},{18,... | collective-permute-start | bytes 393224 | tf_op jit(solution)/shard_map/ppermute | solution.py:373
  20.4 7.7 %collective-permute-start.7 = (bf16[128,512]{1,0:T(8,128)(2,1)S(1)}, bf16[128,512]{1,0:T(8,128)(2,1)S(1)}, u32[]{:S(2)}, u32[]{:S(2)}) collective-permute-start(bf16[128,512]{1,0:T(8,128)(2,1)S(1)} %shard_map.95), channel_id=1, source_target_pairs={{0,8},{2,10},{4,12},{6,14},{8,0},{10,2},{12,4},{14,6},{16,24},{18,... | collective-permute-start | bytes 393224 | tf_op jit(solution)/shard_map/ppermute | solution.py:373
  21.7 6.3 %collective-permute-start.8 = (bf16[80,512]{1,0:T(8,128)(2,1)S(1)}, bf16[80,512]{1,0:T(8,128)(2,1)S(1)}, u32[]{:S(2)}, u32[]{:S(2)}) collective-permute-start(bf16[80,512]{1,0:T(8,128)(2,1)S(1)} %grow.1.refs_1_), channel_id=1, source_target_pairs={{0,16},{2,18},{4,20},{6,22},{8,24},{10,26},{12,28},{14,30},{16,0},... | collective-permute-start | bytes 245768 | tf_op jit(solution)/shard_map/ppermute | solution.py:373
  28.1 1.4 %collective-permute-start.12 = (bf16[128,512]{1,0:T(8,128)(2,1)S(1)}, bf16[128,512]{1,0:T(8,128)(2,1)S(1)}, u32[]{:S(2)}, u32[]{:S(2)}) collective-permute-start(bf16[128,512]{1,0:T(8,128)(2,1)S(1)} %pass_on.1.refs_1_), channel_id=1, source_target_pairs={{0,2},{2,0},{4,6},{6,4},{8,10},{10,8},{12,14},{14,12},{16,18},{18,... | collective-permute-start | bytes 393224 | tf_op jit(solution)/shard_map/ppermute | solution.py:373
  28.2 4.5 %collective-permute-start.14 = (bf16[64,512]{1,0:T(8,128)(2,1)S(1)}, bf16[64,512]{1,0:T(8,128)(2,1)S(1)}, u32[]{:S(2)}, u32[]{:S(2)}) collective-permute-start(bf16[64,512]{1,0:T(8,128)(2,1)S(1)} %get-tuple-element.37.refs_1_), channel_id=1, source_target_pairs={{0,4},{2,6},{4,0},{6,2},{8,12},{10,14},{12,8},{14,10},{16,20},{18,... | collective-permute-start | bytes 196616 | tf_op jit(solution)/shard_map/ppermute | solution.py:373
  30.5 6.3 %collective-permute-start.13 = (bf16[128,640]{1,0:T(8,128)(2,1)S(1)}, bf16[128,640]{1,0:T(8,128)(2,1)S(1)}, u32[]{:S(2)}, u32[]{:S(2)}) collective-permute-start(bf16[128,640]{1,0:T(8,128)(2,1)S(1)} %attend_far.1), channel_id=1, source_target_pairs={{0,4},{2,6},{4,0},{6,2},{8,12},{10,14},{12,8},{14,10},{16,20},{18,... | collective-permute-start | bytes 491528 | tf_op jit(solution)/shard_map/ppermute | solution.py:373
  32.9 1.4 %collective-permute-start.15 = (bf16[128,512]{1,0:T(8,128)(2,1)S(1)}, bf16[128,512]{1,0:T(8,128)(2,1)S(1)}, u32[]{:S(2)}, u32[]{:S(2)}) collective-permute-start(bf16[128,512]{1,0:T(8,128)(2,1)S(1)} %get-tuple-element.45), channel_id=1, source_target_pairs={{0,2},{2,0},{4,6},{6,4},{8,10},{10,8},{12,14},{14,12},{16,18},{18,... | collective-permute-start | bytes 393224 | tf_op jit(solution)/shard_map/ppermute | solution.py:373

commit v6 on v5

--- a/solution.py
+++ b/solution.py
@@ -372,8 +372,20 @@
     def swap(value, bit):
         return lax.ppermute(value, "ctx", [(b, b ^ bit) for b in range(count)])
 
-    def to_head(value, e):
-        return lax.ppermute(value, "head", [(y, (y + e) % n) for y in range(n)])
+    def to_head(value, e, bit):
+        pairs = [
+            (b * n + y, (b ^ (4 * bit)) * n + (y + e) % n) for b in range(count) for y in range(n)
+        ]
+        return lax.ppermute(value, ("ctx", "head"), pairs)
+
+    def joined(bit):
+        parts = [pieces[e] if e + bit == 0 else to_head(pieces[e], e, bit) for e in range(n)]
+        return call(
+            functools.partial(join_rows, n),
+            [shape((n * length, 2 * width))],
+            parts,
+            name="join_rows",
+        )
 
     plain = (k_ret, v_ret, log_decay.T, q_ret, q_cross, gate_ret)
     loaded = call(
@@ -386,7 +398,6 @@
     )
     pieces = loaded[:n]
     k_ret, v_ret, decays, q_ret, q_cross, gate_ret = loaded[n:]
-    arrived = [pieces[0]] + [to_head(pieces[e], e) for e in range(1, n)]
     sum_send, sum_keep = call(
         summarize,
         [shape((half + PAD, wide)), shape((half + PAD, wide), F32)],
@@ -401,7 +412,6 @@
         (sum_keep, sum_other),
         scratch=[pltpu.VMEM((half, wide), F32)],
         name="chip_total",
-        after=arrived[-1:],
     )
     inside, factor = call(
         retain_inside,
@@ -410,22 +420,15 @@
         name="retain_inside",
         after=(chip_send,),
     )
-    blocks = {
-        0: call(
-            functools.partial(join_rows, n),
-            [shape((n * length, 2 * width))],
-            arrived,
-            name="join_rows",
-        )
-    }
     chip_other = swap(chip_send, 2)
     q_other = swap(q_cross, 2)
+    blocks = {0: joined(0)}
     bit = far // 2
     while bit > 1:
         for s in list(blocks):
-            blocks[s ^ bit] = swap(blocks[s], 4 * bit)
+            blocks[s ^ bit] = joined(bit) if s == 0 else swap(blocks[s], 4 * bit)
         bit //= 2
-    blocks[1] = swap(blocks[0], 4)
+    blocks[1] = joined(1)
     window = call(
         plane_total,
         [shape((quarter + PAD, wide))],

time: 38 us -> 39.5 us (1.039)
  starting transfers between devices: 15.5 us -> 19.6 us
  waiting for transfers between devices: 14 us -> 11.3 us
    ppermute x15 -> x13, waiting for transfers between devices: 11.3 us -> 6.81 us  [swap(): return lax.ppermute(value, 'ctx', [(b, b ^ bit) for b in range(count)])]
    ppermute x1 -> x5, starting transfers between devices: 2.6 us -> 6.93 us  [to_head(): return lax.ppermute(value, ('ctx', 'head'), pairs)]
    ppermute x1 -> x5, waiting for transfers between devices: 2.69 us -> 4.48 us  [to_head(): return lax.ppermute(value, ('ctx', 'head'), pairs)]
    ppermute x15 -> x13, starting transfers between devices: 12.9 us -> 12.6 us  [swap(): return lax.ppermute(value, 'ctx', [(b, b ^ bit) for b in range(count)])]
    pallas_call x15 -> x17, Pallas kernels: 7.67 us -> 7.7 us  [call(): pl.pallas_call(kernel, out_shape=outs[0] if single else tuple(outs), in_s...]
  transfers between devices with their start and end apart: 16 -> 18, of which waited for: 10 -> 10; matrix products, arithmetic and copies ran while one was open for 0% -> 0% of each run, Pallas kernels for 12% -> 11%
where the time goes in v6:
time: 39.5 us; the launch traced here: 39.4 us
  starting transfers between devices  19.6 us (50%)
  waiting for transfers between devices  11.3 us (29%)
  Pallas kernels  7.7 us (19%)
  between operations  0.8 us (2%)
    ppermute x13, starting transfers between devices, swap(): return lax.ppermute(value, 'ctx', [(b, b ^ bit) for b in range(count)])  12.6 us
    pallas_call x17, Pallas kernels, call(): pl.pallas_call(kernel, out_shape=outs[0] if single else tuple(outs), in_s...  7.7 us
    ppermute x5, starting transfers between devices, to_head(): return lax.ppermute(value, ('ctx', 'head'), pairs)  6.93 us
    ppermute x13, waiting for transfers between devices, swap(): return lax.ppermute(value, 'ctx', [(b, b ^ bit) for b in range(count)])  6.81 us
    ppermute x5, waiting for transfers between devices, to_head(): return lax.ppermute(value, ('ctx', 'head'), pairs)  4.48 us
  transfers between devices with their start and end apart: 18, of which 10 were waited for; matrix products, arithmetic and copies ran while one was open for 0% of the time, Pallas kernels for 11%

profile of v6, /device:TPU:0, one launch (start us, length us, event | category | flops | bytes accessed | tf_op | source)
XLA Modules:
  0.0 39.4 jit_solution(12008019166438827205)
XLA Ops:
  0.6 1.3 %load_all.1 = (bf16[64,512]{1,0:T(8,128)(2,1)S(1)}, bf16[64,512]{1,0:T(8,128)(2,1)S(1)}, bf16[128,512]{1,0:T(8,128)(2,1)S(1)}, bf16[128,512]{1,0:T(8,128)(2,1)S(...) custom-call(bf16[64,512]{1,0:T(8,128)(2,1)} %refs_0_.1, ...), custom_call_target="tpu_custom_call" | custom-call | flops 1000 | bytes 1000 | tf_op jit(solution)/shard_map/load_all/pallas_call | solution.py:34
  2.0 0.7 %summarize.1 = (bf16[144,512]{1,0:T(8,128)(2,1)S(1)}, f32[144,512]{1,0:T(8,128)S(1)}) custom-call(bf16[128,512]{1,0:T(8,128)(2,1)S(1)} %get-tuple-element.27.refs_0_.refs_1_, bf16[128,512]{1,0:T(8,128)(2,1)S(1)} %get-tuple-element.28.refs_1_.refs_2_, f32[2,128]{1,0:T(2,128)S(1)} %get-tuple-element.29.refs_2_.refs_3_), custom_call_target="tpu_custom_call" | custom-call | flops 1000 | bytes 1000 | tf_op jit(solution)/shard_map/summarize/pallas_call | solution.py:34
  2.6 0.5 %collective-permute-start.2 = (bf16[144,512]{1,0:T(8,128)(2,1)S(1)}, bf16[144,512]{1,0:T(8,128)(2,1)S(1)}, u32[]{:S(2)}, u32[]{:S(2)}) collective-permute-start(bf16[144,512]{1,0:T(8,128)(2,1)S(1)} %get-tuple-element.31), channel_id=1, source_target_pairs={{0,2},{2,0},{4,6},{6,4},{8,10},{10,8},{12,14},{14,12},{16,18},{18,... | collective-permute-start | bytes 442376 | tf_op jit(solution)/shard_map/ppermute | solution.py:373
  3.2 1.0 %collective-permute-done.2.refs_1_ = bf16[144,512]{1,0:T(8,128)(2,1)S(1)} collective-permute-done((bf16[144,512]{1,0:T(8,128)(2,1)S(1)}, bf16[144,512]{1,0:T(8,128)(2,1)S(1)}, u32[]{:S(2)}, u32[]{:S(2)}) %collective-permute-start.2) | collective-permute-done | bytes 147488 | tf_op jit(solution)/shard_map/ppermute | solution.py:373
  4.2 0.1 chip_total.1
  4.3 2.9 %collective-permute-start.3 = (bf16[80,512]{1,0:T(8,128)(2,1)S(1)}, bf16[80,512]{1,0:T(8,128)(2,1)S(1)}, u32[]{:S(2)}, u32[]{:S(2)}) collective-permute-start(bf16[80,512]{1,0:T(8,128)(2,1)S(1)} %get-tuple-element.33.refs_4_), channel_id=1, source_target_pairs={{0,4},{2,6},{4,0},{6,2},{8,12},{10,14},{12,8},{14,10},{16,20},{18,... | collective-permute-start | bytes 245768 | tf_op jit(solution)/shard_map/ppermute | solution.py:373
  7.2 2.6 %collective-permute-start = (bf16[64,512]{1,0:T(8,128)(2,1)S(1)}, bf16[64,512]{1,0:T(8,128)(2,1)S(1)}, u32[]{:S(2)}, u32[]{:S(2)}) collective-permute-start(bf16[64,512]{1,0:T(8,128)(2,1)S(1)} %get-tuple-element.25.refs_0_), channel_id=1, source_target_pairs={{0,16},{1,17},{2,18},{3,19},{4,20},{5,21},{6,22},{7,23},{8,24},{9,... | collective-permute-start | bytes 196616 | tf_op jit(solution)/shard_map/ppermute | solution.py:379
  9.8 1.3 %collective-permute-start.1 = (bf16[64,512]{1,0:T(8,128)(2,1)S(1)}, bf16[64,512]{1,0:T(8,128)(2,1)S(1)}, u32[]{:S(2)}, u32[]{:S(2)}) collective-permute-start(bf16[64,512]{1,0:T(8,128)(2,1)S(1)} %get-tuple-element.26), channel_id=1, source_target_pairs={{0,17},{1,16},{2,19},{3,18},{4,21},{5,20},{6,23},{7,22},{8,25},{9,... | collective-permute-start | bytes 196616 | tf_op jit(solution)/shard_map/ppermute | solution.py:379
  11.1 0.5 %collective-permute-start.5 = (bf16[128,512]{1,0:T(8,128)(2,1)S(1)}, bf16[128,512]{1,0:T(8,128)(2,1)S(1)}, u32[]{:S(2)}, u32[]{:S(2)}) collective-permute-start(bf16[128,512]{1,0:T(8,128)(2,1)S(1)} %get-tuple-element.24.refs_1_.refs_0_), channel_id=1, source_target_pairs={{0,4},{2,6},{4,0},{6,2},{8,12},{10,14},{12,8},{14,10},{16,20},{18,... | collective-permute-start | bytes 393224 | tf_op jit(solution)/shard_map/ppermute | solution.py:373
  11.6 0.6 %retain_inside.1 = (f32[128,512]{1,0:T(8,128)S(1)}, f32[128,2]{1,0:T(8,128)S(1)}) custom-call(bf16[128,512]{1,0:T(8,128)(2,1)S(1)} %get-tuple-element.34.refs_0_.refs_2_, bf16[128,512]{1,0:T(8,128)(2,1)S(1)} %get-tuple-element.27.refs_0_.refs_1_, bf16[128,512]{1,0:T(8,128)(2,1)S(1)} %get-tuple-element.28.refs_1_.refs_2_, ...), custom_call_target="tpu_custom_call" | custom-call | flops 1000 | bytes 1000 | tf_op jit(solution)/shard_map/retain_inside/pallas_call | solution.py:34
  12.2 0.0 collective-permute-done.3.refs_1_
  12.3 1.6 %collective-permute-start.4 = (bf16[80,512]{1,0:T(8,128)(2,1)S(1)}, bf16[80,512]{1,0:T(8,128)(2,1)S(1)}, u32[]{:S(2)}, u32[]{:S(2)}) collective-permute-start(bf16[80,512]{1,0:T(8,128)(2,1)S(1)} %plane_total.1.refs_0_), channel_id=1, source_target_pairs={{0,8},{2,10},{4,12},{6,14},{8,0},{10,2},{12,4},{14,6},{16,24},{18,... | collective-permute-start | bytes 245768 | tf_op jit(solution)/shard_map/ppermute | solution.py:373
  13.9 0.5 %collective-permute-start.6 = (bf16[64,512]{1,0:T(8,128)(2,1)S(1)}, bf16[64,512]{1,0:T(8,128)(2,1)S(1)}, u32[]{:S(2)}, u32[]{:S(2)}) collective-permute-start(bf16[64,512]{1,0:T(8,128)(2,1)S(1)} %get-tuple-element.25.refs_0_), channel_id=1, source_target_pairs={{0,8},{1,9},{2,10},{3,11},{4,12},{5,13},{6,14},{7,15},{8,0},{9,1},... | collective-permute-start | bytes 196616 | tf_op jit(solution)/shard_map/ppermute | solution.py:379
  14.4 0.0 collective-permute-done.refs_0_
  14.4 2.1 %collective-permute-start.7 = (bf16[64,512]{1,0:T(8,128)(2,1)S(1)}, bf16[64,512]{1,0:T(8,128)(2,1)S(1)}, u32[]{:S(2)}, u32[]{:S(2)}) collective-permute-start(bf16[64,512]{1,0:T(8,128)(2,1)S(1)} %get-tuple-element.26), channel_id=1, source_target_pairs={{0,9},{1,8},{2,11},{3,10},{4,13},{5,12},{6,15},{7,14},{8,1},{9,0},... | collective-permute-start | bytes 196616 | tf_op jit(solution)/shard_map/ppermute | solution.py:379
  16.5 0.8 %collective-permute-done.1.refs_1_ = bf16[64,512]{1,0:T(8,128)(2,1)S(1)} collective-permute-done((bf16[64,512]{1,0:T(8,128)(2,1)S(1)}, bf16[64,512]{1,0:T(8,128)(2,1)S(1)}, u32[]{:S(2)}, u32[]{:S(2)}) %collective-permute-start.1) | collective-permute-done | bytes 65568 | tf_op jit(solution)/shard_map/ppermute | solution.py:379
  17.3 0.5 %collective-permute-start.10 = (bf16[64,512]{1,0:T(8,128)(2,1)S(1)}, bf16[64,512]{1,0:T(8,128)(2,1)S(1)}, u32[]{:S(2)}, u32[]{:S(2)}) collective-permute-start(bf16[64,512]{1,0:T(8,128)(2,1)S(1)} %get-tuple-element.26), channel_id=1, source_target_pairs={{0,1},{1,0},{2,3},{3,2},{4,5},{5,4},{6,7},{7,6},{8,9},{9,8},{10,11... | collective-permute-start | bytes 196616 | tf_op jit(solution)/shard_map/ppermute | solution.py:379
  17.8 1.3 %collective-permute-done.6.refs_0_ = bf16[64,512]{1,0:T(8,128)(2,1)S(1)} collective-permute-done((bf16[64,512]{1,0:T(8,128)(2,1)S(1)}, bf16[64,512]{1,0:T(8,128)(2,1)S(1)}, u32[]{:S(2)}, u32[]{:S(2)}) %collective-permute-start.6) | collective-permute-done | bytes 65568 | tf_op jit(solution)/shard_map/ppermute | solution.py:379
  19.1 0.0 collective-permute-start.12
  19.1 1.2 %collective-permute-done.7.refs_1_ = bf16[64,512]{1,0:T(8,128)(2,1)S(1)} collective-permute-done((bf16[64,512]{1,0:T(8,128)(2,1)S(1)}, bf16[64,512]{1,0:T(8,128)(2,1)S(1)}, u32[]{:S(2)}, u32[]{:S(2)}) %collective-permute-start.7) | collective-permute-done | bytes 65568 | tf_op jit(solution)/shard_map/ppermute | solution.py:379
  20.3 0.1 collective-permute-start.13
  20.4 1.2 %collective-permute-done.10.refs_1_ = bf16[64,512]{1,0:T(8,128)(2,1)S(1)} collective-permute-done((bf16[64,512]{1,0:T(8,128)(2,1)S(1)}, bf16[64,512]{1,0:T(8,128)(2,1)S(1)}, u32[]{:S(2)}, u32[]{:S(2)}) %collective-permute-start.10) | collective-permute-done | bytes 65568 | tf_op jit(solution)/shard_map/ppermute | solution.py:379
  21.6 0.1 collective-permute-start.11
  21.7 0.0 collective-permute-done.5.refs_2_.refs_0_
  21.7 0.0 collective-permute-done.4.refs_1_.refs_2_
  21.7 0.1 grow.1.refs_1_
  21.8 0.9 %collective-permute-start.8 = (bf16[128,512]{1,0:T(8,128)(2,1)S(1)}, bf16[128,512]{1,0:T(8,128)(2,1)S(1)}, u32[]{:S(2)}, u32[]{:S(2)}) collective-permute-start(bf16[128,512]{1,0:T(8,128)(2,1)S(1)} %shard_map.95), channel_id=1, source_target_pairs={{0,8},{2,10},{4,12},{6,14},{8,0},{10,2},{12,4},{14,6},{16,24},{18,... | collective-permute-start | bytes 393224 | tf_op jit(solution)/shard_map/ppermute | solution.py:373
  22.7 4.0 %collective-permute-start.9 = (bf16[80,512]{1,0:T(8,128)(2,1)S(1)}, bf16[80,512]{1,0:T(8,128)(2,1)S(1)}, u32[]{:S(2)}, u32[]{:S(2)}) collective-permute-start(bf16[80,512]{1,0:T(8,128)(2,1)S(1)} %grow.1.refs_1_), channel_id=1, source_target_pairs={{0,16},{2,18},{4,20},{6,22},{8,24},{10,26},{12,28},{14,30},{16,0},... | collective-permute-start | bytes 245768 | tf_op jit(solution)/shard_map/ppermute | solution.py:373
  26.7 0.0 collective-permute-done.12.refs_5_
  26.7 0.0 collective-permute-done.13.refs_7_
  26.7 0.0 collective-permute-done.11.refs_3_
  26.7 1.7 %attend_near.1 = (f32[128,512]{1,0:T(8,128)S(1)}, f32[128,128]{1,0:T(8,128)S(1)}, f32[128,512]{1,0:T(8,128)S(1)}, f32[128,128]{1,0:T(8,128)S(1)}) custom-call(bf16[128,512]{1,0:T(8,128)(2,1)S(1)} %collective-permute-done.5.refs_2_.refs_0_, bf16[128,512]{1,0:T(8,128)(2,1)S(1)} %get-tuple-element.24.refs_1_.refs_0_, bf16[128,512]{1,0:T(8,128)(2,1)S(1)} %join_rows.5.refs_2_, ...), custom_call_target="tpu_custom_call" | custom-call | flops 1000 | bytes 1000 | tf_op jit(solution)/shard_map/attend_near/pallas_call | solution.py:34
  28.3 1.2 %collective-permute-done.9.refs_3_ = bf16[80,512]{1,0:T(8,128)(2,1)S(1)} collective-permute-done((bf16[80,512]{1,0:T(8,128)(2,1)S(1)}, bf16[80,512]{1,0:T(8,128)(2,1)S(1)}, u32[]{:S(2)}, u32[]{:S(2)}) %collective-permute-start.9) | collective-permute-done | bytes 81952 | tf_op jit(solution)/shard_map/ppermute | solution.py:373
  29.5 0.1 chip_priors.1
  29.6 0.0 collective-permute-done.8.refs_0_
  29.6 0.1 collective-permute-start.14
  29.7 0.9 %collective-permute-start.16 = (bf16[64,512]{1,0:T(8,128)(2,1)S(1)}, bf16[64,512]{1,0:T(8,128)(2,1)S(1)}, u32[]{:S(2)}, u32[]{:S(2)}) collective-permute-start(bf16[64,512]{1,0:T(8,128)(2,1)S(1)} %get-tuple-element.37.refs_1_), channel_id=1, source_target_pairs={{0,4},{2,6},{4,0},{6,2},{8,12},{10,14},{12,8},{14,10},{16,20},{18,... | collective-permute-start | bytes 196616 | tf_op jit(solution)/shard_map/ppermute | solution.py:373
  30.6 0.4 collective-permute-done.14.refs_2_
  31.0 0.9 %attend_far.1 = bf16[128,640]{1,0:T(8,128)(2,1)S(1)} custom-call(bf16[128,512]{1,0:T(8,128)(2,1)S(1)} %collective-permute-done.5.refs_2_.refs_0_, bf16[128,512]{1,0:T(8,128)(2,1)S(1)} %pass_on.1.refs_1_, bf16[128,512]{1,0:T(8,128)(2,1)S(1)} %collective-permute-done.14.refs_2_, f32[128,512]{1,0:T(8,128)S(1)} %get-tuple-element.40.refs_3_, ...), custom_call_target="tpu_custom_call" | custom-call | flops 1000 | bytes 1000 | tf_op jit(solution)/shard_map/attend_far/pallas_call | solution.py:34
  31.9 0.9 %collective-permute-start.15 = (bf16[128,640]{1,0:T(8,128)(2,1)S(1)}, bf16[128,640]{1,0:T(8,128)(2,1)S(1)}, u32[]{:S(2)}, u32[]{:S(2)}) collective-permute-start(bf16[128,640]{1,0:T(8,128)(2,1)S(1)} %attend_far.1), channel_id=1, source_target_pairs={{0,4},{2,6},{4,0},{6,2},{8,12},{10,14},{12,8},{14,10},{16,20},{18,... | collective-permute-start | bytes 491528 | tf_op jit(solution)/shard_map/ppermute | solution.py:373
  32.9 1.3 %collective-permute-done.16.refs_3_ = bf16[64,512]{1,0:T(8,128)(2,1)S(1)} collective-permute-done((bf16[64,512]{1,0:T(8,128)(2,1)S(1)}, bf16[64,512]{1,0:T(8,128)(2,1)S(1)}, u32[]{:S(2)}, u32[]{:S(2)}) %collective-permute-start.16) | collective-permute-done | bytes 65568 | tf_op jit(solution)/shard_map/ppermute | solution.py:373
  34.2 0.1 block_priors.1
  34.4 0.1 collective-permute-start.17
  34.4 0.9 %attend_own.1.refs_0_ = f32[128,640]{1,0:T(8,128)S(1)} custom-call(bf16[128,512]{1,0:T(8,128)(2,1)S(1)} %get-tuple-element.24.refs_1_.refs_0_, bf16[128,512]{1,0:T(8,128)(2,1)S(1)} %pass_on.1.refs_1_, bf16[128,512]{1,0:T(8,128)(2,1)S(1)} %collective-permute-done.14.refs_2_, f32[128,512]{1,0:T(8,128)S(1)} %get-tuple-element.38.refs_3_, ...), custom_call_target="tpu_custom_call" | custom-call | flops 1000 | bytes 1000 | tf_op jit(solution)/shard_map/attend_own/pallas_call | solution.py:34
  35.4 0.4 %collective-permute-done.17.refs_7_ = bf16[128,512]{1,0:T(8,128)(2,1)S(1)} collective-permute-done((bf16[128,512]{1,0:T(8,128)(2,1)S(1)}, bf16[128,512]{1,0:T(8,128)(2,1)S(1)}, u32[]{:S(2)}, u32[]{:S(2)}) %collective-permute-start.17) | collective-permute-done | bytes 131104 | tf_op jit(solution)/shard_map/ppermute | solution.py:373
  35.8 2.5 %collective-permute-done.15.refs_1_ = bf16[128,640]{1,0:T(8,128)(2,1)S(1)} collective-permute-done((bf16[128,640]{1,0:T(8,128)(2,1)S(1)}, bf16[128,640]{1,0:T(8,128)(2,1)S(1)}, u32[]{:S(2)}, u32[]{:S(2)}) %collective-permute-start.15) | collective-permute-done | bytes 163872 | tf_op jit(solution)/shard_map/ppermute | solution.py:373
  38.3 1.1 %finish.1 = (bf16[128,512]{1,0:T(8,128)(2,1)}, bf16[128,512]{1,0:T(8,128)(2,1)}) custom-call(f32[128,640]{1,0:T(8,128)S(1)} %attend_own.1.refs_0_, bf16[128,640]{1,0:T(8,128)(2,1)S(1)} %collective-permute-done.15.refs_1_, bf16[128,512]{1,0:T(8,128)(2,1)S(1)} %get-tuple-element.34.refs_0_.refs_2_, bf16[128,512]{1,0:T(8,128)(2,1)S(1)} %get-tuple-element.41.refs_3_, ...), custom_call_target="tpu_custom_call" | custom-call | flops 1000 | bytes 1000 | tf_op jit(solution)/shard_map/finish/pallas_call | solution.py:34
  (6 shorter events, 0.1 us)
Async XLA Ops:
  2.6 1.5 %collective-permute-start.2 = (bf16[144,512]{1,0:T(8,128)(2,1)S(1)}, bf16[144,512]{1,0:T(8,128)(2,1)S(1)}, u32[]{:S(2)}, u32[]{:S(2)}) collective-permute-start(bf16[144,512]{1,0:T(8,128)(2,1)S(1)} %get-tuple-element.31), channel_id=1, source_target_pairs={{0,2},{2,0},{4,6},{6,4},{8,10},{10,8},{12,14},{14,12},{16,18},{18,... | collective-permute-start | bytes 442376 | tf_op jit(solution)/shard_map/ppermute | solution.py:373
  4.3 7.9 %collective-permute-start.3 = (bf16[80,512]{1,0:T(8,128)(2,1)S(1)}, bf16[80,512]{1,0:T(8,128)(2,1)S(1)}, u32[]{:S(2)}, u32[]{:S(2)}) collective-permute-start(bf16[80,512]{1,0:T(8,128)(2,1)S(1)} %get-tuple-element.33.refs_4_), channel_id=1, source_target_pairs={{0,4},{2,6},{4,0},{6,2},{8,12},{10,14},{12,8},{14,10},{16,20},{18,... | collective-permute-start | bytes 245768 | tf_op jit(solution)/shard_map/ppermute | solution.py:373
  7.2 7.2 %collective-permute-start = (bf16[64,512]{1,0:T(8,128)(2,1)S(1)}, bf16[64,512]{1,0:T(8,128)(2,1)S(1)}, u32[]{:S(2)}, u32[]{:S(2)}) collective-permute-start(bf16[64,512]{1,0:T(8,128)(2,1)S(1)} %get-tuple-element.25.refs_0_), channel_id=1, source_target_pairs={{0,16},{1,17},{2,18},{3,19},{4,20},{5,21},{6,22},{7,23},{8,24},{9,... | collective-permute-start | bytes 196616 | tf_op jit(solution)/shard_map/ppermute | solution.py:379
  9.8 7.5 %collective-permute-start.1 = (bf16[64,512]{1,0:T(8,128)(2,1)S(1)}, bf16[64,512]{1,0:T(8,128)(2,1)S(1)}, u32[]{:S(2)}, u32[]{:S(2)}) collective-permute-start(bf16[64,512]{1,0:T(8,128)(2,1)S(1)} %get-tuple-element.26), channel_id=1, source_target_pairs={{0,17},{1,16},{2,19},{3,18},{4,21},{5,20},{6,23},{7,22},{8,25},{9,... | collective-permute-start | bytes 196616 | tf_op jit(solution)/shard_map/ppermute | solution.py:379
  11.1 10.6 %collective-permute-start.5 = (bf16[128,512]{1,0:T(8,128)(2,1)S(1)}, bf16[128,512]{1,0:T(8,128)(2,1)S(1)}, u32[]{:S(2)}, u32[]{:S(2)}) collective-permute-start(bf16[128,512]{1,0:T(8,128)(2,1)S(1)} %get-tuple-element.24.refs_1_.refs_0_), channel_id=1, source_target_pairs={{0,4},{2,6},{4,0},{6,2},{8,12},{10,14},{12,8},{14,10},{16,20},{18,... | collective-permute-start | bytes 393224 | tf_op jit(solution)/shard_map/ppermute | solution.py:373
  12.3 9.4 %collective-permute-start.4 = (bf16[80,512]{1,0:T(8,128)(2,1)S(1)}, bf16[80,512]{1,0:T(8,128)(2,1)S(1)}, u32[]{:S(2)}, u32[]{:S(2)}) collective-permute-start(bf16[80,512]{1,0:T(8,128)(2,1)S(1)} %plane_total.1.refs_0_), channel_id=1, source_target_pairs={{0,8},{2,10},{4,12},{6,14},{8,0},{10,2},{12,4},{14,6},{16,24},{18,... | collective-permute-start | bytes 245768 | tf_op jit(solution)/shard_map/ppermute | solution.py:373
  13.9 5.2 %collective-permute-start.6 = (bf16[64,512]{1,0:T(8,128)(2,1)S(1)}, bf16[64,512]{1,0:T(8,128)(2,1)S(1)}, u32[]{:S(2)}, u32[]{:S(2)}) collective-permute-start(bf16[64,512]{1,0:T(8,128)(2,1)S(1)} %get-tuple-element.25.refs_0_), channel_id=1, source_target_pairs={{0,8},{1,9},{2,10},{3,11},{4,12},{5,13},{6,14},{7,15},{8,0},{9,1},... | collective-permute-start | bytes 196616 | tf_op jit(solution)/shard_map/ppermute | solution.py:379
  14.4 5.9 %collective-permute-start.7 = (bf16[64,512]{1,0:T(8,128)(2,1)S(1)}, bf16[64,512]{1,0:T(8,128)(2,1)S(1)}, u32[]{:S(2)}, u32[]{:S(2)}) collective-permute-start(bf16[64,512]{1,0:T(8,128)(2,1)S(1)} %get-tuple-element.26), channel_id=1, source_target_pairs={{0,9},{1,8},{2,11},{3,10},{4,13},{5,12},{6,15},{7,14},{8,1},{9,0},... | collective-permute-start | bytes 196616 | tf_op jit(solution)/shard_map/ppermute | solution.py:379
  17.3 4.3 %collective-permute-start.10 = (bf16[64,512]{1,0:T(8,128)(2,1)S(1)}, bf16[64,512]{1,0:T(8,128)(2,1)S(1)}, u32[]{:S(2)}, u32[]{:S(2)}) collective-permute-start(bf16[64,512]{1,0:T(8,128)(2,1)S(1)} %get-tuple-element.26), channel_id=1, source_target_pairs={{0,1},{1,0},{2,3},{3,2},{4,5},{5,4},{6,7},{7,6},{8,9},{9,8},{10,11... | collective-permute-start | bytes 196616 | tf_op jit(solution)/shard_map/ppermute | solution.py:379
  19.1 7.6 %collective-permute-start.12 = (bf16[128,512]{1,0:T(8,128)(2,1)S(1)}, bf16[128,512]{1,0:T(8,128)(2,1)S(1)}, u32[]{:S(2)}, u32[]{:S(2)}) collective-permute-start(bf16[128,512]{1,0:T(8,128)(2,1)S(1)} %join_rows.3.refs_3_.refs_0_.refs_4_), channel_id=1, source_target_pairs={{0,2},{2,0},{4,6},{6,4},{8,10},{10,8},{12,14},{14,12},{16,18},{18,... | collective-permute-start | bytes 393224 | tf_op jit(solution)/shard_map/ppermute | solution.py:373
  20.3 6.4 %collective-permute-start.13 = (bf16[128,512]{1,0:T(8,128)(2,1)S(1)}, bf16[128,512]{1,0:T(8,128)(2,1)S(1)}, u32[]{:S(2)}, u32[]{:S(2)}) collective-permute-start(bf16[128,512]{1,0:T(8,128)(2,1)S(1)} %join_rows.4.refs_4_.refs_6_), channel_id=1, source_target_pairs={{0,2},{2,0},{4,6},{6,4},{8,10},{10,8},{12,14},{14,12},{16,18},{18,... | collective-permute-start | bytes 393224 | tf_op jit(solution)/shard_map/ppermute | solution.py:373
  21.6 5.1 %collective-permute-start.11 = (bf16[128,512]{1,0:T(8,128)(2,1)S(1)}, bf16[128,512]{1,0:T(8,128)(2,1)S(1)}, u32[]{:S(2)}, u32[]{:S(2)}) collective-permute-start(bf16[128,512]{1,0:T(8,128)(2,1)S(1)} %join_rows.5.refs_2_), channel_id=1, source_target_pairs={{0,2},{2,0},{4,6},{6,4},{8,10},{10,8},{12,14},{14,12},{16,18},{18,... | collective-permute-start | bytes 393224 | tf_op jit(solution)/shard_map/ppermute | solution.py:373
  21.8 7.8 %collective-permute-start.8 = (bf16[128,512]{1,0:T(8,128)(2,1)S(1)}, bf16[128,512]{1,0:T(8,128)(2,1)S(1)}, u32[]{:S(2)}, u32[]{:S(2)}) collective-permute-start(bf16[128,512]{1,0:T(8,128)(2,1)S(1)} %shard_map.95), channel_id=1, source_target_pairs={{0,8},{2,10},{4,12},{6,14},{8,0},{10,2},{12,4},{14,6},{16,24},{18,... | collective-permute-start | bytes 393224 | tf_op jit(solution)/shard_map/ppermute | solution.py:373
  22.7 6.8 %collective-permute-start.9 = (bf16[80,512]{1,0:T(8,128)(2,1)S(1)}, bf16[80,512]{1,0:T(8,128)(2,1)S(1)}, u32[]{:S(2)}, u32[]{:S(2)}) collective-permute-start(bf16[80,512]{1,0:T(8,128)(2,1)S(1)} %grow.1.refs_1_), channel_id=1, source_target_pairs={{0,16},{2,18},{4,20},{6,22},{8,24},{10,26},{12,28},{14,30},{16,0},... | collective-permute-start | bytes 245768 | tf_op jit(solution)/shard_map/ppermute | solution.py:373
  29.6 1.4 %collective-permute-start.14 = (bf16[128,512]{1,0:T(8,128)(2,1)S(1)}, bf16[128,512]{1,0:T(8,128)(2,1)S(1)}, u32[]{:S(2)}, u32[]{:S(2)}) collective-permute-start(bf16[128,512]{1,0:T(8,128)(2,1)S(1)} %pass_on.1.refs_1_), channel_id=1, source_target_pairs={{0,2},{2,0},{4,6},{6,4},{8,10},{10,8},{12,14},{14,12},{16,18},{18,... | collective-permute-start | bytes 393224 | tf_op jit(solution)/shard_map/ppermute | solution.py:373
  29.7 4.5 %collective-permute-start.16 = (bf16[64,512]{1,0:T(8,128)(2,1)S(1)}, bf16[64,512]{1,0:T(8,128)(2,1)S(1)}, u32[]{:S(2)}, u32[]{:S(2)}) collective-permute-start(bf16[64,512]{1,0:T(8,128)(2,1)S(1)} %get-tuple-element.37.refs_1_), channel_id=1, source_target_pairs={{0,4},{2,6},{4,0},{6,2},{8,12},{10,14},{12,8},{14,10},{16,20},{18,... | collective-permute-start | bytes 196616 | tf_op jit(solution)/shard_map/ppermute | solution.py:373
  31.9 6.3 %collective-permute-start.15 = (bf16[128,640]{1,0:T(8,128)(2,1)S(1)}, bf16[128,640]{1,0:T(8,128)(2,1)S(1)}, u32[]{:S(2)}, u32[]{:S(2)}) collective-permute-start(bf16[128,640]{1,0:T(8,128)(2,1)S(1)} %attend_far.1), channel_id=1, source_target_pairs={{0,4},{2,6},{4,0},{6,2},{8,12},{10,14},{12,8},{14,10},{16,20},{18,... | collective-permute-start | bytes 491528 | tf_op jit(solution)/shard_map/ppermute | solution.py:373
  34.4 1.4 %collective-permute-start.17 = (bf16[128,512]{1,0:T(8,128)(2,1)S(1)}, bf16[128,512]{1,0:T(8,128)(2,1)S(1)}, u32[]{:S(2)}, u32[]{:S(2)}) collective-permute-start(bf16[128,512]{1,0:T(8,128)(2,1)S(1)} %get-tuple-element.45), channel_id=1, source_target_pairs={{0,2},{2,0},{4,6},{6,4},{8,10},{10,8},{12,14},{14,12},{16,18},{18,... | collective-permute-start | bytes 393224 | tf_op jit(solution)/shard_map/ppermute | solution.py:373

commit v7 on v5

--- a/solution.py
+++ b/solution.py
@@ -22,7 +22,7 @@
 
 
 def call(
-    body, outs, args, scratch=(), name=None, takes=VMEM, gives=VMEM, after=(),
+    body, outs, args, scratch=(), name=None, flops=1000, takes=VMEM, gives=VMEM, after=(),
     aliases=None,
 ):
     single = len(outs) == 1
@@ -39,7 +39,7 @@
         scratch_shapes=scratch,
         input_output_aliases=aliases or {},
         compiler_params=pltpu.CompilerParams(vmem_limit_bytes=40 * 1024 * 1024),
-        cost_estimate=pl.CostEstimate(flops=1000, bytes_accessed=1000, transcendentals=0),
+        cost_estimate=pl.CostEstimate(flops=flops, bytes_accessed=1000, transcendentals=0),
         name=name,
     )(*args, *after)
 
@@ -178,7 +178,8 @@
         put_total(out, quarter, total)
 
 
-def plane_total(keep_ref, other_ref, out):
+def plane_total(keep_ref, other_ref, block_ref, out, block_out):
+    block_out[...] = block_ref[...]
     _, high, _ = bits()
     state, total = pair_total(high == 0, keep_ref, other_ref)
     out[pl.ds(0, state.shape[0]), :] = state.astype(out.dtype)
@@ -393,6 +394,7 @@
         (k_ret, v_ret, decays),
         scratch=[pltpu.VMEM((HD, wide), F32)],
         name="summarize",
+        flops=3000000000,
     )
     sum_other = swap(sum_send, 1)
     chip_send, chip_keep = call(
@@ -401,7 +403,6 @@
         (sum_keep, sum_other),
         scratch=[pltpu.VMEM((half, wide), F32)],
         name="chip_total",
-        after=arrived[-1:],
     )
     inside, factor = call(
         retain_inside,
@@ -416,6 +417,7 @@
             [shape((n * length, 2 * width))],
             arrived,
             name="join_rows",
+            flops=3000000000,
         )
     }
     chip_other = swap(chip_send, 2)
@@ -425,14 +427,14 @@
         for s in list(blocks):
             blocks[s ^ bit] = swap(blocks[s], 4 * bit)
         bit //= 2
-    blocks[1] = swap(blocks[0], 4)
-    window = call(
+    window, handed = call(
         plane_total,
-        [shape((quarter + PAD, wide))],
-        (chip_keep, chip_other),
+        [shape((quarter + PAD, wide)), shape(blocks[0].shape)],
+        (chip_keep, chip_other, blocks[0]),
         name="plane_total",
         after=(factor,),
     )
+    blocks[1] = swap(handed, 4)
     planes, bit = [], 1
     while bit < far:
         planes.append(swap(window, 4 * bit))
@@ -442,6 +444,7 @@
                 [shape(window.shape)],
                 (window, planes[-1]),
                 name="grow",
+                flops=3000000000,
                 after=(q_other, *[blocks[s] for s in blocks if s]),
             )
         bit *= 2

time: 38 us -> 37.5 us (0.987)
  waiting for transfers between devices: 14 us -> 11 us
  starting transfers between devices: 15.5 us -> 18 us
    ppermute x15, starting transfers between devices: 12.9 us -> 15.4 us  [swap(): return lax.ppermute(value, 'ctx', [(b, b ^ bit) for b in range(count)])]
    ppermute x1, waiting for transfers between devices: 2.69 us -> 1 us  [to_head(): return lax.ppermute(value, 'head', [(y, (y + e) % n) for y in range(n)])]
    ppermute x15, waiting for transfers between devices: 11.3 us -> 10 us  [swap(): return lax.ppermute(value, 'ctx', [(b, b ^ bit) for b in range(count)])]
  transfers between devices with their start and end apart: 16 -> 16, of which waited for: 10 -> 8; matrix products, arithmetic and copies ran while one was open for 0% -> 0% of each run, Pallas kernels for 12% -> 12%
where the time goes in v7:
time: 37.5 us; the launch traced here: 37.4 us
  starting transfers between devices  18 us (48%)
  waiting for transfers between devices  11 us (29%)
  Pallas kernels  7.67 us (20%)
  between operations  0.77 us (2%)
    ppermute x15, starting transfers between devices, swap(): return lax.ppermute(value, 'ctx', [(b, b ^ bit) for b in range(count)])  15.4 us
    ppermute x15, waiting for transfers between devices, swap(): return lax.ppermute(value, 'ctx', [(b, b ^ bit) for b in range(count)])  10 us
    pallas_call x15, Pallas kernels, call(): pl.pallas_call(kernel, out_shape=outs[0] if single else tuple(outs), in_s...  7.67 us
    ppermute x1, starting transfers between devices, to_head(): return lax.ppermute(value, 'head', [(y, (y + e) % n) for y in range(n)])  2.6 us
    ppermute x1, waiting for transfers between devices, to_head(): return lax.ppermute(value, 'head', [(y, (y + e) % n) for y in range(n)])  1 us
  transfers between devices with their start and end apart: 16, of which 8 were waited for; matrix products, arithmetic and copies ran while one was open for 0% of the time, Pallas kernels for 12%

profile of v7, /device:TPU:0, one launch (start us, length us, event | category | flops | bytes accessed | tf_op | source)
XLA Modules:
  0.0 37.4 jit_solution(4464724980750923564)
XLA Ops:
  0.6 1.3 %load_all.1 = (bf16[64,512]{1,0:T(8,128)(2,1)S(1)}, bf16[64,512]{1,0:T(8,128)(2,1)S(1)}, bf16[128,512]{1,0:T(8,128)(2,1)S(1)}, bf16[128,512]{1,0:T(8,128)(2,1)S(...) custom-call(bf16[64,512]{1,0:T(8,128)(2,1)} %refs_0_.1, ...), custom_call_target="tpu_custom_call" | custom-call | flops 1000 | bytes 1000 | tf_op jit(solution)/shard_map/load_all/pallas_call | solution.py:34
  2.0 0.7 %summarize.1 = (bf16[144,512]{1,0:T(8,128)(2,1)S(1)}, f32[144,512]{1,0:T(8,128)S(1)}) custom-call(bf16[128,512]{1,0:T(8,128)(2,1)S(1)} %get-tuple-element.29.refs_0_.refs_1_, bf16[128,512]{1,0:T(8,128)(2,1)S(1)} %get-tuple-element.30.refs_1_.refs_2_, f32[2,128]{1,0:T(2,128)S(1)} %get-tuple-element.31.refs_2_.refs_3_), custom_call_target="tpu_custom_call" | custom-call | flops 3000000000 | bytes 1000 | tf_op jit(solution)/shard_map/summarize/pallas_call | solution.py:34
  2.6 0.5 %collective-permute-start.2 = (bf16[144,512]{1,0:T(8,128)(2,1)S(1)}, bf16[144,512]{1,0:T(8,128)(2,1)S(1)}, u32[]{:S(2)}, u32[]{:S(2)}) collective-permute-start(bf16[144,512]{1,0:T(8,128)(2,1)S(1)} %get-tuple-element.33), channel_id=1, source_target_pairs={{0,2},{2,0},{4,6},{6,4},{8,10},{10,8},{12,14},{14,12},{16,18},{18,... | collective-permute-start | bytes 442376 | tf_op jit(solution)/shard_map/ppermute | solution.py:374
  3.2 2.6 %collective-permute-start = (bf16[64,512]{1,0:T(8,128)(2,1)S(1)}, bf16[64,512]{1,0:T(8,128)(2,1)S(1)}, u32[]{:S(2)}, u32[]{:S(2)}) collective-permute-start(bf16[64,512]{1,0:T(8,128)(2,1)S(1)} %get-tuple-element.28), channel_id=1, source_target_pairs={{0,1},{1,0},{2,3},{3,2},{4,5},{5,4},{6,7},{7,6},{8,9},{9,8},{10,11... | collective-permute-start | bytes 196616 | tf_op jit(solution)/shard_map/ppermute | solution.py:377
  5.8 0.0 collective-permute-done.2.refs_1_
  5.8 0.1 chip_total.1
  5.9 1.6 %collective-permute-start.3 = (bf16[80,512]{1,0:T(8,128)(2,1)S(1)}, bf16[80,512]{1,0:T(8,128)(2,1)S(1)}, u32[]{:S(2)}, u32[]{:S(2)}) collective-permute-start(bf16[80,512]{1,0:T(8,128)(2,1)S(1)} %get-tuple-element.35.refs_4_), channel_id=1, source_target_pairs={{0,4},{2,6},{4,0},{6,2},{8,12},{10,14},{12,8},{14,10},{16,20},{18,... | collective-permute-start | bytes 245768 | tf_op jit(solution)/shard_map/ppermute | solution.py:374
  7.4 1.0 %collective-permute-done.refs_1_ = bf16[64,512]{1,0:T(8,128)(2,1)S(1)} collective-permute-done((bf16[64,512]{1,0:T(8,128)(2,1)S(1)}, bf16[64,512]{1,0:T(8,128)(2,1)S(1)}, u32[]{:S(2)}, u32[]{:S(2)}) %collective-permute-start) | collective-permute-done | bytes 65568 | tf_op jit(solution)/shard_map/ppermute | solution.py:377
  8.5 2.9 %collective-permute-start.1 = (bf16[128,512]{1,0:T(8,128)(2,1)S(1)}, bf16[128,512]{1,0:T(8,128)(2,1)S(1)}, u32[]{:S(2)}, u32[]{:S(2)}) collective-permute-start(bf16[128,512]{1,0:T(8,128)(2,1)S(1)} %join_rows.1.refs_2_), channel_id=1, source_target_pairs={{0,16},{2,18},{4,20},{6,22},{8,24},{10,26},{12,28},{14,30},{16,0},... | collective-permute-start | bytes 393224 | tf_op jit(solution)/shard_map/ppermute | solution.py:374
  11.4 0.6 %retain_inside.1 = (f32[128,512]{1,0:T(8,128)S(1)}, f32[128,2]{1,0:T(8,128)S(1)}) custom-call(bf16[128,512]{1,0:T(8,128)(2,1)S(1)} %get-tuple-element.36.refs_0_.refs_2_, bf16[128,512]{1,0:T(8,128)(2,1)S(1)} %get-tuple-element.29.refs_0_.refs_1_, bf16[128,512]{1,0:T(8,128)(2,1)S(1)} %get-tuple-element.30.refs_1_.refs_2_, ...), custom_call_target="tpu_custom_call" | custom-call | flops 1000 | bytes 1000 | tf_op jit(solution)/shard_map/retain_inside/pallas_call | solution.py:34
  12.0 0.0 collective-permute-done.3.refs_1_
  12.0 0.1 plane_total.1
  12.0 1.6 %collective-permute-start.6 = (bf16[128,512]{1,0:T(8,128)(2,1)S(1)}, bf16[128,512]{1,0:T(8,128)(2,1)S(1)}, u32[]{:S(2)}, u32[]{:S(2)}) collective-permute-start(bf16[128,512]{1,0:T(8,128)(2,1)S(1)} %get-tuple-element.39), channel_id=1, source_target_pairs={{0,8},{2,10},{4,12},{6,14},{8,0},{10,2},{12,4},{14,6},{16,24},{18,... | collective-permute-start | bytes 393224 | tf_op jit(solution)/shard_map/ppermute | solution.py:374
  13.7 1.5 %collective-permute-start.5 = (bf16[128,512]{1,0:T(8,128)(2,1)S(1)}, bf16[128,512]{1,0:T(8,128)(2,1)S(1)}, u32[]{:S(2)}, u32[]{:S(2)}) collective-permute-start(bf16[128,512]{1,0:T(8,128)(2,1)S(1)} %get-tuple-element.26.refs_1_.refs_0_), channel_id=1, source_target_pairs={{0,4},{2,6},{4,0},{6,2},{8,12},{10,14},{12,8},{14,10},{16,20},{18,... | collective-permute-start | bytes 393224 | tf_op jit(solution)/shard_map/ppermute | solution.py:374
  15.2 0.4 %collective-permute-start.4 = (bf16[80,512]{1,0:T(8,128)(2,1)S(1)}, bf16[80,512]{1,0:T(8,128)(2,1)S(1)}, u32[]{:S(2)}, u32[]{:S(2)}) collective-permute-start(bf16[80,512]{1,0:T(8,128)(2,1)S(1)} %get-tuple-element.38.refs_0_), channel_id=1, source_target_pairs={{0,8},{2,10},{4,12},{6,14},{8,0},{10,2},{12,4},{14,6},{16,24},{18,... | collective-permute-start | bytes 245768 | tf_op jit(solution)/shard_map/ppermute | solution.py:374
  15.6 0.0 collective-permute-start.9
  15.6 2.0 %collective-permute-done.1.refs_3_.refs_0_.refs_4_ = bf16[128,512]{1,0:T(8,128)(2,1)S(1)} collective-permute-done((bf16[128,512]{1,0:T(8,128)(2,1)S(1)}, bf16[128,512]{1,0:T(8,128)(2,1)S(1)}, u32[]{:S(2)}, u32[]{:S(2)}) %collective-permute-start.1) | collective-permute-done | bytes 131104 | tf_op jit(solution)/shard_map/ppermute | solution.py:374
  17.6 0.0 collective-permute-start.10
  17.6 1.8 %collective-permute-done.6.refs_4_.refs_6_ = bf16[128,512]{1,0:T(8,128)(2,1)S(1)} collective-permute-done((bf16[128,512]{1,0:T(8,128)(2,1)S(1)}, bf16[128,512]{1,0:T(8,128)(2,1)S(1)}, u32[]{:S(2)}, u32[]{:S(2)}) %collective-permute-start.6) | collective-permute-done | bytes 131104 | tf_op jit(solution)/shard_map/ppermute | solution.py:374
  19.4 0.0 collective-permute-start.11
  19.4 0.0 collective-permute-done.5.refs_2_.refs_0_
  19.4 0.9 %collective-permute-done.4.refs_1_.refs_2_ = bf16[80,512]{1,0:T(8,128)(2,1)S(1)} collective-permute-done((bf16[80,512]{1,0:T(8,128)(2,1)S(1)}, bf16[80,512]{1,0:T(8,128)(2,1)S(1)}, u32[]{:S(2)}, u32[]{:S(2)}) %collective-permute-start.4) | collective-permute-done | bytes 81952 | tf_op jit(solution)/shard_map/ppermute | solution.py:374
  20.3 0.1 grow.1.refs_1_
  20.4 0.8 %collective-permute-start.7 = (bf16[128,512]{1,0:T(8,128)(2,1)S(1)}, bf16[128,512]{1,0:T(8,128)(2,1)S(1)}, u32[]{:S(2)}, u32[]{:S(2)}) collective-permute-start(bf16[128,512]{1,0:T(8,128)(2,1)S(1)} %shard_map.95), channel_id=1, source_target_pairs={{0,8},{2,10},{4,12},{6,14},{8,0},{10,2},{12,4},{14,6},{16,24},{18,... | collective-permute-start | bytes 393224 | tf_op jit(solution)/shard_map/ppermute | solution.py:374
  21.2 3.0 %collective-permute-start.8 = (bf16[80,512]{1,0:T(8,128)(2,1)S(1)}, bf16[80,512]{1,0:T(8,128)(2,1)S(1)}, u32[]{:S(2)}, u32[]{:S(2)}) collective-permute-start(bf16[80,512]{1,0:T(8,128)(2,1)S(1)} %grow.1.refs_1_), channel_id=1, source_target_pairs={{0,16},{2,18},{4,20},{6,22},{8,24},{10,26},{12,28},{14,30},{16,0},... | collective-permute-start | bytes 245768 | tf_op jit(solution)/shard_map/ppermute | solution.py:374
  24.2 0.0 collective-permute-done.9.refs_3_
  24.2 0.0 collective-permute-done.10.refs_5_
  24.2 0.0 collective-permute-done.11.refs_7_
  24.2 1.6 %attend_near.1 = (f32[128,512]{1,0:T(8,128)S(1)}, f32[128,128]{1,0:T(8,128)S(1)}, f32[128,512]{1,0:T(8,128)S(1)}, f32[128,128]{1,0:T(8,128)S(1)}) custom-call(bf16[128,512]{1,0:T(8,128)(2,1)S(1)} %collective-permute-done.5.refs_2_.refs_0_, bf16[128,512]{1,0:T(8,128)(2,1)S(1)} %get-tuple-element.26.refs_1_.refs_0_, bf16[128,512]{1,0:T(8,128)(2,1)S(1)} %join_rows.1.refs_2_, ...), custom_call_target="tpu_custom_call" | custom-call | flops 1000 | bytes 1000 | tf_op jit(solution)/shard_map/attend_near/pallas_call | solution.py:34
  25.8 1.5 %collective-permute-done.8.refs_3_ = bf16[80,512]{1,0:T(8,128)(2,1)S(1)} collective-permute-done((bf16[80,512]{1,0:T(8,128)(2,1)S(1)}, bf16[80,512]{1,0:T(8,128)(2,1)S(1)}, u32[]{:S(2)}, u32[]{:S(2)}) %collective-permute-start.8) | collective-permute-done | bytes 81952 | tf_op jit(solution)/shard_map/ppermute | solution.py:374
  27.3 0.1 chip_priors.1
  27.4 0.0 collective-permute-done.7.refs_0_
  27.4 0.1 collective-permute-start.12
  27.5 1.6 %collective-permute-start.14 = (bf16[64,512]{1,0:T(8,128)(2,1)S(1)}, bf16[64,512]{1,0:T(8,128)(2,1)S(1)}, u32[]{:S(2)}, u32[]{:S(2)}) collective-permute-start(bf16[64,512]{1,0:T(8,128)(2,1)S(1)} %get-tuple-element.41.refs_1_), channel_id=1, source_target_pairs={{0,4},{2,6},{4,0},{6,2},{8,12},{10,14},{12,8},{14,10},{16,20},{18,... | collective-permute-start | bytes 196616 | tf_op jit(solution)/shard_map/ppermute | solution.py:374
  29.0 0.0 collective-permute-done.12.refs_2_
  29.1 0.9 %attend_far.1 = bf16[128,640]{1,0:T(8,128)(2,1)S(1)} custom-call(bf16[128,512]{1,0:T(8,128)(2,1)S(1)} %collective-permute-done.5.refs_2_.refs_0_, bf16[128,512]{1,0:T(8,128)(2,1)S(1)} %pass_on.1.refs_1_, bf16[128,512]{1,0:T(8,128)(2,1)S(1)} %collective-permute-done.12.refs_2_, f32[128,512]{1,0:T(8,128)S(1)} %get-tuple-element.44.refs_3_, ...), custom_call_target="tpu_custom_call" | custom-call | flops 1000 | bytes 1000 | tf_op jit(solution)/shard_map/attend_far/pallas_call | solution.py:34
  30.0 1.3 %collective-permute-start.13 = (bf16[128,640]{1,0:T(8,128)(2,1)S(1)}, bf16[128,640]{1,0:T(8,128)(2,1)S(1)}, u32[]{:S(2)}, u32[]{:S(2)}) collective-permute-start(bf16[128,640]{1,0:T(8,128)(2,1)S(1)} %attend_far.1), channel_id=1, source_target_pairs={{0,4},{2,6},{4,0},{6,2},{8,12},{10,14},{12,8},{14,10},{16,20},{18,... | collective-permute-start | bytes 491528 | tf_op jit(solution)/shard_map/ppermute | solution.py:374
  31.3 0.7 %collective-permute-done.14.refs_3_ = bf16[64,512]{1,0:T(8,128)(2,1)S(1)} collective-permute-done((bf16[64,512]{1,0:T(8,128)(2,1)S(1)}, bf16[64,512]{1,0:T(8,128)(2,1)S(1)}, u32[]{:S(2)}, u32[]{:S(2)}) %collective-permute-start.14) | collective-permute-done | bytes 65568 | tf_op jit(solution)/shard_map/ppermute | solution.py:374
  32.0 0.1 block_priors.1
  32.1 0.1 collective-permute-start.15
  32.2 0.9 %attend_own.1.refs_0_ = f32[128,640]{1,0:T(8,128)S(1)} custom-call(bf16[128,512]{1,0:T(8,128)(2,1)S(1)} %get-tuple-element.26.refs_1_.refs_0_, bf16[128,512]{1,0:T(8,128)(2,1)S(1)} %pass_on.1.refs_1_, bf16[128,512]{1,0:T(8,128)(2,1)S(1)} %collective-permute-done.12.refs_2_, f32[128,512]{1,0:T(8,128)S(1)} %get-tuple-element.42.refs_3_, ...), custom_call_target="tpu_custom_call" | custom-call | flops 1000 | bytes 1000 | tf_op jit(solution)/shard_map/attend_own/pallas_call | solution.py:34
  33.2 0.4 %collective-permute-done.15.refs_7_ = bf16[128,512]{1,0:T(8,128)(2,1)S(1)} collective-permute-done((bf16[128,512]{1,0:T(8,128)(2,1)S(1)}, bf16[128,512]{1,0:T(8,128)(2,1)S(1)}, u32[]{:S(2)}, u32[]{:S(2)}) %collective-permute-start.15) | collective-permute-done | bytes 131104 | tf_op jit(solution)/shard_map/ppermute | solution.py:374
  33.6 2.7 %collective-permute-done.13.refs_1_ = bf16[128,640]{1,0:T(8,128)(2,1)S(1)} collective-permute-done((bf16[128,640]{1,0:T(8,128)(2,1)S(1)}, bf16[128,640]{1,0:T(8,128)(2,1)S(1)}, u32[]{:S(2)}, u32[]{:S(2)}) %collective-permute-start.13) | collective-permute-done | bytes 163872 | tf_op jit(solution)/shard_map/ppermute | solution.py:374
  36.3 1.1 %finish.1 = (bf16[128,512]{1,0:T(8,128)(2,1)}, bf16[128,512]{1,0:T(8,128)(2,1)}) custom-call(f32[128,640]{1,0:T(8,128)S(1)} %attend_own.1.refs_0_, bf16[128,640]{1,0:T(8,128)(2,1)S(1)} %collective-permute-done.13.refs_1_, bf16[128,512]{1,0:T(8,128)(2,1)S(1)} %get-tuple-element.36.refs_0_.refs_2_, bf16[128,512]{1,0:T(8,128)(2,1)S(1)} %get-tuple-element.45.refs_3_, ...), custom_call_target="tpu_custom_call" | custom-call | flops 1000 | bytes 1000 | tf_op jit(solution)/shard_map/finish/pallas_call | solution.py:34
  (3 shorter events, 0.0 us)
Async XLA Ops:
  2.6 3.1 %collective-permute-start.2 = (bf16[144,512]{1,0:T(8,128)(2,1)S(1)}, bf16[144,512]{1,0:T(8,128)(2,1)S(1)}, u32[]{:S(2)}, u32[]{:S(2)}) collective-permute-start(bf16[144,512]{1,0:T(8,128)(2,1)S(1)} %get-tuple-element.33), channel_id=1, source_target_pairs={{0,2},{2,0},{4,6},{6,4},{8,10},{10,8},{12,14},{14,12},{16,18},{18,... | collective-permute-start | bytes 442376 | tf_op jit(solution)/shard_map/ppermute | solution.py:374
  3.2 5.3 %collective-permute-start = (bf16[64,512]{1,0:T(8,128)(2,1)S(1)}, bf16[64,512]{1,0:T(8,128)(2,1)S(1)}, u32[]{:S(2)}, u32[]{:S(2)}) collective-permute-start(bf16[64,512]{1,0:T(8,128)(2,1)S(1)} %get-tuple-element.28), channel_id=1, source_target_pairs={{0,1},{1,0},{2,3},{3,2},{4,5},{5,4},{6,7},{7,6},{8,9},{9,8},{10,11... | collective-permute-start | bytes 196616 | tf_op jit(solution)/shard_map/ppermute | solution.py:377
  5.9 6.1 %collective-permute-start.3 = (bf16[80,512]{1,0:T(8,128)(2,1)S(1)}, bf16[80,512]{1,0:T(8,128)(2,1)S(1)}, u32[]{:S(2)}, u32[]{:S(2)}) collective-permute-start(bf16[80,512]{1,0:T(8,128)(2,1)S(1)} %get-tuple-element.35.refs_4_), channel_id=1, source_target_pairs={{0,4},{2,6},{4,0},{6,2},{8,12},{10,14},{12,8},{14,10},{16,20},{18,... | collective-permute-start | bytes 245768 | tf_op jit(solution)/shard_map/ppermute | solution.py:374
  8.5 9.1 %collective-permute-start.1 = (bf16[128,512]{1,0:T(8,128)(2,1)S(1)}, bf16[128,512]{1,0:T(8,128)(2,1)S(1)}, u32[]{:S(2)}, u32[]{:S(2)}) collective-permute-start(bf16[128,512]{1,0:T(8,128)(2,1)S(1)} %join_rows.1.refs_2_), channel_id=1, source_target_pairs={{0,16},{2,18},{4,20},{6,22},{8,24},{10,26},{12,28},{14,30},{16,0},... | collective-permute-start | bytes 393224 | tf_op jit(solution)/shard_map/ppermute | solution.py:374
  12.0 7.4 %collective-permute-start.6 = (bf16[128,512]{1,0:T(8,128)(2,1)S(1)}, bf16[128,512]{1,0:T(8,128)(2,1)S(1)}, u32[]{:S(2)}, u32[]{:S(2)}) collective-permute-start(bf16[128,512]{1,0:T(8,128)(2,1)S(1)} %get-tuple-element.39), channel_id=1, source_target_pairs={{0,8},{2,10},{4,12},{6,14},{8,0},{10,2},{12,4},{14,6},{16,24},{18,... | collective-permute-start | bytes 393224 | tf_op jit(solution)/shard_map/ppermute | solution.py:374
  13.7 5.7 %collective-permute-start.5 = (bf16[128,512]{1,0:T(8,128)(2,1)S(1)}, bf16[128,512]{1,0:T(8,128)(2,1)S(1)}, u32[]{:S(2)}, u32[]{:S(2)}) collective-permute-start(bf16[128,512]{1,0:T(8,128)(2,1)S(1)} %get-tuple-element.26.refs_1_.refs_0_), channel_id=1, source_target_pairs={{0,4},{2,6},{4,0},{6,2},{8,12},{10,14},{12,8},{14,10},{16,20},{18,... | collective-permute-start | bytes 393224 | tf_op jit(solution)/shard_map/ppermute | solution.py:374
  15.2 5.1 %collective-permute-start.4 = (bf16[80,512]{1,0:T(8,128)(2,1)S(1)}, bf16[80,512]{1,0:T(8,128)(2,1)S(1)}, u32[]{:S(2)}, u32[]{:S(2)}) collective-permute-start(bf16[80,512]{1,0:T(8,128)(2,1)S(1)} %get-tuple-element.38.refs_0_), channel_id=1, source_target_pairs={{0,8},{2,10},{4,12},{6,14},{8,0},{10,2},{12,4},{14,6},{16,24},{18,... | collective-permute-start | bytes 245768 | tf_op jit(solution)/shard_map/ppermute | solution.py:374
  15.6 8.5 %collective-permute-start.9 = (bf16[128,512]{1,0:T(8,128)(2,1)S(1)}, bf16[128,512]{1,0:T(8,128)(2,1)S(1)}, u32[]{:S(2)}, u32[]{:S(2)}) collective-permute-start(bf16[128,512]{1,0:T(8,128)(2,1)S(1)} %join_rows.1.refs_2_), channel_id=1, source_target_pairs={{0,2},{2,0},{4,6},{6,4},{8,10},{10,8},{12,14},{14,12},{16,18},{18,... | collective-permute-start | bytes 393224 | tf_op jit(solution)/shard_map/ppermute | solution.py:374
  17.6 6.6 %collective-permute-start.10 = (bf16[128,512]{1,0:T(8,128)(2,1)S(1)}, bf16[128,512]{1,0:T(8,128)(2,1)S(1)}, u32[]{:S(2)}, u32[]{:S(2)}) collective-permute-start(bf16[128,512]{1,0:T(8,128)(2,1)S(1)} %collective-permute-done.1.refs_3_.refs_0_.refs_4_), channel_id=1, source_target_pairs={{0,2},{2,0},{4,6},{6,4},{8,10},{10,8},{12,14},{14,12},{16,18},{18,... | collective-permute-start | bytes 393224 | tf_op jit(solution)/shard_map/ppermute | solution.py:374
  19.4 4.8 %collective-permute-start.11 = (bf16[128,512]{1,0:T(8,128)(2,1)S(1)}, bf16[128,512]{1,0:T(8,128)(2,1)S(1)}, u32[]{:S(2)}, u32[]{:S(2)}) collective-permute-start(bf16[128,512]{1,0:T(8,128)(2,1)S(1)} %collective-permute-done.6.refs_4_.refs_6_), channel_id=1, source_target_pairs={{0,2},{2,0},{4,6},{6,4},{8,10},{10,8},{12,14},{14,12},{16,18},{18,... | collective-permute-start | bytes 393224 | tf_op jit(solution)/shard_map/ppermute | solution.py:374
  20.4 7.0 %collective-permute-start.7 = (bf16[128,512]{1,0:T(8,128)(2,1)S(1)}, bf16[128,512]{1,0:T(8,128)(2,1)S(1)}, u32[]{:S(2)}, u32[]{:S(2)}) collective-permute-start(bf16[128,512]{1,0:T(8,128)(2,1)S(1)} %shard_map.95), channel_id=1, source_target_pairs={{0,8},{2,10},{4,12},{6,14},{8,0},{10,2},{12,4},{14,6},{16,24},{18,... | collective-permute-start | bytes 393224 | tf_op jit(solution)/shard_map/ppermute | solution.py:374
  21.2 6.1 %collective-permute-start.8 = (bf16[80,512]{1,0:T(8,128)(2,1)S(1)}, bf16[80,512]{1,0:T(8,128)(2,1)S(1)}, u32[]{:S(2)}, u32[]{:S(2)}) collective-permute-start(bf16[80,512]{1,0:T(8,128)(2,1)S(1)} %grow.1.refs_1_), channel_id=1, source_target_pairs={{0,16},{2,18},{4,20},{6,22},{8,24},{10,26},{12,28},{14,30},{16,0},... | collective-permute-start | bytes 245768 | tf_op jit(solution)/shard_map/ppermute | solution.py:374
  27.4 1.6 %collective-permute-start.12 = (bf16[128,512]{1,0:T(8,128)(2,1)S(1)}, bf16[128,512]{1,0:T(8,128)(2,1)S(1)}, u32[]{:S(2)}, u32[]{:S(2)}) collective-permute-start(bf16[128,512]{1,0:T(8,128)(2,1)S(1)} %pass_on.1.refs_1_), channel_id=1, source_target_pairs={{0,2},{2,0},{4,6},{6,4},{8,10},{10,8},{12,14},{14,12},{16,18},{18,... | collective-permute-start | bytes 393224 | tf_op jit(solution)/shard_map/ppermute | solution.py:374
  27.5 4.5 %collective-permute-start.14 = (bf16[64,512]{1,0:T(8,128)(2,1)S(1)}, bf16[64,512]{1,0:T(8,128)(2,1)S(1)}, u32[]{:S(2)}, u32[]{:S(2)}) collective-permute-start(bf16[64,512]{1,0:T(8,128)(2,1)S(1)} %get-tuple-element.41.refs_1_), channel_id=1, source_target_pairs={{0,4},{2,6},{4,0},{6,2},{8,12},{10,14},{12,8},{14,10},{16,20},{18,... | collective-permute-start | bytes 196616 | tf_op jit(solution)/shard_map/ppermute | solution.py:374
  30.0 6.3 %collective-permute-start.13 = (bf16[128,640]{1,0:T(8,128)(2,1)S(1)}, bf16[128,640]{1,0:T(8,128)(2,1)S(1)}, u32[]{:S(2)}, u32[]{:S(2)}) collective-permute-start(bf16[128,640]{1,0:T(8,128)(2,1)S(1)} %attend_far.1), channel_id=1, source_target_pairs={{0,4},{2,6},{4,0},{6,2},{8,12},{10,14},{12,8},{14,10},{16,20},{18,... | collective-permute-start | bytes 491528 | tf_op jit(solution)/shard_map/ppermute | solution.py:374
  32.1 1.4 %collective-permute-start.15 = (bf16[128,512]{1,0:T(8,128)(2,1)S(1)}, bf16[128,512]{1,0:T(8,128)(2,1)S(1)}, u32[]{:S(2)}, u32[]{:S(2)}) collective-permute-start(bf16[128,512]{1,0:T(8,128)(2,1)S(1)} %get-tuple-element.49), channel_id=1, source_target_pairs={{0,2},{2,0},{4,6},{6,4},{8,10},{10,8},{12,14},{14,12},{16,18},{18,... | collective-permute-start | bytes 393224 | tf_op jit(solution)/shard_map/ppermute | solution.py:374

commit v8 on v7

--- a/solution.py
+++ b/solution.py
@@ -79,26 +79,6 @@
         jnp.int32, (rows, rows), 1
     )
     return below, jnp.where(below, 1.0, 0.0).astype(F32)
-
-
-def load_all(n, count, *refs):
-    k_ref, v_ref, *plain = refs[:count]
-    outs, sems = refs[count:-1], refs[-1]
-    pieces, copies = outs[:n], outs[n:]
-    width = k_ref.shape[1] // n
-    here = lax.axis_index("head")
-    moves = []
-    for e, piece in enumerate(pieces):
-        target = lax.rem(here + e, n)
-        columns = pl.ds(pl.multiple_of(target * width, LANES), width)
-        moves.append((k_ref.at[:, columns], piece.at[:, pl.ds(0, width)]))
-        moves.append((v_ref.at[:, columns], piece.at[:, pl.ds(width, width)]))
-    moves += list(zip(plain, copies))
-    running = [pltpu.make_async_copy(a, b, sems.at[i]) for i, (a, b) in enumerate(moves)]
-    for one in running:
-        one.start()
-    for one in running:
-        one.wait()
 
 
 def join_rows(n, *refs):
@@ -159,6 +139,28 @@
     for out, which in ((send, 1 - low), (keep, low)):
         out[pl.ds(0, half), :] = part_of(held, which, half).astype(out.dtype)
         put_total(out, half, total)
+
+
+def load_all(n, count, *refs):
+    k_ref, v_ref, *plain = refs[:count]
+    outs, (held, sems) = refs[count:-2], refs[-2:]
+    pieces, copies, (send, keep) = outs[:n], outs[n:-2], outs[-2:]
+    width = k_ref.shape[1] // n
+    here = lax.axis_index("head")
+    moves = list(zip(plain, copies))
+    for e, piece in enumerate(pieces):
+        target = lax.rem(here + e, n)
+        columns = pl.ds(pl.multiple_of(target * width, LANES), width)
+        moves.append((k_ref.at[:, columns], piece.at[:, pl.ds(0, width)]))
+        moves.append((v_ref.at[:, columns], piece.at[:, pl.ds(width, width)]))
+    running = [pltpu.make_async_copy(a, b, sems.at[i]) for i, (a, b) in enumerate(moves)]
+    for one in running:
+        one.start()
+    for one in running[:3]:
+        one.wait()
+    summarize(*copies[:3], send, keep, held)
+    for one in running[3:]:
+        one.wait()
 
 
 def pair_total(first, keep_ref, other_ref):
@@ -379,23 +381,17 @@
     plain = (k_ret, v_ret, log_decay.T, q_ret, q_cross, gate_ret)
     loaded = call(
         functools.partial(load_all, n, 2 + len(plain)),
-        [pltpu.VMEM((length, 2 * width), BF16)] * n + [pltpu.VMEM(a.shape, a.dtype) for a in plain],
+        [pltpu.VMEM((length, 2 * width), BF16)] * n
+        + [pltpu.VMEM(a.shape, a.dtype) for a in plain]
+        + [pltpu.VMEM((half + PAD, wide), BF16), pltpu.VMEM((half + PAD, wide), F32)],
         [pltpu.with_memory_space_constraint(a, pltpu.HBM) for a in (cache_k, cache_v, *plain)],
-        scratch=[pltpu.SemaphoreType.DMA((2 * n + len(plain),))],
+        scratch=[pltpu.VMEM((HD, wide), F32), pltpu.SemaphoreType.DMA((2 * n + len(plain),))],
         name="load_all",
         takes=HBM,
     )
     pieces = loaded[:n]
-    k_ret, v_ret, decays, q_ret, q_cross, gate_ret = loaded[n:]
+    k_ret, v_ret, decays, q_ret, q_cross, gate_ret, sum_send, sum_keep = loaded[n:]
     arrived = [pieces[0]] + [to_head(pieces[e], e) for e in range(1, n)]
-    sum_send, sum_keep = call(
-        summarize,
-        [shape((half + PAD, wide)), shape((half + PAD, wide), F32)],
-        (k_ret, v_ret, decays),
-        scratch=[pltpu.VMEM((HD, wide), F32)],
-        name="summarize",
-        flops=3000000000,
-    )
     sum_other = swap(sum_send, 1)
     chip_send, chip_keep = call(
         chip_total,
@@ -421,7 +417,6 @@
         )
     }
     chip_other = swap(chip_send, 2)
-    q_other = swap(q_cross, 2)
     bit = far // 2
     while bit > 1:
         for s in list(blocks):
@@ -435,6 +430,8 @@
         after=(factor,),
     )
     blocks[1] = swap(handed, 4)
+    q_cross = pass_on(q_cross, blocks[far // 2])
+    q_other = swap(q_cross, 2)
     planes, bit = [], 1
     while bit < far:
         planes.append(swap(window, 4 * bit))
@@ -445,7 +442,7 @@
                 (window, planes[-1]),
                 name="grow",
                 flops=3000000000,
-                after=(q_other, *[blocks[s] for s in blocks if s]),
+                after=tuple(blocks[s] for s in blocks if s),
             )
         bit *= 2
 

time: 37.5 us -> 37.3 us (level)
  waiting for transfers between devices: 11 us -> 10.6 us
  starting transfers between devices: 18 us -> 18.4 us
    ppermute x15, starting transfers between devices: 15.4 us -> 15.8 us  [swap(): return lax.ppermute(value, 'ctx', [(b, b ^ bit) for b in range(count)])]
    ppermute x15, waiting for transfers between devices: 10 us -> 9.58 us  [swap(): return lax.ppermute(value, 'ctx', [(b, b ^ bit) for b in range(count)])]
where the time goes in v8:
time: 37.3 us; the launch traced here: 37.2 us
  starting transfers between devices  18.4 us (49%)
  waiting for transfers between devices  10.6 us (28%)
  Pallas kernels  7.43 us (20%)
  between operations  0.76 us (2%)
    ppermute x15, starting transfers between devices, swap(): return lax.ppermute(value, 'ctx', [(b, b ^ bit) for b in range(count)])  15.8 us
    ppermute x15, waiting for transfers between devices, swap(): return lax.ppermute(value, 'ctx', [(b, b ^ bit) for b in range(count)])  9.58 us
    pallas_call x15, Pallas kernels, call(): pl.pallas_call(kernel, out_shape=outs[0] if single else tuple(outs), in_s...  7.43 us
    ppermute x1, starting transfers between devices, to_head(): return lax.ppermute(value, 'head', [(y, (y + e) % n) for y in range(n)])  2.6 us
    ppermute x1, waiting for transfers between devices, to_head(): return lax.ppermute(value, 'head', [(y, (y + e) % n) for y in range(n)])  1 us
  transfers between devices with their start and end apart: 16, of which 8 were waited for; matrix products, arithmetic and copies ran while one was open for 0% of the time, Pallas kernels for 12%

profile of v8, /device:TPU:0, one launch (start us, length us, event | category | flops | bytes accessed | tf_op | source)
XLA Modules:
  0.0 37.2 jit_solution(13547216621092478794)
XLA Ops:
  0.6 1.8 %load_all.1 = (bf16[64,512]{1,0:T(8,128)(2,1)S(1)}, bf16[64,512]{1,0:T(8,128)(2,1)S(1)}, bf16[128,512]{1,0:T(8,128)(2,1)S(1)}, bf16[128,512]{1,0:T(8,128)(2,1)S(...) custom-call(bf16[64,512]{1,0:T(8,128)(2,1)} %refs_0_.1, ...), custom_call_target="tpu_custom_call" | custom-call | flops 1000 | bytes 1000 | tf_op jit(solution)/shard_map/load_all/pallas_call | solution.py:34
  2.4 0.5 %collective-permute-start.2 = (bf16[144,512]{1,0:T(8,128)(2,1)S(1)}, bf16[144,512]{1,0:T(8,128)(2,1)S(1)}, u32[]{:S(2)}, u32[]{:S(2)}) collective-permute-start(bf16[144,512]{1,0:T(8,128)(2,1)S(1)} %get-tuple-element.30), channel_id=1, source_target_pairs={{0,2},{2,0},{4,6},{6,4},{8,10},{10,8},{12,14},{14,12},{16,18},{18,... | collective-permute-start | bytes 442376 | tf_op jit(solution)/shard_map/ppermute | solution.py:376
  2.9 2.6 %collective-permute-start = (bf16[64,512]{1,0:T(8,128)(2,1)S(1)}, bf16[64,512]{1,0:T(8,128)(2,1)S(1)}, u32[]{:S(2)}, u32[]{:S(2)}) collective-permute-start(bf16[64,512]{1,0:T(8,128)(2,1)S(1)} %get-tuple-element.28), channel_id=1, source_target_pairs={{0,1},{1,0},{2,3},{3,2},{4,5},{5,4},{6,7},{7,6},{8,9},{9,8},{10,11... | collective-permute-start | bytes 196616 | tf_op jit(solution)/shard_map/ppermute | solution.py:379
  5.5 0.0 collective-permute-done.2.refs_1_
  5.5 0.1 chip_total.1
  5.6 1.6 %collective-permute-start.3 = (bf16[80,512]{1,0:T(8,128)(2,1)S(1)}, bf16[80,512]{1,0:T(8,128)(2,1)S(1)}, u32[]{:S(2)}, u32[]{:S(2)}) collective-permute-start(bf16[80,512]{1,0:T(8,128)(2,1)S(1)} %get-tuple-element.32.refs_4_), channel_id=1, source_target_pairs={{0,4},{2,6},{4,0},{6,2},{8,12},{10,14},{12,8},{14,10},{16,20},{18,... | collective-permute-start | bytes 245768 | tf_op jit(solution)/shard_map/ppermute | solution.py:376
  7.2 1.0 %collective-permute-done.refs_1_ = bf16[64,512]{1,0:T(8,128)(2,1)S(1)} collective-permute-done((bf16[64,512]{1,0:T(8,128)(2,1)S(1)}, bf16[64,512]{1,0:T(8,128)(2,1)S(1)}, u32[]{:S(2)}, u32[]{:S(2)}) %collective-permute-start) | collective-permute-done | bytes 65568 | tf_op jit(solution)/shard_map/ppermute | solution.py:379
  8.2 2.9 %collective-permute-start.1 = (bf16[128,512]{1,0:T(8,128)(2,1)S(1)}, bf16[128,512]{1,0:T(8,128)(2,1)S(1)}, u32[]{:S(2)}, u32[]{:S(2)}) collective-permute-start(bf16[128,512]{1,0:T(8,128)(2,1)S(1)} %join_rows.1.refs_2_), channel_id=1, source_target_pairs={{0,16},{2,18},{4,20},{6,22},{8,24},{10,26},{12,28},{14,30},{16,0},... | collective-permute-start | bytes 393224 | tf_op jit(solution)/shard_map/ppermute | solution.py:376
  11.1 0.6 %retain_inside.1 = (f32[128,512]{1,0:T(8,128)S(1)}, f32[128,2]{1,0:T(8,128)S(1)}) custom-call(bf16[128,512]{1,0:T(8,128)(2,1)S(1)} %get-tuple-element.33.refs_0_.refs_2_, bf16[128,512]{1,0:T(8,128)(2,1)S(1)} %get-tuple-element.34.refs_1_, bf16[128,512]{1,0:T(8,128)(2,1)S(1)} %get-tuple-element.35.refs_2_, f32[2,128]{1,0:T(2,128)S(1)} %get-tuple-element.36.refs_3_, ...), custom_call_target="tpu_custom_call" | custom-call | flops 1000 | bytes 1000 | tf_op jit(solution)/shard_map/retain_inside/pallas_call | solution.py:34
  11.7 0.0 collective-permute-done.3.refs_1_
  11.7 0.1 plane_total.1
  11.8 1.6 %collective-permute-start.5 = (bf16[128,512]{1,0:T(8,128)(2,1)S(1)}, bf16[128,512]{1,0:T(8,128)(2,1)S(1)}, u32[]{:S(2)}, u32[]{:S(2)}) collective-permute-start(bf16[128,512]{1,0:T(8,128)(2,1)S(1)} %get-tuple-element.39), channel_id=1, source_target_pairs={{0,8},{2,10},{4,12},{6,14},{8,0},{10,2},{12,4},{14,6},{16,24},{18,... | collective-permute-start | bytes 393224 | tf_op jit(solution)/shard_map/ppermute | solution.py:376
  13.4 0.4 %collective-permute-start.4 = (bf16[80,512]{1,0:T(8,128)(2,1)S(1)}, bf16[80,512]{1,0:T(8,128)(2,1)S(1)}, u32[]{:S(2)}, u32[]{:S(2)}) collective-permute-start(bf16[80,512]{1,0:T(8,128)(2,1)S(1)} %get-tuple-element.38.refs_0_), channel_id=1, source_target_pairs={{0,8},{2,10},{4,12},{6,14},{8,0},{10,2},{12,4},{14,6},{16,24},{18,... | collective-permute-start | bytes 245768 | tf_op jit(solution)/shard_map/ppermute | solution.py:376
  13.9 0.0 collective-permute-start.9
  13.9 3.5 %collective-permute-done.1.refs_1_.refs_2_.refs_0_.refs_4_ = bf16[128,512]{1,0:T(8,128)(2,1)S(1)} collective-permute-done((bf16[128,512]{1,0:T(8,128)(2,1)S(1)}, bf16[128,512]{1,0:T(8,128)(2,1)S(1)}, u32[]{:S(2)}, u32[]{:S(2)}) %collective-permute-start.1) | collective-permute-done | bytes 131104 | tf_op jit(solution)/shard_map/ppermute | solution.py:376
  17.4 1.5 %collective-permute-start.8 = (bf16[128,512]{1,0:T(8,128)(2,1)S(1)}, bf16[128,512]{1,0:T(8,128)(2,1)S(1)}, u32[]{:S(2)}, u32[]{:S(2)}) collective-permute-start(bf16[128,512]{1,0:T(8,128)(2,1)S(1)} %pass_on.2.refs_1_.refs_0_), channel_id=1, source_target_pairs={{0,4},{2,6},{4,0},{6,2},{8,12},{10,14},{12,8},{14,10},{16,20},{18,... | collective-permute-start | bytes 393224 | tf_op jit(solution)/shard_map/ppermute | solution.py:376
  18.9 0.0 collective-permute-start.10
  18.9 0.3 collective-permute-done.5.refs_3_.refs_6_
  19.2 0.2 collective-permute-start.11
  19.4 0.6 %collective-permute-done.4.refs_1_.refs_2_ = bf16[80,512]{1,0:T(8,128)(2,1)S(1)} collective-permute-done((bf16[80,512]{1,0:T(8,128)(2,1)S(1)}, bf16[80,512]{1,0:T(8,128)(2,1)S(1)}, u32[]{:S(2)}, u32[]{:S(2)}) %collective-permute-start.4) | collective-permute-done | bytes 81952 | tf_op jit(solution)/shard_map/ppermute | solution.py:376
  20.0 0.1 grow.1.refs_1_
  20.1 0.8 %collective-permute-start.6 = (bf16[128,512]{1,0:T(8,128)(2,1)S(1)}, bf16[128,512]{1,0:T(8,128)(2,1)S(1)}, u32[]{:S(2)}, u32[]{:S(2)}) collective-permute-start(bf16[128,512]{1,0:T(8,128)(2,1)S(1)} %shard_map.95), channel_id=1, source_target_pairs={{0,8},{2,10},{4,12},{6,14},{8,0},{10,2},{12,4},{14,6},{16,24},{18,... | collective-permute-start | bytes 393224 | tf_op jit(solution)/shard_map/ppermute | solution.py:376
  20.9 0.0 collective-permute-done.9.refs_3_
  20.9 3.0 %collective-permute-start.7 = (bf16[80,512]{1,0:T(8,128)(2,1)S(1)}, bf16[80,512]{1,0:T(8,128)(2,1)S(1)}, u32[]{:S(2)}, u32[]{:S(2)}) collective-permute-start(bf16[80,512]{1,0:T(8,128)(2,1)S(1)} %grow.1.refs_1_), channel_id=1, source_target_pairs={{0,16},{2,18},{4,20},{6,22},{8,24},{10,26},{12,28},{14,30},{16,0},... | collective-permute-start | bytes 245768 | tf_op jit(solution)/shard_map/ppermute | solution.py:376
  23.9 0.0 collective-permute-done.8.refs_0_
  23.9 0.0 collective-permute-done.10.refs_5_
  23.9 0.0 collective-permute-done.11.refs_7_
  23.9 1.7 %attend_near.1 = (f32[128,512]{1,0:T(8,128)S(1)}, f32[128,128]{1,0:T(8,128)S(1)}, f32[128,512]{1,0:T(8,128)S(1)}, f32[128,128]{1,0:T(8,128)S(1)}) custom-call(bf16[128,512]{1,0:T(8,128)(2,1)S(1)} %collective-permute-done.8.refs_0_, bf16[128,512]{1,0:T(8,128)(2,1)S(1)} %pass_on.2.refs_1_.refs_0_, bf16[128,512]{1,0:T(8,128)(2,1)S(1)} %join_rows.1.refs_2_, ...), custom_call_target="tpu_custom_call" | custom-call | flops 1000 | bytes 1000 | tf_op jit(solution)/shard_map/attend_near/pallas_call | solution.py:34
  25.6 1.3 %collective-permute-done.7.refs_3_ = bf16[80,512]{1,0:T(8,128)(2,1)S(1)} collective-permute-done((bf16[80,512]{1,0:T(8,128)(2,1)S(1)}, bf16[80,512]{1,0:T(8,128)(2,1)S(1)}, u32[]{:S(2)}, u32[]{:S(2)}) %collective-permute-start.7) | collective-permute-done | bytes 81952 | tf_op jit(solution)/shard_map/ppermute | solution.py:376
  26.9 0.1 chip_priors.1
  27.0 0.0 collective-permute-done.6.refs_0_
  27.0 0.1 collective-permute-start.12
  27.1 1.7 %collective-permute-start.14 = (bf16[64,512]{1,0:T(8,128)(2,1)S(1)}, bf16[64,512]{1,0:T(8,128)(2,1)S(1)}, u32[]{:S(2)}, u32[]{:S(2)}) collective-permute-start(bf16[64,512]{1,0:T(8,128)(2,1)S(1)} %get-tuple-element.41.refs_1_), channel_id=1, source_target_pairs={{0,4},{2,6},{4,0},{6,2},{8,12},{10,14},{12,8},{14,10},{16,20},{18,... | collective-permute-start | bytes 196616 | tf_op jit(solution)/shard_map/ppermute | solution.py:376
  28.8 0.0 collective-permute-done.12.refs_2_
  28.8 0.9 %attend_far.1 = bf16[128,640]{1,0:T(8,128)(2,1)S(1)} custom-call(bf16[128,512]{1,0:T(8,128)(2,1)S(1)} %collective-permute-done.8.refs_0_, bf16[128,512]{1,0:T(8,128)(2,1)S(1)} %pass_on.3.refs_1_, bf16[128,512]{1,0:T(8,128)(2,1)S(1)} %collective-permute-done.12.refs_2_, f32[128,512]{1,0:T(8,128)S(1)} %get-tuple-element.44.refs_3_, ...), custom_call_target="tpu_custom_call" | custom-call | flops 1000 | bytes 1000 | tf_op jit(solution)/shard_map/attend_far/pallas_call | solution.py:34
  29.7 1.3 %collective-permute-start.13 = (bf16[128,640]{1,0:T(8,128)(2,1)S(1)}, bf16[128,640]{1,0:T(8,128)(2,1)S(1)}, u32[]{:S(2)}, u32[]{:S(2)}) collective-permute-start(bf16[128,640]{1,0:T(8,128)(2,1)S(1)} %attend_far.1), channel_id=1, source_target_pairs={{0,4},{2,6},{4,0},{6,2},{8,12},{10,14},{12,8},{14,10},{16,20},{18,... | collective-permute-start | bytes 491528 | tf_op jit(solution)/shard_map/ppermute | solution.py:376
  31.1 0.6 %collective-permute-done.14.refs_3_ = bf16[64,512]{1,0:T(8,128)(2,1)S(1)} collective-permute-done((bf16[64,512]{1,0:T(8,128)(2,1)S(1)}, bf16[64,512]{1,0:T(8,128)(2,1)S(1)}, u32[]{:S(2)}, u32[]{:S(2)}) %collective-permute-start.14) | collective-permute-done | bytes 65568 | tf_op jit(solution)/shard_map/ppermute | solution.py:376
  31.6 0.1 block_priors.1
  31.8 0.1 collective-permute-start.15
  31.8 0.9 %attend_own.1.refs_0_ = f32[128,640]{1,0:T(8,128)S(1)} custom-call(bf16[128,512]{1,0:T(8,128)(2,1)S(1)} %pass_on.2.refs_1_.refs_0_, bf16[128,512]{1,0:T(8,128)(2,1)S(1)} %pass_on.3.refs_1_, bf16[128,512]{1,0:T(8,128)(2,1)S(1)} %collective-permute-done.12.refs_2_, f32[128,512]{1,0:T(8,128)S(1)} %get-tuple-element.42.refs_3_, ...), custom_call_target="tpu_custom_call" | custom-call | flops 1000 | bytes 1000 | tf_op jit(solution)/shard_map/attend_own/pallas_call | solution.py:34
  32.8 0.4 %collective-permute-done.15.refs_7_ = bf16[128,512]{1,0:T(8,128)(2,1)S(1)} collective-permute-done((bf16[128,512]{1,0:T(8,128)(2,1)S(1)}, bf16[128,512]{1,0:T(8,128)(2,1)S(1)}, u32[]{:S(2)}, u32[]{:S(2)}) %collective-permute-start.15) | collective-permute-done | bytes 131104 | tf_op jit(solution)/shard_map/ppermute | solution.py:376
  33.2 2.9 %collective-permute-done.13.refs_1_ = bf16[128,640]{1,0:T(8,128)(2,1)S(1)} collective-permute-done((bf16[128,640]{1,0:T(8,128)(2,1)S(1)}, bf16[128,640]{1,0:T(8,128)(2,1)S(1)}, u32[]{:S(2)}, u32[]{:S(2)}) %collective-permute-start.13) | collective-permute-done | bytes 163872 | tf_op jit(solution)/shard_map/ppermute | solution.py:376
  36.1 1.1 %finish.1 = (bf16[128,512]{1,0:T(8,128)(2,1)}, bf16[128,512]{1,0:T(8,128)(2,1)}) custom-call(f32[128,640]{1,0:T(8,128)S(1)} %attend_own.1.refs_0_, bf16[128,640]{1,0:T(8,128)(2,1)S(1)} %collective-permute-done.13.refs_1_, bf16[128,512]{1,0:T(8,128)(2,1)S(1)} %get-tuple-element.33.refs_0_.refs_2_, bf16[128,512]{1,0:T(8,128)(2,1)S(1)} %get-tuple-element.45.refs_3_, ...), custom_call_target="tpu_custom_call" | custom-call | flops 1000 | bytes 1000 | tf_op jit(solution)/shard_map/finish/pallas_call | solution.py:34
  (4 shorter events, 0.0 us)
Async XLA Ops:
  2.4 3.1 %collective-permute-start.2 = (bf16[144,512]{1,0:T(8,128)(2,1)S(1)}, bf16[144,512]{1,0:T(8,128)(2,1)S(1)}, u32[]{:S(2)}, u32[]{:S(2)}) collective-permute-start(bf16[144,512]{1,0:T(8,128)(2,1)S(1)} %get-tuple-element.30), channel_id=1, source_target_pairs={{0,2},{2,0},{4,6},{6,4},{8,10},{10,8},{12,14},{14,12},{16,18},{18,... | collective-permute-start | bytes 442376 | tf_op jit(solution)/shard_map/ppermute | solution.py:376
  2.9 5.3 %collective-permute-start = (bf16[64,512]{1,0:T(8,128)(2,1)S(1)}, bf16[64,512]{1,0:T(8,128)(2,1)S(1)}, u32[]{:S(2)}, u32[]{:S(2)}) collective-permute-start(bf16[64,512]{1,0:T(8,128)(2,1)S(1)} %get-tuple-element.28), channel_id=1, source_target_pairs={{0,1},{1,0},{2,3},{3,2},{4,5},{5,4},{6,7},{7,6},{8,9},{9,8},{10,11... | collective-permute-start | bytes 196616 | tf_op jit(solution)/shard_map/ppermute | solution.py:379
  5.6 6.1 %collective-permute-start.3 = (bf16[80,512]{1,0:T(8,128)(2,1)S(1)}, bf16[80,512]{1,0:T(8,128)(2,1)S(1)}, u32[]{:S(2)}, u32[]{:S(2)}) collective-permute-start(bf16[80,512]{1,0:T(8,128)(2,1)S(1)} %get-tuple-element.32.refs_4_), channel_id=1, source_target_pairs={{0,4},{2,6},{4,0},{6,2},{8,12},{10,14},{12,8},{14,10},{16,20},{18,... | collective-permute-start | bytes 245768 | tf_op jit(solution)/shard_map/ppermute | solution.py:376
  8.2 9.1 %collective-permute-start.1 = (bf16[128,512]{1,0:T(8,128)(2,1)S(1)}, bf16[128,512]{1,0:T(8,128)(2,1)S(1)}, u32[]{:S(2)}, u32[]{:S(2)}) collective-permute-start(bf16[128,512]{1,0:T(8,128)(2,1)S(1)} %join_rows.1.refs_2_), channel_id=1, source_target_pairs={{0,16},{2,18},{4,20},{6,22},{8,24},{10,26},{12,28},{14,30},{16,0},... | collective-permute-start | bytes 393224 | tf_op jit(solution)/shard_map/ppermute | solution.py:376
  11.8 7.4 %collective-permute-start.5 = (bf16[128,512]{1,0:T(8,128)(2,1)S(1)}, bf16[128,512]{1,0:T(8,128)(2,1)S(1)}, u32[]{:S(2)}, u32[]{:S(2)}) collective-permute-start(bf16[128,512]{1,0:T(8,128)(2,1)S(1)} %get-tuple-element.39), channel_id=1, source_target_pairs={{0,8},{2,10},{4,12},{6,14},{8,0},{10,2},{12,4},{14,6},{16,24},{18,... | collective-permute-start | bytes 393224 | tf_op jit(solution)/shard_map/ppermute | solution.py:376
  13.4 6.6 %collective-permute-start.4 = (bf16[80,512]{1,0:T(8,128)(2,1)S(1)}, bf16[80,512]{1,0:T(8,128)(2,1)S(1)}, u32[]{:S(2)}, u32[]{:S(2)}) collective-permute-start(bf16[80,512]{1,0:T(8,128)(2,1)S(1)} %get-tuple-element.38.refs_0_), channel_id=1, source_target_pairs={{0,8},{2,10},{4,12},{6,14},{8,0},{10,2},{12,4},{14,6},{16,24},{18,... | collective-permute-start | bytes 245768 | tf_op jit(solution)/shard_map/ppermute | solution.py:376
  13.9 7.1 %collective-permute-start.9 = (bf16[128,512]{1,0:T(8,128)(2,1)S(1)}, bf16[128,512]{1,0:T(8,128)(2,1)S(1)}, u32[]{:S(2)}, u32[]{:S(2)}) collective-permute-start(bf16[128,512]{1,0:T(8,128)(2,1)S(1)} %join_rows.1.refs_2_), channel_id=1, source_target_pairs={{0,2},{2,0},{4,6},{6,4},{8,10},{10,8},{12,14},{14,12},{16,18},{18,... | collective-permute-start | bytes 393224 | tf_op jit(solution)/shard_map/ppermute | solution.py:376
  17.4 6.6 %collective-permute-start.8 = (bf16[128,512]{1,0:T(8,128)(2,1)S(1)}, bf16[128,512]{1,0:T(8,128)(2,1)S(1)}, u32[]{:S(2)}, u32[]{:S(2)}) collective-permute-start(bf16[128,512]{1,0:T(8,128)(2,1)S(1)} %pass_on.2.refs_1_.refs_0_), channel_id=1, source_target_pairs={{0,4},{2,6},{4,0},{6,2},{8,12},{10,14},{12,8},{14,10},{16,20},{18,... | collective-permute-start | bytes 393224 | tf_op jit(solution)/shard_map/ppermute | solution.py:376
  18.9 5.0 %collective-permute-start.10 = (bf16[128,512]{1,0:T(8,128)(2,1)S(1)}, bf16[128,512]{1,0:T(8,128)(2,1)S(1)}, u32[]{:S(2)}, u32[]{:S(2)}) collective-permute-start(bf16[128,512]{1,0:T(8,128)(2,1)S(1)} %collective-permute-done.1.refs_1_.refs_2_.refs_0_.refs_4_), channel_id=1, source_target_pairs={{0,2},{2,0},{4,6},{6,4},{8,10},{10,8},{12,14},{14,12},{16,18},{18,... | collective-permute-start | bytes 393224 | tf_op jit(solution)/shard_map/ppermute | solution.py:376
  19.2 4.8 %collective-permute-start.11 = (bf16[128,512]{1,0:T(8,128)(2,1)S(1)}, bf16[128,512]{1,0:T(8,128)(2,1)S(1)}, u32[]{:S(2)}, u32[]{:S(2)}) collective-permute-start(bf16[128,512]{1,0:T(8,128)(2,1)S(1)} %collective-permute-done.5.refs_3_.refs_6_), channel_id=1, source_target_pairs={{0,2},{2,0},{4,6},{6,4},{8,10},{10,8},{12,14},{14,12},{16,18},{18,... | collective-permute-start | bytes 393224 | tf_op jit(solution)/shard_map/ppermute | solution.py:376
  20.1 6.9 %collective-permute-start.6 = (bf16[128,512]{1,0:T(8,128)(2,1)S(1)}, bf16[128,512]{1,0:T(8,128)(2,1)S(1)}, u32[]{:S(2)}, u32[]{:S(2)}) collective-permute-start(bf16[128,512]{1,0:T(8,128)(2,1)S(1)} %shard_map.95), channel_id=1, source_target_pairs={{0,8},{2,10},{4,12},{6,14},{8,0},{10,2},{12,4},{14,6},{16,24},{18,... | collective-permute-start | bytes 393224 | tf_op jit(solution)/shard_map/ppermute | solution.py:376
  20.9 6.0 %collective-permute-start.7 = (bf16[80,512]{1,0:T(8,128)(2,1)S(1)}, bf16[80,512]{1,0:T(8,128)(2,1)S(1)}, u32[]{:S(2)}, u32[]{:S(2)}) collective-permute-start(bf16[80,512]{1,0:T(8,128)(2,1)S(1)} %grow.1.refs_1_), channel_id=1, source_target_pairs={{0,16},{2,18},{4,20},{6,22},{8,24},{10,26},{12,28},{14,30},{16,0},... | collective-permute-start | bytes 245768 | tf_op jit(solution)/shard_map/ppermute | solution.py:376
  27.0 1.8 %collective-permute-start.12 = (bf16[128,512]{1,0:T(8,128)(2,1)S(1)}, bf16[128,512]{1,0:T(8,128)(2,1)S(1)}, u32[]{:S(2)}, u32[]{:S(2)}) collective-permute-start(bf16[128,512]{1,0:T(8,128)(2,1)S(1)} %pass_on.3.refs_1_), channel_id=1, source_target_pairs={{0,2},{2,0},{4,6},{6,4},{8,10},{10,8},{12,14},{14,12},{16,18},{18,... | collective-permute-start | bytes 393224 | tf_op jit(solution)/shard_map/ppermute | solution.py:376
  27.1 4.5 %collective-permute-start.14 = (bf16[64,512]{1,0:T(8,128)(2,1)S(1)}, bf16[64,512]{1,0:T(8,128)(2,1)S(1)}, u32[]{:S(2)}, u32[]{:S(2)}) collective-permute-start(bf16[64,512]{1,0:T(8,128)(2,1)S(1)} %get-tuple-element.41.refs_1_), channel_id=1, source_target_pairs={{0,4},{2,6},{4,0},{6,2},{8,12},{10,14},{12,8},{14,10},{16,20},{18,... | collective-permute-start | bytes 196616 | tf_op jit(solution)/shard_map/ppermute | solution.py:376
  29.7 6.3 %collective-permute-start.13 = (bf16[128,640]{1,0:T(8,128)(2,1)S(1)}, bf16[128,640]{1,0:T(8,128)(2,1)S(1)}, u32[]{:S(2)}, u32[]{:S(2)}) collective-permute-start(bf16[128,640]{1,0:T(8,128)(2,1)S(1)} %attend_far.1), channel_id=1, source_target_pairs={{0,4},{2,6},{4,0},{6,2},{8,12},{10,14},{12,8},{14,10},{16,20},{18,... | collective-permute-start | bytes 491528 | tf_op jit(solution)/shard_map/ppermute | solution.py:376
  31.8 1.4 %collective-permute-start.15 = (bf16[128,512]{1,0:T(8,128)(2,1)S(1)}, bf16[128,512]{1,0:T(8,128)(2,1)S(1)}, u32[]{:S(2)}, u32[]{:S(2)}) collective-permute-start(bf16[128,512]{1,0:T(8,128)(2,1)S(1)} %get-tuple-element.49), channel_id=1, source_target_pairs={{0,2},{2,0},{4,6},{6,4},{8,10},{10,8},{12,14},{14,12},{16,18},{18,... | collective-permute-start | bytes 393224 | tf_op jit(solution)/shard_map/ppermute | solution.py:376

commit v9 on v8

--- a/solution.py
+++ b/solution.py
@@ -245,13 +245,7 @@
         inside_ref[:, columns] = dot(weights, v_ref[:, columns], ((1,), (0,)))
 
 
-def finish(
-    part_ref, part_other_ref, q_ref, gate_ref, inside_ref, factor_ref, keep_ref, other_ref,
-    o_ret, o_cross, held, ret_held, cross_held, sems,
-):
-    merge(part_ref, part_other_ref, cross_held)
-    cross_out = pltpu.make_async_copy(cross_held, o_cross, sems.at[0])
-    cross_out.start()
+def retain_finish(q_ref, gate_ref, inside_ref, factor_ref, keep_ref, other_ref, o_ret, held, done, sem):
     low, _, _ = bits()
     half = keep_ref.shape[0]
     for ref, which in ((keep_ref, low), (other_ref, 1 - low)):
@@ -263,11 +257,22 @@
         scale = lax.rsqrt(jnp.mean(retained * retained, axis=1, keepdims=True) + EPS)
         gate = gate_ref[:, columns].astype(F32)
         silu = gate / (1.0 + jnp.exp(-gate))
-        ret_held[:, columns] = (retained * scale * silu).astype(BF16)
-    ret_out = pltpu.make_async_copy(ret_held, o_ret, sems.at[1])
-    ret_out.start()
-    cross_out.wait()
-    ret_out.wait()
+        done[:, columns] = (retained * scale * silu).astype(BF16)
+    out = pltpu.make_async_copy(done, o_ret, sem)
+    out.start()
+    out.wait()
+
+
+def finish(part_ref, part_other_ref, o_cross, done, sems):
+    wide = done.shape[1]
+    moves = []
+    for head in range(wide // HD):
+        merge(head, part_ref, part_other_ref, done)
+        columns = pl.ds(head * HD, HD)
+        moves.append(pltpu.make_async_copy(done.at[:, columns], o_cross.at[:, columns], sems.at[head]))
+        moves[-1].start()
+    for move in moves:
+        move.wait()
 
 
 def copy_after(source, out):
@@ -344,25 +349,24 @@
             stats_out[...] = stats
 
 
-def merge(keep_ref, other_ref, out):
+def merge(head, keep_ref, other_ref, out):
     wide = out.shape[1]
     ins = (keep_ref, other_ref)
-    stats = [ref[:, pl.ds(wide, LANES)].astype(F32) for ref in ins]
-    for head in range(wide // HD):
-        columns = pl.ds(head * HD, HD)
-        levels = [
-            tile[:, 3 * head : 3 * head + 1]
-            + tile[:, 3 * head + 1 : 3 * head + 2]
-            + tile[:, 3 * head + 2 : 3 * head + 3]
-            for tile in stats
-        ]
-        top = functools.reduce(jnp.maximum, levels)
-        weights = [jnp.exp2(level - top) for level in levels]
-        share = 1.0 / functools.reduce(jnp.add, weights)
-        mixed = functools.reduce(
-            jnp.add, [(w * share) * ref[:, columns].astype(F32) for w, ref in zip(weights, ins)]
-        )
-        out[:, columns] = mixed.astype(BF16)
+    columns = pl.ds(head * HD, HD)
+    tiles = [ref[:, pl.ds(wide, LANES)].astype(F32) for ref in ins]
+    levels = [
+        tile[:, 3 * head : 3 * head + 1]
+        + tile[:, 3 * head + 1 : 3 * head + 2]
+        + tile[:, 3 * head + 2 : 3 * head + 3]
+        for tile in tiles
+    ]
+    top = functools.reduce(jnp.maximum, levels)
+    weights = [jnp.exp2(level - top) for level in levels]
+    share = 1.0 / functools.reduce(jnp.add, weights)
+    mixed = functools.reduce(
+        jnp.add, [(w * share) * ref[:, columns].astype(F32) for w, ref in zip(weights, ins)]
+    )
+    out[:, columns] = mixed.astype(BF16)
 
 
 def per_device(count, n, q_ret, k_ret, v_ret, gate_ret, log_decay, q_cross, cache_k, cache_v):
@@ -476,6 +480,7 @@
         [shape((quarter, wide)), shape((quarter, wide), F32)],
         (chip_keep, chip_other, *planes),
         name="chip_priors",
+        flops=3000000000,
         after=so_far[1:2],
     )
     for s in near:
@@ -496,15 +501,24 @@
         name="block_priors",
     )
     state_other = swap(state_send, 1)
-    held = pltpu.VMEM((rows, wide), BF16)
-    return call(
+    done = pltpu.VMEM((rows, wide), BF16)
+    o_ret = call(
+        retain_finish,
+        [shape((rows, wide))],
+        (q_ret, gate_ret, inside, factor, state_keep, state_other),
+        scratch=[pltpu.VMEM((HD, wide), BF16), done, pltpu.SemaphoreType.DMA],
+        name="retain_finish",
+        gives=HBM,
+    )
+    o_cross = call(
         finish,
-        [shape((rows, wide))] * 2,
-        (part_keep, part_other, q_ret, gate_ret, inside, factor, state_keep, state_other),
-        scratch=[pltpu.VMEM((HD, wide), BF16), held, held, pltpu.SemaphoreType.DMA((2,))],
+        [shape((rows, wide))],
+        (part_keep, part_other),
+        scratch=[done, pltpu.SemaphoreType.DMA((heads,))],
         name="finish",
         gives=HBM,
     )
+    return o_ret, o_cross
 
 
 def solution(mesh):

time: 37.3 us -> 38.2 us (1.024)
  Pallas kernels: 7.43 us -> 8.37 us
    pallas_call x15 -> x16, Pallas kernels: 7.43 us -> 8.37 us  [call(): pl.pallas_call(kernel, out_shape=outs[0] if single else tuple(outs), in_s...]
  transfers between devices with their start and end apart: 16 -> 16, of which waited for: 8 -> 9; matrix products, arithmetic and copies ran while one was open for 0% -> 0% of each run, Pallas kernels for 12% -> 15%
where the time goes in v9:
time: 38.2 us; the launch traced here: 38 us
  starting transfers between devices  18.3 us (48%)
  waiting for transfers between devices  10.6 us (28%)
  Pallas kernels  8.37 us (22%)
  between operations  0.75 us (2%)
    ppermute x15, starting transfers between devices, swap(): return lax.ppermute(value, 'ctx', [(b, b ^ bit) for b in range(count)])  15.7 us
    ppermute x15, waiting for transfers between devices, swap(): return lax.ppermute(value, 'ctx', [(b, b ^ bit) for b in range(count)])  9.62 us
    pallas_call x16, Pallas kernels, call(): pl.pallas_call(kernel, out_shape=outs[0] if single else tuple(outs), in_s...  8.37 us
    ppermute x1, starting transfers between devices, to_head(): return lax.ppermute(value, 'head', [(y, (y + e) % n) for y in range(n)])  2.6 us
    ppermute x1, waiting for transfers between devices, to_head(): return lax.ppermute(value, 'head', [(y, (y + e) % n) for y in range(n)])  1 us
  transfers between devices with their start and end apart: 16, of which 9 were waited for; matrix products, arithmetic and copies ran while one was open for 0% of the time, Pallas kernels for 15%

profile of v9, /device:TPU:0, one launch (start us, length us, event | category | flops | bytes accessed | tf_op | source)
XLA Modules:
  0.0 38.0 jit_solution(13175690554905246957)
XLA Ops:
  0.6 1.8 %load_all.1 = (bf16[64,512]{1,0:T(8,128)(2,1)S(1)}, bf16[64,512]{1,0:T(8,128)(2,1)S(1)}, bf16[128,512]{1,0:T(8,128)(2,1)S(1)}, bf16[128,512]{1,0:T(8,128)(2,1)S(...) custom-call(bf16[64,512]{1,0:T(8,128)(2,1)} %refs_0_.1, ...), custom_call_target="tpu_custom_call" | custom-call | flops 1000 | bytes 1000 | tf_op jit(solution)/shard_map/load_all/pallas_call | solution.py:34
  2.4 0.5 %collective-permute-start = (bf16[144,512]{1,0:T(8,128)(2,1)S(1)}, bf16[144,512]{1,0:T(8,128)(2,1)S(1)}, u32[]{:S(2)}, u32[]{:S(2)}) collective-permute-start(bf16[144,512]{1,0:T(8,128)(2,1)S(1)} %get-tuple-element.32), channel_id=1, source_target_pairs={{0,2},{2,0},{4,6},{6,4},{8,10},{10,8},{12,14},{14,12},{16,18},{18,... | collective-permute-start | bytes 442376 | tf_op jit(solution)/shard_map/ppermute | solution.py:380
  2.9 2.6 %collective-permute-start.2 = (bf16[64,512]{1,0:T(8,128)(2,1)S(1)}, bf16[64,512]{1,0:T(8,128)(2,1)S(1)}, u32[]{:S(2)}, u32[]{:S(2)}) collective-permute-start(bf16[64,512]{1,0:T(8,128)(2,1)S(1)} %get-tuple-element.38), channel_id=1, source_target_pairs={{0,1},{1,0},{2,3},{3,2},{4,5},{5,4},{6,7},{7,6},{8,9},{9,8},{10,11... | collective-permute-start | bytes 196616 | tf_op jit(solution)/shard_map/ppermute | solution.py:383
  5.5 0.0 collective-permute-done.refs_1_
  5.5 0.1 chip_total.1
  5.6 1.6 %collective-permute-start.1 = (bf16[80,512]{1,0:T(8,128)(2,1)S(1)}, bf16[80,512]{1,0:T(8,128)(2,1)S(1)}, u32[]{:S(2)}, u32[]{:S(2)}) collective-permute-start(bf16[80,512]{1,0:T(8,128)(2,1)S(1)} %get-tuple-element.33.refs_4_), channel_id=1, source_target_pairs={{0,4},{2,6},{4,0},{6,2},{8,12},{10,14},{12,8},{14,10},{16,20},{18,... | collective-permute-start | bytes 245768 | tf_op jit(solution)/shard_map/ppermute | solution.py:380
  7.2 1.0 %collective-permute-done.2.refs_1_ = bf16[64,512]{1,0:T(8,128)(2,1)S(1)} collective-permute-done((bf16[64,512]{1,0:T(8,128)(2,1)S(1)}, bf16[64,512]{1,0:T(8,128)(2,1)S(1)}, u32[]{:S(2)}, u32[]{:S(2)}) %collective-permute-start.2) | collective-permute-done | bytes 65568 | tf_op jit(solution)/shard_map/ppermute | solution.py:383
  8.2 2.9 %collective-permute-start.4 = (bf16[128,512]{1,0:T(8,128)(2,1)S(1)}, bf16[128,512]{1,0:T(8,128)(2,1)S(1)}, u32[]{:S(2)}, u32[]{:S(2)}) collective-permute-start(bf16[128,512]{1,0:T(8,128)(2,1)S(1)} %join_rows.1.refs_2_), channel_id=1, source_target_pairs={{0,16},{2,18},{4,20},{6,22},{8,24},{10,26},{12,28},{14,30},{16,0},... | collective-permute-start | bytes 393224 | tf_op jit(solution)/shard_map/ppermute | solution.py:380
  11.1 0.6 %retain_inside.1 = (f32[128,512]{1,0:T(8,128)S(1)}, f32[128,2]{1,0:T(8,128)S(1)}) custom-call(bf16[128,512]{1,0:T(8,128)(2,1)S(1)} %get-tuple-element.26.refs_0_, bf16[128,512]{1,0:T(8,128)(2,1)S(1)} %get-tuple-element.28.refs_1_, bf16[128,512]{1,0:T(8,128)(2,1)S(1)} %get-tuple-element.29.refs_2_, f32[2,128]{1,0:T(2,128)S(1)} %get-tuple-element.30.refs_3_, ...), custom_call_target="tpu_custom_call" | custom-call | flops 1000 | bytes 1000 | tf_op jit(solution)/shard_map/retain_inside/pallas_call | solution.py:34
  11.7 0.0 collective-permute-done.1.refs_1_
  11.7 0.1 plane_total.1
  11.8 1.6 %collective-permute-start.5 = (bf16[128,512]{1,0:T(8,128)(2,1)S(1)}, bf16[128,512]{1,0:T(8,128)(2,1)S(1)}, u32[]{:S(2)}, u32[]{:S(2)}) collective-permute-start(bf16[128,512]{1,0:T(8,128)(2,1)S(1)} %get-tuple-element.40), channel_id=1, source_target_pairs={{0,8},{2,10},{4,12},{6,14},{8,0},{10,2},{12,4},{14,6},{16,24},{18,... | collective-permute-start | bytes 393224 | tf_op jit(solution)/shard_map/ppermute | solution.py:380
  13.4 0.4 %collective-permute-start.3 = (bf16[80,512]{1,0:T(8,128)(2,1)S(1)}, bf16[80,512]{1,0:T(8,128)(2,1)S(1)}, u32[]{:S(2)}, u32[]{:S(2)}) collective-permute-start(bf16[80,512]{1,0:T(8,128)(2,1)S(1)} %get-tuple-element.39.refs_0_), channel_id=1, source_target_pairs={{0,8},{2,10},{4,12},{6,14},{8,0},{10,2},{12,4},{14,6},{16,24},{18,... | collective-permute-start | bytes 245768 | tf_op jit(solution)/shard_map/ppermute | solution.py:380
  13.9 0.0 collective-permute-start.8
  13.9 3.5 %collective-permute-done.4.refs_2_.refs_1_.refs_4_.refs_0_ = bf16[128,512]{1,0:T(8,128)(2,1)S(1)} collective-permute-done((bf16[128,512]{1,0:T(8,128)(2,1)S(1)}, bf16[128,512]{1,0:T(8,128)(2,1)S(1)}, u32[]{:S(2)}, u32[]{:S(2)}) %collective-permute-start.4) | collective-permute-done | bytes 131104 | tf_op jit(solution)/shard_map/ppermute | solution.py:380
  17.4 1.5 %collective-permute-start.7 = (bf16[128,512]{1,0:T(8,128)(2,1)S(1)}, bf16[128,512]{1,0:T(8,128)(2,1)S(1)}, u32[]{:S(2)}, u32[]{:S(2)}) collective-permute-start(bf16[128,512]{1,0:T(8,128)(2,1)S(1)} %pass_on.2.refs_1_.refs_0_), channel_id=1, source_target_pairs={{0,4},{2,6},{4,0},{6,2},{8,12},{10,14},{12,8},{14,10},{16,20},{18,... | collective-permute-start | bytes 393224 | tf_op jit(solution)/shard_map/ppermute | solution.py:380
  18.9 0.0 collective-permute-start.9
  18.9 0.3 collective-permute-done.5.refs_3_.refs_6_
  19.2 0.2 collective-permute-start.10
  19.4 0.6 %collective-permute-done.3.refs_1_.refs_2_ = bf16[80,512]{1,0:T(8,128)(2,1)S(1)} collective-permute-done((bf16[80,512]{1,0:T(8,128)(2,1)S(1)}, bf16[80,512]{1,0:T(8,128)(2,1)S(1)}, u32[]{:S(2)}, u32[]{:S(2)}) %collective-permute-start.3) | collective-permute-done | bytes 81952 | tf_op jit(solution)/shard_map/ppermute | solution.py:380
  20.0 0.1 grow.1.refs_1_
  20.1 1.3 %collective-permute-start.6 = (bf16[80,512]{1,0:T(8,128)(2,1)S(1)}, bf16[80,512]{1,0:T(8,128)(2,1)S(1)}, u32[]{:S(2)}, u32[]{:S(2)}) collective-permute-start(bf16[80,512]{1,0:T(8,128)(2,1)S(1)} %grow.1.refs_1_), channel_id=1, source_target_pairs={{0,16},{2,18},{4,20},{6,22},{8,24},{10,26},{12,28},{14,30},{16,0},... | collective-permute-start | bytes 245768 | tf_op jit(solution)/shard_map/ppermute | solution.py:380
  21.4 0.0 collective-permute-done.8.refs_3_
  21.4 2.5 %collective-permute-start.13 = (bf16[128,512]{1,0:T(8,128)(2,1)S(1)}, bf16[128,512]{1,0:T(8,128)(2,1)S(1)}, u32[]{:S(2)}, u32[]{:S(2)}) collective-permute-start(bf16[128,512]{1,0:T(8,128)(2,1)S(1)} %shard_map.95), channel_id=1, source_target_pairs={{0,8},{2,10},{4,12},{6,14},{8,0},{10,2},{12,4},{14,6},{16,24},{18,... | collective-permute-start | bytes 393224 | tf_op jit(solution)/shard_map/ppermute | solution.py:380
  24.0 0.0 collective-permute-done.7.refs_0_
  24.0 0.0 collective-permute-done.9.refs_5_
  24.0 0.0 collective-permute-done.10.refs_7_
  24.0 1.7 %attend_near.1 = (f32[128,512]{1,0:T(8,128)S(1)}, f32[128,128]{1,0:T(8,128)S(1)}, f32[128,512]{1,0:T(8,128)S(1)}, f32[128,128]{1,0:T(8,128)S(1)}) custom-call(bf16[128,512]{1,0:T(8,128)(2,1)S(1)} %collective-permute-done.7.refs_0_, bf16[128,512]{1,0:T(8,128)(2,1)S(1)} %pass_on.2.refs_1_.refs_0_, bf16[128,512]{1,0:T(8,128)(2,1)S(1)} %join_rows.1.refs_2_, ...), custom_call_target="tpu_custom_call" | custom-call | flops 1000 | bytes 1000 | tf_op jit(solution)/shard_map/attend_near/pallas_call | solution.py:34
  25.6 1.3 %collective-permute-done.6.refs_3_ = bf16[80,512]{1,0:T(8,128)(2,1)S(1)} collective-permute-done((bf16[80,512]{1,0:T(8,128)(2,1)S(1)}, bf16[80,512]{1,0:T(8,128)(2,1)S(1)}, u32[]{:S(2)}, u32[]{:S(2)}) %collective-permute-start.6) | collective-permute-done | bytes 81952 | tf_op jit(solution)/shard_map/ppermute | solution.py:380
  26.9 0.1 chip_priors.1
  27.0 1.1 %collective-permute-done.13.refs_0_ = bf16[128,512]{1,0:T(8,128)(2,1)S(1)} collective-permute-done((bf16[128,512]{1,0:T(8,128)(2,1)S(1)}, bf16[128,512]{1,0:T(8,128)(2,1)S(1)}, u32[]{:S(2)}, u32[]{:S(2)}) %collective-permute-start.13) | collective-permute-done | bytes 131104 | tf_op jit(solution)/shard_map/ppermute | solution.py:380
  28.1 0.0 collective-permute-start.14
  28.1 1.5 %collective-permute-start.11 = (bf16[64,512]{1,0:T(8,128)(2,1)S(1)}, bf16[64,512]{1,0:T(8,128)(2,1)S(1)}, u32[]{:S(2)}, u32[]{:S(2)}) collective-permute-start(bf16[64,512]{1,0:T(8,128)(2,1)S(1)} %get-tuple-element.44.refs_1_), channel_id=1, source_target_pairs={{0,4},{2,6},{4,0},{6,2},{8,12},{10,14},{12,8},{14,10},{16,20},{18,... | collective-permute-start | bytes 196616 | tf_op jit(solution)/shard_map/ppermute | solution.py:380
  29.7 0.0 collective-permute-done.14.refs_2_
  29.7 0.9 %attend_far.1 = bf16[128,640]{1,0:T(8,128)(2,1)S(1)} custom-call(bf16[128,512]{1,0:T(8,128)(2,1)S(1)} %collective-permute-done.7.refs_0_, bf16[128,512]{1,0:T(8,128)(2,1)S(1)} %pass_on.3.refs_1_, bf16[128,512]{1,0:T(8,128)(2,1)S(1)} %collective-permute-done.14.refs_2_, f32[128,512]{1,0:T(8,128)S(1)} %get-tuple-element.49.refs_3_, ...), custom_call_target="tpu_custom_call" | custom-call | flops 1000 | bytes 1000 | tf_op jit(solution)/shard_map/attend_far/pallas_call | solution.py:34
  30.6 1.4 %collective-permute-start.15 = (bf16[128,640]{1,0:T(8,128)(2,1)S(1)}, bf16[128,640]{1,0:T(8,128)(2,1)S(1)}, u32[]{:S(2)}, u32[]{:S(2)}) collective-permute-start(bf16[128,640]{1,0:T(8,128)(2,1)S(1)} %attend_far.1), channel_id=1, source_target_pairs={{0,4},{2,6},{4,0},{6,2},{8,12},{10,14},{12,8},{14,10},{16,20},{18,... | collective-permute-start | bytes 491528 | tf_op jit(solution)/shard_map/ppermute | solution.py:380
  32.0 0.6 %collective-permute-done.11.refs_3_ = bf16[64,512]{1,0:T(8,128)(2,1)S(1)} collective-permute-done((bf16[64,512]{1,0:T(8,128)(2,1)S(1)}, bf16[64,512]{1,0:T(8,128)(2,1)S(1)}, u32[]{:S(2)}, u32[]{:S(2)}) %collective-permute-start.11) | collective-permute-done | bytes 65568 | tf_op jit(solution)/shard_map/ppermute | solution.py:380
  32.6 0.1 block_priors.1
  32.8 0.1 collective-permute-start.12
  32.9 0.9 %attend_own.1.refs_0_ = f32[128,640]{1,0:T(8,128)S(1)} custom-call(bf16[128,512]{1,0:T(8,128)(2,1)S(1)} %pass_on.2.refs_1_.refs_0_, bf16[128,512]{1,0:T(8,128)(2,1)S(1)} %pass_on.3.refs_1_, bf16[128,512]{1,0:T(8,128)(2,1)S(1)} %collective-permute-done.14.refs_2_, f32[128,512]{1,0:T(8,128)S(1)} %get-tuple-element.47.refs_3_, ...), custom_call_target="tpu_custom_call" | custom-call | flops 1000 | bytes 1000 | tf_op jit(solution)/shard_map/attend_own/pallas_call | solution.py:34
  33.8 0.4 %collective-permute-done.12.refs_5_ = bf16[128,512]{1,0:T(8,128)(2,1)S(1)} collective-permute-done((bf16[128,512]{1,0:T(8,128)(2,1)S(1)}, bf16[128,512]{1,0:T(8,128)(2,1)S(1)}, u32[]{:S(2)}, u32[]{:S(2)}) %collective-permute-start.12) | collective-permute-done | bytes 131104 | tf_op jit(solution)/shard_map/ppermute | solution.py:380
  34.2 1.0 %retain_finish.1 = bf16[128,512]{1,0:T(8,128)(2,1)} custom-call(bf16[128,512]{1,0:T(8,128)(2,1)S(1)} %get-tuple-element.26.refs_0_, bf16[128,512]{1,0:T(8,128)(2,1)S(1)} %get-tuple-element.27.refs_1_, f32[128,512]{1,0:T(8,128)S(1)} %get-tuple-element.34.refs_2_, f32[128,2]{1,0:T(8,128)S(1)} %get-tuple-element.35.refs_3_, ...), custom_call_target="tpu_custom_call" | custom-call | flops 1000 | bytes 1000 | tf_op jit(solution)/shard_map/retain_finish/pallas_call | solution.py:34
  35.2 1.8 %collective-permute-done.15.refs_1_ = bf16[128,640]{1,0:T(8,128)(2,1)S(1)} collective-permute-done((bf16[128,640]{1,0:T(8,128)(2,1)S(1)}, bf16[128,640]{1,0:T(8,128)(2,1)S(1)}, u32[]{:S(2)}, u32[]{:S(2)}) %collective-permute-start.15) | collective-permute-done | bytes 163872 | tf_op jit(solution)/shard_map/ppermute | solution.py:380
  37.0 1.1 %finish.1 = bf16[128,512]{1,0:T(8,128)(2,1)} custom-call(f32[128,640]{1,0:T(8,128)S(1)} %attend_own.1.refs_0_, bf16[128,640]{1,0:T(8,128)(2,1)S(1)} %collective-permute-done.15.refs_1_), custom_call_target="tpu_custom_call" | custom-call | flops 1000 | bytes 1000 | tf_op jit(solution)/shard_map/finish/pallas_call | solution.py:34
  (4 shorter events, 0.0 us)
Async XLA Ops:
  2.4 3.1 %collective-permute-start = (bf16[144,512]{1,0:T(8,128)(2,1)S(1)}, bf16[144,512]{1,0:T(8,128)(2,1)S(1)}, u32[]{:S(2)}, u32[]{:S(2)}) collective-permute-start(bf16[144,512]{1,0:T(8,128)(2,1)S(1)} %get-tuple-element.32), channel_id=1, source_target_pairs={{0,2},{2,0},{4,6},{6,4},{8,10},{10,8},{12,14},{14,12},{16,18},{18,... | collective-permute-start | bytes 442376 | tf_op jit(solution)/shard_map/ppermute | solution.py:380
  2.9 5.3 %collective-permute-start.2 = (bf16[64,512]{1,0:T(8,128)(2,1)S(1)}, bf16[64,512]{1,0:T(8,128)(2,1)S(1)}, u32[]{:S(2)}, u32[]{:S(2)}) collective-permute-start(bf16[64,512]{1,0:T(8,128)(2,1)S(1)} %get-tuple-element.38), channel_id=1, source_target_pairs={{0,1},{1,0},{2,3},{3,2},{4,5},{5,4},{6,7},{7,6},{8,9},{9,8},{10,11... | collective-permute-start | bytes 196616 | tf_op jit(solution)/shard_map/ppermute | solution.py:383
  5.6 6.1 %collective-permute-start.1 = (bf16[80,512]{1,0:T(8,128)(2,1)S(1)}, bf16[80,512]{1,0:T(8,128)(2,1)S(1)}, u32[]{:S(2)}, u32[]{:S(2)}) collective-permute-start(bf16[80,512]{1,0:T(8,128)(2,1)S(1)} %get-tuple-element.33.refs_4_), channel_id=1, source_target_pairs={{0,4},{2,6},{4,0},{6,2},{8,12},{10,14},{12,8},{14,10},{16,20},{18,... | collective-permute-start | bytes 245768 | tf_op jit(solution)/shard_map/ppermute | solution.py:380
  8.2 9.1 %collective-permute-start.4 = (bf16[128,512]{1,0:T(8,128)(2,1)S(1)}, bf16[128,512]{1,0:T(8,128)(2,1)S(1)}, u32[]{:S(2)}, u32[]{:S(2)}) collective-permute-start(bf16[128,512]{1,0:T(8,128)(2,1)S(1)} %join_rows.1.refs_2_), channel_id=1, source_target_pairs={{0,16},{2,18},{4,20},{6,22},{8,24},{10,26},{12,28},{14,30},{16,0},... | collective-permute-start | bytes 393224 | tf_op jit(solution)/shard_map/ppermute | solution.py:380
  11.8 7.4 %collective-permute-start.5 = (bf16[128,512]{1,0:T(8,128)(2,1)S(1)}, bf16[128,512]{1,0:T(8,128)(2,1)S(1)}, u32[]{:S(2)}, u32[]{:S(2)}) collective-permute-start(bf16[128,512]{1,0:T(8,128)(2,1)S(1)} %get-tuple-element.40), channel_id=1, source_target_pairs={{0,8},{2,10},{4,12},{6,14},{8,0},{10,2},{12,4},{14,6},{16,24},{18,... | collective-permute-start | bytes 393224 | tf_op jit(solution)/shard_map/ppermute | solution.py:380
  13.4 6.6 %collective-permute-start.3 = (bf16[80,512]{1,0:T(8,128)(2,1)S(1)}, bf16[80,512]{1,0:T(8,128)(2,1)S(1)}, u32[]{:S(2)}, u32[]{:S(2)}) collective-permute-start(bf16[80,512]{1,0:T(8,128)(2,1)S(1)} %get-tuple-element.39.refs_0_), channel_id=1, source_target_pairs={{0,8},{2,10},{4,12},{6,14},{8,0},{10,2},{12,4},{14,6},{16,24},{18,... | collective-permute-start | bytes 245768 | tf_op jit(solution)/shard_map/ppermute | solution.py:380
  13.9 7.5 %collective-permute-start.8 = (bf16[128,512]{1,0:T(8,128)(2,1)S(1)}, bf16[128,512]{1,0:T(8,128)(2,1)S(1)}, u32[]{:S(2)}, u32[]{:S(2)}) collective-permute-start(bf16[128,512]{1,0:T(8,128)(2,1)S(1)} %join_rows.1.refs_2_), channel_id=1, source_target_pairs={{0,2},{2,0},{4,6},{6,4},{8,10},{10,8},{12,14},{14,12},{16,18},{18,... | collective-permute-start | bytes 393224 | tf_op jit(solution)/shard_map/ppermute | solution.py:380
  17.4 6.6 %collective-permute-start.7 = (bf16[128,512]{1,0:T(8,128)(2,1)S(1)}, bf16[128,512]{1,0:T(8,128)(2,1)S(1)}, u32[]{:S(2)}, u32[]{:S(2)}) collective-permute-start(bf16[128,512]{1,0:T(8,128)(2,1)S(1)} %pass_on.2.refs_1_.refs_0_), channel_id=1, source_target_pairs={{0,4},{2,6},{4,0},{6,2},{8,12},{10,14},{12,8},{14,10},{16,20},{18,... | collective-permute-start | bytes 393224 | tf_op jit(solution)/shard_map/ppermute | solution.py:380
  18.9 5.1 %collective-permute-start.9 = (bf16[128,512]{1,0:T(8,128)(2,1)S(1)}, bf16[128,512]{1,0:T(8,128)(2,1)S(1)}, u32[]{:S(2)}, u32[]{:S(2)}) collective-permute-start(bf16[128,512]{1,0:T(8,128)(2,1)S(1)} %collective-permute-done.4.refs_2_.refs_1_.refs_4_.refs_0_), channel_id=1, source_target_pairs={{0,2},{2,0},{4,6},{6,4},{8,10},{10,8},{12,14},{14,12},{16,18},{18,... | collective-permute-start | bytes 393224 | tf_op jit(solution)/shard_map/ppermute | solution.py:380
  19.2 4.8 %collective-permute-start.10 = (bf16[128,512]{1,0:T(8,128)(2,1)S(1)}, bf16[128,512]{1,0:T(8,128)(2,1)S(1)}, u32[]{:S(2)}, u32[]{:S(2)}) collective-permute-start(bf16[128,512]{1,0:T(8,128)(2,1)S(1)} %collective-permute-done.5.refs_3_.refs_6_), channel_id=1, source_target_pairs={{0,2},{2,0},{4,6},{6,4},{8,10},{10,8},{12,14},{14,12},{16,18},{18,... | collective-permute-start | bytes 393224 | tf_op jit(solution)/shard_map/ppermute | solution.py:380
  20.1 6.8 %collective-permute-start.6 = (bf16[80,512]{1,0:T(8,128)(2,1)S(1)}, bf16[80,512]{1,0:T(8,128)(2,1)S(1)}, u32[]{:S(2)}, u32[]{:S(2)}) collective-permute-start(bf16[80,512]{1,0:T(8,128)(2,1)S(1)} %grow.1.refs_1_), channel_id=1, source_target_pairs={{0,16},{2,18},{4,20},{6,22},{8,24},{10,26},{12,28},{14,30},{16,0},... | collective-permute-start | bytes 245768 | tf_op jit(solution)/shard_map/ppermute | solution.py:380
  21.4 6.7 %collective-permute-start.13 = (bf16[128,512]{1,0:T(8,128)(2,1)S(1)}, bf16[128,512]{1,0:T(8,128)(2,1)S(1)}, u32[]{:S(2)}, u32[]{:S(2)}) collective-permute-start(bf16[128,512]{1,0:T(8,128)(2,1)S(1)} %shard_map.95), channel_id=1, source_target_pairs={{0,8},{2,10},{4,12},{6,14},{8,0},{10,2},{12,4},{14,6},{16,24},{18,... | collective-permute-start | bytes 393224 | tf_op jit(solution)/shard_map/ppermute | solution.py:380
  28.1 1.5 %collective-permute-start.14 = (bf16[128,512]{1,0:T(8,128)(2,1)S(1)}, bf16[128,512]{1,0:T(8,128)(2,1)S(1)}, u32[]{:S(2)}, u32[]{:S(2)}) collective-permute-start(bf16[128,512]{1,0:T(8,128)(2,1)S(1)} %pass_on.3.refs_1_), channel_id=1, source_target_pairs={{0,2},{2,0},{4,6},{6,4},{8,10},{10,8},{12,14},{14,12},{16,18},{18,... | collective-permute-start | bytes 393224 | tf_op jit(solution)/shard_map/ppermute | solution.py:380
  28.1 4.5 %collective-permute-start.11 = (bf16[64,512]{1,0:T(8,128)(2,1)S(1)}, bf16[64,512]{1,0:T(8,128)(2,1)S(1)}, u32[]{:S(2)}, u32[]{:S(2)}) collective-permute-start(bf16[64,512]{1,0:T(8,128)(2,1)S(1)} %get-tuple-element.44.refs_1_), channel_id=1, source_target_pairs={{0,4},{2,6},{4,0},{6,2},{8,12},{10,14},{12,8},{14,10},{16,20},{18,... | collective-permute-start | bytes 196616 | tf_op jit(solution)/shard_map/ppermute | solution.py:380
  30.6 6.4 %collective-permute-start.15 = (bf16[128,640]{1,0:T(8,128)(2,1)S(1)}, bf16[128,640]{1,0:T(8,128)(2,1)S(1)}, u32[]{:S(2)}, u32[]{:S(2)}) collective-permute-start(bf16[128,640]{1,0:T(8,128)(2,1)S(1)} %attend_far.1), channel_id=1, source_target_pairs={{0,4},{2,6},{4,0},{6,2},{8,12},{10,14},{12,8},{14,10},{16,20},{18,... | collective-permute-start | bytes 491528 | tf_op jit(solution)/shard_map/ppermute | solution.py:380
  32.8 1.4 %collective-permute-start.12 = (bf16[128,512]{1,0:T(8,128)(2,1)S(1)}, bf16[128,512]{1,0:T(8,128)(2,1)S(1)}, u32[]{:S(2)}, u32[]{:S(2)}) collective-permute-start(bf16[128,512]{1,0:T(8,128)(2,1)S(1)} %get-tuple-element.46), channel_id=1, source_target_pairs={{0,2},{2,0},{4,6},{6,4},{8,10},{10,8},{12,14},{14,12},{16,18},{18,... | collective-permute-start | bytes 393224 | tf_op jit(solution)/shard_map/ppermute | solution.py:380

commit v10 on v9

--- a/solution.py
+++ b/solution.py
@@ -376,8 +376,9 @@
     length, width = cache_k.shape[0], cache_k.shape[1] // n
     half, quarter = HD // 2, HD // 4
 
-    def swap(value, bit):
-        return lax.ppermute(value, "ctx", [(b, b ^ bit) for b in range(count)])
+    def swap(value, bit, wanted=None):
+        pairs = [(b ^ bit, b) for b in range(count) if wanted is None or wanted(b // 4)]
+        return lax.ppermute(value, "ctx", pairs)
 
     def to_head(value, e):
         return lax.ppermute(value, "head", [(y, (y + e) % n) for y in range(n)])
@@ -438,7 +439,8 @@
     q_other = swap(q_cross, 2)
     planes, bit = [], 1
     while bit < far:
-        planes.append(swap(window, 4 * bit))
+        wanted = (lambda z, bit=bit: z & bit) if bit > 1 else None
+        planes.append(swap(window, 4 * bit, wanted))
         if 2 * bit < far:
             window = call(
                 functools.partial(grow, bit),
@@ -486,7 +488,8 @@
     for s in near:
         if s > 1:
             ready = call(copy_after, [shape(blocks[s].shape)], (blocks[s],), after=(window,))
-            blocks[s ^ 1] = pass_on(swap(ready, 4), prior_send)
+            last = swap(ready, 4, lambda z, s=s: z ^ s ^ 1 < z)
+            blocks[s ^ 1] = pass_on(last, prior_send)
     hops = [s for s in blocks if s not in near]
     packed = (rows, wide + LANES)
     part_send = look(hops, True, [shape(packed)], ((q_other, 1),), so_far[:2], "attend_far")

time: 38.2 us -> 38.1 us (level)
  the two profiles are of different devices: /device:TPU:0 before, /device:TPU:28 now
where the time goes in v10:
time: 38.1 us; the launch traced here: 37.9 us
  waiting for transfers between devices  17.1 us (45%)
  starting transfers between devices  11.6 us (30%)
  Pallas kernels  8.37 us (22%)
  between operations  0.79 us (2%)
    ppermute x15, waiting for transfers between devices, swap(): return lax.ppermute(value, 'ctx', pairs)  15.6 us
    ppermute x15, starting transfers between devices, swap(): return lax.ppermute(value, 'ctx', pairs)  11.1 us
    pallas_call x16, Pallas kernels, call(): pl.pallas_call(kernel, out_shape=outs[0] if single else tuple(outs), in_s...  8.37 us
    ppermute x1, waiting for transfers between devices, to_head(): return lax.ppermute(value, 'head', [(y, (y + e) % n) for y in range(n)])  1.47 us
  transfers between devices with their start and end apart: 16, of which 11 were waited for; matrix products, arithmetic and copies ran while one was open for 0% of the time, Pallas kernels for 15%

profile of v10, /device:TPU:28, one launch (start us, length us, event | category | flops | bytes accessed | tf_op | source)
XLA Modules:
  0.0 37.9 jit_solution(7826701891931721478)
XLA Ops:
  0.6 1.8 %load_all.1 = (bf16[64,512]{1,0:T(8,128)(2,1)S(1)}, bf16[64,512]{1,0:T(8,128)(2,1)S(1)}, bf16[128,512]{1,0:T(8,128)(2,1)S(1)}, bf16[128,512]{1,0:T(8,128)(2,1)S(...) custom-call(bf16[64,512]{1,0:T(8,128)(2,1)} %refs_0_.1, ...), custom_call_target="tpu_custom_call" | custom-call | flops 1000 | bytes 1000 | tf_op jit(solution)/shard_map/load_all/pallas_call | solution.py:34
  2.4 0.1 collective-permute-start
  2.5 0.6 %collective-permute-start.2 = (bf16[64,512]{1,0:T(8,128)(2,1)S(1)}, bf16[64,512]{1,0:T(8,128)(2,1)S(1)}, u32[]{:S(2)}, u32[]{:S(2)}) collective-permute-start(bf16[64,512]{1,0:T(8,128)(2,1)S(1)} %get-tuple-element.38), channel_id=1, source_target_pairs={{0,1},{1,0},{2,3},{3,2},{4,5},{5,4},{6,7},{7,6},{8,9},{9,8},{10,11... | collective-permute-start | bytes 196616 | tf_op jit(solution)/shard_map/ppermute | solution.py:384
  3.0 0.8 %collective-permute-done.refs_1_ = bf16[144,512]{1,0:T(8,128)(2,1)S(1)} collective-permute-done((bf16[144,512]{1,0:T(8,128)(2,1)S(1)}, bf16[144,512]{1,0:T(8,128)(2,1)S(1)}, u32[]{:S(2)}, u32[]{:S(2)}) %collective-permute-start) | collective-permute-done | bytes 147488 | tf_op jit(solution)/shard_map/ppermute | solution.py:381
  3.8 0.1 chip_total.1
  4.0 1.6 %collective-permute-start.1 = (bf16[80,512]{1,0:T(8,128)(2,1)S(1)}, bf16[80,512]{1,0:T(8,128)(2,1)S(1)}, u32[]{:S(2)}, u32[]{:S(2)}) collective-permute-start(bf16[80,512]{1,0:T(8,128)(2,1)S(1)} %get-tuple-element.33.refs_4_), channel_id=1, source_target_pairs={{4,0},{6,2},{0,4},{2,6},{12,8},{14,10},{8,12},{10,14},{20,16},{22,... | collective-permute-start | bytes 245768 | tf_op jit(solution)/shard_map/ppermute | solution.py:381
  5.5 1.5 %collective-permute-done.2.refs_1_ = bf16[64,512]{1,0:T(8,128)(2,1)S(1)} collective-permute-done((bf16[64,512]{1,0:T(8,128)(2,1)S(1)}, bf16[64,512]{1,0:T(8,128)(2,1)S(1)}, u32[]{:S(2)}, u32[]{:S(2)}) %collective-permute-start.2) | collective-permute-done | bytes 65568 | tf_op jit(solution)/shard_map/ppermute | solution.py:384
  7.0 0.4 %collective-permute-start.4 = (bf16[128,512]{1,0:T(8,128)(2,1)S(1)}, bf16[128,512]{1,0:T(8,128)(2,1)S(1)}, u32[]{:S(2)}, u32[]{:S(2)}) collective-permute-start(bf16[128,512]{1,0:T(8,128)(2,1)S(1)} %join_rows.1.refs_2_), channel_id=1, source_target_pairs={{16,0},{18,2},{20,4},{22,6},{24,8},{26,10},{28,12},{30,14},{0,16},... | collective-permute-start | bytes 393224 | tf_op jit(solution)/shard_map/ppermute | solution.py:381
  7.4 0.6 %retain_inside.1 = (f32[128,512]{1,0:T(8,128)S(1)}, f32[128,2]{1,0:T(8,128)S(1)}) custom-call(bf16[128,512]{1,0:T(8,128)(2,1)S(1)} %get-tuple-element.26.refs_0_, bf16[128,512]{1,0:T(8,128)(2,1)S(1)} %get-tuple-element.28.refs_1_, bf16[128,512]{1,0:T(8,128)(2,1)S(1)} %get-tuple-element.29.refs_2_, f32[2,128]{1,0:T(2,128)S(1)} %get-tuple-element.30.refs_3_, ...), custom_call_target="tpu_custom_call" | custom-call | flops 1000 | bytes 1000 | tf_op jit(solution)/shard_map/retain_inside/pallas_call | solution.py:34
  8.0 0.5 %collective-permute-done.1.refs_1_ = bf16[80,512]{1,0:T(8,128)(2,1)S(1)} collective-permute-done((bf16[80,512]{1,0:T(8,128)(2,1)S(1)}, bf16[80,512]{1,0:T(8,128)(2,1)S(1)}, u32[]{:S(2)}, u32[]{:S(2)}) %collective-permute-start.1) | collective-permute-done | bytes 81952 | tf_op jit(solution)/shard_map/ppermute | solution.py:381
  8.5 0.1 plane_total.1
  8.6 0.5 %collective-permute-start.5 = (bf16[128,512]{1,0:T(8,128)(2,1)S(1)}, bf16[128,512]{1,0:T(8,128)(2,1)S(1)}, u32[]{:S(2)}, u32[]{:S(2)}) collective-permute-start(bf16[128,512]{1,0:T(8,128)(2,1)S(1)} %get-tuple-element.40), channel_id=1, source_target_pairs={{8,0},{10,2},{12,4},{14,6},{0,8},{2,10},{4,12},{6,14},{24,16},{26,... | collective-permute-start | bytes 393224 | tf_op jit(solution)/shard_map/ppermute | solution.py:381
  9.1 1.6 %collective-permute-start.3 = (bf16[80,512]{1,0:T(8,128)(2,1)S(1)}, bf16[80,512]{1,0:T(8,128)(2,1)S(1)}, u32[]{:S(2)}, u32[]{:S(2)}) collective-permute-start(bf16[80,512]{1,0:T(8,128)(2,1)S(1)} %get-tuple-element.39.refs_0_), channel_id=1, source_target_pairs={{8,0},{10,2},{12,4},{14,6},{0,8},{2,10},{4,12},{6,14},{24,16},{26,... | collective-permute-start | bytes 245768 | tf_op jit(solution)/shard_map/ppermute | solution.py:381
  10.7 0.0 collective-permute-start.8
  10.7 5.2 %collective-permute-done.4.refs_2_.refs_1_.refs_4_.refs_0_ = bf16[128,512]{1,0:T(8,128)(2,1)S(1)} collective-permute-done((bf16[128,512]{1,0:T(8,128)(2,1)S(1)}, bf16[128,512]{1,0:T(8,128)(2,1)S(1)}, u32[]{:S(2)}, u32[]{:S(2)}) %collective-permute-start.4) | collective-permute-done | bytes 131104 | tf_op jit(solution)/shard_map/ppermute | solution.py:381
  15.8 1.5 %collective-permute-start.7 = (bf16[128,512]{1,0:T(8,128)(2,1)S(1)}, bf16[128,512]{1,0:T(8,128)(2,1)S(1)}, u32[]{:S(2)}, u32[]{:S(2)}) collective-permute-start(bf16[128,512]{1,0:T(8,128)(2,1)S(1)} %pass_on.2.refs_1_.refs_0_), channel_id=1, source_target_pairs={{4,0},{6,2},{0,4},{2,6},{12,8},{14,10},{8,12},{10,14},{20,16},{22,... | collective-permute-start | bytes 393224 | tf_op jit(solution)/shard_map/ppermute | solution.py:381
  17.3 0.0 collective-permute-start.9
  17.3 0.0 collective-permute-done.5.refs_3_.refs_6_
  17.3 0.5 %collective-permute-start.10 = (bf16[128,512]{1,0:T(8,128)(2,1)S(1)}, bf16[128,512]{1,0:T(8,128)(2,1)S(1)}, u32[]{:S(2)}, u32[]{:S(2)}) collective-permute-start(bf16[128,512]{1,0:T(8,128)(2,1)S(1)} %collective-permute-done.5.refs_3_.refs_6_), channel_id=1, source_target_pairs={{2,0},{0,2},{6,4},{4,6},{10,8},{8,10},{14,12},{12,14},{18,16},{16,... | collective-permute-start | bytes 393224 | tf_op jit(solution)/shard_map/ppermute | solution.py:381
  17.8 0.1 collective-permute-done.3.refs_1_.refs_2_
  17.9 0.1 grow.1.refs_1_
  18.0 1.3 %collective-permute-start.6 = (bf16[80,512]{1,0:T(8,128)(2,1)S(1)}, bf16[80,512]{1,0:T(8,128)(2,1)S(1)}, u32[]{:S(2)}, u32[]{:S(2)}) collective-permute-start(bf16[80,512]{1,0:T(8,128)(2,1)S(1)} %grow.1.refs_1_), channel_id=1, source_target_pairs={{0,16},{2,18},{4,20},{6,22},{8,24},{10,26},{12,28},{14,30},{1,17},... | collective-permute-start | bytes 245768 | tf_op jit(solution)/shard_map/ppermute | solution.py:381
  19.3 0.0 collective-permute-done.8.refs_3_
  19.3 1.9 %collective-permute-start.13 = (bf16[128,512]{1,0:T(8,128)(2,1)S(1)}, bf16[128,512]{1,0:T(8,128)(2,1)S(1)}, u32[]{:S(2)}, u32[]{:S(2)}) collective-permute-start(bf16[128,512]{1,0:T(8,128)(2,1)S(1)} %shard_map.95), channel_id=1, source_target_pairs={{24,16},{26,18},{28,20},{30,22},{16,24},{18,26},{20,28},{22,30},{2... | collective-permute-start | bytes 393224 | tf_op jit(solution)/shard_map/ppermute | solution.py:381
  21.2 0.0 collective-permute-done.7.refs_0_
  21.2 0.0 collective-permute-done.9.refs_5_
  21.2 0.0 collective-permute-done.10.refs_7_
  21.3 1.7 %attend_near.1 = (f32[128,512]{1,0:T(8,128)S(1)}, f32[128,128]{1,0:T(8,128)S(1)}, f32[128,512]{1,0:T(8,128)S(1)}, f32[128,128]{1,0:T(8,128)S(1)}) custom-call(bf16[128,512]{1,0:T(8,128)(2,1)S(1)} %collective-permute-done.7.refs_0_, bf16[128,512]{1,0:T(8,128)(2,1)S(1)} %pass_on.2.refs_1_.refs_0_, bf16[128,512]{1,0:T(8,128)(2,1)S(1)} %join_rows.1.refs_2_, ...), custom_call_target="tpu_custom_call" | custom-call | flops 1000 | bytes 1000 | tf_op jit(solution)/shard_map/attend_near/pallas_call | solution.py:34
  22.9 3.1 %collective-permute-done.6.refs_3_ = bf16[80,512]{1,0:T(8,128)(2,1)S(1)} collective-permute-done((bf16[80,512]{1,0:T(8,128)(2,1)S(1)}, bf16[80,512]{1,0:T(8,128)(2,1)S(1)}, u32[]{:S(2)}, u32[]{:S(2)}) %collective-permute-start.6) | collective-permute-done | bytes 81952 | tf_op jit(solution)/shard_map/ppermute | solution.py:381
  26.0 0.1 chip_priors.1
  26.1 2.1 %collective-permute-done.13.refs_0_ = bf16[128,512]{1,0:T(8,128)(2,1)S(1)} collective-permute-done((bf16[128,512]{1,0:T(8,128)(2,1)S(1)}, bf16[128,512]{1,0:T(8,128)(2,1)S(1)}, u32[]{:S(2)}, u32[]{:S(2)}) %collective-permute-start.13) | collective-permute-done | bytes 131104 | tf_op jit(solution)/shard_map/ppermute | solution.py:381
  28.3 0.0 collective-permute-start.14
  28.3 0.8 %collective-permute-start.11 = (bf16[64,512]{1,0:T(8,128)(2,1)S(1)}, bf16[64,512]{1,0:T(8,128)(2,1)S(1)}, u32[]{:S(2)}, u32[]{:S(2)}) collective-permute-start(bf16[64,512]{1,0:T(8,128)(2,1)S(1)} %get-tuple-element.44.refs_1_), channel_id=1, source_target_pairs={{4,0},{6,2},{0,4},{2,6},{12,8},{14,10},{8,12},{10,14},{20,16},{22,... | collective-permute-start | bytes 196616 | tf_op jit(solution)/shard_map/ppermute | solution.py:381
  29.1 0.6 %collective-permute-done.14.refs_2_ = bf16[128,512]{1,0:T(8,128)(2,1)S(1)} collective-permute-done((bf16[128,512]{1,0:T(8,128)(2,1)S(1)}, bf16[128,512]{1,0:T(8,128)(2,1)S(1)}, u32[]{:S(2)}, u32[]{:S(2)}) %collective-permute-start.14) | collective-permute-done | bytes 131104 | tf_op jit(solution)/shard_map/ppermute | solution.py:381
  29.6 0.9 %attend_far.1 = bf16[128,640]{1,0:T(8,128)(2,1)S(1)} custom-call(bf16[128,512]{1,0:T(8,128)(2,1)S(1)} %collective-permute-done.7.refs_0_, bf16[128,512]{1,0:T(8,128)(2,1)S(1)} %pass_on.3.refs_1_, bf16[128,512]{1,0:T(8,128)(2,1)S(1)} %collective-permute-done.14.refs_2_, f32[128,512]{1,0:T(8,128)S(1)} %get-tuple-element.49.refs_3_, ...), custom_call_target="tpu_custom_call" | custom-call | flops 1000 | bytes 1000 | tf_op jit(solution)/shard_map/attend_far/pallas_call | solution.py:34
  30.5 0.9 %collective-permute-start.15 = (bf16[128,640]{1,0:T(8,128)(2,1)S(1)}, bf16[128,640]{1,0:T(8,128)(2,1)S(1)}, u32[]{:S(2)}, u32[]{:S(2)}) collective-permute-start(bf16[128,640]{1,0:T(8,128)(2,1)S(1)} %attend_far.1), channel_id=1, source_target_pairs={{4,0},{6,2},{0,4},{2,6},{12,8},{14,10},{8,12},{10,14},{20,16},{22,... | collective-permute-start | bytes 491528 | tf_op jit(solution)/shard_map/ppermute | solution.py:381
  31.4 1.4 %collective-permute-done.11.refs_3_ = bf16[64,512]{1,0:T(8,128)(2,1)S(1)} collective-permute-done((bf16[64,512]{1,0:T(8,128)(2,1)S(1)}, bf16[64,512]{1,0:T(8,128)(2,1)S(1)}, u32[]{:S(2)}, u32[]{:S(2)}) %collective-permute-start.11) | collective-permute-done | bytes 65568 | tf_op jit(solution)/shard_map/ppermute | solution.py:381
  32.8 0.1 block_priors.1
  32.9 0.1 collective-permute-start.12
  33.0 0.9 %attend_own.1.refs_0_ = f32[128,640]{1,0:T(8,128)S(1)} custom-call(bf16[128,512]{1,0:T(8,128)(2,1)S(1)} %pass_on.2.refs_1_.refs_0_, bf16[128,512]{1,0:T(8,128)(2,1)S(1)} %pass_on.3.refs_1_, bf16[128,512]{1,0:T(8,128)(2,1)S(1)} %collective-permute-done.14.refs_2_, f32[128,512]{1,0:T(8,128)S(1)} %get-tuple-element.47.refs_3_, ...), custom_call_target="tpu_custom_call" | custom-call | flops 1000 | bytes 1000 | tf_op jit(solution)/shard_map/attend_own/pallas_call | solution.py:34
  33.9 0.4 %collective-permute-done.12.refs_5_ = bf16[128,512]{1,0:T(8,128)(2,1)S(1)} collective-permute-done((bf16[128,512]{1,0:T(8,128)(2,1)S(1)}, bf16[128,512]{1,0:T(8,128)(2,1)S(1)}, u32[]{:S(2)}, u32[]{:S(2)}) %collective-permute-start.12) | collective-permute-done | bytes 131104 | tf_op jit(solution)/shard_map/ppermute | solution.py:381
  34.3 1.0 %retain_finish.1 = bf16[128,512]{1,0:T(8,128)(2,1)} custom-call(bf16[128,512]{1,0:T(8,128)(2,1)S(1)} %get-tuple-element.26.refs_0_, bf16[128,512]{1,0:T(8,128)(2,1)S(1)} %get-tuple-element.27.refs_1_, f32[128,512]{1,0:T(8,128)S(1)} %get-tuple-element.34.refs_2_, f32[128,2]{1,0:T(8,128)S(1)} %get-tuple-element.35.refs_3_, ...), custom_call_target="tpu_custom_call" | custom-call | flops 1000 | bytes 1000 | tf_op jit(solution)/shard_map/retain_finish/pallas_call | solution.py:34
  35.3 1.5 %collective-permute-done.15.refs_1_ = bf16[128,640]{1,0:T(8,128)(2,1)S(1)} collective-permute-done((bf16[128,640]{1,0:T(8,128)(2,1)S(1)}, bf16[128,640]{1,0:T(8,128)(2,1)S(1)}, u32[]{:S(2)}, u32[]{:S(2)}) %collective-permute-start.15) | collective-permute-done | bytes 163872 | tf_op jit(solution)/shard_map/ppermute | solution.py:381
  36.8 1.1 %finish.1 = bf16[128,512]{1,0:T(8,128)(2,1)} custom-call(f32[128,640]{1,0:T(8,128)S(1)} %attend_own.1.refs_0_, bf16[128,640]{1,0:T(8,128)(2,1)S(1)} %collective-permute-done.15.refs_1_), custom_call_target="tpu_custom_call" | custom-call | flops 1000 | bytes 1000 | tf_op jit(solution)/shard_map/finish/pallas_call | solution.py:34
  (4 shorter events, 0.0 us)
Async XLA Ops:
  2.4 1.4 %collective-permute-start = (bf16[144,512]{1,0:T(8,128)(2,1)S(1)}, bf16[144,512]{1,0:T(8,128)(2,1)S(1)}, u32[]{:S(2)}, u32[]{:S(2)}) collective-permute-start(bf16[144,512]{1,0:T(8,128)(2,1)S(1)} %get-tuple-element.32), channel_id=1, source_target_pairs={{2,0},{0,2},{6,4},{4,6},{10,8},{8,10},{14,12},{12,14},{18,16},{16,... | collective-permute-start | bytes 442376 | tf_op jit(solution)/shard_map/ppermute | solution.py:381
  2.5 4.5 %collective-permute-start.2 = (bf16[64,512]{1,0:T(8,128)(2,1)S(1)}, bf16[64,512]{1,0:T(8,128)(2,1)S(1)}, u32[]{:S(2)}, u32[]{:S(2)}) collective-permute-start(bf16[64,512]{1,0:T(8,128)(2,1)S(1)} %get-tuple-element.38), channel_id=1, source_target_pairs={{0,1},{1,0},{2,3},{3,2},{4,5},{5,4},{6,7},{7,6},{8,9},{9,8},{10,11... | collective-permute-start | bytes 196616 | tf_op jit(solution)/shard_map/ppermute | solution.py:384
  4.0 4.6 %collective-permute-start.1 = (bf16[80,512]{1,0:T(8,128)(2,1)S(1)}, bf16[80,512]{1,0:T(8,128)(2,1)S(1)}, u32[]{:S(2)}, u32[]{:S(2)}) collective-permute-start(bf16[80,512]{1,0:T(8,128)(2,1)S(1)} %get-tuple-element.33.refs_4_), channel_id=1, source_target_pairs={{4,0},{6,2},{0,4},{2,6},{12,8},{14,10},{8,12},{10,14},{20,16},{22,... | collective-permute-start | bytes 245768 | tf_op jit(solution)/shard_map/ppermute | solution.py:381
  7.0 8.8 %collective-permute-start.4 = (bf16[128,512]{1,0:T(8,128)(2,1)S(1)}, bf16[128,512]{1,0:T(8,128)(2,1)S(1)}, u32[]{:S(2)}, u32[]{:S(2)}) collective-permute-start(bf16[128,512]{1,0:T(8,128)(2,1)S(1)} %join_rows.1.refs_2_), channel_id=1, source_target_pairs={{16,0},{18,2},{20,4},{22,6},{24,8},{26,10},{28,12},{30,14},{0,16},... | collective-permute-start | bytes 393224 | tf_op jit(solution)/shard_map/ppermute | solution.py:381
  8.6 8.8 %collective-permute-start.5 = (bf16[128,512]{1,0:T(8,128)(2,1)S(1)}, bf16[128,512]{1,0:T(8,128)(2,1)S(1)}, u32[]{:S(2)}, u32[]{:S(2)}) collective-permute-start(bf16[128,512]{1,0:T(8,128)(2,1)S(1)} %get-tuple-element.40), channel_id=1, source_target_pairs={{8,0},{10,2},{12,4},{14,6},{0,8},{2,10},{4,12},{6,14},{24,16},{26,... | collective-permute-start | bytes 393224 | tf_op jit(solution)/shard_map/ppermute | solution.py:381
  9.1 8.8 %collective-permute-start.3 = (bf16[80,512]{1,0:T(8,128)(2,1)S(1)}, bf16[80,512]{1,0:T(8,128)(2,1)S(1)}, u32[]{:S(2)}, u32[]{:S(2)}) collective-permute-start(bf16[80,512]{1,0:T(8,128)(2,1)S(1)} %get-tuple-element.39.refs_0_), channel_id=1, source_target_pairs={{8,0},{10,2},{12,4},{14,6},{0,8},{2,10},{4,12},{6,14},{24,16},{26,... | collective-permute-start | bytes 245768 | tf_op jit(solution)/shard_map/ppermute | solution.py:381
  10.7 8.6 %collective-permute-start.8 = (bf16[128,512]{1,0:T(8,128)(2,1)S(1)}, bf16[128,512]{1,0:T(8,128)(2,1)S(1)}, u32[]{:S(2)}, u32[]{:S(2)}) collective-permute-start(bf16[128,512]{1,0:T(8,128)(2,1)S(1)} %join_rows.1.refs_2_), channel_id=1, source_target_pairs={{2,0},{0,2},{6,4},{4,6},{10,8},{8,10},{14,12},{12,14},{18,16},{16,... | collective-permute-start | bytes 393224 | tf_op jit(solution)/shard_map/ppermute | solution.py:381
  15.8 5.4 %collective-permute-start.7 = (bf16[128,512]{1,0:T(8,128)(2,1)S(1)}, bf16[128,512]{1,0:T(8,128)(2,1)S(1)}, u32[]{:S(2)}, u32[]{:S(2)}) collective-permute-start(bf16[128,512]{1,0:T(8,128)(2,1)S(1)} %pass_on.2.refs_1_.refs_0_), channel_id=1, source_target_pairs={{4,0},{6,2},{0,4},{2,6},{12,8},{14,10},{8,12},{10,14},{20,16},{22,... | collective-permute-start | bytes 393224 | tf_op jit(solution)/shard_map/ppermute | solution.py:381
  17.3 3.9 %collective-permute-start.9 = (bf16[128,512]{1,0:T(8,128)(2,1)S(1)}, bf16[128,512]{1,0:T(8,128)(2,1)S(1)}, u32[]{:S(2)}, u32[]{:S(2)}) collective-permute-start(bf16[128,512]{1,0:T(8,128)(2,1)S(1)} %collective-permute-done.4.refs_2_.refs_1_.refs_4_.refs_0_), channel_id=1, source_target_pairs={{2,0},{0,2},{6,4},{4,6},{10,8},{8,10},{14,12},{12,14},{18,16},{16,... | collective-permute-start | bytes 393224 | tf_op jit(solution)/shard_map/ppermute | solution.py:381
  17.3 3.9 %collective-permute-start.10 = (bf16[128,512]{1,0:T(8,128)(2,1)S(1)}, bf16[128,512]{1,0:T(8,128)(2,1)S(1)}, u32[]{:S(2)}, u32[]{:S(2)}) collective-permute-start(bf16[128,512]{1,0:T(8,128)(2,1)S(1)} %collective-permute-done.5.refs_3_.refs_6_), channel_id=1, source_target_pairs={{2,0},{0,2},{6,4},{4,6},{10,8},{8,10},{14,12},{12,14},{18,16},{16,... | collective-permute-start | bytes 393224 | tf_op jit(solution)/shard_map/ppermute | solution.py:381
  18.0 8.1 %collective-permute-start.6 = (bf16[80,512]{1,0:T(8,128)(2,1)S(1)}, bf16[80,512]{1,0:T(8,128)(2,1)S(1)}, u32[]{:S(2)}, u32[]{:S(2)}) collective-permute-start(bf16[80,512]{1,0:T(8,128)(2,1)S(1)} %grow.1.refs_1_), channel_id=1, source_target_pairs={{0,16},{2,18},{4,20},{6,22},{8,24},{10,26},{12,28},{14,30},{1,17},... | collective-permute-start | bytes 245768 | tf_op jit(solution)/shard_map/ppermute | solution.py:381
  19.3 9.0 %collective-permute-start.13 = (bf16[128,512]{1,0:T(8,128)(2,1)S(1)}, bf16[128,512]{1,0:T(8,128)(2,1)S(1)}, u32[]{:S(2)}, u32[]{:S(2)}) collective-permute-start(bf16[128,512]{1,0:T(8,128)(2,1)S(1)} %shard_map.95), channel_id=1, source_target_pairs={{24,16},{26,18},{28,20},{30,22},{16,24},{18,26},{20,28},{22,30},{2... | collective-permute-start | bytes 393224 | tf_op jit(solution)/shard_map/ppermute | solution.py:381
  28.3 1.3 %collective-permute-start.14 = (bf16[128,512]{1,0:T(8,128)(2,1)S(1)}, bf16[128,512]{1,0:T(8,128)(2,1)S(1)}, u32[]{:S(2)}, u32[]{:S(2)}) collective-permute-start(bf16[128,512]{1,0:T(8,128)(2,1)S(1)} %pass_on.3.refs_1_), channel_id=1, source_target_pairs={{2,0},{0,2},{6,4},{4,6},{10,8},{8,10},{14,12},{12,14},{18,16},{16,... | collective-permute-start | bytes 393224 | tf_op jit(solution)/shard_map/ppermute | solution.py:381
  28.3 4.5 %collective-permute-start.11 = (bf16[64,512]{1,0:T(8,128)(2,1)S(1)}, bf16[64,512]{1,0:T(8,128)(2,1)S(1)}, u32[]{:S(2)}, u32[]{:S(2)}) collective-permute-start(bf16[64,512]{1,0:T(8,128)(2,1)S(1)} %get-tuple-element.44.refs_1_), channel_id=1, source_target_pairs={{4,0},{6,2},{0,4},{2,6},{12,8},{14,10},{8,12},{10,14},{20,16},{22,... | collective-permute-start | bytes 196616 | tf_op jit(solution)/shard_map/ppermute | solution.py:381
  30.5 6.3 %collective-permute-start.15 = (bf16[128,640]{1,0:T(8,128)(2,1)S(1)}, bf16[128,640]{1,0:T(8,128)(2,1)S(1)}, u32[]{:S(2)}, u32[]{:S(2)}) collective-permute-start(bf16[128,640]{1,0:T(8,128)(2,1)S(1)} %attend_far.1), channel_id=1, source_target_pairs={{4,0},{6,2},{0,4},{2,6},{12,8},{14,10},{8,12},{10,14},{20,16},{22,... | collective-permute-start | bytes 491528 | tf_op jit(solution)/shard_map/ppermute | solution.py:381
  32.9 1.4 %collective-permute-start.12 = (bf16[128,512]{1,0:T(8,128)(2,1)S(1)}, bf16[128,512]{1,0:T(8,128)(2,1)S(1)}, u32[]{:S(2)}, u32[]{:S(2)}) collective-permute-start(bf16[128,512]{1,0:T(8,128)(2,1)S(1)} %get-tuple-element.46), channel_id=1, source_target_pairs={{2,0},{0,2},{6,4},{4,6},{10,8},{8,10},{14,12},{12,14},{18,16},{16,... | collective-permute-start | bytes 393224 | tf_op jit(solution)/shard_map/ppermute | solution.py:381

commit v11 on v10

--- a/solution.py
+++ b/solution.py
@@ -377,7 +377,9 @@
     half, quarter = HD // 2, HD // 4
 
     def swap(value, bit, wanted=None):
-        pairs = [(b ^ bit, b) for b in range(count) if wanted is None or wanted(b // 4)]
+        pairs = [
+            (b ^ bit if wanted is None or wanted(b // 4) else b, b) for b in range(count)
+        ]
         return lax.ppermute(value, "ctx", pairs)
 
     def to_head(value, e):
@@ -439,8 +441,7 @@
     q_other = swap(q_cross, 2)
     planes, bit = [], 1
     while bit < far:
-        wanted = (lambda z, bit=bit: z & bit) if bit > 1 else None
-        planes.append(swap(window, 4 * bit, wanted))
+        planes.append(swap(window, 4 * bit))
         if 2 * bit < far:
             window = call(
                 functools.partial(grow, bit),
@@ -488,7 +489,7 @@
     for s in near:
         if s > 1:
             ready = call(copy_after, [shape(blocks[s].shape)], (blocks[s],), after=(window,))
-            last = swap(ready, 4, lambda z, s=s: z ^ s ^ 1 < z)
+            last = swap(ready, 4, lambda z, s=s: (z ^ s ^ 1) < z)
             blocks[s ^ 1] = pass_on(last, prior_send)
     hops = [s for s in blocks if s not in near]
     packed = (rows, wide + LANES)

time: 38.1 us -> 37 us (0.971)
  the two profiles are of different devices: /device:TPU:28 before, /device:TPU:0 now
where the time goes in v11:
time: 37 us; the launch traced here: 36.9 us
  starting transfers between devices  16.5 us (45%)
  waiting for transfers between devices  11.3 us (31%)
  Pallas kernels  8.37 us (23%)
  between operations  0.78 us (2%)
    ppermute x15, starting transfers between devices, swap(): return lax.ppermute(value, 'ctx', pairs)  13.9 us
    ppermute x15, waiting for transfers between devices, swap(): return lax.ppermute(value, 'ctx', pairs)  10.3 us
    pallas_call x16, Pallas kernels, call(): pl.pallas_call(kernel, out_shape=outs[0] if single else tuple(outs), in_s...  8.37 us
    ppermute x1, starting transfers between devices, to_head(): return lax.ppermute(value, 'head', [(y, (y + e) % n) for y in range(n)])  2.6 us
    ppermute x1, waiting for transfers between devices, to_head(): return lax.ppermute(value, 'head', [(y, (y + e) % n) for y in range(n)])  1 us
  transfers between devices with their start and end apart: 16, of which 9 were waited for; matrix products, arithmetic and copies ran while one was open for 0% of the time, Pallas kernels for 15%

profile of v11, /device:TPU:0, one launch (start us, length us, event | category | flops | bytes accessed | tf_op | source)
XLA Modules:
  0.0 36.9 jit_solution(8807679378691616442)
XLA Ops:
  0.6 1.8 %load_all.1 = (bf16[64,512]{1,0:T(8,128)(2,1)S(1)}, bf16[64,512]{1,0:T(8,128)(2,1)S(1)}, bf16[128,512]{1,0:T(8,128)(2,1)S(1)}, bf16[128,512]{1,0:T(8,128)(2,1)S(...) custom-call(bf16[64,512]{1,0:T(8,128)(2,1)} %refs_0_.1, ...), custom_call_target="tpu_custom_call" | custom-call | flops 1000 | bytes 1000 | tf_op jit(solution)/shard_map/load_all/pallas_call | solution.py:34
  2.4 0.5 %collective-permute-start = (bf16[144,512]{1,0:T(8,128)(2,1)S(1)}, bf16[144,512]{1,0:T(8,128)(2,1)S(1)}, u32[]{:S(2)}, u32[]{:S(2)}) collective-permute-start(bf16[144,512]{1,0:T(8,128)(2,1)S(1)} %get-tuple-element.32), channel_id=1, source_target_pairs={{2,0},{0,2},{6,4},{4,6},{10,8},{8,10},{14,12},{12,14},{18,16},{16,... | collective-permute-start | bytes 442376 | tf_op jit(solution)/shard_map/ppermute | solution.py:383
  2.9 2.6 %collective-permute-start.2 = (bf16[64,512]{1,0:T(8,128)(2,1)S(1)}, bf16[64,512]{1,0:T(8,128)(2,1)S(1)}, u32[]{:S(2)}, u32[]{:S(2)}) collective-permute-start(bf16[64,512]{1,0:T(8,128)(2,1)S(1)} %get-tuple-element.38), channel_id=1, source_target_pairs={{0,1},{1,0},{2,3},{3,2},{4,5},{5,4},{6,7},{7,6},{8,9},{9,8},{10,11... | collective-permute-start | bytes 196616 | tf_op jit(solution)/shard_map/ppermute | solution.py:386
  5.5 0.0 collective-permute-done.refs_1_
  5.5 0.1 chip_total.1
  5.6 1.6 %collective-permute-start.1 = (bf16[80,512]{1,0:T(8,128)(2,1)S(1)}, bf16[80,512]{1,0:T(8,128)(2,1)S(1)}, u32[]{:S(2)}, u32[]{:S(2)}) collective-permute-start(bf16[80,512]{1,0:T(8,128)(2,1)S(1)} %get-tuple-element.33.refs_4_), channel_id=1, source_target_pairs={{4,0},{6,2},{0,4},{2,6},{12,8},{14,10},{8,12},{10,14},{20,16},{22,... | collective-permute-start | bytes 245768 | tf_op jit(solution)/shard_map/ppermute | solution.py:383
  7.2 1.0 %collective-permute-done.2.refs_1_ = bf16[64,512]{1,0:T(8,128)(2,1)S(1)} collective-permute-done((bf16[64,512]{1,0:T(8,128)(2,1)S(1)}, bf16[64,512]{1,0:T(8,128)(2,1)S(1)}, u32[]{:S(2)}, u32[]{:S(2)}) %collective-permute-start.2) | collective-permute-done | bytes 65568 | tf_op jit(solution)/shard_map/ppermute | solution.py:386
  8.2 2.9 %collective-permute-start.4 = (bf16[128,512]{1,0:T(8,128)(2,1)S(1)}, bf16[128,512]{1,0:T(8,128)(2,1)S(1)}, u32[]{:S(2)}, u32[]{:S(2)}) collective-permute-start(bf16[128,512]{1,0:T(8,128)(2,1)S(1)} %join_rows.1.refs_2_), channel_id=1, source_target_pairs={{16,0},{18,2},{20,4},{22,6},{24,8},{26,10},{28,12},{30,14},{0,16},... | collective-permute-start | bytes 393224 | tf_op jit(solution)/shard_map/ppermute | solution.py:383
  11.1 0.6 %retain_inside.1 = (f32[128,512]{1,0:T(8,128)S(1)}, f32[128,2]{1,0:T(8,128)S(1)}) custom-call(bf16[128,512]{1,0:T(8,128)(2,1)S(1)} %get-tuple-element.26.refs_0_, bf16[128,512]{1,0:T(8,128)(2,1)S(1)} %get-tuple-element.28.refs_1_, bf16[128,512]{1,0:T(8,128)(2,1)S(1)} %get-tuple-element.29.refs_2_, f32[2,128]{1,0:T(2,128)S(1)} %get-tuple-element.30.refs_3_, ...), custom_call_target="tpu_custom_call" | custom-call | flops 1000 | bytes 1000 | tf_op jit(solution)/shard_map/retain_inside/pallas_call | solution.py:34
  11.7 0.0 collective-permute-done.1.refs_1_
  11.7 0.1 plane_total.1
  11.8 1.6 %collective-permute-start.5 = (bf16[128,512]{1,0:T(8,128)(2,1)S(1)}, bf16[128,512]{1,0:T(8,128)(2,1)S(1)}, u32[]{:S(2)}, u32[]{:S(2)}) collective-permute-start(bf16[128,512]{1,0:T(8,128)(2,1)S(1)} %get-tuple-element.40), channel_id=1, source_target_pairs={{8,0},{10,2},{12,4},{14,6},{0,8},{2,10},{4,12},{6,14},{24,16},{26,... | collective-permute-start | bytes 393224 | tf_op jit(solution)/shard_map/ppermute | solution.py:383
  13.4 0.4 %collective-permute-start.3 = (bf16[80,512]{1,0:T(8,128)(2,1)S(1)}, bf16[80,512]{1,0:T(8,128)(2,1)S(1)}, u32[]{:S(2)}, u32[]{:S(2)}) collective-permute-start(bf16[80,512]{1,0:T(8,128)(2,1)S(1)} %get-tuple-element.39.refs_0_), channel_id=1, source_target_pairs={{8,0},{10,2},{12,4},{14,6},{0,8},{2,10},{4,12},{6,14},{24,16},{26,... | collective-permute-start | bytes 245768 | tf_op jit(solution)/shard_map/ppermute | solution.py:383
  13.9 0.0 collective-permute-start.8
  13.9 3.5 %collective-permute-done.4.refs_2_.refs_1_.refs_4_.refs_0_ = bf16[128,512]{1,0:T(8,128)(2,1)S(1)} collective-permute-done((bf16[128,512]{1,0:T(8,128)(2,1)S(1)}, bf16[128,512]{1,0:T(8,128)(2,1)S(1)}, u32[]{:S(2)}, u32[]{:S(2)}) %collective-permute-start.4) | collective-permute-done | bytes 131104 | tf_op jit(solution)/shard_map/ppermute | solution.py:383
  17.4 1.5 %collective-permute-start.7 = (bf16[128,512]{1,0:T(8,128)(2,1)S(1)}, bf16[128,512]{1,0:T(8,128)(2,1)S(1)}, u32[]{:S(2)}, u32[]{:S(2)}) collective-permute-start(bf16[128,512]{1,0:T(8,128)(2,1)S(1)} %pass_on.2.refs_1_.refs_0_), channel_id=1, source_target_pairs={{4,0},{6,2},{0,4},{2,6},{12,8},{14,10},{8,12},{10,14},{20,16},{22,... | collective-permute-start | bytes 393224 | tf_op jit(solution)/shard_map/ppermute | solution.py:383
  18.9 0.0 collective-permute-start.9
  18.9 0.3 collective-permute-done.5.refs_3_.refs_6_
  19.2 0.2 collective-permute-start.10
  19.4 0.6 %collective-permute-done.3.refs_1_.refs_2_ = bf16[80,512]{1,0:T(8,128)(2,1)S(1)} collective-permute-done((bf16[80,512]{1,0:T(8,128)(2,1)S(1)}, bf16[80,512]{1,0:T(8,128)(2,1)S(1)}, u32[]{:S(2)}, u32[]{:S(2)}) %collective-permute-start.3) | collective-permute-done | bytes 81952 | tf_op jit(solution)/shard_map/ppermute | solution.py:383
  20.0 0.1 grow.1.refs_1_
  20.1 1.3 %collective-permute-start.6 = (bf16[80,512]{1,0:T(8,128)(2,1)S(1)}, bf16[80,512]{1,0:T(8,128)(2,1)S(1)}, u32[]{:S(2)}, u32[]{:S(2)}) collective-permute-start(bf16[80,512]{1,0:T(8,128)(2,1)S(1)} %grow.1.refs_1_), channel_id=1, source_target_pairs={{16,0},{18,2},{20,4},{22,6},{24,8},{26,10},{28,12},{30,14},{0,16},... | collective-permute-start | bytes 245768 | tf_op jit(solution)/shard_map/ppermute | solution.py:383
  21.4 0.0 collective-permute-done.8.refs_3_
  21.4 0.7 %collective-permute-start.13 = (bf16[128,512]{1,0:T(8,128)(2,1)S(1)}, bf16[128,512]{1,0:T(8,128)(2,1)S(1)}, u32[]{:S(2)}, u32[]{:S(2)}) collective-permute-start(bf16[128,512]{1,0:T(8,128)(2,1)S(1)} %shard_map.95), channel_id=1, source_target_pairs={{0,0},{2,2},{4,4},{6,6},{8,8},{10,10},{12,12},{14,14},{24,16},{26,... | collective-permute-start | bytes 393224 | tf_op jit(solution)/shard_map/ppermute | solution.py:383
  22.1 0.2 collective-permute-done.7.refs_0_
  22.3 0.0 collective-permute-done.9.refs_5_
  22.3 0.0 collective-permute-done.10.refs_7_
  22.3 1.6 %attend_near.1 = (f32[128,512]{1,0:T(8,128)S(1)}, f32[128,128]{1,0:T(8,128)S(1)}, f32[128,512]{1,0:T(8,128)S(1)}, f32[128,128]{1,0:T(8,128)S(1)}) custom-call(bf16[128,512]{1,0:T(8,128)(2,1)S(1)} %collective-permute-done.7.refs_0_, bf16[128,512]{1,0:T(8,128)(2,1)S(1)} %pass_on.2.refs_1_.refs_0_, bf16[128,512]{1,0:T(8,128)(2,1)S(1)} %join_rows.1.refs_2_, ...), custom_call_target="tpu_custom_call" | custom-call | flops 1000 | bytes 1000 | tf_op jit(solution)/shard_map/attend_near/pallas_call | solution.py:34
  24.0 2.8 %collective-permute-done.6.refs_3_ = bf16[80,512]{1,0:T(8,128)(2,1)S(1)} collective-permute-done((bf16[80,512]{1,0:T(8,128)(2,1)S(1)}, bf16[80,512]{1,0:T(8,128)(2,1)S(1)}, u32[]{:S(2)}, u32[]{:S(2)}) %collective-permute-start.6) | collective-permute-done | bytes 81952 | tf_op jit(solution)/shard_map/ppermute | solution.py:383
  26.8 0.1 chip_priors.1
  26.9 0.0 collective-permute-done.13.refs_0_
  26.9 0.1 collective-permute-start.14
  27.0 1.6 %collective-permute-start.11 = (bf16[64,512]{1,0:T(8,128)(2,1)S(1)}, bf16[64,512]{1,0:T(8,128)(2,1)S(1)}, u32[]{:S(2)}, u32[]{:S(2)}) collective-permute-start(bf16[64,512]{1,0:T(8,128)(2,1)S(1)} %get-tuple-element.44.refs_1_), channel_id=1, source_target_pairs={{4,0},{6,2},{0,4},{2,6},{12,8},{14,10},{8,12},{10,14},{20,16},{22,... | collective-permute-start | bytes 196616 | tf_op jit(solution)/shard_map/ppermute | solution.py:383
  28.6 0.0 collective-permute-done.14.refs_2_
  28.6 0.9 %attend_far.1 = bf16[128,640]{1,0:T(8,128)(2,1)S(1)} custom-call(bf16[128,512]{1,0:T(8,128)(2,1)S(1)} %collective-permute-done.7.refs_0_, bf16[128,512]{1,0:T(8,128)(2,1)S(1)} %pass_on.3.refs_1_, bf16[128,512]{1,0:T(8,128)(2,1)S(1)} %collective-permute-done.14.refs_2_, f32[128,512]{1,0:T(8,128)S(1)} %get-tuple-element.49.refs_3_, ...), custom_call_target="tpu_custom_call" | custom-call | flops 1000 | bytes 1000 | tf_op jit(solution)/shard_map/attend_far/pallas_call | solution.py:34
  29.5 1.3 %collective-permute-start.15 = (bf16[128,640]{1,0:T(8,128)(2,1)S(1)}, bf16[128,640]{1,0:T(8,128)(2,1)S(1)}, u32[]{:S(2)}, u32[]{:S(2)}) collective-permute-start(bf16[128,640]{1,0:T(8,128)(2,1)S(1)} %attend_far.1), channel_id=1, source_target_pairs={{4,0},{6,2},{0,4},{2,6},{12,8},{14,10},{8,12},{10,14},{20,16},{22,... | collective-permute-start | bytes 491528 | tf_op jit(solution)/shard_map/ppermute | solution.py:383
  30.8 0.7 %collective-permute-done.11.refs_3_ = bf16[64,512]{1,0:T(8,128)(2,1)S(1)} collective-permute-done((bf16[64,512]{1,0:T(8,128)(2,1)S(1)}, bf16[64,512]{1,0:T(8,128)(2,1)S(1)}, u32[]{:S(2)}, u32[]{:S(2)}) %collective-permute-start.11) | collective-permute-done | bytes 65568 | tf_op jit(solution)/shard_map/ppermute | solution.py:383
  31.5 0.1 block_priors.1
  31.7 0.1 collective-permute-start.12
  31.7 0.9 %attend_own.1.refs_0_ = f32[128,640]{1,0:T(8,128)S(1)} custom-call(bf16[128,512]{1,0:T(8,128)(2,1)S(1)} %pass_on.2.refs_1_.refs_0_, bf16[128,512]{1,0:T(8,128)(2,1)S(1)} %pass_on.3.refs_1_, bf16[128,512]{1,0:T(8,128)(2,1)S(1)} %collective-permute-done.14.refs_2_, f32[128,512]{1,0:T(8,128)S(1)} %get-tuple-element.47.refs_3_, ...), custom_call_target="tpu_custom_call" | custom-call | flops 1000 | bytes 1000 | tf_op jit(solution)/shard_map/attend_own/pallas_call | solution.py:34
  32.7 0.4 %collective-permute-done.12.refs_5_ = bf16[128,512]{1,0:T(8,128)(2,1)S(1)} collective-permute-done((bf16[128,512]{1,0:T(8,128)(2,1)S(1)}, bf16[128,512]{1,0:T(8,128)(2,1)S(1)}, u32[]{:S(2)}, u32[]{:S(2)}) %collective-permute-start.12) | collective-permute-done | bytes 131104 | tf_op jit(solution)/shard_map/ppermute | solution.py:383
  33.1 1.0 %retain_finish.1 = bf16[128,512]{1,0:T(8,128)(2,1)} custom-call(bf16[128,512]{1,0:T(8,128)(2,1)S(1)} %get-tuple-element.26.refs_0_, bf16[128,512]{1,0:T(8,128)(2,1)S(1)} %get-tuple-element.27.refs_1_, f32[128,512]{1,0:T(8,128)S(1)} %get-tuple-element.34.refs_2_, f32[128,2]{1,0:T(8,128)S(1)} %get-tuple-element.35.refs_3_, ...), custom_call_target="tpu_custom_call" | custom-call | flops 1000 | bytes 1000 | tf_op jit(solution)/shard_map/retain_finish/pallas_call | solution.py:34
  34.1 1.8 %collective-permute-done.15.refs_1_ = bf16[128,640]{1,0:T(8,128)(2,1)S(1)} collective-permute-done((bf16[128,640]{1,0:T(8,128)(2,1)S(1)}, bf16[128,640]{1,0:T(8,128)(2,1)S(1)}, u32[]{:S(2)}, u32[]{:S(2)}) %collective-permute-start.15) | collective-permute-done | bytes 163872 | tf_op jit(solution)/shard_map/ppermute | solution.py:383
  35.8 1.1 %finish.1 = bf16[128,512]{1,0:T(8,128)(2,1)} custom-call(f32[128,640]{1,0:T(8,128)S(1)} %attend_own.1.refs_0_, bf16[128,640]{1,0:T(8,128)(2,1)S(1)} %collective-permute-done.15.refs_1_), custom_call_target="tpu_custom_call" | custom-call | flops 1000 | bytes 1000 | tf_op jit(solution)/shard_map/finish/pallas_call | solution.py:34
  (4 shorter events, 0.0 us)
Async XLA Ops:
  2.4 3.1 %collective-permute-start = (bf16[144,512]{1,0:T(8,128)(2,1)S(1)}, bf16[144,512]{1,0:T(8,128)(2,1)S(1)}, u32[]{:S(2)}, u32[]{:S(2)}) collective-permute-start(bf16[144,512]{1,0:T(8,128)(2,1)S(1)} %get-tuple-element.32), channel_id=1, source_target_pairs={{2,0},{0,2},{6,4},{4,6},{10,8},{8,10},{14,12},{12,14},{18,16},{16,... | collective-permute-start | bytes 442376 | tf_op jit(solution)/shard_map/ppermute | solution.py:383
  2.9 5.3 %collective-permute-start.2 = (bf16[64,512]{1,0:T(8,128)(2,1)S(1)}, bf16[64,512]{1,0:T(8,128)(2,1)S(1)}, u32[]{:S(2)}, u32[]{:S(2)}) collective-permute-start(bf16[64,512]{1,0:T(8,128)(2,1)S(1)} %get-tuple-element.38), channel_id=1, source_target_pairs={{0,1},{1,0},{2,3},{3,2},{4,5},{5,4},{6,7},{7,6},{8,9},{9,8},{10,11... | collective-permute-start | bytes 196616 | tf_op jit(solution)/shard_map/ppermute | solution.py:386
  5.6 6.1 %collective-permute-start.1 = (bf16[80,512]{1,0:T(8,128)(2,1)S(1)}, bf16[80,512]{1,0:T(8,128)(2,1)S(1)}, u32[]{:S(2)}, u32[]{:S(2)}) collective-permute-start(bf16[80,512]{1,0:T(8,128)(2,1)S(1)} %get-tuple-element.33.refs_4_), channel_id=1, source_target_pairs={{4,0},{6,2},{0,4},{2,6},{12,8},{14,10},{8,12},{10,14},{20,16},{22,... | collective-permute-start | bytes 245768 | tf_op jit(solution)/shard_map/ppermute | solution.py:383
  8.2 9.1 %collective-permute-start.4 = (bf16[128,512]{1,0:T(8,128)(2,1)S(1)}, bf16[128,512]{1,0:T(8,128)(2,1)S(1)}, u32[]{:S(2)}, u32[]{:S(2)}) collective-permute-start(bf16[128,512]{1,0:T(8,128)(2,1)S(1)} %join_rows.1.refs_2_), channel_id=1, source_target_pairs={{16,0},{18,2},{20,4},{22,6},{24,8},{26,10},{28,12},{30,14},{0,16},... | collective-permute-start | bytes 393224 | tf_op jit(solution)/shard_map/ppermute | solution.py:383
  11.8 7.4 %collective-permute-start.5 = (bf16[128,512]{1,0:T(8,128)(2,1)S(1)}, bf16[128,512]{1,0:T(8,128)(2,1)S(1)}, u32[]{:S(2)}, u32[]{:S(2)}) collective-permute-start(bf16[128,512]{1,0:T(8,128)(2,1)S(1)} %get-tuple-element.40), channel_id=1, source_target_pairs={{8,0},{10,2},{12,4},{14,6},{0,8},{2,10},{4,12},{6,14},{24,16},{26,... | collective-permute-start | bytes 393224 | tf_op jit(solution)/shard_map/ppermute | solution.py:383
  13.4 6.6 %collective-permute-start.3 = (bf16[80,512]{1,0:T(8,128)(2,1)S(1)}, bf16[80,512]{1,0:T(8,128)(2,1)S(1)}, u32[]{:S(2)}, u32[]{:S(2)}) collective-permute-start(bf16[80,512]{1,0:T(8,128)(2,1)S(1)} %get-tuple-element.39.refs_0_), channel_id=1, source_target_pairs={{8,0},{10,2},{12,4},{14,6},{0,8},{2,10},{4,12},{6,14},{24,16},{26,... | collective-permute-start | bytes 245768 | tf_op jit(solution)/shard_map/ppermute | solution.py:383
  13.9 7.5 %collective-permute-start.8 = (bf16[128,512]{1,0:T(8,128)(2,1)S(1)}, bf16[128,512]{1,0:T(8,128)(2,1)S(1)}, u32[]{:S(2)}, u32[]{:S(2)}) collective-permute-start(bf16[128,512]{1,0:T(8,128)(2,1)S(1)} %join_rows.1.refs_2_), channel_id=1, source_target_pairs={{2,0},{0,2},{6,4},{4,6},{10,8},{8,10},{14,12},{12,14},{18,16},{16,... | collective-permute-start | bytes 393224 | tf_op jit(solution)/shard_map/ppermute | solution.py:383
  17.4 5.0 %collective-permute-start.7 = (bf16[128,512]{1,0:T(8,128)(2,1)S(1)}, bf16[128,512]{1,0:T(8,128)(2,1)S(1)}, u32[]{:S(2)}, u32[]{:S(2)}) collective-permute-start(bf16[128,512]{1,0:T(8,128)(2,1)S(1)} %pass_on.2.refs_1_.refs_0_), channel_id=1, source_target_pairs={{4,0},{6,2},{0,4},{2,6},{12,8},{14,10},{8,12},{10,14},{20,16},{22,... | collective-permute-start | bytes 393224 | tf_op jit(solution)/shard_map/ppermute | solution.py:383
  18.9 3.4 %collective-permute-start.9 = (bf16[128,512]{1,0:T(8,128)(2,1)S(1)}, bf16[128,512]{1,0:T(8,128)(2,1)S(1)}, u32[]{:S(2)}, u32[]{:S(2)}) collective-permute-start(bf16[128,512]{1,0:T(8,128)(2,1)S(1)} %collective-permute-done.4.refs_2_.refs_1_.refs_4_.refs_0_), channel_id=1, source_target_pairs={{2,0},{0,2},{6,4},{4,6},{10,8},{8,10},{14,12},{12,14},{18,16},{16,... | collective-permute-start | bytes 393224 | tf_op jit(solution)/shard_map/ppermute | solution.py:383
  19.2 3.2 %collective-permute-start.10 = (bf16[128,512]{1,0:T(8,128)(2,1)S(1)}, bf16[128,512]{1,0:T(8,128)(2,1)S(1)}, u32[]{:S(2)}, u32[]{:S(2)}) collective-permute-start(bf16[128,512]{1,0:T(8,128)(2,1)S(1)} %collective-permute-done.5.refs_3_.refs_6_), channel_id=1, source_target_pairs={{2,0},{0,2},{6,4},{4,6},{10,8},{8,10},{14,12},{12,14},{18,16},{16,... | collective-permute-start | bytes 393224 | tf_op jit(solution)/shard_map/ppermute | solution.py:383
  20.1 6.7 %collective-permute-start.6 = (bf16[80,512]{1,0:T(8,128)(2,1)S(1)}, bf16[80,512]{1,0:T(8,128)(2,1)S(1)}, u32[]{:S(2)}, u32[]{:S(2)}) collective-permute-start(bf16[80,512]{1,0:T(8,128)(2,1)S(1)} %grow.1.refs_1_), channel_id=1, source_target_pairs={{16,0},{18,2},{20,4},{22,6},{24,8},{26,10},{28,12},{30,14},{0,16},... | collective-permute-start | bytes 245768 | tf_op jit(solution)/shard_map/ppermute | solution.py:383
  21.4 5.5 %collective-permute-start.13 = (bf16[128,512]{1,0:T(8,128)(2,1)S(1)}, bf16[128,512]{1,0:T(8,128)(2,1)S(1)}, u32[]{:S(2)}, u32[]{:S(2)}) collective-permute-start(bf16[128,512]{1,0:T(8,128)(2,1)S(1)} %shard_map.95), channel_id=1, source_target_pairs={{0,0},{2,2},{4,4},{6,6},{8,8},{10,10},{12,12},{14,14},{24,16},{26,... | collective-permute-start | bytes 393224 | tf_op jit(solution)/shard_map/ppermute | solution.py:383
  26.9 1.7 %collective-permute-start.14 = (bf16[128,512]{1,0:T(8,128)(2,1)S(1)}, bf16[128,512]{1,0:T(8,128)(2,1)S(1)}, u32[]{:S(2)}, u32[]{:S(2)}) collective-permute-start(bf16[128,512]{1,0:T(8,128)(2,1)S(1)} %pass_on.3.refs_1_), channel_id=1, source_target_pairs={{2,0},{0,2},{6,4},{4,6},{10,8},{8,10},{14,12},{12,14},{18,16},{16,... | collective-permute-start | bytes 393224 | tf_op jit(solution)/shard_map/ppermute | solution.py:383
  27.0 4.5 %collective-permute-start.11 = (bf16[64,512]{1,0:T(8,128)(2,1)S(1)}, bf16[64,512]{1,0:T(8,128)(2,1)S(1)}, u32[]{:S(2)}, u32[]{:S(2)}) collective-permute-start(bf16[64,512]{1,0:T(8,128)(2,1)S(1)} %get-tuple-element.44.refs_1_), channel_id=1, source_target_pairs={{4,0},{6,2},{0,4},{2,6},{12,8},{14,10},{8,12},{10,14},{20,16},{22,... | collective-permute-start | bytes 196616 | tf_op jit(solution)/shard_map/ppermute | solution.py:383
  29.5 6.3 %collective-permute-start.15 = (bf16[128,640]{1,0:T(8,128)(2,1)S(1)}, bf16[128,640]{1,0:T(8,128)(2,1)S(1)}, u32[]{:S(2)}, u32[]{:S(2)}) collective-permute-start(bf16[128,640]{1,0:T(8,128)(2,1)S(1)} %attend_far.1), channel_id=1, source_target_pairs={{4,0},{6,2},{0,4},{2,6},{12,8},{14,10},{8,12},{10,14},{20,16},{22,... | collective-permute-start | bytes 491528 | tf_op jit(solution)/shard_map/ppermute | solution.py:383
  31.7 1.4 %collective-permute-start.12 = (bf16[128,512]{1,0:T(8,128)(2,1)S(1)}, bf16[128,512]{1,0:T(8,128)(2,1)S(1)}, u32[]{:S(2)}, u32[]{:S(2)}) collective-permute-start(bf16[128,512]{1,0:T(8,128)(2,1)S(1)} %get-tuple-element.46), channel_id=1, source_target_pairs={{2,0},{0,2},{6,4},{4,6},{10,8},{8,10},{14,12},{12,14},{18,16},{16,... | collective-permute-start | bytes 393224 | tf_op jit(solution)/shard_map/ppermute | solution.py:383

commit v12 on v11

--- a/solution.py
+++ b/solution.py
@@ -306,7 +306,7 @@
             at = jnp.where(jnp.bitwise_xor(depth, s) < depth, -1, 4 * rows)
         limit = jnp.where(column >= i * length, at, limit)
     scale = 1.0 / (math.sqrt(HD) * math.log(2.0))
-    row = lax.broadcasted_iota(jnp.int32, (rows, total), 0)
+    row = lax.rem(lax.broadcasted_iota(jnp.int32, (group * rows, total), 0), rows)
     lane = lax.broadcasted_iota(jnp.int32, (rows, LANES), 1)
     for which, (query, side) in enumerate(zip(queries, sides)):
         place = jnp.bitwise_xor(high, side)
@@ -317,32 +317,36 @@
             out = outs[which]
         else:
             out, stats_out = outs[2 * which : 2 * which + 2]
-        for head in range(heads):
-            columns = pl.ds(head * HD, HD)
-            shared = pl.ds((head // group) * HD, HD)
-            scores = dot(query[:, columns], keys[:, shared], ((1,), (1,))) * scale
+        for first in range(0, heads, group):
+            members = range(first, first + group)
+            shared = pl.ds((first // group) * HD, HD)
+            stacked = jnp.concatenate([query[:, pl.ds(h * HD, HD)] for h in members], axis=0)
+            scores = dot(stacked, keys[:, shared], ((1,), (1,))) * scale
             masked = jnp.where(allowed, scores, FAR)
             top = jnp.maximum(jnp.max(masked, axis=1, keepdims=True), NEAR)
             if last:
-                old = stats_ref[:, 2 * head : 2 * head + 1]
+                old = jnp.concatenate([stats_ref[:, 2 * h : 2 * h + 1] for h in members], axis=0)
                 top = jnp.maximum(top, old)
             weights = jnp.exp2(masked - top)
             summed = jnp.sum(weights, axis=1, keepdims=True)
             mixed = dot(weights.astype(BF16), values[:, shared], ((1,), (0,)))
-            if not last:
-                out[:, columns] = mixed
-                stats = jnp.where(lane == 2 * head, top, stats)
-                stats = jnp.where(lane == 2 * head + 1, summed, stats)
-                continue
-            shrink = jnp.exp2(old - top)
-            summed = summed + shrink * stats_ref[:, 2 * head + 1 : 2 * head + 2]
-            mixed = mixed + shrink * mixed_ref[:, columns]
-            some = summed > 0.0
-            safe = jnp.where(some, summed, 1.0)
-            out[:, columns] = (mixed / safe).astype(out.dtype)
-            level = jnp.where(some, top + jnp.log2(safe), FAR)
-            for i, third in enumerate(thirds(level)):
-                stats = jnp.where(lane == 3 * head + i, third, stats)
+            for i, h in enumerate(members):
+                columns, part = pl.ds(h * HD, HD), slice(i * rows, (i + 1) * rows)
+                if not last:
+                    out[:, columns] = mixed[part]
+                    stats = jnp.where(lane == 2 * h, top[part], stats)
+                    stats = jnp.where(lane == 2 * h + 1, summed[part], stats)
+                    continue
+                shrink = jnp.exp2(old[part] - top[part])
+                whole = summed[part] + shrink * stats_ref[:, 2 * h + 1 : 2 * h + 2]
+                some = whole > 0.0
+                safe = jnp.where(some, whole, 1.0)
+                out[:, columns] = ((mixed[part] + shrink * mixed_ref[:, columns]) / safe).astype(
+                    out.dtype
+                )
+                level = jnp.where(some, top[part] + jnp.log2(safe), FAR)
+                for k, third in enumerate(thirds(level)):
+                    stats = jnp.where(lane == 3 * h + k, third, stats)
         if last:
             out[:, pl.ds(wide, LANES)] = stats.astype(out.dtype)
         else:

time: 37 us -> 36.7 us (level)
  Pallas kernels: 8.37 us -> 7.13 us
  waiting for transfers between devices: 11.3 us -> 12.2 us
    pallas_call x16, Pallas kernels: 8.37 us -> 7.13 us  [call(): pl.pallas_call(kernel, out_shape=outs[0] if single else tuple(outs), in_s...]
    ppermute x15, waiting for transfers between devices: 10.3 us -> 11.2 us  [swap(): return lax.ppermute(value, 'ctx', pairs)]
  transfers between devices with their start and end apart: 16 -> 16, of which waited for: 9 -> 9; matrix products, arithmetic and copies ran while one was open for 0% -> 0% of each run, Pallas kernels for 15% -> 12%
where the time goes in v12:
time: 36.7 us; the launch traced here: 36.6 us
  starting transfers between devices  16.5 us (45%)
  waiting for transfers between devices  12.2 us (33%)
  Pallas kernels  7.13 us (19%)
  between operations  0.78 us (2%)
    ppermute x15, starting transfers between devices, swap(): return lax.ppermute(value, 'ctx', pairs)  13.9 us
    ppermute x15, waiting for transfers between devices, swap(): return lax.ppermute(value, 'ctx', pairs)  11.2 us
    pallas_call x16, Pallas kernels, call(): pl.pallas_call(kernel, out_shape=outs[0] if single else tuple(outs), in_s...  7.13 us
    ppermute x1, starting transfers between devices, to_head(): return lax.ppermute(value, 'head', [(y, (y + e) % n) for y in range(n)])  2.6 us
    ppermute x1, waiting for transfers between devices, to_head(): return lax.ppermute(value, 'head', [(y, (y + e) % n) for y in range(n)])  1 us
  transfers between devices with their start and end apart: 16, of which 9 were waited for; matrix products, arithmetic and copies ran while one was open for 0% of the time, Pallas kernels for 12%

profile of v12, /device:TPU:0, one launch (start us, length us, event | category | flops | bytes accessed | tf_op | source)
XLA Modules:
  0.0 36.6 jit_solution(6312978611896061757)
XLA Ops:
  0.6 1.8 %load_all.1 = (bf16[64,512]{1,0:T(8,128)(2,1)S(1)}, bf16[64,512]{1,0:T(8,128)(2,1)S(1)}, bf16[128,512]{1,0:T(8,128)(2,1)S(1)}, bf16[128,512]{1,0:T(8,128)(2,1)S(...) custom-call(bf16[64,512]{1,0:T(8,128)(2,1)} %refs_0_.1, ...), custom_call_target="tpu_custom_call" | custom-call | flops 1000 | bytes 1000 | tf_op jit(solution)/shard_map/load_all/pallas_call | solution.py:34
  2.4 0.5 %collective-permute-start = (bf16[144,512]{1,0:T(8,128)(2,1)S(1)}, bf16[144,512]{1,0:T(8,128)(2,1)S(1)}, u32[]{:S(2)}, u32[]{:S(2)}) collective-permute-start(bf16[144,512]{1,0:T(8,128)(2,1)S(1)} %get-tuple-element.32), channel_id=1, source_target_pairs={{2,0},{0,2},{6,4},{4,6},{10,8},{8,10},{14,12},{12,14},{18,16},{16,... | collective-permute-start | bytes 442376 | tf_op jit(solution)/shard_map/ppermute | solution.py:387
  2.9 2.6 %collective-permute-start.2 = (bf16[64,512]{1,0:T(8,128)(2,1)S(1)}, bf16[64,512]{1,0:T(8,128)(2,1)S(1)}, u32[]{:S(2)}, u32[]{:S(2)}) collective-permute-start(bf16[64,512]{1,0:T(8,128)(2,1)S(1)} %get-tuple-element.38), channel_id=1, source_target_pairs={{0,1},{1,0},{2,3},{3,2},{4,5},{5,4},{6,7},{7,6},{8,9},{9,8},{10,11... | collective-permute-start | bytes 196616 | tf_op jit(solution)/shard_map/ppermute | solution.py:390
  5.5 0.0 collective-permute-done.refs_1_
  5.5 0.1 chip_total.1
  5.6 1.6 %collective-permute-start.1 = (bf16[80,512]{1,0:T(8,128)(2,1)S(1)}, bf16[80,512]{1,0:T(8,128)(2,1)S(1)}, u32[]{:S(2)}, u32[]{:S(2)}) collective-permute-start(bf16[80,512]{1,0:T(8,128)(2,1)S(1)} %get-tuple-element.33.refs_4_), channel_id=1, source_target_pairs={{4,0},{6,2},{0,4},{2,6},{12,8},{14,10},{8,12},{10,14},{20,16},{22,... | collective-permute-start | bytes 245768 | tf_op jit(solution)/shard_map/ppermute | solution.py:387
  7.2 1.0 %collective-permute-done.2.refs_1_ = bf16[64,512]{1,0:T(8,128)(2,1)S(1)} collective-permute-done((bf16[64,512]{1,0:T(8,128)(2,1)S(1)}, bf16[64,512]{1,0:T(8,128)(2,1)S(1)}, u32[]{:S(2)}, u32[]{:S(2)}) %collective-permute-start.2) | collective-permute-done | bytes 65568 | tf_op jit(solution)/shard_map/ppermute | solution.py:390
  8.2 2.9 %collective-permute-start.4 = (bf16[128,512]{1,0:T(8,128)(2,1)S(1)}, bf16[128,512]{1,0:T(8,128)(2,1)S(1)}, u32[]{:S(2)}, u32[]{:S(2)}) collective-permute-start(bf16[128,512]{1,0:T(8,128)(2,1)S(1)} %join_rows.1.refs_2_), channel_id=1, source_target_pairs={{16,0},{18,2},{20,4},{22,6},{24,8},{26,10},{28,12},{30,14},{0,16},... | collective-permute-start | bytes 393224 | tf_op jit(solution)/shard_map/ppermute | solution.py:387
  11.1 0.6 %retain_inside.1 = (f32[128,512]{1,0:T(8,128)S(1)}, f32[128,2]{1,0:T(8,128)S(1)}) custom-call(bf16[128,512]{1,0:T(8,128)(2,1)S(1)} %get-tuple-element.26.refs_0_, bf16[128,512]{1,0:T(8,128)(2,1)S(1)} %get-tuple-element.28.refs_1_, bf16[128,512]{1,0:T(8,128)(2,1)S(1)} %get-tuple-element.29.refs_2_, f32[2,128]{1,0:T(2,128)S(1)} %get-tuple-element.30.refs_3_, ...), custom_call_target="tpu_custom_call" | custom-call | flops 1000 | bytes 1000 | tf_op jit(solution)/shard_map/retain_inside/pallas_call | solution.py:34
  11.7 0.0 collective-permute-done.1.refs_1_
  11.7 0.1 plane_total.1
  11.8 1.6 %collective-permute-start.5 = (bf16[128,512]{1,0:T(8,128)(2,1)S(1)}, bf16[128,512]{1,0:T(8,128)(2,1)S(1)}, u32[]{:S(2)}, u32[]{:S(2)}) collective-permute-start(bf16[128,512]{1,0:T(8,128)(2,1)S(1)} %get-tuple-element.40), channel_id=1, source_target_pairs={{8,0},{10,2},{12,4},{14,6},{0,8},{2,10},{4,12},{6,14},{24,16},{26,... | collective-permute-start | bytes 393224 | tf_op jit(solution)/shard_map/ppermute | solution.py:387
  13.4 0.4 %collective-permute-start.3 = (bf16[80,512]{1,0:T(8,128)(2,1)S(1)}, bf16[80,512]{1,0:T(8,128)(2,1)S(1)}, u32[]{:S(2)}, u32[]{:S(2)}) collective-permute-start(bf16[80,512]{1,0:T(8,128)(2,1)S(1)} %get-tuple-element.39.refs_0_), channel_id=1, source_target_pairs={{8,0},{10,2},{12,4},{14,6},{0,8},{2,10},{4,12},{6,14},{24,16},{26,... | collective-permute-start | bytes 245768 | tf_op jit(solution)/shard_map/ppermute | solution.py:387
  13.9 0.0 collective-permute-start.8
  13.9 3.5 %collective-permute-done.4.refs_2_.refs_1_.refs_4_.refs_0_ = bf16[128,512]{1,0:T(8,128)(2,1)S(1)} collective-permute-done((bf16[128,512]{1,0:T(8,128)(2,1)S(1)}, bf16[128,512]{1,0:T(8,128)(2,1)S(1)}, u32[]{:S(2)}, u32[]{:S(2)}) %collective-permute-start.4) | collective-permute-done | bytes 131104 | tf_op jit(solution)/shard_map/ppermute | solution.py:387
  17.4 1.5 %collective-permute-start.7 = (bf16[128,512]{1,0:T(8,128)(2,1)S(1)}, bf16[128,512]{1,0:T(8,128)(2,1)S(1)}, u32[]{:S(2)}, u32[]{:S(2)}) collective-permute-start(bf16[128,512]{1,0:T(8,128)(2,1)S(1)} %pass_on.2.refs_1_.refs_0_), channel_id=1, source_target_pairs={{4,0},{6,2},{0,4},{2,6},{12,8},{14,10},{8,12},{10,14},{20,16},{22,... | collective-permute-start | bytes 393224 | tf_op jit(solution)/shard_map/ppermute | solution.py:387
  18.9 0.0 collective-permute-start.9
  18.9 0.3 collective-permute-done.5.refs_3_.refs_6_
  19.2 0.2 collective-permute-start.10
  19.4 0.6 %collective-permute-done.3.refs_1_.refs_2_ = bf16[80,512]{1,0:T(8,128)(2,1)S(1)} collective-permute-done((bf16[80,512]{1,0:T(8,128)(2,1)S(1)}, bf16[80,512]{1,0:T(8,128)(2,1)S(1)}, u32[]{:S(2)}, u32[]{:S(2)}) %collective-permute-start.3) | collective-permute-done | bytes 81952 | tf_op jit(solution)/shard_map/ppermute | solution.py:387
  20.0 0.1 grow.1.refs_1_
  20.1 1.3 %collective-permute-start.6 = (bf16[80,512]{1,0:T(8,128)(2,1)S(1)}, bf16[80,512]{1,0:T(8,128)(2,1)S(1)}, u32[]{:S(2)}, u32[]{:S(2)}) collective-permute-start(bf16[80,512]{1,0:T(8,128)(2,1)S(1)} %grow.1.refs_1_), channel_id=1, source_target_pairs={{16,0},{18,2},{20,4},{22,6},{24,8},{26,10},{28,12},{30,14},{0,16},... | collective-permute-start | bytes 245768 | tf_op jit(solution)/shard_map/ppermute | solution.py:387
  21.4 0.0 collective-permute-done.8.refs_3_
  21.4 0.7 %collective-permute-start.13 = (bf16[128,512]{1,0:T(8,128)(2,1)S(1)}, bf16[128,512]{1,0:T(8,128)(2,1)S(1)}, u32[]{:S(2)}, u32[]{:S(2)}) collective-permute-start(bf16[128,512]{1,0:T(8,128)(2,1)S(1)} %shard_map.95), channel_id=1, source_target_pairs={{0,0},{2,2},{4,4},{6,6},{8,8},{10,10},{12,12},{14,14},{24,16},{26,... | collective-permute-start | bytes 393224 | tf_op jit(solution)/shard_map/ppermute | solution.py:387
  22.1 0.2 collective-permute-done.7.refs_0_
  22.3 0.0 collective-permute-done.9.refs_5_
  22.3 0.0 collective-permute-done.10.refs_7_
  22.3 1.0 %attend_near.1 = (f32[128,512]{1,0:T(8,128)S(1)}, f32[128,128]{1,0:T(8,128)S(1)}, f32[128,512]{1,0:T(8,128)S(1)}, f32[128,128]{1,0:T(8,128)S(1)}) custom-call(bf16[128,512]{1,0:T(8,128)(2,1)S(1)} %collective-permute-done.7.refs_0_, bf16[128,512]{1,0:T(8,128)(2,1)S(1)} %pass_on.2.refs_1_.refs_0_, bf16[128,512]{1,0:T(8,128)(2,1)S(1)} %join_rows.1.refs_2_, ...), custom_call_target="tpu_custom_call" | custom-call | flops 1000 | bytes 1000 | tf_op jit(solution)/shard_map/attend_near/pallas_call | solution.py:34
  23.4 3.4 %collective-permute-done.6.refs_3_ = bf16[80,512]{1,0:T(8,128)(2,1)S(1)} collective-permute-done((bf16[80,512]{1,0:T(8,128)(2,1)S(1)}, bf16[80,512]{1,0:T(8,128)(2,1)S(1)}, u32[]{:S(2)}, u32[]{:S(2)}) %collective-permute-start.6) | collective-permute-done | bytes 81952 | tf_op jit(solution)/shard_map/ppermute | solution.py:387
  26.8 0.1 chip_priors.1
  26.9 0.0 collective-permute-done.13.refs_0_
  26.9 0.1 collective-permute-start.14
  27.0 1.6 %collective-permute-start.11 = (bf16[64,512]{1,0:T(8,128)(2,1)S(1)}, bf16[64,512]{1,0:T(8,128)(2,1)S(1)}, u32[]{:S(2)}, u32[]{:S(2)}) collective-permute-start(bf16[64,512]{1,0:T(8,128)(2,1)S(1)} %get-tuple-element.44.refs_1_), channel_id=1, source_target_pairs={{4,0},{6,2},{0,4},{2,6},{12,8},{14,10},{8,12},{10,14},{20,16},{22,... | collective-permute-start | bytes 196616 | tf_op jit(solution)/shard_map/ppermute | solution.py:387
  28.6 0.0 collective-permute-done.14.refs_2_
  28.6 0.6 %attend_far.1 = bf16[128,640]{1,0:T(8,128)(2,1)S(1)} custom-call(bf16[128,512]{1,0:T(8,128)(2,1)S(1)} %collective-permute-done.7.refs_0_, bf16[128,512]{1,0:T(8,128)(2,1)S(1)} %pass_on.3.refs_1_, bf16[128,512]{1,0:T(8,128)(2,1)S(1)} %collective-permute-done.14.refs_2_, f32[128,512]{1,0:T(8,128)S(1)} %get-tuple-element.49.refs_3_, ...), custom_call_target="tpu_custom_call" | custom-call | flops 1000 | bytes 1000 | tf_op jit(solution)/shard_map/attend_far/pallas_call | solution.py:34
  29.2 1.3 %collective-permute-start.15 = (bf16[128,640]{1,0:T(8,128)(2,1)S(1)}, bf16[128,640]{1,0:T(8,128)(2,1)S(1)}, u32[]{:S(2)}, u32[]{:S(2)}) collective-permute-start(bf16[128,640]{1,0:T(8,128)(2,1)S(1)} %attend_far.1), channel_id=1, source_target_pairs={{4,0},{6,2},{0,4},{2,6},{12,8},{14,10},{8,12},{10,14},{20,16},{22,... | collective-permute-start | bytes 491528 | tf_op jit(solution)/shard_map/ppermute | solution.py:387
  30.5 1.0 %collective-permute-done.11.refs_3_ = bf16[64,512]{1,0:T(8,128)(2,1)S(1)} collective-permute-done((bf16[64,512]{1,0:T(8,128)(2,1)S(1)}, bf16[64,512]{1,0:T(8,128)(2,1)S(1)}, u32[]{:S(2)}, u32[]{:S(2)}) %collective-permute-start.11) | collective-permute-done | bytes 65568 | tf_op jit(solution)/shard_map/ppermute | solution.py:387
  31.5 0.1 block_priors.1
  31.7 0.1 collective-permute-start.12
  31.7 0.6 %attend_own.1.refs_0_ = f32[128,640]{1,0:T(8,128)S(1)} custom-call(bf16[128,512]{1,0:T(8,128)(2,1)S(1)} %pass_on.2.refs_1_.refs_0_, bf16[128,512]{1,0:T(8,128)(2,1)S(1)} %pass_on.3.refs_1_, bf16[128,512]{1,0:T(8,128)(2,1)S(1)} %collective-permute-done.14.refs_2_, f32[128,512]{1,0:T(8,128)S(1)} %get-tuple-element.47.refs_3_, ...), custom_call_target="tpu_custom_call" | custom-call | flops 1000 | bytes 1000 | tf_op jit(solution)/shard_map/attend_own/pallas_call | solution.py:34
  32.3 0.7 %collective-permute-done.12.refs_5_ = bf16[128,512]{1,0:T(8,128)(2,1)S(1)} collective-permute-done((bf16[128,512]{1,0:T(8,128)(2,1)S(1)}, bf16[128,512]{1,0:T(8,128)(2,1)S(1)}, u32[]{:S(2)}, u32[]{:S(2)}) %collective-permute-start.12) | collective-permute-done | bytes 131104 | tf_op jit(solution)/shard_map/ppermute | solution.py:387
  33.1 1.0 %retain_finish.1 = bf16[128,512]{1,0:T(8,128)(2,1)} custom-call(bf16[128,512]{1,0:T(8,128)(2,1)S(1)} %get-tuple-element.26.refs_0_, bf16[128,512]{1,0:T(8,128)(2,1)S(1)} %get-tuple-element.27.refs_1_, f32[128,512]{1,0:T(8,128)S(1)} %get-tuple-element.34.refs_2_, f32[128,2]{1,0:T(8,128)S(1)} %get-tuple-element.35.refs_3_, ...), custom_call_target="tpu_custom_call" | custom-call | flops 1000 | bytes 1000 | tf_op jit(solution)/shard_map/retain_finish/pallas_call | solution.py:34
  34.1 1.5 %collective-permute-done.15.refs_1_ = bf16[128,640]{1,0:T(8,128)(2,1)S(1)} collective-permute-done((bf16[128,640]{1,0:T(8,128)(2,1)S(1)}, bf16[128,640]{1,0:T(8,128)(2,1)S(1)}, u32[]{:S(2)}, u32[]{:S(2)}) %collective-permute-start.15) | collective-permute-done | bytes 163872 | tf_op jit(solution)/shard_map/ppermute | solution.py:387
  35.5 1.1 %finish.1 = bf16[128,512]{1,0:T(8,128)(2,1)} custom-call(f32[128,640]{1,0:T(8,128)S(1)} %attend_own.1.refs_0_, bf16[128,640]{1,0:T(8,128)(2,1)S(1)} %collective-permute-done.15.refs_1_), custom_call_target="tpu_custom_call" | custom-call | flops 1000 | bytes 1000 | tf_op jit(solution)/shard_map/finish/pallas_call | solution.py:34
  (4 shorter events, 0.0 us)
Async XLA Ops:
  2.4 3.1 %collective-permute-start = (bf16[144,512]{1,0:T(8,128)(2,1)S(1)}, bf16[144,512]{1,0:T(8,128)(2,1)S(1)}, u32[]{:S(2)}, u32[]{:S(2)}) collective-permute-start(bf16[144,512]{1,0:T(8,128)(2,1)S(1)} %get-tuple-element.32), channel_id=1, source_target_pairs={{2,0},{0,2},{6,4},{4,6},{10,8},{8,10},{14,12},{12,14},{18,16},{16,... | collective-permute-start | bytes 442376 | tf_op jit(solution)/shard_map/ppermute | solution.py:387
  2.9 5.3 %collective-permute-start.2 = (bf16[64,512]{1,0:T(8,128)(2,1)S(1)}, bf16[64,512]{1,0:T(8,128)(2,1)S(1)}, u32[]{:S(2)}, u32[]{:S(2)}) collective-permute-start(bf16[64,512]{1,0:T(8,128)(2,1)S(1)} %get-tuple-element.38), channel_id=1, source_target_pairs={{0,1},{1,0},{2,3},{3,2},{4,5},{5,4},{6,7},{7,6},{8,9},{9,8},{10,11... | collective-permute-start | bytes 196616 | tf_op jit(solution)/shard_map/ppermute | solution.py:390
  5.6 6.1 %collective-permute-start.1 = (bf16[80,512]{1,0:T(8,128)(2,1)S(1)}, bf16[80,512]{1,0:T(8,128)(2,1)S(1)}, u32[]{:S(2)}, u32[]{:S(2)}) collective-permute-start(bf16[80,512]{1,0:T(8,128)(2,1)S(1)} %get-tuple-element.33.refs_4_), channel_id=1, source_target_pairs={{4,0},{6,2},{0,4},{2,6},{12,8},{14,10},{8,12},{10,14},{20,16},{22,... | collective-permute-start | bytes 245768 | tf_op jit(solution)/shard_map/ppermute | solution.py:387
  8.2 9.1 %collective-permute-start.4 = (bf16[128,512]{1,0:T(8,128)(2,1)S(1)}, bf16[128,512]{1,0:T(8,128)(2,1)S(1)}, u32[]{:S(2)}, u32[]{:S(2)}) collective-permute-start(bf16[128,512]{1,0:T(8,128)(2,1)S(1)} %join_rows.1.refs_2_), channel_id=1, source_target_pairs={{16,0},{18,2},{20,4},{22,6},{24,8},{26,10},{28,12},{30,14},{0,16},... | collective-permute-start | bytes 393224 | tf_op jit(solution)/shard_map/ppermute | solution.py:387
  11.8 7.4 %collective-permute-start.5 = (bf16[128,512]{1,0:T(8,128)(2,1)S(1)}, bf16[128,512]{1,0:T(8,128)(2,1)S(1)}, u32[]{:S(2)}, u32[]{:S(2)}) collective-permute-start(bf16[128,512]{1,0:T(8,128)(2,1)S(1)} %get-tuple-element.40), channel_id=1, source_target_pairs={{8,0},{10,2},{12,4},{14,6},{0,8},{2,10},{4,12},{6,14},{24,16},{26,... | collective-permute-start | bytes 393224 | tf_op jit(solution)/shard_map/ppermute | solution.py:387
  13.4 6.6 %collective-permute-start.3 = (bf16[80,512]{1,0:T(8,128)(2,1)S(1)}, bf16[80,512]{1,0:T(8,128)(2,1)S(1)}, u32[]{:S(2)}, u32[]{:S(2)}) collective-permute-start(bf16[80,512]{1,0:T(8,128)(2,1)S(1)} %get-tuple-element.39.refs_0_), channel_id=1, source_target_pairs={{8,0},{10,2},{12,4},{14,6},{0,8},{2,10},{4,12},{6,14},{24,16},{26,... | collective-permute-start | bytes 245768 | tf_op jit(solution)/shard_map/ppermute | solution.py:387
  13.9 7.5 %collective-permute-start.8 = (bf16[128,512]{1,0:T(8,128)(2,1)S(1)}, bf16[128,512]{1,0:T(8,128)(2,1)S(1)}, u32[]{:S(2)}, u32[]{:S(2)}) collective-permute-start(bf16[128,512]{1,0:T(8,128)(2,1)S(1)} %join_rows.1.refs_2_), channel_id=1, source_target_pairs={{2,0},{0,2},{6,4},{4,6},{10,8},{8,10},{14,12},{12,14},{18,16},{16,... | collective-permute-start | bytes 393224 | tf_op jit(solution)/shard_map/ppermute | solution.py:387
  17.4 5.0 %collective-permute-start.7 = (bf16[128,512]{1,0:T(8,128)(2,1)S(1)}, bf16[128,512]{1,0:T(8,128)(2,1)S(1)}, u32[]{:S(2)}, u32[]{:S(2)}) collective-permute-start(bf16[128,512]{1,0:T(8,128)(2,1)S(1)} %pass_on.2.refs_1_.refs_0_), channel_id=1, source_target_pairs={{4,0},{6,2},{0,4},{2,6},{12,8},{14,10},{8,12},{10,14},{20,16},{22,... | collective-permute-start | bytes 393224 | tf_op jit(solution)/shard_map/ppermute | solution.py:387
  18.9 3.4 %collective-permute-start.9 = (bf16[128,512]{1,0:T(8,128)(2,1)S(1)}, bf16[128,512]{1,0:T(8,128)(2,1)S(1)}, u32[]{:S(2)}, u32[]{:S(2)}) collective-permute-start(bf16[128,512]{1,0:T(8,128)(2,1)S(1)} %collective-permute-done.4.refs_2_.refs_1_.refs_4_.refs_0_), channel_id=1, source_target_pairs={{2,0},{0,2},{6,4},{4,6},{10,8},{8,10},{14,12},{12,14},{18,16},{16,... | collective-permute-start | bytes 393224 | tf_op jit(solution)/shard_map/ppermute | solution.py:387
  19.2 3.2 %collective-permute-start.10 = (bf16[128,512]{1,0:T(8,128)(2,1)S(1)}, bf16[128,512]{1,0:T(8,128)(2,1)S(1)}, u32[]{:S(2)}, u32[]{:S(2)}) collective-permute-start(bf16[128,512]{1,0:T(8,128)(2,1)S(1)} %collective-permute-done.5.refs_3_.refs_6_), channel_id=1, source_target_pairs={{2,0},{0,2},{6,4},{4,6},{10,8},{8,10},{14,12},{12,14},{18,16},{16,... | collective-permute-start | bytes 393224 | tf_op jit(solution)/shard_map/ppermute | solution.py:387
  20.1 6.7 %collective-permute-start.6 = (bf16[80,512]{1,0:T(8,128)(2,1)S(1)}, bf16[80,512]{1,0:T(8,128)(2,1)S(1)}, u32[]{:S(2)}, u32[]{:S(2)}) collective-permute-start(bf16[80,512]{1,0:T(8,128)(2,1)S(1)} %grow.1.refs_1_), channel_id=1, source_target_pairs={{16,0},{18,2},{20,4},{22,6},{24,8},{26,10},{28,12},{30,14},{0,16},... | collective-permute-start | bytes 245768 | tf_op jit(solution)/shard_map/ppermute | solution.py:387
  21.4 5.5 %collective-permute-start.13 = (bf16[128,512]{1,0:T(8,128)(2,1)S(1)}, bf16[128,512]{1,0:T(8,128)(2,1)S(1)}, u32[]{:S(2)}, u32[]{:S(2)}) collective-permute-start(bf16[128,512]{1,0:T(8,128)(2,1)S(1)} %shard_map.95), channel_id=1, source_target_pairs={{0,0},{2,2},{4,4},{6,6},{8,8},{10,10},{12,12},{14,14},{24,16},{26,... | collective-permute-start | bytes 393224 | tf_op jit(solution)/shard_map/ppermute | solution.py:387
  26.9 1.7 %collective-permute-start.14 = (bf16[128,512]{1,0:T(8,128)(2,1)S(1)}, bf16[128,512]{1,0:T(8,128)(2,1)S(1)}, u32[]{:S(2)}, u32[]{:S(2)}) collective-permute-start(bf16[128,512]{1,0:T(8,128)(2,1)S(1)} %pass_on.3.refs_1_), channel_id=1, source_target_pairs={{2,0},{0,2},{6,4},{4,6},{10,8},{8,10},{14,12},{12,14},{18,16},{16,... | collective-permute-start | bytes 393224 | tf_op jit(solution)/shard_map/ppermute | solution.py:387
  27.0 4.5 %collective-permute-start.11 = (bf16[64,512]{1,0:T(8,128)(2,1)S(1)}, bf16[64,512]{1,0:T(8,128)(2,1)S(1)}, u32[]{:S(2)}, u32[]{:S(2)}) collective-permute-start(bf16[64,512]{1,0:T(8,128)(2,1)S(1)} %get-tuple-element.44.refs_1_), channel_id=1, source_target_pairs={{4,0},{6,2},{0,4},{2,6},{12,8},{14,10},{8,12},{10,14},{20,16},{22,... | collective-permute-start | bytes 196616 | tf_op jit(solution)/shard_map/ppermute | solution.py:387
  29.2 6.3 %collective-permute-start.15 = (bf16[128,640]{1,0:T(8,128)(2,1)S(1)}, bf16[128,640]{1,0:T(8,128)(2,1)S(1)}, u32[]{:S(2)}, u32[]{:S(2)}) collective-permute-start(bf16[128,640]{1,0:T(8,128)(2,1)S(1)} %attend_far.1), channel_id=1, source_target_pairs={{4,0},{6,2},{0,4},{2,6},{12,8},{14,10},{8,12},{10,14},{20,16},{22,... | collective-permute-start | bytes 491528 | tf_op jit(solution)/shard_map/ppermute | solution.py:387
  31.7 1.4 %collective-permute-start.12 = (bf16[128,512]{1,0:T(8,128)(2,1)S(1)}, bf16[128,512]{1,0:T(8,128)(2,1)S(1)}, u32[]{:S(2)}, u32[]{:S(2)}) collective-permute-start(bf16[128,512]{1,0:T(8,128)(2,1)S(1)} %get-tuple-element.46), channel_id=1, source_target_pairs={{2,0},{0,2},{6,4},{4,6},{10,8},{8,10},{14,12},{12,14},{18,16},{16,... | collective-permute-start | bytes 393224 | tf_op jit(solution)/shard_map/ppermute | solution.py:387

commit v13 on v12

--- a/solution.py
+++ b/solution.py
@@ -277,6 +277,11 @@
 
 def copy_after(source, out):
     out[...] = source[...]
+
+
+def diagonal(rows):
+    dims = (rows, rows)
+    return lax.broadcasted_iota(jnp.int32, dims, 0) == lax.broadcasted_iota(jnp.int32, dims, 1)
 
 
 def attend(hops, last, sides, *refs):
@@ -312,6 +317,8 @@
         place = jnp.bitwise_xor(high, side)
         allowed = row + (2 * place + low) * rows >= limit
         stats = jnp.zeros((rows, LANES), F32)
+        levels = jnp.zeros((PAD, rows), F32)
+        line = lax.broadcasted_iota(jnp.int32, (PAD, rows), 0)
         if last:
             mixed_ref, stats_ref = carried[2 * which : 2 * which + 2]
             out = outs[which]
@@ -341,14 +348,16 @@
                 whole = summed[part] + shrink * stats_ref[:, 2 * h + 1 : 2 * h + 2]
                 some = whole > 0.0
                 safe = jnp.where(some, whole, 1.0)
-                out[:, columns] = ((mixed[part] + shrink * mixed_ref[:, columns]) / safe).astype(
+                out[pl.ds(0, rows), columns] = ((mixed[part] + shrink * mixed_ref[:, columns]) / safe).astype(
                     out.dtype
                 )
                 level = jnp.where(some, top[part] + jnp.log2(safe), FAR)
-                for k, third in enumerate(thirds(level)):
-                    stats = jnp.where(lane == 3 * h + k, third, stats)
+                across = jnp.sum(jnp.where(diagonal(rows), level, 0.0), axis=0, keepdims=True)
+                for k, third in enumerate(thirds(across)):
+                    levels = jnp.where(line == 3 * h + k, third, levels)
         if last:
-            out[:, pl.ds(wide, LANES)] = stats.astype(out.dtype)
+            out[pl.ds(rows, PAD), :] = jnp.zeros((PAD, wide), out.dtype)
+            out[pl.ds(rows, PAD), pl.ds(0, rows)] = levels.astype(out.dtype)
         else:
             stats_out[...] = stats
 
@@ -357,18 +366,22 @@
     wide = out.shape[1]
     ins = (keep_ref, other_ref)
     columns = pl.ds(head * HD, HD)
-    tiles = [ref[:, pl.ds(wide, LANES)].astype(F32) for ref in ins]
+    rows = out.shape[0]
+    tiles = [ref[pl.ds(rows, PAD), pl.ds(0, rows)].astype(F32) for ref in ins]
+    across = [
+        tile[3 * head : 3 * head + 1, :]
+        + tile[3 * head + 1 : 3 * head + 2, :]
+        + tile[3 * head + 2 : 3 * head + 3, :]
+        for tile in tiles
+    ]
     levels = [
-        tile[:, 3 * head : 3 * head + 1]
-        + tile[:, 3 * head + 1 : 3 * head + 2]
-        + tile[:, 3 * head + 2 : 3 * head + 3]
-        for tile in tiles
+        jnp.sum(jnp.where(diagonal(rows), row, 0.0), axis=1, keepdims=True) for row in across
     ]
     top = functools.reduce(jnp.maximum, levels)
     weights = [jnp.exp2(level - top) for level in levels]
     share = 1.0 / functools.reduce(jnp.add, weights)
     mixed = functools.reduce(
-        jnp.add, [(w * share) * ref[:, columns].astype(F32) for w, ref in zip(weights, ins)]
+        jnp.add, [(w * share) * ref[pl.ds(0, rows), columns].astype(F32) for w, ref in zip(weights, ins)]
     )
     out[:, columns] = mixed.astype(BF16)
 
@@ -496,7 +509,7 @@
             last = swap(ready, 4, lambda z, s=s: (z ^ s ^ 1) < z)
             blocks[s ^ 1] = pass_on(last, prior_send)
     hops = [s for s in blocks if s not in near]
-    packed = (rows, wide + LANES)
+    packed = (rows + PAD, wide)
     part_send = look(hops, True, [shape(packed)], ((q_other, 1),), so_far[:2], "attend_far")
     part_keep = look(hops, True, [shape(packed, F32)], ((q_cross, 0),), so_far[2:], "attend_own")
     part_other = swap(part_send, 2)

time: 36.7 us -> 36.2 us (0.986)
  no operation moved by 1% of the time
where the time goes in v13:
time: 36.2 us; the launch traced here: 36 us
  starting transfers between devices  16.5 us (46%)
  waiting for transfers between devices  11.9 us (33%)
  Pallas kernels  6.92 us (19%)
  between operations  0.78 us (2%)
    ppermute x15, starting transfers between devices, swap(): return lax.ppermute(value, 'ctx', pairs)  13.9 us
    ppermute x15, waiting for transfers between devices, swap(): return lax.ppermute(value, 'ctx', pairs)  10.9 us
    pallas_call x16, Pallas kernels, call(): pl.pallas_call(kernel, out_shape=outs[0] if single else tuple(outs), in_s...  6.92 us
    ppermute x1, starting transfers between devices, to_head(): return lax.ppermute(value, 'head', [(y, (y + e) % n) for y in range(n)])  2.6 us
    ppermute x1, waiting for transfers between devices, to_head(): return lax.ppermute(value, 'head', [(y, (y + e) % n) for y in range(n)])  1 us
  transfers between devices with their start and end apart: 16, of which 9 were waited for; matrix products, arithmetic and copies ran while one was open for 0% of the time, Pallas kernels for 12%

profile of v13, /device:TPU:0, one launch (start us, length us, event | category | flops | bytes accessed | tf_op | source)
XLA Modules:
  0.0 36.0 jit_solution(13244099984799794830)
XLA Ops:
  0.6 1.8 %load_all.1 = (bf16[64,512]{1,0:T(8,128)(2,1)S(1)}, bf16[64,512]{1,0:T(8,128)(2,1)S(1)}, bf16[128,512]{1,0:T(8,128)(2,1)S(1)}, bf16[128,512]{1,0:T(8,128)(2,1)S(...) custom-call(bf16[64,512]{1,0:T(8,128)(2,1)} %refs_0_.1, ...), custom_call_target="tpu_custom_call" | custom-call | flops 1000 | bytes 1000 | tf_op jit(solution)/shard_map/load_all/pallas_call | solution.py:34
  2.4 0.5 %collective-permute-start = (bf16[144,512]{1,0:T(8,128)(2,1)S(1)}, bf16[144,512]{1,0:T(8,128)(2,1)S(1)}, u32[]{:S(2)}, u32[]{:S(2)}) collective-permute-start(bf16[144,512]{1,0:T(8,128)(2,1)S(1)} %get-tuple-element.32), channel_id=1, source_target_pairs={{2,0},{0,2},{6,4},{4,6},{10,8},{8,10},{14,12},{12,14},{18,16},{16,... | collective-permute-start | bytes 442376 | tf_op jit(solution)/shard_map/ppermute | solution.py:400
  2.9 2.6 %collective-permute-start.2 = (bf16[64,512]{1,0:T(8,128)(2,1)S(1)}, bf16[64,512]{1,0:T(8,128)(2,1)S(1)}, u32[]{:S(2)}, u32[]{:S(2)}) collective-permute-start(bf16[64,512]{1,0:T(8,128)(2,1)S(1)} %get-tuple-element.38), channel_id=1, source_target_pairs={{0,1},{1,0},{2,3},{3,2},{4,5},{5,4},{6,7},{7,6},{8,9},{9,8},{10,11... | collective-permute-start | bytes 196616 | tf_op jit(solution)/shard_map/ppermute | solution.py:403
  5.5 0.0 collective-permute-done.refs_1_
  5.5 0.1 chip_total.1
  5.6 1.6 %collective-permute-start.1 = (bf16[80,512]{1,0:T(8,128)(2,1)S(1)}, bf16[80,512]{1,0:T(8,128)(2,1)S(1)}, u32[]{:S(2)}, u32[]{:S(2)}) collective-permute-start(bf16[80,512]{1,0:T(8,128)(2,1)S(1)} %get-tuple-element.33.refs_4_), channel_id=1, source_target_pairs={{4,0},{6,2},{0,4},{2,6},{12,8},{14,10},{8,12},{10,14},{20,16},{22,... | collective-permute-start | bytes 245768 | tf_op jit(solution)/shard_map/ppermute | solution.py:400
  7.2 1.0 %collective-permute-done.2.refs_1_ = bf16[64,512]{1,0:T(8,128)(2,1)S(1)} collective-permute-done((bf16[64,512]{1,0:T(8,128)(2,1)S(1)}, bf16[64,512]{1,0:T(8,128)(2,1)S(1)}, u32[]{:S(2)}, u32[]{:S(2)}) %collective-permute-start.2) | collective-permute-done | bytes 65568 | tf_op jit(solution)/shard_map/ppermute | solution.py:403
  8.2 2.9 %collective-permute-start.4 = (bf16[128,512]{1,0:T(8,128)(2,1)S(1)}, bf16[128,512]{1,0:T(8,128)(2,1)S(1)}, u32[]{:S(2)}, u32[]{:S(2)}) collective-permute-start(bf16[128,512]{1,0:T(8,128)(2,1)S(1)} %join_rows.1.refs_2_), channel_id=1, source_target_pairs={{16,0},{18,2},{20,4},{22,6},{24,8},{26,10},{28,12},{30,14},{0,16},... | collective-permute-start | bytes 393224 | tf_op jit(solution)/shard_map/ppermute | solution.py:400
  11.1 0.6 %retain_inside.1 = (f32[128,512]{1,0:T(8,128)S(1)}, f32[128,2]{1,0:T(8,128)S(1)}) custom-call(bf16[128,512]{1,0:T(8,128)(2,1)S(1)} %get-tuple-element.26.refs_0_, bf16[128,512]{1,0:T(8,128)(2,1)S(1)} %get-tuple-element.28.refs_1_, bf16[128,512]{1,0:T(8,128)(2,1)S(1)} %get-tuple-element.29.refs_2_, f32[2,128]{1,0:T(2,128)S(1)} %get-tuple-element.30.refs_3_, ...), custom_call_target="tpu_custom_call" | custom-call | flops 1000 | bytes 1000 | tf_op jit(solution)/shard_map/retain_inside/pallas_call | solution.py:34
  11.7 0.0 collective-permute-done.1.refs_1_
  11.7 0.1 plane_total.1
  11.8 1.6 %collective-permute-start.5 = (bf16[128,512]{1,0:T(8,128)(2,1)S(1)}, bf16[128,512]{1,0:T(8,128)(2,1)S(1)}, u32[]{:S(2)}, u32[]{:S(2)}) collective-permute-start(bf16[128,512]{1,0:T(8,128)(2,1)S(1)} %get-tuple-element.40), channel_id=1, source_target_pairs={{8,0},{10,2},{12,4},{14,6},{0,8},{2,10},{4,12},{6,14},{24,16},{26,... | collective-permute-start | bytes 393224 | tf_op jit(solution)/shard_map/ppermute | solution.py:400
  13.4 0.4 %collective-permute-start.3 = (bf16[80,512]{1,0:T(8,128)(2,1)S(1)}, bf16[80,512]{1,0:T(8,128)(2,1)S(1)}, u32[]{:S(2)}, u32[]{:S(2)}) collective-permute-start(bf16[80,512]{1,0:T(8,128)(2,1)S(1)} %get-tuple-element.39.refs_0_), channel_id=1, source_target_pairs={{8,0},{10,2},{12,4},{14,6},{0,8},{2,10},{4,12},{6,14},{24,16},{26,... | collective-permute-start | bytes 245768 | tf_op jit(solution)/shard_map/ppermute | solution.py:400
  13.9 0.0 collective-permute-start.8
  13.9 3.5 %collective-permute-done.4.refs_2_.refs_1_.refs_4_.refs_0_ = bf16[128,512]{1,0:T(8,128)(2,1)S(1)} collective-permute-done((bf16[128,512]{1,0:T(8,128)(2,1)S(1)}, bf16[128,512]{1,0:T(8,128)(2,1)S(1)}, u32[]{:S(2)}, u32[]{:S(2)}) %collective-permute-start.4) | collective-permute-done | bytes 131104 | tf_op jit(solution)/shard_map/ppermute | solution.py:400
  17.4 1.5 %collective-permute-start.7 = (bf16[128,512]{1,0:T(8,128)(2,1)S(1)}, bf16[128,512]{1,0:T(8,128)(2,1)S(1)}, u32[]{:S(2)}, u32[]{:S(2)}) collective-permute-start(bf16[128,512]{1,0:T(8,128)(2,1)S(1)} %pass_on.2.refs_1_.refs_0_), channel_id=1, source_target_pairs={{4,0},{6,2},{0,4},{2,6},{12,8},{14,10},{8,12},{10,14},{20,16},{22,... | collective-permute-start | bytes 393224 | tf_op jit(solution)/shard_map/ppermute | solution.py:400
  18.9 0.0 collective-permute-start.9
  18.9 0.3 collective-permute-done.5.refs_3_.refs_6_
  19.2 0.2 collective-permute-start.10
  19.4 0.6 %collective-permute-done.3.refs_1_.refs_2_ = bf16[80,512]{1,0:T(8,128)(2,1)S(1)} collective-permute-done((bf16[80,512]{1,0:T(8,128)(2,1)S(1)}, bf16[80,512]{1,0:T(8,128)(2,1)S(1)}, u32[]{:S(2)}, u32[]{:S(2)}) %collective-permute-start.3) | collective-permute-done | bytes 81952 | tf_op jit(solution)/shard_map/ppermute | solution.py:400
  20.0 0.1 grow.1.refs_1_
  20.1 1.3 %collective-permute-start.6 = (bf16[80,512]{1,0:T(8,128)(2,1)S(1)}, bf16[80,512]{1,0:T(8,128)(2,1)S(1)}, u32[]{:S(2)}, u32[]{:S(2)}) collective-permute-start(bf16[80,512]{1,0:T(8,128)(2,1)S(1)} %grow.1.refs_1_), channel_id=1, source_target_pairs={{16,0},{18,2},{20,4},{22,6},{24,8},{26,10},{28,12},{30,14},{0,16},... | collective-permute-start | bytes 245768 | tf_op jit(solution)/shard_map/ppermute | solution.py:400
  21.4 0.0 collective-permute-done.8.refs_3_
  21.4 0.7 %collective-permute-start.13 = (bf16[128,512]{1,0:T(8,128)(2,1)S(1)}, bf16[128,512]{1,0:T(8,128)(2,1)S(1)}, u32[]{:S(2)}, u32[]{:S(2)}) collective-permute-start(bf16[128,512]{1,0:T(8,128)(2,1)S(1)} %shard_map.95), channel_id=1, source_target_pairs={{0,0},{2,2},{4,4},{6,6},{8,8},{10,10},{12,12},{14,14},{24,16},{26,... | collective-permute-start | bytes 393224 | tf_op jit(solution)/shard_map/ppermute | solution.py:400
  22.1 0.2 collective-permute-done.7.refs_0_
  22.3 0.0 collective-permute-done.9.refs_5_
  22.3 0.0 collective-permute-done.10.refs_7_
  22.3 1.0 %attend_near.1 = (f32[128,512]{1,0:T(8,128)S(1)}, f32[128,128]{1,0:T(8,128)S(1)}, f32[128,512]{1,0:T(8,128)S(1)}, f32[128,128]{1,0:T(8,128)S(1)}) custom-call(bf16[128,512]{1,0:T(8,128)(2,1)S(1)} %collective-permute-done.7.refs_0_, bf16[128,512]{1,0:T(8,128)(2,1)S(1)} %pass_on.2.refs_1_.refs_0_, bf16[128,512]{1,0:T(8,128)(2,1)S(1)} %join_rows.1.refs_2_, ...), custom_call_target="tpu_custom_call" | custom-call | flops 1000 | bytes 1000 | tf_op jit(solution)/shard_map/attend_near/pallas_call | solution.py:34
  23.4 3.4 %collective-permute-done.6.refs_3_ = bf16[80,512]{1,0:T(8,128)(2,1)S(1)} collective-permute-done((bf16[80,512]{1,0:T(8,128)(2,1)S(1)}, bf16[80,512]{1,0:T(8,128)(2,1)S(1)}, u32[]{:S(2)}, u32[]{:S(2)}) %collective-permute-start.6) | collective-permute-done | bytes 81952 | tf_op jit(solution)/shard_map/ppermute | solution.py:400
  26.8 0.1 chip_priors.1
  26.9 0.0 collective-permute-done.13.refs_0_
  26.9 0.1 collective-permute-start.14
  27.0 1.6 %collective-permute-start.11 = (bf16[64,512]{1,0:T(8,128)(2,1)S(1)}, bf16[64,512]{1,0:T(8,128)(2,1)S(1)}, u32[]{:S(2)}, u32[]{:S(2)}) collective-permute-start(bf16[64,512]{1,0:T(8,128)(2,1)S(1)} %get-tuple-element.44.refs_1_), channel_id=1, source_target_pairs={{4,0},{6,2},{0,4},{2,6},{12,8},{14,10},{8,12},{10,14},{20,16},{22,... | collective-permute-start | bytes 196616 | tf_op jit(solution)/shard_map/ppermute | solution.py:400
  28.6 0.0 collective-permute-done.14.refs_2_
  28.6 0.6 %attend_far.1 = bf16[144,512]{1,0:T(8,128)(2,1)S(1)} custom-call(bf16[128,512]{1,0:T(8,128)(2,1)S(1)} %collective-permute-done.7.refs_0_, bf16[128,512]{1,0:T(8,128)(2,1)S(1)} %pass_on.3.refs_1_, bf16[128,512]{1,0:T(8,128)(2,1)S(1)} %collective-permute-done.14.refs_2_, f32[128,512]{1,0:T(8,128)S(1)} %get-tuple-element.49.refs_3_, ...), custom_call_target="tpu_custom_call" | custom-call | flops 1000 | bytes 1000 | tf_op jit(solution)/shard_map/attend_far/pallas_call | solution.py:34
  29.2 1.3 %collective-permute-start.15 = (bf16[144,512]{1,0:T(8,128)(2,1)S(1)}, bf16[144,512]{1,0:T(8,128)(2,1)S(1)}, u32[]{:S(2)}, u32[]{:S(2)}) collective-permute-start(bf16[144,512]{1,0:T(8,128)(2,1)S(1)} %attend_far.1), channel_id=1, source_target_pairs={{4,0},{6,2},{0,4},{2,6},{12,8},{14,10},{8,12},{10,14},{20,16},{22,... | collective-permute-start | bytes 442376 | tf_op jit(solution)/shard_map/ppermute | solution.py:400
  30.5 1.0 %collective-permute-done.11.refs_3_ = bf16[64,512]{1,0:T(8,128)(2,1)S(1)} collective-permute-done((bf16[64,512]{1,0:T(8,128)(2,1)S(1)}, bf16[64,512]{1,0:T(8,128)(2,1)S(1)}, u32[]{:S(2)}, u32[]{:S(2)}) %collective-permute-start.11) | collective-permute-done | bytes 65568 | tf_op jit(solution)/shard_map/ppermute | solution.py:400
  31.5 0.1 block_priors.1
  31.7 0.1 collective-permute-start.12
  31.7 0.6 %attend_own.1.refs_0_ = f32[144,512]{1,0:T(8,128)S(1)} custom-call(bf16[128,512]{1,0:T(8,128)(2,1)S(1)} %pass_on.2.refs_1_.refs_0_, bf16[128,512]{1,0:T(8,128)(2,1)S(1)} %pass_on.3.refs_1_, bf16[128,512]{1,0:T(8,128)(2,1)S(1)} %collective-permute-done.14.refs_2_, f32[128,512]{1,0:T(8,128)S(1)} %get-tuple-element.47.refs_3_, ...), custom_call_target="tpu_custom_call" | custom-call | flops 1000 | bytes 1000 | tf_op jit(solution)/shard_map/attend_own/pallas_call | solution.py:34
  32.3 0.7 %collective-permute-done.12.refs_5_ = bf16[128,512]{1,0:T(8,128)(2,1)S(1)} collective-permute-done((bf16[128,512]{1,0:T(8,128)(2,1)S(1)}, bf16[128,512]{1,0:T(8,128)(2,1)S(1)}, u32[]{:S(2)}, u32[]{:S(2)}) %collective-permute-start.12) | collective-permute-done | bytes 131104 | tf_op jit(solution)/shard_map/ppermute | solution.py:400
  33.1 1.0 %retain_finish.1 = bf16[128,512]{1,0:T(8,128)(2,1)} custom-call(bf16[128,512]{1,0:T(8,128)(2,1)S(1)} %get-tuple-element.26.refs_0_, bf16[128,512]{1,0:T(8,128)(2,1)S(1)} %get-tuple-element.27.refs_1_, f32[128,512]{1,0:T(8,128)S(1)} %get-tuple-element.34.refs_2_, f32[128,2]{1,0:T(8,128)S(1)} %get-tuple-element.35.refs_3_, ...), custom_call_target="tpu_custom_call" | custom-call | flops 1000 | bytes 1000 | tf_op jit(solution)/shard_map/retain_finish/pallas_call | solution.py:34
  34.1 1.1 %collective-permute-done.15.refs_1_ = bf16[144,512]{1,0:T(8,128)(2,1)S(1)} collective-permute-done((bf16[144,512]{1,0:T(8,128)(2,1)S(1)}, bf16[144,512]{1,0:T(8,128)(2,1)S(1)}, u32[]{:S(2)}, u32[]{:S(2)}) %collective-permute-start.15) | collective-permute-done | bytes 147488 | tf_op jit(solution)/shard_map/ppermute | solution.py:400
  35.2 0.8 %finish.1 = bf16[128,512]{1,0:T(8,128)(2,1)} custom-call(f32[144,512]{1,0:T(8,128)S(1)} %attend_own.1.refs_0_, bf16[144,512]{1,0:T(8,128)(2,1)S(1)} %collective-permute-done.15.refs_1_), custom_call_target="tpu_custom_call" | custom-call | flops 1000 | bytes 1000 | tf_op jit(solution)/shard_map/finish/pallas_call | solution.py:34
  (4 shorter events, 0.0 us)
Async XLA Ops:
  2.4 3.1 %collective-permute-start = (bf16[144,512]{1,0:T(8,128)(2,1)S(1)}, bf16[144,512]{1,0:T(8,128)(2,1)S(1)}, u32[]{:S(2)}, u32[]{:S(2)}) collective-permute-start(bf16[144,512]{1,0:T(8,128)(2,1)S(1)} %get-tuple-element.32), channel_id=1, source_target_pairs={{2,0},{0,2},{6,4},{4,6},{10,8},{8,10},{14,12},{12,14},{18,16},{16,... | collective-permute-start | bytes 442376 | tf_op jit(solution)/shard_map/ppermute | solution.py:400
  2.9 5.3 %collective-permute-start.2 = (bf16[64,512]{1,0:T(8,128)(2,1)S(1)}, bf16[64,512]{1,0:T(8,128)(2,1)S(1)}, u32[]{:S(2)}, u32[]{:S(2)}) collective-permute-start(bf16[64,512]{1,0:T(8,128)(2,1)S(1)} %get-tuple-element.38), channel_id=1, source_target_pairs={{0,1},{1,0},{2,3},{3,2},{4,5},{5,4},{6,7},{7,6},{8,9},{9,8},{10,11... | collective-permute-start | bytes 196616 | tf_op jit(solution)/shard_map/ppermute | solution.py:403
  5.6 6.1 %collective-permute-start.1 = (bf16[80,512]{1,0:T(8,128)(2,1)S(1)}, bf16[80,512]{1,0:T(8,128)(2,1)S(1)}, u32[]{:S(2)}, u32[]{:S(2)}) collective-permute-start(bf16[80,512]{1,0:T(8,128)(2,1)S(1)} %get-tuple-element.33.refs_4_), channel_id=1, source_target_pairs={{4,0},{6,2},{0,4},{2,6},{12,8},{14,10},{8,12},{10,14},{20,16},{22,... | collective-permute-start | bytes 245768 | tf_op jit(solution)/shard_map/ppermute | solution.py:400
  8.2 9.1 %collective-permute-start.4 = (bf16[128,512]{1,0:T(8,128)(2,1)S(1)}, bf16[128,512]{1,0:T(8,128)(2,1)S(1)}, u32[]{:S(2)}, u32[]{:S(2)}) collective-permute-start(bf16[128,512]{1,0:T(8,128)(2,1)S(1)} %join_rows.1.refs_2_), channel_id=1, source_target_pairs={{16,0},{18,2},{20,4},{22,6},{24,8},{26,10},{28,12},{30,14},{0,16},... | collective-permute-start | bytes 393224 | tf_op jit(solution)/shard_map/ppermute | solution.py:400
  11.8 7.4 %collective-permute-start.5 = (bf16[128,512]{1,0:T(8,128)(2,1)S(1)}, bf16[128,512]{1,0:T(8,128)(2,1)S(1)}, u32[]{:S(2)}, u32[]{:S(2)}) collective-permute-start(bf16[128,512]{1,0:T(8,128)(2,1)S(1)} %get-tuple-element.40), channel_id=1, source_target_pairs={{8,0},{10,2},{12,4},{14,6},{0,8},{2,10},{4,12},{6,14},{24,16},{26,... | collective-permute-start | bytes 393224 | tf_op jit(solution)/shard_map/ppermute | solution.py:400
  13.4 6.6 %collective-permute-start.3 = (bf16[80,512]{1,0:T(8,128)(2,1)S(1)}, bf16[80,512]{1,0:T(8,128)(2,1)S(1)}, u32[]{:S(2)}, u32[]{:S(2)}) collective-permute-start(bf16[80,512]{1,0:T(8,128)(2,1)S(1)} %get-tuple-element.39.refs_0_), channel_id=1, source_target_pairs={{8,0},{10,2},{12,4},{14,6},{0,8},{2,10},{4,12},{6,14},{24,16},{26,... | collective-permute-start | bytes 245768 | tf_op jit(solution)/shard_map/ppermute | solution.py:400
  13.9 7.5 %collective-permute-start.8 = (bf16[128,512]{1,0:T(8,128)(2,1)S(1)}, bf16[128,512]{1,0:T(8,128)(2,1)S(1)}, u32[]{:S(2)}, u32[]{:S(2)}) collective-permute-start(bf16[128,512]{1,0:T(8,128)(2,1)S(1)} %join_rows.1.refs_2_), channel_id=1, source_target_pairs={{2,0},{0,2},{6,4},{4,6},{10,8},{8,10},{14,12},{12,14},{18,16},{16,... | collective-permute-start | bytes 393224 | tf_op jit(solution)/shard_map/ppermute | solution.py:400
  17.4 5.0 %collective-permute-start.7 = (bf16[128,512]{1,0:T(8,128)(2,1)S(1)}, bf16[128,512]{1,0:T(8,128)(2,1)S(1)}, u32[]{:S(2)}, u32[]{:S(2)}) collective-permute-start(bf16[128,512]{1,0:T(8,128)(2,1)S(1)} %pass_on.2.refs_1_.refs_0_), channel_id=1, source_target_pairs={{4,0},{6,2},{0,4},{2,6},{12,8},{14,10},{8,12},{10,14},{20,16},{22,... | collective-permute-start | bytes 393224 | tf_op jit(solution)/shard_map/ppermute | solution.py:400
  18.9 3.4 %collective-permute-start.9 = (bf16[128,512]{1,0:T(8,128)(2,1)S(1)}, bf16[128,512]{1,0:T(8,128)(2,1)S(1)}, u32[]{:S(2)}, u32[]{:S(2)}) collective-permute-start(bf16[128,512]{1,0:T(8,128)(2,1)S(1)} %collective-permute-done.4.refs_2_.refs_1_.refs_4_.refs_0_), channel_id=1, source_target_pairs={{2,0},{0,2},{6,4},{4,6},{10,8},{8,10},{14,12},{12,14},{18,16},{16,... | collective-permute-start | bytes 393224 | tf_op jit(solution)/shard_map/ppermute | solution.py:400
  19.2 3.2 %collective-permute-start.10 = (bf16[128,512]{1,0:T(8,128)(2,1)S(1)}, bf16[128,512]{1,0:T(8,128)(2,1)S(1)}, u32[]{:S(2)}, u32[]{:S(2)}) collective-permute-start(bf16[128,512]{1,0:T(8,128)(2,1)S(1)} %collective-permute-done.5.refs_3_.refs_6_), channel_id=1, source_target_pairs={{2,0},{0,2},{6,4},{4,6},{10,8},{8,10},{14,12},{12,14},{18,16},{16,... | collective-permute-start | bytes 393224 | tf_op jit(solution)/shard_map/ppermute | solution.py:400
  20.1 6.7 %collective-permute-start.6 = (bf16[80,512]{1,0:T(8,128)(2,1)S(1)}, bf16[80,512]{1,0:T(8,128)(2,1)S(1)}, u32[]{:S(2)}, u32[]{:S(2)}) collective-permute-start(bf16[80,512]{1,0:T(8,128)(2,1)S(1)} %grow.1.refs_1_), channel_id=1, source_target_pairs={{16,0},{18,2},{20,4},{22,6},{24,8},{26,10},{28,12},{30,14},{0,16},... | collective-permute-start | bytes 245768 | tf_op jit(solution)/shard_map/ppermute | solution.py:400
  21.4 5.5 %collective-permute-start.13 = (bf16[128,512]{1,0:T(8,128)(2,1)S(1)}, bf16[128,512]{1,0:T(8,128)(2,1)S(1)}, u32[]{:S(2)}, u32[]{:S(2)}) collective-permute-start(bf16[128,512]{1,0:T(8,128)(2,1)S(1)} %shard_map.95), channel_id=1, source_target_pairs={{0,0},{2,2},{4,4},{6,6},{8,8},{10,10},{12,12},{14,14},{24,16},{26,... | collective-permute-start | bytes 393224 | tf_op jit(solution)/shard_map/ppermute | solution.py:400
  26.9 1.7 %collective-permute-start.14 = (bf16[128,512]{1,0:T(8,128)(2,1)S(1)}, bf16[128,512]{1,0:T(8,128)(2,1)S(1)}, u32[]{:S(2)}, u32[]{:S(2)}) collective-permute-start(bf16[128,512]{1,0:T(8,128)(2,1)S(1)} %pass_on.3.refs_1_), channel_id=1, source_target_pairs={{2,0},{0,2},{6,4},{4,6},{10,8},{8,10},{14,12},{12,14},{18,16},{16,... | collective-permute-start | bytes 393224 | tf_op jit(solution)/shard_map/ppermute | solution.py:400
  27.0 4.5 %collective-permute-start.11 = (bf16[64,512]{1,0:T(8,128)(2,1)S(1)}, bf16[64,512]{1,0:T(8,128)(2,1)S(1)}, u32[]{:S(2)}, u32[]{:S(2)}) collective-permute-start(bf16[64,512]{1,0:T(8,128)(2,1)S(1)} %get-tuple-element.44.refs_1_), channel_id=1, source_target_pairs={{4,0},{6,2},{0,4},{2,6},{12,8},{14,10},{8,12},{10,14},{20,16},{22,... | collective-permute-start | bytes 196616 | tf_op jit(solution)/shard_map/ppermute | solution.py:400
  29.2 6.0 %collective-permute-start.15 = (bf16[144,512]{1,0:T(8,128)(2,1)S(1)}, bf16[144,512]{1,0:T(8,128)(2,1)S(1)}, u32[]{:S(2)}, u32[]{:S(2)}) collective-permute-start(bf16[144,512]{1,0:T(8,128)(2,1)S(1)} %attend_far.1), channel_id=1, source_target_pairs={{4,0},{6,2},{0,4},{2,6},{12,8},{14,10},{8,12},{10,14},{20,16},{22,... | collective-permute-start | bytes 442376 | tf_op jit(solution)/shard_map/ppermute | solution.py:400
  31.7 1.4 %collective-permute-start.12 = (bf16[128,512]{1,0:T(8,128)(2,1)S(1)}, bf16[128,512]{1,0:T(8,128)(2,1)S(1)}, u32[]{:S(2)}, u32[]{:S(2)}) collective-permute-start(bf16[128,512]{1,0:T(8,128)(2,1)S(1)} %get-tuple-element.46), channel_id=1, source_target_pairs={{2,0},{0,2},{6,4},{4,6},{10,8},{8,10},{14,12},{12,14},{18,16},{16,... | collective-permute-start | bytes 393224 | tf_op jit(solution)/shard_map/ppermute | solution.py:400

commit v14 on v13

--- a/solution.py
+++ b/solution.py
@@ -424,13 +424,6 @@
         scratch=[pltpu.VMEM((half, wide), F32)],
         name="chip_total",
     )
-    inside, factor = call(
-        retain_inside,
-        [shape((rows, wide), F32), shape((rows, heads), F32)],
-        (q_ret, k_ret, v_ret, decays),
-        name="retain_inside",
-        after=(chip_send,),
-    )
     blocks = {
         0: call(
             functools.partial(join_rows, n),
@@ -451,7 +444,6 @@
         [shape((quarter + PAD, wide)), shape(blocks[0].shape)],
         (chip_keep, chip_other, blocks[0]),
         name="plane_total",
-        after=(factor,),
     )
     blocks[1] = swap(handed, 4)
     q_cross = pass_on(q_cross, blocks[far // 2])
@@ -495,13 +487,20 @@
         (),
         "attend_near",
     )
+    inside, factor = call(
+        retain_inside,
+        [shape((rows, wide), F32), shape((rows, heads), F32)],
+        (q_ret, k_ret, v_ret, decays),
+        name="retain_inside",
+        after=so_far[1:2],
+    )
     prior_send, prior_keep = call(
         chip_priors,
         [shape((quarter, wide)), shape((quarter, wide), F32)],
         (chip_keep, chip_other, *planes),
         name="chip_priors",
         flops=3000000000,
-        after=so_far[1:2],
+        after=(so_far[1], factor),
     )
     for s in near:
         if s > 1:

time: 36.2 us -> 35.8 us (0.989)
  waiting for transfers between devices: 11.9 us -> 10.7 us
  starting transfers between devices: 16.5 us -> 17.2 us
    ppermute x15, waiting for transfers between devices: 10.9 us -> 9.71 us  [swap(): return lax.ppermute(value, 'ctx', pairs)]
    ppermute x15, starting transfers between devices: 13.9 us -> 14.6 us  [swap(): return lax.ppermute(value, 'ctx', pairs)]
  transfers between devices with their start and end apart: 16 -> 16, of which waited for: 9 -> 7; matrix products, arithmetic and copies ran while one was open for 0% -> 0% of each run, Pallas kernels for 12% -> 12%
where the time goes in v14:
time: 35.8 us; the launch traced here: 35.6 us
  starting transfers between devices  17.2 us (48%)
  waiting for transfers between devices  10.7 us (30%)
  Pallas kernels  6.92 us (19%)
  between operations  0.77 us (2%)
    ppermute x15, starting transfers between devices, swap(): return lax.ppermute(value, 'ctx', pairs)  14.6 us
    ppermute x15, waiting for transfers between devices, swap(): return lax.ppermute(value, 'ctx', pairs)  9.71 us
    pallas_call x16, Pallas kernels, call(): pl.pallas_call(kernel, out_shape=outs[0] if single else tuple(outs), in_s...  6.92 us
    ppermute x1, starting transfers between devices, to_head(): return lax.ppermute(value, 'head', [(y, (y + e) % n) for y in range(n)])  2.6 us
    ppermute x1, waiting for transfers between devices, to_head(): return lax.ppermute(value, 'head', [(y, (y + e) % n) for y in range(n)])  1 us
  transfers between devices with their start and end apart: 16, of which 7 were waited for; matrix products, arithmetic and copies ran while one was open for 0% of the time, Pallas kernels for 12%

profile of v14, /device:TPU:0, one launch (start us, length us, event | category | flops | bytes accessed | tf_op | source)
XLA Modules:
  0.0 35.6 jit_solution(11629425182438729181)
XLA Ops:
  0.6 1.8 %load_all.1 = (bf16[64,512]{1,0:T(8,128)(2,1)S(1)}, bf16[64,512]{1,0:T(8,128)(2,1)S(1)}, bf16[128,512]{1,0:T(8,128)(2,1)S(1)}, bf16[128,512]{1,0:T(8,128)(2,1)S(...) custom-call(bf16[64,512]{1,0:T(8,128)(2,1)} %refs_0_.1, ...), custom_call_target="tpu_custom_call" | custom-call | flops 1000 | bytes 1000 | tf_op jit(solution)/shard_map/load_all/pallas_call | solution.py:34
  2.4 0.5 %collective-permute-start.5 = (bf16[144,512]{1,0:T(8,128)(2,1)S(1)}, bf16[144,512]{1,0:T(8,128)(2,1)S(1)}, u32[]{:S(2)}, u32[]{:S(2)}) collective-permute-start(bf16[144,512]{1,0:T(8,128)(2,1)S(1)} %get-tuple-element.35), channel_id=1, source_target_pairs={{2,0},{0,2},{6,4},{4,6},{10,8},{8,10},{14,12},{12,14},{18,16},{16,... | collective-permute-start | bytes 442376 | tf_op jit(solution)/shard_map/ppermute | solution.py:400
  2.9 2.6 %collective-permute-start = (bf16[64,512]{1,0:T(8,128)(2,1)S(1)}, bf16[64,512]{1,0:T(8,128)(2,1)S(1)}, u32[]{:S(2)}, u32[]{:S(2)}) collective-permute-start(bf16[64,512]{1,0:T(8,128)(2,1)S(1)} %get-tuple-element.33), channel_id=1, source_target_pairs={{0,1},{1,0},{2,3},{3,2},{4,5},{5,4},{6,7},{7,6},{8,9},{9,8},{10,11... | collective-permute-start | bytes 196616 | tf_op jit(solution)/shard_map/ppermute | solution.py:403
  5.5 0.0 collective-permute-done.5.refs_1_
  5.5 0.1 chip_total.1
  5.6 1.6 %collective-permute-start.6 = (bf16[80,512]{1,0:T(8,128)(2,1)S(1)}, bf16[80,512]{1,0:T(8,128)(2,1)S(1)}, u32[]{:S(2)}, u32[]{:S(2)}) collective-permute-start(bf16[80,512]{1,0:T(8,128)(2,1)S(1)} %get-tuple-element.37), channel_id=1, source_target_pairs={{4,0},{6,2},{0,4},{2,6},{12,8},{14,10},{8,12},{10,14},{20,16},{22,... | collective-permute-start | bytes 245768 | tf_op jit(solution)/shard_map/ppermute | solution.py:400
  7.2 1.0 %collective-permute-done.refs_1_ = bf16[64,512]{1,0:T(8,128)(2,1)S(1)} collective-permute-done((bf16[64,512]{1,0:T(8,128)(2,1)S(1)}, bf16[64,512]{1,0:T(8,128)(2,1)S(1)}, u32[]{:S(2)}, u32[]{:S(2)}) %collective-permute-start) | collective-permute-done | bytes 65568 | tf_op jit(solution)/shard_map/ppermute | solution.py:403
  8.2 2.9 %collective-permute-start.1 = (bf16[128,512]{1,0:T(8,128)(2,1)S(1)}, bf16[128,512]{1,0:T(8,128)(2,1)S(1)}, u32[]{:S(2)}, u32[]{:S(2)}) collective-permute-start(bf16[128,512]{1,0:T(8,128)(2,1)S(1)} %join_rows.1.refs_2_), channel_id=1, source_target_pairs={{16,0},{18,2},{20,4},{22,6},{24,8},{26,10},{28,12},{30,14},{0,16},... | collective-permute-start | bytes 393224 | tf_op jit(solution)/shard_map/ppermute | solution.py:400
  11.1 0.0 collective-permute-done.6.refs_1_
  11.1 0.1 plane_total.1
  11.2 1.6 %collective-permute-start.7 = (bf16[128,512]{1,0:T(8,128)(2,1)S(1)}, bf16[128,512]{1,0:T(8,128)(2,1)S(1)}, u32[]{:S(2)}, u32[]{:S(2)}) collective-permute-start(bf16[128,512]{1,0:T(8,128)(2,1)S(1)} %get-tuple-element.38), channel_id=1, source_target_pairs={{8,0},{10,2},{12,4},{14,6},{0,8},{2,10},{4,12},{6,14},{24,16},{26,... | collective-permute-start | bytes 393224 | tf_op jit(solution)/shard_map/ppermute | solution.py:400
  12.8 0.4 %collective-permute-start.9 = (bf16[80,512]{1,0:T(8,128)(2,1)S(1)}, bf16[80,512]{1,0:T(8,128)(2,1)S(1)}, u32[]{:S(2)}, u32[]{:S(2)}) collective-permute-start(bf16[80,512]{1,0:T(8,128)(2,1)S(1)} %get-tuple-element.42.refs_0_), channel_id=1, source_target_pairs={{8,0},{10,2},{12,4},{14,6},{0,8},{2,10},{4,12},{6,14},{24,16},{26,... | collective-permute-start | bytes 245768 | tf_op jit(solution)/shard_map/ppermute | solution.py:400
  13.3 0.0 collective-permute-start.3
  13.3 4.1 %collective-permute-done.1.refs_1_.refs_4_.refs_2_.refs_0_ = bf16[128,512]{1,0:T(8,128)(2,1)S(1)} collective-permute-done((bf16[128,512]{1,0:T(8,128)(2,1)S(1)}, bf16[128,512]{1,0:T(8,128)(2,1)S(1)}, u32[]{:S(2)}, u32[]{:S(2)}) %collective-permute-start.1) | collective-permute-done | bytes 131104 | tf_op jit(solution)/shard_map/ppermute | solution.py:400
  17.3 1.5 %collective-permute-start.2 = (bf16[128,512]{1,0:T(8,128)(2,1)S(1)}, bf16[128,512]{1,0:T(8,128)(2,1)S(1)}, u32[]{:S(2)}, u32[]{:S(2)}) collective-permute-start(bf16[128,512]{1,0:T(8,128)(2,1)S(1)} %pass_on.2.refs_1_.refs_0_), channel_id=1, source_target_pairs={{4,0},{6,2},{0,4},{2,6},{12,8},{14,10},{8,12},{10,14},{20,16},{22,... | collective-permute-start | bytes 393224 | tf_op jit(solution)/shard_map/ppermute | solution.py:400
  18.9 0.0 collective-permute-start.4
  18.9 0.0 collective-permute-done.7.refs_6_.refs_3_
  18.9 0.5 %collective-permute-start.8 = (bf16[128,512]{1,0:T(8,128)(2,1)S(1)}, bf16[128,512]{1,0:T(8,128)(2,1)S(1)}, u32[]{:S(2)}, u32[]{:S(2)}) collective-permute-start(bf16[128,512]{1,0:T(8,128)(2,1)S(1)} %collective-permute-done.7.refs_6_.refs_3_), channel_id=1, source_target_pairs={{2,0},{0,2},{6,4},{4,6},{10,8},{8,10},{14,12},{12,14},{18,16},{16,... | collective-permute-start | bytes 393224 | tf_op jit(solution)/shard_map/ppermute | solution.py:400
  19.4 0.0 collective-permute-done.9.refs_1_.refs_2_
  19.4 0.1 grow.1.refs_1_
  19.5 1.9 %collective-permute-start.10 = (bf16[80,512]{1,0:T(8,128)(2,1)S(1)}, bf16[80,512]{1,0:T(8,128)(2,1)S(1)}, u32[]{:S(2)}, u32[]{:S(2)}) collective-permute-start(bf16[80,512]{1,0:T(8,128)(2,1)S(1)} %grow.1.refs_1_), channel_id=1, source_target_pairs={{16,0},{18,2},{20,4},{22,6},{24,8},{26,10},{28,12},{30,14},{0,16},... | collective-permute-start | bytes 245768 | tf_op jit(solution)/shard_map/ppermute | solution.py:400
  21.4 0.0 collective-permute-done.3.refs_3_
  21.4 0.7 %collective-permute-start.13 = (bf16[128,512]{1,0:T(8,128)(2,1)S(1)}, bf16[128,512]{1,0:T(8,128)(2,1)S(1)}, u32[]{:S(2)}, u32[]{:S(2)}) collective-permute-start(bf16[128,512]{1,0:T(8,128)(2,1)S(1)} %shard_map.95), channel_id=1, source_target_pairs={{0,0},{2,2},{4,4},{6,6},{8,8},{10,10},{12,12},{14,14},{24,16},{26,... | collective-permute-start | bytes 393224 | tf_op jit(solution)/shard_map/ppermute | solution.py:400
  22.1 0.2 collective-permute-done.2.refs_0_
  22.3 0.0 collective-permute-done.4.refs_5_
  22.3 0.0 collective-permute-done.8.refs_7_
  22.3 1.0 %attend_near.1 = (f32[128,512]{1,0:T(8,128)S(1)}, f32[128,128]{1,0:T(8,128)S(1)}, f32[128,512]{1,0:T(8,128)S(1)}, f32[128,128]{1,0:T(8,128)S(1)}) custom-call(bf16[128,512]{1,0:T(8,128)(2,1)S(1)} %collective-permute-done.2.refs_0_, bf16[128,512]{1,0:T(8,128)(2,1)S(1)} %pass_on.2.refs_1_.refs_0_, bf16[128,512]{1,0:T(8,128)(2,1)S(1)} %join_rows.1.refs_2_, ...), custom_call_target="tpu_custom_call" | custom-call | flops 1000 | bytes 1000 | tf_op jit(solution)/shard_map/attend_near/pallas_call | solution.py:34
  23.4 0.6 %retain_inside.1 = (f32[128,512]{1,0:T(8,128)S(1)}, f32[128,2]{1,0:T(8,128)S(1)}) custom-call(bf16[128,512]{1,0:T(8,128)(2,1)S(1)} %get-tuple-element.26.refs_0_, bf16[128,512]{1,0:T(8,128)(2,1)S(1)} %get-tuple-element.28.refs_1_, bf16[128,512]{1,0:T(8,128)(2,1)S(1)} %get-tuple-element.29.refs_2_, f32[2,128]{1,0:T(2,128)S(1)} %get-tuple-element.30.refs_3_, ...), custom_call_target="tpu_custom_call" | custom-call | flops 1000 | bytes 1000 | tf_op jit(solution)/shard_map/retain_inside/pallas_call | solution.py:34
  24.0 2.6 %collective-permute-done.10.refs_3_ = bf16[80,512]{1,0:T(8,128)(2,1)S(1)} collective-permute-done((bf16[80,512]{1,0:T(8,128)(2,1)S(1)}, bf16[80,512]{1,0:T(8,128)(2,1)S(1)}, u32[]{:S(2)}, u32[]{:S(2)}) %collective-permute-start.10) | collective-permute-done | bytes 81952 | tf_op jit(solution)/shard_map/ppermute | solution.py:400
  26.6 0.1 chip_priors.1
  26.6 0.0 collective-permute-done.13.refs_0_
  26.7 0.1 collective-permute-start.14
  26.7 1.5 %collective-permute-start.11 = (bf16[64,512]{1,0:T(8,128)(2,1)S(1)}, bf16[64,512]{1,0:T(8,128)(2,1)S(1)}, u32[]{:S(2)}, u32[]{:S(2)}) collective-permute-start(bf16[64,512]{1,0:T(8,128)(2,1)S(1)} %get-tuple-element.44.refs_1_), channel_id=1, source_target_pairs={{4,0},{6,2},{0,4},{2,6},{12,8},{14,10},{8,12},{10,14},{20,16},{22,... | collective-permute-start | bytes 196616 | tf_op jit(solution)/shard_map/ppermute | solution.py:400
  28.2 0.0 collective-permute-done.14.refs_2_
  28.2 0.6 %attend_far.1 = bf16[144,512]{1,0:T(8,128)(2,1)S(1)} custom-call(bf16[128,512]{1,0:T(8,128)(2,1)S(1)} %collective-permute-done.2.refs_0_, bf16[128,512]{1,0:T(8,128)(2,1)S(1)} %pass_on.3.refs_1_, bf16[128,512]{1,0:T(8,128)(2,1)S(1)} %collective-permute-done.14.refs_2_, f32[128,512]{1,0:T(8,128)S(1)} %get-tuple-element.49.refs_3_, ...), custom_call_target="tpu_custom_call" | custom-call | flops 1000 | bytes 1000 | tf_op jit(solution)/shard_map/attend_far/pallas_call | solution.py:34
  28.8 1.3 %collective-permute-start.15 = (bf16[144,512]{1,0:T(8,128)(2,1)S(1)}, bf16[144,512]{1,0:T(8,128)(2,1)S(1)}, u32[]{:S(2)}, u32[]{:S(2)}) collective-permute-start(bf16[144,512]{1,0:T(8,128)(2,1)S(1)} %attend_far.1), channel_id=1, source_target_pairs={{4,0},{6,2},{0,4},{2,6},{12,8},{14,10},{8,12},{10,14},{20,16},{22,... | collective-permute-start | bytes 442376 | tf_op jit(solution)/shard_map/ppermute | solution.py:400
  30.1 1.1 %collective-permute-done.11.refs_3_ = bf16[64,512]{1,0:T(8,128)(2,1)S(1)} collective-permute-done((bf16[64,512]{1,0:T(8,128)(2,1)S(1)}, bf16[64,512]{1,0:T(8,128)(2,1)S(1)}, u32[]{:S(2)}, u32[]{:S(2)}) %collective-permute-start.11) | collective-permute-done | bytes 65568 | tf_op jit(solution)/shard_map/ppermute | solution.py:400
  31.2 0.1 block_priors.1
  31.4 0.1 collective-permute-start.12
  31.5 0.6 %attend_own.1.refs_0_ = f32[144,512]{1,0:T(8,128)S(1)} custom-call(bf16[128,512]{1,0:T(8,128)(2,1)S(1)} %pass_on.2.refs_1_.refs_0_, bf16[128,512]{1,0:T(8,128)(2,1)S(1)} %pass_on.3.refs_1_, bf16[128,512]{1,0:T(8,128)(2,1)S(1)} %collective-permute-done.14.refs_2_, f32[128,512]{1,0:T(8,128)S(1)} %get-tuple-element.47.refs_3_, ...), custom_call_target="tpu_custom_call" | custom-call | flops 1000 | bytes 1000 | tf_op jit(solution)/shard_map/attend_own/pallas_call | solution.py:34
  32.1 0.7 %collective-permute-done.12.refs_5_ = bf16[128,512]{1,0:T(8,128)(2,1)S(1)} collective-permute-done((bf16[128,512]{1,0:T(8,128)(2,1)S(1)}, bf16[128,512]{1,0:T(8,128)(2,1)S(1)}, u32[]{:S(2)}, u32[]{:S(2)}) %collective-permute-start.12) | collective-permute-done | bytes 131104 | tf_op jit(solution)/shard_map/ppermute | solution.py:400
  32.8 1.0 %retain_finish.1 = bf16[128,512]{1,0:T(8,128)(2,1)} custom-call(bf16[128,512]{1,0:T(8,128)(2,1)S(1)} %get-tuple-element.26.refs_0_, bf16[128,512]{1,0:T(8,128)(2,1)S(1)} %get-tuple-element.27.refs_1_, f32[128,512]{1,0:T(8,128)S(1)} %get-tuple-element.40.refs_2_, f32[128,2]{1,0:T(8,128)S(1)} %get-tuple-element.41.refs_5_.refs_3_, ...), custom_call_target="tpu_custom_call" | custom-call | flops 1000 | bytes 1000 | tf_op jit(solution)/shard_map/retain_finish/pallas_call | solution.py:34
  33.8 1.0 %collective-permute-done.15.refs_1_ = bf16[144,512]{1,0:T(8,128)(2,1)S(1)} collective-permute-done((bf16[144,512]{1,0:T(8,128)(2,1)S(1)}, bf16[144,512]{1,0:T(8,128)(2,1)S(1)}, u32[]{:S(2)}, u32[]{:S(2)}) %collective-permute-start.15) | collective-permute-done | bytes 147488 | tf_op jit(solution)/shard_map/ppermute | solution.py:400
  34.8 0.8 %finish.1 = bf16[128,512]{1,0:T(8,128)(2,1)} custom-call(f32[144,512]{1,0:T(8,128)S(1)} %attend_own.1.refs_0_, bf16[144,512]{1,0:T(8,128)(2,1)S(1)} %collective-permute-done.15.refs_1_), custom_call_target="tpu_custom_call" | custom-call | flops 1000 | bytes 1000 | tf_op jit(solution)/shard_map/finish/pallas_call | solution.py:34
  (4 shorter events, 0.0 us)
Async XLA Ops:
  2.4 3.1 %collective-permute-start.5 = (bf16[144,512]{1,0:T(8,128)(2,1)S(1)}, bf16[144,512]{1,0:T(8,128)(2,1)S(1)}, u32[]{:S(2)}, u32[]{:S(2)}) collective-permute-start(bf16[144,512]{1,0:T(8,128)(2,1)S(1)} %get-tuple-element.35), channel_id=1, source_target_pairs={{2,0},{0,2},{6,4},{4,6},{10,8},{8,10},{14,12},{12,14},{18,16},{16,... | collective-permute-start | bytes 442376 | tf_op jit(solution)/shard_map/ppermute | solution.py:400
  2.9 5.3 %collective-permute-start = (bf16[64,512]{1,0:T(8,128)(2,1)S(1)}, bf16[64,512]{1,0:T(8,128)(2,1)S(1)}, u32[]{:S(2)}, u32[]{:S(2)}) collective-permute-start(bf16[64,512]{1,0:T(8,128)(2,1)S(1)} %get-tuple-element.33), channel_id=1, source_target_pairs={{0,1},{1,0},{2,3},{3,2},{4,5},{5,4},{6,7},{7,6},{8,9},{9,8},{10,11... | collective-permute-start | bytes 196616 | tf_op jit(solution)/shard_map/ppermute | solution.py:403
  5.6 5.5 %collective-permute-start.6 = (bf16[80,512]{1,0:T(8,128)(2,1)S(1)}, bf16[80,512]{1,0:T(8,128)(2,1)S(1)}, u32[]{:S(2)}, u32[]{:S(2)}) collective-permute-start(bf16[80,512]{1,0:T(8,128)(2,1)S(1)} %get-tuple-element.37), channel_id=1, source_target_pairs={{4,0},{6,2},{0,4},{2,6},{12,8},{14,10},{8,12},{10,14},{20,16},{22,... | collective-permute-start | bytes 245768 | tf_op jit(solution)/shard_map/ppermute | solution.py:400
  8.2 9.1 %collective-permute-start.1 = (bf16[128,512]{1,0:T(8,128)(2,1)S(1)}, bf16[128,512]{1,0:T(8,128)(2,1)S(1)}, u32[]{:S(2)}, u32[]{:S(2)}) collective-permute-start(bf16[128,512]{1,0:T(8,128)(2,1)S(1)} %join_rows.1.refs_2_), channel_id=1, source_target_pairs={{16,0},{18,2},{20,4},{22,6},{24,8},{26,10},{28,12},{30,14},{0,16},... | collective-permute-start | bytes 393224 | tf_op jit(solution)/shard_map/ppermute | solution.py:400
  11.2 7.7 %collective-permute-start.7 = (bf16[128,512]{1,0:T(8,128)(2,1)S(1)}, bf16[128,512]{1,0:T(8,128)(2,1)S(1)}, u32[]{:S(2)}, u32[]{:S(2)}) collective-permute-start(bf16[128,512]{1,0:T(8,128)(2,1)S(1)} %get-tuple-element.38), channel_id=1, source_target_pairs={{8,0},{10,2},{12,4},{14,6},{0,8},{2,10},{4,12},{6,14},{24,16},{26,... | collective-permute-start | bytes 393224 | tf_op jit(solution)/shard_map/ppermute | solution.py:400
  12.8 6.6 %collective-permute-start.9 = (bf16[80,512]{1,0:T(8,128)(2,1)S(1)}, bf16[80,512]{1,0:T(8,128)(2,1)S(1)}, u32[]{:S(2)}, u32[]{:S(2)}) collective-permute-start(bf16[80,512]{1,0:T(8,128)(2,1)S(1)} %get-tuple-element.42.refs_0_), channel_id=1, source_target_pairs={{8,0},{10,2},{12,4},{14,6},{0,8},{2,10},{4,12},{6,14},{24,16},{26,... | collective-permute-start | bytes 245768 | tf_op jit(solution)/shard_map/ppermute | solution.py:400
  13.3 8.2 %collective-permute-start.3 = (bf16[128,512]{1,0:T(8,128)(2,1)S(1)}, bf16[128,512]{1,0:T(8,128)(2,1)S(1)}, u32[]{:S(2)}, u32[]{:S(2)}) collective-permute-start(bf16[128,512]{1,0:T(8,128)(2,1)S(1)} %join_rows.1.refs_2_), channel_id=1, source_target_pairs={{2,0},{0,2},{6,4},{4,6},{10,8},{8,10},{14,12},{12,14},{18,16},{16,... | collective-permute-start | bytes 393224 | tf_op jit(solution)/shard_map/ppermute | solution.py:400
  17.3 5.0 %collective-permute-start.2 = (bf16[128,512]{1,0:T(8,128)(2,1)S(1)}, bf16[128,512]{1,0:T(8,128)(2,1)S(1)}, u32[]{:S(2)}, u32[]{:S(2)}) collective-permute-start(bf16[128,512]{1,0:T(8,128)(2,1)S(1)} %pass_on.2.refs_1_.refs_0_), channel_id=1, source_target_pairs={{4,0},{6,2},{0,4},{2,6},{12,8},{14,10},{8,12},{10,14},{20,16},{22,... | collective-permute-start | bytes 393224 | tf_op jit(solution)/shard_map/ppermute | solution.py:400
  18.9 3.4 %collective-permute-start.4 = (bf16[128,512]{1,0:T(8,128)(2,1)S(1)}, bf16[128,512]{1,0:T(8,128)(2,1)S(1)}, u32[]{:S(2)}, u32[]{:S(2)}) collective-permute-start(bf16[128,512]{1,0:T(8,128)(2,1)S(1)} %collective-permute-done.1.refs_1_.refs_4_.refs_2_.refs_0_), channel_id=1, source_target_pairs={{2,0},{0,2},{6,4},{4,6},{10,8},{8,10},{14,12},{12,14},{18,16},{16,... | collective-permute-start | bytes 393224 | tf_op jit(solution)/shard_map/ppermute | solution.py:400
  18.9 3.4 %collective-permute-start.8 = (bf16[128,512]{1,0:T(8,128)(2,1)S(1)}, bf16[128,512]{1,0:T(8,128)(2,1)S(1)}, u32[]{:S(2)}, u32[]{:S(2)}) collective-permute-start(bf16[128,512]{1,0:T(8,128)(2,1)S(1)} %collective-permute-done.7.refs_6_.refs_3_), channel_id=1, source_target_pairs={{2,0},{0,2},{6,4},{4,6},{10,8},{8,10},{14,12},{12,14},{18,16},{16,... | collective-permute-start | bytes 393224 | tf_op jit(solution)/shard_map/ppermute | solution.py:400
  19.5 7.1 %collective-permute-start.10 = (bf16[80,512]{1,0:T(8,128)(2,1)S(1)}, bf16[80,512]{1,0:T(8,128)(2,1)S(1)}, u32[]{:S(2)}, u32[]{:S(2)}) collective-permute-start(bf16[80,512]{1,0:T(8,128)(2,1)S(1)} %grow.1.refs_1_), channel_id=1, source_target_pairs={{16,0},{18,2},{20,4},{22,6},{24,8},{26,10},{28,12},{30,14},{0,16},... | collective-permute-start | bytes 245768 | tf_op jit(solution)/shard_map/ppermute | solution.py:400
  21.4 5.2 %collective-permute-start.13 = (bf16[128,512]{1,0:T(8,128)(2,1)S(1)}, bf16[128,512]{1,0:T(8,128)(2,1)S(1)}, u32[]{:S(2)}, u32[]{:S(2)}) collective-permute-start(bf16[128,512]{1,0:T(8,128)(2,1)S(1)} %shard_map.95), channel_id=1, source_target_pairs={{0,0},{2,2},{4,4},{6,6},{8,8},{10,10},{12,12},{14,14},{24,16},{26,... | collective-permute-start | bytes 393224 | tf_op jit(solution)/shard_map/ppermute | solution.py:400
  26.7 1.5 %collective-permute-start.14 = (bf16[128,512]{1,0:T(8,128)(2,1)S(1)}, bf16[128,512]{1,0:T(8,128)(2,1)S(1)}, u32[]{:S(2)}, u32[]{:S(2)}) collective-permute-start(bf16[128,512]{1,0:T(8,128)(2,1)S(1)} %pass_on.3.refs_1_), channel_id=1, source_target_pairs={{2,0},{0,2},{6,4},{4,6},{10,8},{8,10},{14,12},{12,14},{18,16},{16,... | collective-permute-start | bytes 393224 | tf_op jit(solution)/shard_map/ppermute | solution.py:400
  26.7 4.5 %collective-permute-start.11 = (bf16[64,512]{1,0:T(8,128)(2,1)S(1)}, bf16[64,512]{1,0:T(8,128)(2,1)S(1)}, u32[]{:S(2)}, u32[]{:S(2)}) collective-permute-start(bf16[64,512]{1,0:T(8,128)(2,1)S(1)} %get-tuple-element.44.refs_1_), channel_id=1, source_target_pairs={{4,0},{6,2},{0,4},{2,6},{12,8},{14,10},{8,12},{10,14},{20,16},{22,... | collective-permute-start | bytes 196616 | tf_op jit(solution)/shard_map/ppermute | solution.py:400
  28.8 6.0 %collective-permute-start.15 = (bf16[144,512]{1,0:T(8,128)(2,1)S(1)}, bf16[144,512]{1,0:T(8,128)(2,1)S(1)}, u32[]{:S(2)}, u32[]{:S(2)}) collective-permute-start(bf16[144,512]{1,0:T(8,128)(2,1)S(1)} %attend_far.1), channel_id=1, source_target_pairs={{4,0},{6,2},{0,4},{2,6},{12,8},{14,10},{8,12},{10,14},{20,16},{22,... | collective-permute-start | bytes 442376 | tf_op jit(solution)/shard_map/ppermute | solution.py:400
  31.4 1.4 %collective-permute-start.12 = (bf16[128,512]{1,0:T(8,128)(2,1)S(1)}, bf16[128,512]{1,0:T(8,128)(2,1)S(1)}, u32[]{:S(2)}, u32[]{:S(2)}) collective-permute-start(bf16[128,512]{1,0:T(8,128)(2,1)S(1)} %get-tuple-element.46), channel_id=1, source_target_pairs={{2,0},{0,2},{6,4},{4,6},{10,8},{8,10},{14,12},{12,14},{18,16},{16,... | collective-permute-start | bytes 393224 | tf_op jit(solution)/shard_map/ppermute | solution.py:400
